TPU v7x, 32 devices: a whole 2x2x4 slice. The times are simulated.
32 devices in a mesh: row: 4 (over z), col: 8 (over y, x, core).
Axes of the slice: x: 2, y: 2, z: 4, core: 2. Of those that a mesh axis runs over, the one named last changes fastest.
Arguments:
- image_feats: bfloat16 [18432, 6144], P(('row', 'col')), may hold values from -6 to 6
- text_feats: bfloat16 [18432, 4096], P(('row', 'col')), may hold values from -6 to 6
- probe_image: bfloat16 [6144, 128], P('row'), may hold values from -0.078125 to 0.078125
- probe_text: bfloat16 [4096, 128], P('col'), may hold values from -0.09375 to 0.09375
Outputs:
- image_basis: float32 [6144, 128], P('row')
- text_basis: float32 [4096, 128], P('col')
All inputs are finite; a program needn't handle non-finite values.
Results may differ from a plain program's by a relative error of at most 0.0031.
Values may be sent and summed in bfloat16 or wider, within the bound.
No kernel may reach another device: no remote copies, remote signals or barrier semaphores. Data moves between devices by JAX's collectives and lax.ppermute only.
A program may use at most 64 MiB of HBM per device.

v0:
```python
import math

import jax
import jax.numpy as jnp
from jax import lax
from jax.sharding import PartitionSpec as P


def finish(panel, gram, width):
    factor = jnp.linalg.cholesky(gram)
    basis = lax.linalg.triangular_solve(
        factor, panel, left_side=False, lower=True, transpose_a=True
    )
    return basis * math.sqrt(width)


def local_gram(panel):
    return jnp.dot(
        panel.T, panel, precision=lax.Precision.HIGHEST, preferred_element_type=jnp.float32
    )


def per_device(image_feats, text_feats, probe_image, probe_text):
    image_width = image_feats.shape[1]
    text_width = text_feats.shape[1]
    columns = text_feats
    sketch_text = jnp.dot(
        columns,
        lax.all_gather(probe_text, "col", axis=0, tiled=True),
        preferred_element_type=jnp.float32,
    ).astype(jnp.bfloat16)
    columns = image_feats
    sketch_image = jnp.dot(
        columns,
        lax.all_gather(probe_image, "row", axis=0, tiled=True),
        preferred_element_type=jnp.float32,
    ).astype(jnp.bfloat16)
    dims = (((0,), (0,)), ((), ()))
    columns = image_feats
    partial_panel = lax.psum_scatter(
        lax.dot_general(columns, sketch_text, dims, preferred_element_type=jnp.float32),
        "row",
        scatter_dimension=0,
        tiled=True,
    )
    image_panel = lax.psum(partial_panel, "col")
    columns = text_feats
    partial_text = lax.psum_scatter(
        lax.dot_general(columns, sketch_image, dims, preferred_element_type=jnp.float32),
        "col",
        scatter_dimension=0,
        tiled=True,
    )
    text_panel = lax.psum(partial_text, "row")
    image_local = local_gram(image_panel)
    text_local = local_gram(text_panel)
    image_gram = lax.psum(image_local, "row")
    text_gram = lax.psum(text_local, "col")
    return (finish(image_panel, image_gram, image_width), finish(text_panel, text_gram, text_width))


def solution(mesh):
    in_specs = (P(("row", "col"), None), P(("row", "col"), None), P("row", None), P("col", None))
    out_specs = (P("row", None), P("col", None))
    return jax.shard_map(
        per_device, mesh=mesh, in_specs=in_specs, out_specs=out_specs, check_vma=False
    )
```

profile of v0, /device:TPU:0, one launch (start us, length us, event | category | flops | bytes accessed | tf_op | source)
XLA Modules:
  0.0 356.9 jit_solution(9680591499118282490)
XLA Ops:
  7.2 0.7 all-gather.5.cloned.1.call-update
  7.9 0.0 reduce-scatter.5.cloned.1.call-start
  7.9 41.4 %all-gather.5.cloned.1.call-done = bf16[6144,128]{1,0:T(8,128)(2,1)} async-done(((bf16[1536,128]{1,0:T(8,128)(2,1)}), bf16[6144,128]{1,0:T(8,128)(2,1)}) %all-gather.5.cloned.1.call-update) | async-done | bytes 1572880 | tf_op jit(solution)/shard_map/all_gather | solution.py:35
  49.4 10.7 %convolution_bitcast_fusion.1 = f32[4096,128]{0,1:T(8,128)} fusion(bf16[576,4096]{1,0:T(8,128)(2,1)} %param.6, bf16[576,6144]{1,0:T(8,128)(2,1)} %param.5, bf16[6144,128]{1,0:T(8,128)(2,1)} %all-gather.5.cloned.1.call-done), kind=kOutput, calls=%fused_computation.1 | convolution fusion | flops 1510023168 | bytes 15466496 | tf_op jit(solution)/shard_map/dot_general | solution.py:49
  60.1 0.0 all-gather.3.cloned.1.call-start
  60.1 0.7 all-gather.3.cloned.1.call-update
  60.9 39.4 %reduce-scatter.5.cloned.1.call-done = f32[512,128]{0,1:T(8,128)} async-done(((f32[4096,128]{0,1:T(8,128)}), f32[512,128]{0,1:T(8,128)}) %reduce-scatter.5.cloned.1.call-update) | async-done | bytes 262160 | tf_op jit(solution)/shard_map/reduce_scatter | solution.py:48
  100.3 0.0 reduce-scatter.3.cloned.1.call-start
  100.4 25.5 %all-gather.3.cloned.1.call-done = bf16[4096,128]{1,0:T(8,128)(2,1)} async-done(((bf16[512,128]{1,0:T(8,128)(2,1)}), bf16[4096,128]{1,0:T(8,128)(2,1)}) %all-gather.3.cloned.1.call-update) | async-done | bytes 1048592 | tf_op jit(solution)/shard_map/all_gather | solution.py:29
  125.9 11.5 %convolution_bitcast_fusion = f32[6144,128]{0,1:T(8,128)} fusion(bf16[576,6144]{1,0:T(8,128)(2,1)} %param.5, bf16[576,4096]{1,0:T(8,128)(2,1)} %param.6, bf16[4096,128]{1,0:T(8,128)(2,1)} %all-gather.3.cloned.1.call-done), kind=kOutput, calls=%fused_computation | convolution fusion | flops 1510023168 | bytes 15990784 | tf_op jit(solution)/shard_map/dot_general | solution.py:41
  137.4 0.0 all-reduce.9.cloned.1.call-start
  137.5 26.1 %all-reduce.7.cloned.1.call-done = f32[512,128]{0,1:T(8,128)} async-done(((f32[512,128]{0,1:T(8,128)}), f32[512,128]{0,1:T(8,128)}) %all-reduce.7.cloned.1.call-update) | async-done | bytes 262160 | tf_op jit(solution)/shard_map/psum | solution.py:54
  163.5 2.0 fusion.7
  165.6 60.1 %reduce-scatter.3.cloned.1.call-done = f32[1536,128]{0,1:T(8,128)} async-done(((f32[6144,128]{0,1:T(8,128)}), f32[1536,128]{0,1:T(8,128)}) %reduce-scatter.3.cloned.1.call-update) | async-done | bytes 786448 | tf_op jit(solution)/shard_map/reduce_scatter | solution.py:40
  225.7 0.2 all-reduce.5.cloned.1.call-start
  226.0 59.4 %all-reduce.9.cloned.1.call-done = (f32[1536,128]{0,1:T(8,128)}, f32[128,128]{0,1:T(8,128)}) async-done(((f32[1536,128]{0,1:T(8,128)}, f32[128,128]{0,1:T(8,128)}), (f32[1536,128]{0,1:T(8,128)}, f32[128,128]{0,1:T(8,128)})) %all-reduce.9.cloned.1.call-update) | async-done | bytes 851984 | tf_op jit(solution)/shard_map/psum | solution.py:46
  285.3 2.8 fusion.6
  288.2 0.9 copy.9
  289.1 0.9 fusion.3
  290.0 11.7 %cholesky.55 = f32[128,128]{1,0:T(8,128)S(1)} custom-call(f32[128,128]{1,0:T(8,128)S(1)} %fusion.3), custom_call_target="Cholesky" | custom-call | tf_op jit(solution)/shard_map/jit(cholesky)/cholesky | solution.py:10
  301.7 0.6 compare_reduce_fusion
  302.3 0.7 fusion.1
  303.0 9.8 %custom-call.9 = f32[1,128,128]{1,2,0:T(8,128)S(1)} custom-call(f32[1,128,128]{2,1,0:T(8,128)S(1)} %fusion.1), custom_call_target="InvertDiagBlocksLowerTriangular" | custom-call | tf_op jit(solution)/shard_map/triangular_solve | solution.py:11
  312.8 2.2 convolution_multiply_fusion.1
  315.1 6.7 %all-reduce.5.cloned.1.call-done = f32[128,128]{0,1:T(8,128)} async-done(((f32[128,128]{0,1:T(8,128)}), f32[128,128]{0,1:T(8,128)}) %all-reduce.5.cloned.1.call-update) | async-done | bytes 65552 | tf_op jit(solution)/shard_map/psum | solution.py:57
  321.8 0.9 copy.7
  322.7 0.9 fusion.5
  323.6 11.7 %cholesky.44 = f32[128,128]{1,0:T(8,128)S(1)} custom-call(f32[128,128]{1,0:T(8,128)S(1)} %fusion.5), custom_call_target="Cholesky" | custom-call | tf_op jit(solution)/shard_map/jit(cholesky)/cholesky | solution.py:10
  335.3 0.6 compare_reduce_fusion.1
  335.9 0.7 fusion
  336.6 10.0 %custom-call.8 = f32[1,128,128]{1,2,0:T(8,128)S(1)} custom-call(f32[1,128,128]{2,1,0:T(8,128)S(1)} %fusion), custom_call_target="InvertDiagBlocksLowerTriangular" | custom-call | tf_op jit(solution)/shard_map/triangular_solve | solution.py:11
  346.6 3.4 convolution_multiply_fusion
  (9 shorter events, 0.2 us)
Async XLA Ops:
  7.2 42.2 %all-gather.5.cloned.1.call-start = ((), (), s32[]{:S(2)}) async-start(), calls=%async_computation.5 | async-start | bytes 1966080 | tf_op jit(solution)/shard_map/all_gather | solution.py:35
  7.9 92.4 %reduce-scatter.5.cloned.1.call-start = ((), (), s32[]{:S(2)}) async-start(), calls=%async_computation.6 | async-start | bytes 2359296 | tf_op jit(solution)/shard_map/reduce_scatter | solution.py:48
  60.1 65.8 %all-gather.3.cloned.1.call-start = ((), (), s32[]{:S(2)}) async-start(), calls=%async_computation.2 | async-start | bytes 1179648 | tf_op jit(solution)/shard_map/all_gather | solution.py:29
  60.8 102.7 %all-reduce.7.cloned.1.call-start = ((), (), s32[]{:S(2)}) async-start(), calls=%async_computation.7 | async-start | bytes 524288 | tf_op jit(solution)/shard_map/psum | solution.py:54
  100.3 125.4 %reduce-scatter.3.cloned.1.call-start = ((), (), s32[]{:S(2)}) async-start(), calls=%async_computation.3 | async-start | bytes 3932160 | tf_op jit(solution)/shard_map/reduce_scatter | solution.py:40
  137.4 147.9 %all-reduce.9.cloned.1.call-start = ((), (), s32[]{:S(2)}) async-start(), calls=%async_computation.8 | async-start | bytes 1703936 | tf_op jit(solution)/shard_map/psum | solution.py:46
  225.7 96.0 %all-reduce.5.cloned.1.call-start = ((), (), s32[]{:S(2)}) async-start(), calls=%async_computation.4 | async-start | bytes 131072 | tf_op jit(solution)/shard_map/psum | solution.py:57
Sparse Core Ops, SparseCore 0:
  9.6 39.7 all-gather.4
  60.2 40.0 reduce-scatter.4
  102.4 23.4 all-gather.2
  128.2 35.2 all-reduce.6
  165.7 59.9 reduce-scatter.2
  229.4 55.9 all-reduce.8
  288.3 33.4 all-reduce.4
where the time goes:
time: 357 us
  waiting for transfers between devices  260 us (73%)
  other arithmetic  47.6 us (13%)
  matrix products  32.7 us (9%)
  between operations  14.2 us (4%)
    reduce_scatter x1, waiting for transfers between devices, per_device(): lax.psum_scatter(lax.dot_general(columns, sketch_text, dims, preferred_el...  60.1 us
    psum x1, waiting for transfers between devices, per_device(): image_panel = lax.psum(partial_panel, 'col')  59.4 us
    all_gather x1, waiting for transfers between devices, per_device(): lax.all_gather(probe_image, 'row', axis=0, tiled=True)  41.4 us
    reduce_scatter x1, waiting for transfers between devices, per_device(): lax.psum_scatter(lax.dot_general(columns, sketch_image, dims, preferred_e...  39.4 us
    psum x1, waiting for transfers between devices, per_device(): text_panel = lax.psum(partial_text, 'row')  26.1 us
    all_gather x1, waiting for transfers between devices, per_device(): lax.all_gather(probe_text, 'col', axis=0, tiled=True)  25.5 us
    another operation x6, other arithmetic, finish(): factor = jnp.linalg.cholesky(gram)  24.8 us
    another operation x4, other arithmetic, finish(): lax.linalg.triangular_solve(factor, panel, left_side=False, lower=True, t...  21.1 us
  transfers between devices with their start and end apart: 7, of which 7 were waited for; matrix products, arithmetic and copies ran while one was open for 11% of the time, Pallas kernels for 0%

commit v1 on v0

v1 whole, which is shorter than its diff:
```python
import functools
import math

import jax
import jax.numpy as jnp
from jax import lax
from jax.experimental import pallas as pl
from jax.experimental.pallas import tpu as pltpu
from jax.sharding import PartitionSpec as P

F32 = jnp.float32
BF16 = jnp.bfloat16
VMEM = pl.BlockSpec(memory_space=pltpu.VMEM)
SMEM = pl.BlockSpec(memory_space=pltpu.SMEM)
LIMIT = 48 * 1024 * 1024


def sds(shape, dtype):
    return jax.ShapeDtypeStruct(shape, dtype)


def params(**kw):
    return pltpu.CompilerParams(vmem_limit_bytes=LIMIT, **kw)


def cost(flops, nbytes):
    return pl.CostEstimate(flops=int(flops), bytes_accessed=int(nbytes), transcendentals=0)


def swap(x, axis, n, s):
    return lax.ppermute(x, axis, [(i, i ^ s) for i in range(n)])


def panel_kernel(n_in, me_ref, probe_ref, a_ref, b_ref, keep_ref, send_ref, acc, sketch, tile):
    step = pl.program_id(0)
    depth = a_ref.shape[1]

    @pl.when(step < n_in)
    def _():
        rows = pl.ds(pl.multiple_of(step * depth, depth), depth)
        part = jnp.dot(a_ref[...], probe_ref[rows, :], preferred_element_type=F32)

        @pl.when(step == 0)
        def _():
            acc[...] = part

        @pl.when(step > 0)
        def _():
            acc[...] += part

    @pl.when(step == n_in - 1)
    def _():
        sketch[...] = acc[...].T.astype(BF16)

    @pl.when(step >= n_in)
    def _():
        core = me_ref[0] % 2
        _, groups, rows, _ = keep_ref.shape
        out = jnp.dot(sketch[...], b_ref[...], preferred_element_type=F32)
        tile[...] = out.T.reshape(tile.shape)
        for g in range(groups):
            keep_ref[0, g] = tile[2 * g + core]
            send_ref[0, g] = tile[2 * g + 1 - core]


def panel_call(me, probe, a, b, n_in, n_out, groups):
    pairs, width_a = a.shape
    width_b = b.shape[1]
    rank = probe.shape[1]
    depth = width_a // n_in
    cols = width_b // n_out
    rows = cols // groups // 2
    out = sds((n_out, groups, rows, rank), F32)
    spec = pl.BlockSpec((1, groups, rows, rank), lambda i: (jnp.maximum(i - n_in, 0), 0, 0, 0))
    return pl.pallas_call(
        functools.partial(panel_kernel, n_in),
        grid=(n_in + n_out,),
        in_specs=[
            SMEM,
            VMEM,
            pl.BlockSpec((pairs, depth), lambda i: (0, jnp.minimum(i, n_in - 1))),
            pl.BlockSpec((pairs, cols), lambda i: (0, jnp.maximum(i - n_in, 0))),
        ],
        out_specs=[spec, spec],
        out_shape=[out, out],
        scratch_shapes=[
            pltpu.VMEM((pairs, rank), F32),
            pltpu.VMEM((rank, pairs), BF16),
            pltpu.VMEM((2 * groups, rows, rank), F32),
        ],
        compiler_params=params(),
        cost_estimate=cost(2 * pairs * rank * (width_a + width_b), 2 * pairs * (width_a + width_b)),
        name="panel",
    )(me, probe, a, b)


def place_kernel(order, me_ref, *refs):
    *parts, out_ref = refs
    for part, spot in zip(parts, order):
        for i, (r, c) in enumerate(spot):
            row, col = me_ref[1] ^ r, me_ref[0] ^ c
            out_ref[row, col] = part[i]


def plane_kernel(axis, shifts, me_ref, keep_ref, recv_ref, own_ref, *send_refs):
    spot = me_ref[0] // 2

    def total(i):
        if axis == 1:
            return keep_ref[:, i] + recv_ref[:, i]
        return keep_ref[i] + recv_ref[i]

    own_ref[...] = total(spot)
    for s, ref in zip(shifts, send_refs):
        ref[...] = total(spot ^ (s // 2)).astype(BF16)


def plane_call(axis, shifts, me, keep, recv):
    shape = list(keep.shape)
    del shape[axis]
    return pl.pallas_call(
        functools.partial(plane_kernel, axis, shifts),
        in_specs=[SMEM, VMEM, VMEM],
        out_specs=[VMEM] * (1 + len(shifts)),
        out_shape=[sds(shape, F32)] + [sds(shape, BF16)] * len(shifts),
        compiler_params=params(),
        cost_estimate=cost(keep.size, 3 * 4 * keep.size),
        name="plane",
    )(me, keep, recv)


def depth_kernel(shifts, n, me_ref, own_ref, *refs):
    recv, (keep_ref, *send) = refs[:n], refs[n:]

    def total(r):
        value = own_ref[r]
        for ref in recv:
            value = value + ref[r].astype(F32)
        return value

    keep_ref[...] = total(me_ref[1])
    for s, ref in zip(shifts, send):
        ref[...] = total(me_ref[1] ^ s).astype(BF16)


def depth_call(shifts, me, own, recv):
    shape = own.shape[1:]
    return pl.pallas_call(
        functools.partial(depth_kernel, shifts, len(recv)),
        in_specs=[SMEM] + [VMEM] * (1 + len(recv)),
        out_specs=[VMEM] * (1 + len(shifts)),
        out_shape=[sds(shape, F32)] + [sds(shape, BF16)] * len(shifts),
        compiler_params=params(),
        cost_estimate=cost(own.size, 12 * own.size),
        name="depth",
    )(me, own, *recv)


def last_kernel(own_ref, *refs):
    *recv, out_ref = refs
    value = own_ref[...]
    for ref in recv:
        value = value + ref[...].astype(F32)
    out_ref[...] = value.astype(BF16)


def last_call(own, recv):
    return pl.pallas_call(
        last_kernel,
        in_specs=[VMEM] * (1 + len(recv)),
        out_specs=VMEM,
        out_shape=sds(own.shape, BF16),
        compiler_params=params(),
        cost_estimate=cost(own.size, 12 * own.size),
        name="last",
    )(own, *recv)


def gram_kernel(which, n, me_ref, *refs):
    parts, (panel_ref, gram_ref) = refs[:n], refs[n:]
    me = me_ref[which]
    for s, part in enumerate(parts):
        panel_ref[me ^ s] = part[...]
    rank = gram_ref.shape[0]
    panel = panel_ref[...].reshape(-1, rank)
    gram_ref[...] = lax.dot_general(
        panel, panel, (((0,), (0,)), ((), ())), preferred_element_type=F32
    )


def gram_call(which, me, parts):
    n = len(parts)
    rows, rank = parts[0].shape
    return pl.pallas_call(
        functools.partial(gram_kernel, which, n),
        in_specs=[SMEM] + [VMEM] * n,
        out_specs=[VMEM, VMEM],
        out_shape=[sds((n, rows, rank), BF16), sds((rank, rank), F32)],
        compiler_params=params(),
        cost_estimate=cost(2 * n * rows * rank * rank, 4 * n * rows * rank),
        name="gram",
    )(me, *parts)


def inverse_factor(gram):
    n = gram.shape[0]
    lane = lax.broadcasted_iota(jnp.int32, (8, n), 1)
    sub = lax.broadcasted_iota(jnp.int32, (8, n), 0)
    rows = [gram[8 * i : 8 * i + 8, :] for i in range(n // 8)]
    for b in range(n // 8):
        cols = [
            [jnp.broadcast_to(rows[i][:, 8 * b + j : 8 * b + j + 1], (8, n)) for i in range(b, n // 8)]
            for j in range(8)
        ]
        scale = jnp.ones((8, n), F32)
        for j in range(8):
            k = 8 * b + j
            pivot = jnp.broadcast_to(cols[j][0][j : j + 1, :], (8, n))
            inv = 1.0 / pivot
            scale = jnp.where(sub == j, pivot, scale)
            pivot_row = jnp.where(lane == k, 1.0, jnp.broadcast_to(rows[b][j : j + 1, :], (8, n)))
            below = sub > j
            mult = [c * inv for c in cols[j]]
            mult[0] = jnp.where(below, mult[0], 0.0)
            for jj in range(j + 1, 8):
                entry = jnp.broadcast_to(cols[jj][0][j : j + 1, :], (8, n))
                cols[jj] = [c - m * entry for c, m in zip(cols[jj], mult)]
            for i in range(b, n // 8):
                here = lane == k
                if i == b:
                    here = jnp.logical_and(here, below)
                rows[i] = jnp.where(here, 0.0, rows[i]) - mult[i - b] * pivot_row
        unit = jnp.where(lane == sub + 8 * b, 1.0, jnp.where(lane < sub + 8 * b, rows[b], 0.0))
        rows[b] = unit * lax.rsqrt(scale)
    return jnp.concatenate(rows, axis=0)


def finish_kernel(width, panel_ref, own_ref, *refs):
    *recv, out_ref = refs
    gram = own_ref[...]
    for ref in recv:
        gram = gram + ref[...]
    inverse = inverse_factor(gram) * math.sqrt(width)
    high = inverse.astype(BF16)
    low = (inverse - high.astype(F32)).astype(BF16)
    dims = (((1,), (1,)), ((), ()))
    panel = panel_ref[...].reshape(out_ref.shape)
    out_ref[...] = lax.dot_general(panel, high, dims, preferred_element_type=F32) + lax.dot_general(
        panel, low, dims, preferred_element_type=F32
    )


def finish_call(width, panel, own, recv):
    n, rows, rank = panel.shape
    return pl.pallas_call(
        functools.partial(finish_kernel, width),
        in_specs=[VMEM] * (2 + len(recv)),
        out_specs=VMEM,
        out_shape=sds((n * rows, rank), F32),
        compiler_params=params(),
        cost_estimate=cost(10**10, 6 * n * rows * rank),
        name="finish",
    )(panel, own, *recv)


def per_device(n_row, n_col, image_feats, text_feats, probe_image, probe_text):
    col_swap = lambda x, s: swap(x, "col", n_col, s)
    row_swap = lambda x, s: swap(x, "row", n_row, s)
    me = jnp.stack([lax.axis_index("col"), lax.axis_index("row")]).astype(jnp.int32)
    chips = list(range(2, n_col, 2))
    depths = list(range(1, n_row))
    rank = probe_text.shape[1]
    groups = n_col // 2

    parts = {0: probe_text}
    for s in chips:
        parts[s] = col_swap(probe_text, s)
    for s in list(parts):
        parts[s ^ 1] = col_swap(parts[s], 1)
    order = sorted(parts)
    text_whole = pl.pallas_call(
        functools.partial(place_kernel, [[(0, s)] for s in order]),
        in_specs=[SMEM] + [VMEM] * n_col,
        out_specs=VMEM,
        out_shape=sds((1, n_col) + probe_text.shape, BF16),
        compiler_params=params(),
        name="place_text",
    )(me * jnp.array([1, 0], jnp.int32), *[parts[s][None] for s in order]).reshape(-1, rank)

    depth_rows, _ = probe_image.shape
    piece = depth_rows // n_col
    if piece % 16 == 0:
        mine = lax.dynamic_slice_in_dim(probe_image, me[0] * piece, piece, 0)
        got = jnp.stack([row_swap(mine, t) for t in depths])
        sets = {0: got}
        for s in chips:
            sets[s] = col_swap(got, s)
        for s in list(sets):
            sets[s ^ 1] = col_swap(sets[s], 1)
        order = sorted(sets)
        spots = [[(0, c) for c in range(n_col)]] + [[(t, s) for t in depths] for s in order]

        def image_place(me_ref, own_ref, *refs):
            *parts, out_ref = refs
            for c in range(n_col):
                out_ref[me_ref[1], c] = own_ref[c]
            for part, s in zip(parts, order):
                for i, t in enumerate(depths):
                    out_ref[me_ref[1] ^ t, me_ref[0] ^ s] = part[i]

        image_whole = pl.pallas_call(
            image_place,
            in_specs=[SMEM] + [VMEM] * (1 + n_col),
            out_specs=VMEM,
            out_shape=sds((n_row, n_col, piece, rank), BF16),
            compiler_params=params(),
            name="place_image",
        )(me, probe_image.reshape(n_col, piece, rank), *[sets[s] for s in order]).reshape(-1, rank)
    else:
        image_whole = lax.all_gather(probe_image, "row", axis=0, tiled=True)

    n_text = max(1, text_feats.shape[1] // 1024)
    n_image = max(1, image_feats.shape[1] // 1536)
    keep, send = panel_call(me, text_whole, text_feats, image_feats, n_text, n_row, groups)
    recv = col_swap(send, 1)
    own, *sends = plane_call(1, chips, me, keep, recv)
    recv = [col_swap(x, s) for x, s in zip(sends, chips)]
    own, *sends = depth_call(depths, me, own, recv)
    recv = [row_swap(x, s) for x, s in zip(sends, depths)]
    mine = last_call(own, recv)
    image_parts = [mine] + [col_swap(mine, s) for s in range(1, n_col)]
    image_panel, image_local = gram_call(0, me, image_parts)
    image_grams = [row_swap(image_local, s) for s in depths]
    image_basis = finish_call(image_feats.shape[1], image_panel, image_local, image_grams)

    keep, send = panel_call(me, image_whole, image_feats, text_feats, n_image, groups, 1)
    split = (groups, n_row, keep.shape[2] // n_row, rank)
    keep, send = keep.reshape(split), send.reshape(split)
    recv = col_swap(send, 1)
    own, *sends = plane_call(0, chips, me, keep, recv)
    recv = [col_swap(x, s) for x, s in zip(sends, chips)]
    own, *sends = depth_call(depths, me, own, recv)
    recv = [row_swap(x, s) for x, s in zip(sends, depths)]
    mine = last_call(own, recv)
    text_parts = [mine] + [row_swap(mine, s) for s in depths]
    text_panel, text_local = gram_call(1, me, text_parts)
    text_grams = [col_swap(text_local, s) for s in range(1, n_col)]
    text_basis = finish_call(text_feats.shape[1], text_panel, text_local, text_grams)
    return image_basis, text_basis


def solution(mesh):
    in_specs = (P(("row", "col"), None), P(("row", "col"), None), P("row", None), P("col", None))
    out_specs = (P("row", None), P("col", None))
    body = functools.partial(per_device, mesh.shape["row"], mesh.shape["col"])
    return jax.shard_map(body, mesh=mesh, in_specs=in_specs, out_specs=out_specs, check_vma=False)
```

time: 357 us -> 114 us (0.32)
  waiting for transfers between devices: 260 us -> 22.3 us
  starting transfers between devices: 0.46 us -> 53.2 us
  other arithmetic: 47.6 us -> 0.75 us
  Pallas kernels: 0 us -> 34.8 us
  matrix products: 32.7 us -> 0 us
  between operations: 14.2 us -> 0.86 us
    reduce_scatter x2 -> x0, waiting for transfers between devices: 99.6 us -> none  [the longest x1 60.1 us: per_device(): lax.psum_scatter(lax.dot_general(columns, sketch_text, dims, preferred_el...]
    psum x3 -> x0, waiting for transfers between devices: 92.1 us -> none  [the longest x1 59.4 us: per_device(): image_panel = lax.psum(partial_panel, 'col')]
    all_gather x2 -> x0, waiting for transfers between devices: 67 us -> none  [the longest x1 41.4 us: per_device(): lax.all_gather(probe_image, 'row', axis=0, tiled=True)]
    ppermute x0 -> x51, starting transfers between devices: none -> 53.2 us  [swap(): return lax.ppermute(x, axis, [(i, i ^ s) for i in range(n)])]
    another operation x10 -> x1, other arithmetic: 45.9 us -> 0.02 us  [per_device(): got = jnp.stack([row_swap(mine, t) for t in depths])]
    pallas_call x0 -> x14, Pallas kernels: none -> 34.8 us  [the longest x2 19 us: panel_call(): pl.pallas_call(functools.partial(panel_kernel, n_in), grid=(n_in + n_out,...]
    dot_general x4 -> x0, matrix products: 27 us -> none  [the longest x1 11.5 us: per_device(): lax.dot_general(columns, sketch_text, dims, preferred_element_type=jnp.fl...]
    ppermute x0 -> x51, waiting for transfers between devices: none -> 22.3 us  [swap(): return lax.ppermute(x, axis, [(i, i ^ s) for i in range(n)])]
  transfers between devices with their start and end apart: 7 -> 51, of which waited for: 7 -> 13; matrix products, arithmetic and copies ran while one was open for 11% -> 1% of each run, Pallas kernels for 0% -> 26%
where the time goes in v1:
time: 114 us
  starting transfers between devices  53.2 us (47%)
  Pallas kernels  34.8 us (31%)
  waiting for transfers between devices  22.3 us (20%)
  local copies, waits for them, and re-layouts  1.71 us (2%)
    ppermute x51, starting transfers between devices, swap(): return lax.ppermute(x, axis, [(i, i ^ s) for i in range(n)])  53.2 us
    ppermute x51, waiting for transfers between devices, swap(): return lax.ppermute(x, axis, [(i, i ^ s) for i in range(n)])  22.3 us
    pallas_call x2, Pallas kernels, panel_call(): pl.pallas_call(functools.partial(panel_kernel, n_in), grid=(n_in + n_out,...  19 us
    pallas_call x2, Pallas kernels, finish_call(): pl.pallas_call(functools.partial(finish_kernel, width), in_specs=[VMEM] *...  10.3 us
  transfers between devices with their start and end apart: 51, of which 13 were waited for; matrix products, arithmetic and copies ran while one was open for 1% of the time, Pallas kernels for 26%

profile of v1, /device:TPU:0, one launch (start us, length us, event | category | flops | bytes accessed | tf_op | source)
XLA Modules:
  0.0 113.6 jit_solution(3118581171501399178)
XLA Ops:
  0.6 3.0 %collective-permute-start.1 = (bf16[512,128]{1,0:T(8,128)(2,1)}, bf16[512,128]{1,0:T(8,128)(2,1)S(1)}, u32[]{:S(2)}, u32[]{:S(2)}) collective-permute-start(bf16[512,128]{1,0:T(8,128)(2,1)} %param.8), channel_id=1, source_target_pairs={{0,2},{1,3},{2,0},{3,1},{4,6},{5,7},{6,4},{7,5},{8,10},{9,11},{10,... | collective-permute-start | bytes 393224 | tf_op jit(solution)/shard_map/ppermute | solution.py:31
  3.6 1.5 %collective-permute-start.3 = (bf16[512,128]{1,0:T(8,128)(2,1)}, bf16[512,128]{1,0:T(8,128)(2,1)S(1)}, u32[]{:S(2)}, u32[]{:S(2)}) collective-permute-start(bf16[512,128]{1,0:T(8,128)(2,1)} %param.8), channel_id=1, source_target_pairs={{0,4},{1,5},{2,6},{3,7},{4,0},{5,1},{6,2},{7,3},{8,12},{9,13},{10,... | collective-permute-start | bytes 393224 | tf_op jit(solution)/shard_map/ppermute | solution.py:31
  6.0 4.1 %collective-permute-start.26 = (bf16[192,128]{1,0:T(8,128)(2,1)S(1)}, bf16[192,128]{1,0:T(8,128)(2,1)S(1)}, u32[]{:S(2)}, u32[]{:S(2)}) collective-permute-start(bf16[192,128]{1,0:T(8,128)(2,1)S(1)} %constant_dynamic-slice_fusion), channel_id=1, source_target_pairs={{0,24},{8,16},{16,8},{24,0},{1,25},{9,17},{17,9},{25,1},{2,26},{10... | collective-permute-start | bytes 147464 | tf_op jit(solution)/shard_map/ppermute | solution.py:31
  10.0 2.3 %collective-permute-done.26 = bf16[192,128]{1,0:T(8,128)(2,1)S(1)} collective-permute-done((bf16[192,128]{1,0:T(8,128)(2,1)S(1)}, bf16[192,128]{1,0:T(8,128)(2,1)S(1)}, u32[]{:S(2)}, u32[]{:S(2)}) %collective-permute-start.26) | collective-permute-done | bytes 49184 | tf_op jit(solution)/shard_map/ppermute | solution.py:31
  12.4 2.6 %collective-permute-done.25 = bf16[192,128]{1,0:T(8,128)(2,1)S(1)} collective-permute-done((bf16[192,128]{1,0:T(8,128)(2,1)S(1)}, bf16[192,128]{1,0:T(8,128)(2,1)S(1)}, u32[]{:S(2)}, u32[]{:S(2)}) %collective-permute-start.25) | collective-permute-done | bytes 49184 | tf_op jit(solution)/shard_map/ppermute | solution.py:31
  16.4 2.8 %collective-permute-done.24 = bf16[192,128]{1,0:T(8,128)(2,1)S(1)} collective-permute-done((bf16[192,128]{1,0:T(8,128)(2,1)S(1)}, bf16[192,128]{1,0:T(8,128)(2,1)S(1)}, u32[]{:S(2)}, u32[]{:S(2)}) %collective-permute-start.24) | collective-permute-done | bytes 49184 | tf_op jit(solution)/shard_map/ppermute | solution.py:31
  19.1 1.6 %collective-permute-start.28 = (bf16[3,192,128]{2,1,0:T(8,128)(2,1)S(1)}, bf16[3,192,128]{2,1,0:T(8,128)(2,1)S(1)}, u32[]{:S(2)}, u32[]{:S(2)}) collective-permute-start(bf16[3,192,128]{2,1,0:T(8,128)(2,1)S(1)} %pad_maximum_fusion.refs_0_), channel_id=1, source_target_pairs={{0,2},{1,3},{2,0},{3,1},{4,6},{5,7},{6,4},{7,5},{8,10},{9,11},{10,... | collective-permute-start | bytes 442376 | tf_op jit(solution)/shard_map/ppermute | solution.py:31
  20.7 1.5 %collective-permute-start.30 = (bf16[3,192,128]{2,1,0:T(8,128)(2,1)S(1)}, bf16[3,192,128]{2,1,0:T(8,128)(2,1)S(1)}, u32[]{:S(2)}, u32[]{:S(2)}) collective-permute-start(bf16[3,192,128]{2,1,0:T(8,128)(2,1)S(1)} %pad_maximum_fusion.refs_0_), channel_id=1, source_target_pairs={{0,4},{1,5},{2,6},{3,7},{4,0},{5,1},{6,2},{7,3},{8,12},{9,13},{10,... | collective-permute-start | bytes 442376 | tf_op jit(solution)/shard_map/ppermute | solution.py:31
  24.2 9.4 %panel.2 = (f32[4,4,192,128]{3,2,1,0:T(8,128)S(1)}, f32[4,4,192,128]{3,2,1,0:T(8,128)S(1)}) custom-call(s32[2]{0:T(128)S(1)} %get-tuple-element.51.me_ref, bf16[4096,128]{1,0:T(8,128)(2,1)S(1)} %bitcast.19, bf16[576,4096]{1,0:T(8,128)(2,1)} %b_ref.3, bf16[576,6144]{1,0:T(8,128)(2,1)} %a_ref.3), custom_call_target="tpu_custom_call" | custom-call | flops 1509949440 | bytes 11796480 | tf_op jit(solution)/shard_map/panel/pallas_call | solution.py:75
  34.9 2.5 %collective-permute-done.27.refs_1_ = bf16[3,192,128]{2,1,0:T(8,128)(2,1)S(1)} collective-permute-done((bf16[3,192,128]{2,1,0:T(8,128)(2,1)S(1)}, bf16[3,192,128]{2,1,0:T(8,128)(2,1)S(1)}, u32[]{:S(2)}, u32[]{:S(2)}) %collective-permute-start.27) | collective-permute-done | bytes 147488 | tf_op jit(solution)/shard_map/ppermute | solution.py:31
  38.6 9.5 %panel.3 = (f32[4,1,512,128]{3,2,1,0:T(8,128)S(1)}, f32[4,1,512,128]{3,2,1,0:T(8,128)S(1)}) custom-call(s32[2]{0:T(128)S(1)} %get-tuple-element.51.me_ref, bf16[6144,128]{1,0:T(8,128)(2,1)S(1)} %bitcast.18, bf16[576,6144]{1,0:T(8,128)(2,1)} %a_ref.3, bf16[576,4096]{1,0:T(8,128)(2,1)} %b_ref.3), custom_call_target="tpu_custom_call" | custom-call | flops 1509949440 | bytes 11796480 | tf_op jit(solution)/shard_map/panel/pallas_call | solution.py:75
  48.4 2.5 %collective-permute-done.34.recv_ref = f32[4,4,128,128]{3,2,1,0:T(8,128)S(1)} collective-permute-done((f32[4,4,128,128]{3,2,1,0:T(8,128)S(1)}, f32[4,4,128,128]{3,2,1,0:T(8,128)S(1)}, u32[]{:S(2)}, u32[]{:S(2)}) %collective-permute-start.34) | collective-permute-done | bytes 1048608 | tf_op jit(solution)/shard_map/ppermute | solution.py:31
  51.6 1.6 %collective-permute-start.35 = (bf16[4,128,128]{2,1,0:T(8,128)(2,1)S(1)}, bf16[4,128,128]{2,1,0:T(8,128)(2,1)S(1)}, u32[]{:S(2)}, u32[]{:S(2)}) collective-permute-start(bf16[4,128,128]{2,1,0:T(8,128)(2,1)S(1)} %get-tuple-element.41), channel_id=1, source_target_pairs={{0,2},{1,3},{2,0},{3,1},{4,6},{5,7},{6,4},{7,5},{8,10},{9,11},{10,... | collective-permute-start | bytes 393224 | tf_op jit(solution)/shard_map/ppermute | solution.py:31
  53.1 1.5 %collective-permute-start.36 = (bf16[4,128,128]{2,1,0:T(8,128)(2,1)S(1)}, bf16[4,128,128]{2,1,0:T(8,128)(2,1)S(1)}, u32[]{:S(2)}, u32[]{:S(2)}) collective-permute-start(bf16[4,128,128]{2,1,0:T(8,128)(2,1)S(1)} %get-tuple-element.42), channel_id=1, source_target_pairs={{0,4},{1,5},{2,6},{3,7},{4,0},{5,1},{6,2},{7,3},{8,12},{9,13},{10,... | collective-permute-start | bytes 393224 | tf_op jit(solution)/shard_map/ppermute | solution.py:31
  55.8 1.6 %collective-permute-start.8 = (bf16[4,192,128]{2,1,0:T(8,128)(2,1)S(1)}, bf16[4,192,128]{2,1,0:T(8,128)(2,1)S(1)}, u32[]{:S(2)}, u32[]{:S(2)}) collective-permute-start(bf16[4,192,128]{2,1,0:T(8,128)(2,1)S(1)} %get-tuple-element.29), channel_id=1, source_target_pairs={{0,2},{1,3},{2,0},{3,1},{4,6},{5,7},{6,4},{7,5},{8,10},{9,11},{10,... | collective-permute-start | bytes 589832 | tf_op jit(solution)/shard_map/ppermute | solution.py:31
  57.4 1.5 %collective-permute-start.9 = (bf16[4,192,128]{2,1,0:T(8,128)(2,1)S(1)}, bf16[4,192,128]{2,1,0:T(8,128)(2,1)S(1)}, u32[]{:S(2)}, u32[]{:S(2)}) collective-permute-start(bf16[4,192,128]{2,1,0:T(8,128)(2,1)S(1)} %get-tuple-element.30), channel_id=1, source_target_pairs={{0,4},{1,5},{2,6},{3,7},{4,0},{5,1},{6,2},{7,3},{8,12},{9,13},{10,... | collective-permute-start | bytes 589832 | tf_op jit(solution)/shard_map/ppermute | solution.py:31
  58.9 1.5 %collective-permute-start.10 = (bf16[4,192,128]{2,1,0:T(8,128)(2,1)S(1)}, bf16[4,192,128]{2,1,0:T(8,128)(2,1)S(1)}, u32[]{:S(2)}, u32[]{:S(2)}) collective-permute-start(bf16[4,192,128]{2,1,0:T(8,128)(2,1)S(1)} %get-tuple-element.31), channel_id=1, source_target_pairs={{0,6},{1,7},{2,4},{3,5},{4,2},{5,3},{6,0},{7,1},{8,14},{9,15},{10,... | collective-permute-start | bytes 589832 | tf_op jit(solution)/shard_map/ppermute | solution.py:31
  62.7 2.1 %collective-permute-start.39 = (bf16[128,128]{1,0:T(8,128)(2,1)S(1)}, bf16[128,128]{1,0:T(8,128)(2,1)S(1)}, u32[]{:S(2)}, u32[]{:S(2)}) collective-permute-start(bf16[128,128]{1,0:T(8,128)(2,1)S(1)} %get-tuple-element.46), channel_id=1, source_target_pairs={{0,16},{8,24},{16,0},{24,8},{1,17},{9,25},{17,1},{25,9},{2,18},{10... | collective-permute-start | bytes 98312 | tf_op jit(solution)/shard_map/ppermute | solution.py:31
  64.8 1.8 %collective-permute-done.38.refs_0_ = bf16[128,128]{1,0:T(8,128)(2,1)S(1)} collective-permute-done((bf16[128,128]{1,0:T(8,128)(2,1)S(1)}, bf16[128,128]{1,0:T(8,128)(2,1)S(1)}, u32[]{:S(2)}, u32[]{:S(2)}) %collective-permute-start.38) | collective-permute-done | bytes 32800 | tf_op jit(solution)/shard_map/ppermute | solution.py:31
  66.6 1.6 %collective-permute-start.40 = (bf16[128,128]{1,0:T(8,128)(2,1)S(1)}, bf16[128,128]{1,0:T(8,128)(2,1)S(1)}, u32[]{:S(2)}, u32[]{:S(2)}) collective-permute-start(bf16[128,128]{1,0:T(8,128)(2,1)S(1)} %get-tuple-element.47), channel_id=1, source_target_pairs={{0,24},{8,16},{16,8},{24,0},{1,25},{9,17},{17,9},{25,1},{2,26},{10... | collective-permute-start | bytes 98312 | tf_op jit(solution)/shard_map/ppermute | solution.py:31
  68.2 4.2 %collective-permute-done.40.refs_2_ = bf16[128,128]{1,0:T(8,128)(2,1)S(1)} collective-permute-done((bf16[128,128]{1,0:T(8,128)(2,1)S(1)}, bf16[128,128]{1,0:T(8,128)(2,1)S(1)}, u32[]{:S(2)}, u32[]{:S(2)}) %collective-permute-start.40) | collective-permute-done | bytes 32800 | tf_op jit(solution)/shard_map/ppermute | solution.py:31
  72.4 2.1 %collective-permute-start.42 = (bf16[128,128]{1,0:T(8,128)(2,1)S(1)}, bf16[128,128]{1,0:T(8,128)(2,1)S(1)}, u32[]{:S(2)}, u32[]{:S(2)}) collective-permute-start(bf16[128,128]{1,0:T(8,128)(2,1)S(1)} %last.3.refs_0_), channel_id=1, source_target_pairs={{0,16},{8,24},{16,0},{24,8},{1,17},{9,25},{17,1},{25,9},{2,18},{10... | collective-permute-start | bytes 98312 | tf_op jit(solution)/shard_map/ppermute | solution.py:31
  74.6 2.3 %collective-permute-start.43 = (bf16[128,128]{1,0:T(8,128)(2,1)S(1)}, bf16[128,128]{1,0:T(8,128)(2,1)S(1)}, u32[]{:S(2)}, u32[]{:S(2)}) collective-permute-start(bf16[128,128]{1,0:T(8,128)(2,1)S(1)} %last.3.refs_0_), channel_id=1, source_target_pairs={{0,24},{8,16},{16,8},{24,0},{1,25},{9,17},{17,9},{25,1},{2,26},{10... | collective-permute-start | bytes 98312 | tf_op jit(solution)/shard_map/ppermute | solution.py:31
  77.5 2.1 %collective-permute-start.12 = (bf16[192,128]{1,0:T(8,128)(2,1)S(1)}, bf16[192,128]{1,0:T(8,128)(2,1)S(1)}, u32[]{:S(2)}, u32[]{:S(2)}) collective-permute-start(bf16[192,128]{1,0:T(8,128)(2,1)S(1)} %get-tuple-element.34), channel_id=1, source_target_pairs={{0,16},{8,24},{16,0},{24,8},{1,17},{9,25},{17,1},{25,9},{2,18},{10... | collective-permute-start | bytes 147464 | tf_op jit(solution)/shard_map/ppermute | solution.py:31
  79.7 2.3 %collective-permute-start.13 = (bf16[192,128]{1,0:T(8,128)(2,1)S(1)}, bf16[192,128]{1,0:T(8,128)(2,1)S(1)}, u32[]{:S(2)}, u32[]{:S(2)}) collective-permute-start(bf16[192,128]{1,0:T(8,128)(2,1)S(1)} %get-tuple-element.35), channel_id=1, source_target_pairs={{0,24},{8,16},{16,8},{24,0},{1,25},{9,17},{17,9},{25,1},{2,26},{10... | collective-permute-start | bytes 147464 | tf_op jit(solution)/shard_map/ppermute | solution.py:31
  87.5 2.1 %collective-permute-start.17 = (bf16[192,128]{1,0:T(8,128)(2,1)S(1)}, bf16[192,128]{1,0:T(8,128)(2,1)S(1)}, u32[]{:S(2)}, u32[]{:S(2)}) collective-permute-start(bf16[192,128]{1,0:T(8,128)(2,1)S(1)} %last.2.refs_0_), channel_id=1, source_target_pairs={{0,4},{1,5},{2,6},{3,7},{4,0},{5,1},{6,2},{7,3},{8,12},{9,13},{10,... | collective-permute-start | bytes 147464 | tf_op jit(solution)/shard_map/ppermute | solution.py:31
  92.1 1.5 %collective-permute-start.46 = (f32[128,128]{1,0:T(8,128)S(1)}, f32[128,128]{1,0:T(8,128)S(1)}, u32[]{:S(2)}, u32[]{:S(2)}) collective-permute-start(f32[128,128]{1,0:T(8,128)S(1)} %get-tuple-element.49.own_ref), channel_id=1, source_target_pairs={{0,3},{1,2},{2,1},{3,0},{4,7},{5,6},{6,5},{7,4},{8,11},{9,10},{10,... | collective-permute-start | bytes 196616 | tf_op jit(solution)/shard_map/ppermute | solution.py:31
  94.7 2.2 %collective-permute-start.49 = (f32[128,128]{1,0:T(8,128)S(1)}, f32[128,128]{1,0:T(8,128)S(1)}, u32[]{:S(2)}, u32[]{:S(2)}) collective-permute-start(f32[128,128]{1,0:T(8,128)S(1)} %get-tuple-element.49.own_ref), channel_id=1, source_target_pairs={{0,6},{1,7},{2,4},{3,5},{4,2},{5,3},{6,0},{7,1},{8,14},{9,15},{10,... | collective-permute-start | bytes 196616 | tf_op jit(solution)/shard_map/ppermute | solution.py:31
  99.0 2.7 %collective-permute-start.22 = (f32[128,128]{1,0:T(8,128)S(1)}, f32[128,128]{1,0:T(8,128)S(1)}, u32[]{:S(2)}, u32[]{:S(2)}) collective-permute-start(f32[128,128]{1,0:T(8,128)S(1)} %get-tuple-element.37.own_ref), channel_id=1, source_target_pairs={{0,16},{8,24},{16,0},{24,8},{1,17},{9,25},{17,1},{25,9},{2,18},{10... | collective-permute-start | bytes 196616 | tf_op jit(solution)/shard_map/ppermute | solution.py:31
  101.7 1.7 %collective-permute-start.23 = (f32[128,128]{1,0:T(8,128)S(1)}, f32[128,128]{1,0:T(8,128)S(1)}, u32[]{:S(2)}, u32[]{:S(2)}) collective-permute-start(f32[128,128]{1,0:T(8,128)S(1)} %get-tuple-element.37.own_ref), channel_id=1, source_target_pairs={{0,24},{8,16},{16,8},{24,0},{1,25},{9,17},{17,9},{25,1},{2,26},{10... | collective-permute-start | bytes 196616 | tf_op jit(solution)/shard_map/ppermute | solution.py:31
  103.3 5.0 %finish.3 = f32[512,128]{1,0:T(8,128)} custom-call(bf16[4,128,128]{2,1,0:T(8,128)(2,1)S(1)} %get-tuple-element.48.panel_ref, f32[128,128]{1,0:T(8,128)S(1)} %get-tuple-element.49.own_ref, f32[128,128]{1,0:T(8,128)S(1)} %collective-permute-done.44.refs_0_, f32[128,128]{1,0:T(8,128)S(1)} %collective-permute-done.45.refs_1_, ...), custom_call_target="tpu_custom_call" | custom-call | flops 10000000000 | bytes 393216 | tf_op jit(solution)/shard_map/finish/pallas_call | solution.py:255
  108.3 5.3 %finish.2 = f32[1536,128]{1,0:T(8,128)} custom-call(bf16[8,192,128]{2,1,0:T(8,128)(2,1)S(1)} %get-tuple-element.36.panel_ref, f32[128,128]{1,0:T(8,128)S(1)} %get-tuple-element.37.own_ref, f32[128,128]{1,0:T(8,128)S(1)} %collective-permute-done.21.refs_0_, f32[128,128]{1,0:T(8,128)S(1)} %collective-permute-done.22.refs_1_, ...), custom_call_target="tpu_custom_call" | custom-call | flops 10000000000 | bytes 1179648 | tf_op jit(solution)/shard_map/finish/pallas_call | solution.py:255
  (91 shorter events, 22.9 us)
Async XLA Ops:
  0.6 14.4 %collective-permute-start.1 = (bf16[512,128]{1,0:T(8,128)(2,1)}, bf16[512,128]{1,0:T(8,128)(2,1)S(1)}, u32[]{:S(2)}, u32[]{:S(2)}) collective-permute-start(bf16[512,128]{1,0:T(8,128)(2,1)} %param.8), channel_id=1, source_target_pairs={{0,2},{1,3},{2,0},{3,1},{4,6},{5,7},{6,4},{7,5},{8,10},{9,11},{10,... | collective-permute-start | bytes 393224 | tf_op jit(solution)/shard_map/ppermute | solution.py:31
  3.6 11.4 %collective-permute-start.3 = (bf16[512,128]{1,0:T(8,128)(2,1)}, bf16[512,128]{1,0:T(8,128)(2,1)S(1)}, u32[]{:S(2)}, u32[]{:S(2)}) collective-permute-start(bf16[512,128]{1,0:T(8,128)(2,1)} %param.8), channel_id=1, source_target_pairs={{0,4},{1,5},{2,6},{3,7},{4,0},{5,1},{6,2},{7,3},{8,12},{9,13},{10,... | collective-permute-start | bytes 393224 | tf_op jit(solution)/shard_map/ppermute | solution.py:31
  5.2 10.4 %collective-permute-start.5 = (bf16[512,128]{1,0:T(8,128)(2,1)}, bf16[512,128]{1,0:T(8,128)(2,1)S(1)}, u32[]{:S(2)}, u32[]{:S(2)}) collective-permute-start(bf16[512,128]{1,0:T(8,128)(2,1)} %param.8), channel_id=1, source_target_pairs={{0,6},{1,7},{2,4},{3,5},{4,2},{5,3},{6,0},{7,1},{8,14},{9,15},{10,... | collective-permute-start | bytes 393224 | tf_op jit(solution)/shard_map/ppermute | solution.py:31
  6.0 6.4 %collective-permute-start.26 = (bf16[192,128]{1,0:T(8,128)(2,1)S(1)}, bf16[192,128]{1,0:T(8,128)(2,1)S(1)}, u32[]{:S(2)}, u32[]{:S(2)}) collective-permute-start(bf16[192,128]{1,0:T(8,128)(2,1)S(1)} %constant_dynamic-slice_fusion), channel_id=1, source_target_pairs={{0,24},{8,16},{16,8},{24,0},{1,25},{9,17},{17,9},{25,1},{2,26},{10... | collective-permute-start | bytes 147464 | tf_op jit(solution)/shard_map/ppermute | solution.py:31
  12.4 8.3 %collective-permute-start = (bf16[512,128]{1,0:T(8,128)(2,1)}, bf16[512,128]{1,0:T(8,128)(2,1)S(1)}, u32[]{:S(2)}, u32[]{:S(2)}) collective-permute-start(bf16[512,128]{1,0:T(8,128)(2,1)} %param.8), channel_id=1, source_target_pairs={{0,1},{1,0},{2,3},{3,2},{4,5},{5,4},{6,7},{7,6},{8,9},{9,8},{10,11... | collective-permute-start | bytes 393224 | tf_op jit(solution)/shard_map/ppermute | solution.py:31
  15.0 7.2 %collective-permute-start.2 = (bf16[512,128]{1,0:T(8,128)(2,1)S(1)}, bf16[512,128]{1,0:T(8,128)(2,1)S(1)}, u32[]{:S(2)}, u32[]{:S(2)}) collective-permute-start(bf16[512,128]{1,0:T(8,128)(2,1)S(1)} %collective-permute-done.1), channel_id=1, source_target_pairs={{0,1},{1,0},{2,3},{3,2},{4,5},{5,4},{6,7},{7,6},{8,9},{9,8},{10,11... | collective-permute-start | bytes 393224 | tf_op jit(solution)/shard_map/ppermute | solution.py:31
  15.1 7.7 %collective-permute-start.4 = (bf16[512,128]{1,0:T(8,128)(2,1)S(1)}, bf16[512,128]{1,0:T(8,128)(2,1)S(1)}, u32[]{:S(2)}, u32[]{:S(2)}) collective-permute-start(bf16[512,128]{1,0:T(8,128)(2,1)S(1)} %collective-permute-done.3), channel_id=1, source_target_pairs={{0,1},{1,0},{2,3},{3,2},{4,5},{5,4},{6,7},{7,6},{8,9},{9,8},{10,11... | collective-permute-start | bytes 393224 | tf_op jit(solution)/shard_map/ppermute | solution.py:31
  15.6 7.2 %collective-permute-start.6 = (bf16[512,128]{1,0:T(8,128)(2,1)S(1)}, bf16[512,128]{1,0:T(8,128)(2,1)S(1)}, u32[]{:S(2)}, u32[]{:S(2)}) collective-permute-start(bf16[512,128]{1,0:T(8,128)(2,1)S(1)} %collective-permute-done.5), channel_id=1, source_target_pairs={{0,1},{1,0},{2,3},{3,2},{4,5},{5,4},{6,7},{7,6},{8,9},{9,8},{10,11... | collective-permute-start | bytes 393224 | tf_op jit(solution)/shard_map/ppermute | solution.py:31
  19.1 15.1 %collective-permute-start.28 = (bf16[3,192,128]{2,1,0:T(8,128)(2,1)S(1)}, bf16[3,192,128]{2,1,0:T(8,128)(2,1)S(1)}, u32[]{:S(2)}, u32[]{:S(2)}) collective-permute-start(bf16[3,192,128]{2,1,0:T(8,128)(2,1)S(1)} %pad_maximum_fusion.refs_0_), channel_id=1, source_target_pairs={{0,2},{1,3},{2,0},{3,1},{4,6},{5,7},{6,4},{7,5},{8,10},{9,11},{10,... | collective-permute-start | bytes 442376 | tf_op jit(solution)/shard_map/ppermute | solution.py:31
  20.7 13.6 %collective-permute-start.30 = (bf16[3,192,128]{2,1,0:T(8,128)(2,1)S(1)}, bf16[3,192,128]{2,1,0:T(8,128)(2,1)S(1)}, u32[]{:S(2)}, u32[]{:S(2)}) collective-permute-start(bf16[3,192,128]{2,1,0:T(8,128)(2,1)S(1)} %pad_maximum_fusion.refs_0_), channel_id=1, source_target_pairs={{0,4},{1,5},{2,6},{3,7},{4,0},{5,1},{6,2},{7,3},{8,12},{9,13},{10,... | collective-permute-start | bytes 442376 | tf_op jit(solution)/shard_map/ppermute | solution.py:31
  22.2 12.5 %collective-permute-start.32 = (bf16[3,192,128]{2,1,0:T(8,128)(2,1)S(1)}, bf16[3,192,128]{2,1,0:T(8,128)(2,1)S(1)}, u32[]{:S(2)}, u32[]{:S(2)}) collective-permute-start(bf16[3,192,128]{2,1,0:T(8,128)(2,1)S(1)} %pad_maximum_fusion.refs_0_), channel_id=1, source_target_pairs={{0,6},{1,7},{2,4},{3,5},{4,2},{5,3},{6,0},{7,1},{8,14},{9,15},{10,... | collective-permute-start | bytes 442376 | tf_op jit(solution)/shard_map/ppermute | solution.py:31
  33.7 21.5 %collective-permute-start.7 = (f32[4,4,192,128]{3,2,1,0:T(8,128)S(1)}, f32[4,4,192,128]{3,2,1,0:T(8,128)S(1)}, u32[]{:S(2)}, u32[]{:S(2)}) collective-permute-start(f32[4,4,192,128]{3,2,1,0:T(8,128)S(1)} %get-tuple-element.27), channel_id=1, source_target_pairs={{0,1},{1,0},{2,3},{3,2},{4,5},{5,4},{6,7},{7,6},{8,9},{9,8},{10,11... | collective-permute-start | bytes 4718600 | tf_op jit(solution)/shard_map/ppermute | solution.py:31
  51.6 7.3 %collective-permute-start.35 = (bf16[4,128,128]{2,1,0:T(8,128)(2,1)S(1)}, bf16[4,128,128]{2,1,0:T(8,128)(2,1)S(1)}, u32[]{:S(2)}, u32[]{:S(2)}) collective-permute-start(bf16[4,128,128]{2,1,0:T(8,128)(2,1)S(1)} %get-tuple-element.41), channel_id=1, source_target_pairs={{0,2},{1,3},{2,0},{3,1},{4,6},{5,7},{6,4},{7,5},{8,10},{9,11},{10,... | collective-permute-start | bytes 393224 | tf_op jit(solution)/shard_map/ppermute | solution.py:31
  53.1 8.2 %collective-permute-start.36 = (bf16[4,128,128]{2,1,0:T(8,128)(2,1)S(1)}, bf16[4,128,128]{2,1,0:T(8,128)(2,1)S(1)}, u32[]{:S(2)}, u32[]{:S(2)}) collective-permute-start(bf16[4,128,128]{2,1,0:T(8,128)(2,1)S(1)} %get-tuple-element.42), channel_id=1, source_target_pairs={{0,4},{1,5},{2,6},{3,7},{4,0},{5,1},{6,2},{7,3},{8,12},{9,13},{10,... | collective-permute-start | bytes 393224 | tf_op jit(solution)/shard_map/ppermute | solution.py:31
  54.6 7.4 %collective-permute-start.37 = (bf16[4,128,128]{2,1,0:T(8,128)(2,1)S(1)}, bf16[4,128,128]{2,1,0:T(8,128)(2,1)S(1)}, u32[]{:S(2)}, u32[]{:S(2)}) collective-permute-start(bf16[4,128,128]{2,1,0:T(8,128)(2,1)S(1)} %get-tuple-element.43), channel_id=1, source_target_pairs={{0,6},{1,7},{2,4},{3,5},{4,2},{5,3},{6,0},{7,1},{8,14},{9,15},{10,... | collective-permute-start | bytes 393224 | tf_op jit(solution)/shard_map/ppermute | solution.py:31
  55.8 18.7 %collective-permute-start.8 = (bf16[4,192,128]{2,1,0:T(8,128)(2,1)S(1)}, bf16[4,192,128]{2,1,0:T(8,128)(2,1)S(1)}, u32[]{:S(2)}, u32[]{:S(2)}) collective-permute-start(bf16[4,192,128]{2,1,0:T(8,128)(2,1)S(1)} %get-tuple-element.29), channel_id=1, source_target_pairs={{0,2},{1,3},{2,0},{3,1},{4,6},{5,7},{6,4},{7,5},{8,10},{9,11},{10,... | collective-permute-start | bytes 589832 | tf_op jit(solution)/shard_map/ppermute | solution.py:31
  57.4 19.4 %collective-permute-start.9 = (bf16[4,192,128]{2,1,0:T(8,128)(2,1)S(1)}, bf16[4,192,128]{2,1,0:T(8,128)(2,1)S(1)}, u32[]{:S(2)}, u32[]{:S(2)}) collective-permute-start(bf16[4,192,128]{2,1,0:T(8,128)(2,1)S(1)} %get-tuple-element.30), channel_id=1, source_target_pairs={{0,4},{1,5},{2,6},{3,7},{4,0},{5,1},{6,2},{7,3},{8,12},{9,13},{10,... | collective-permute-start | bytes 589832 | tf_op jit(solution)/shard_map/ppermute | solution.py:31
  58.9 17.9 %collective-permute-start.10 = (bf16[4,192,128]{2,1,0:T(8,128)(2,1)S(1)}, bf16[4,192,128]{2,1,0:T(8,128)(2,1)S(1)}, u32[]{:S(2)}, u32[]{:S(2)}) collective-permute-start(bf16[4,192,128]{2,1,0:T(8,128)(2,1)S(1)} %get-tuple-element.31), channel_id=1, source_target_pairs={{0,6},{1,7},{2,4},{3,5},{4,2},{5,3},{6,0},{7,1},{8,14},{9,15},{10,... | collective-permute-start | bytes 589832 | tf_op jit(solution)/shard_map/ppermute | solution.py:31
  72.4 7.3 %collective-permute-start.41 = (bf16[128,128]{1,0:T(8,128)(2,1)S(1)}, bf16[128,128]{1,0:T(8,128)(2,1)S(1)}, u32[]{:S(2)}, u32[]{:S(2)}) collective-permute-start(bf16[128,128]{1,0:T(8,128)(2,1)S(1)} %last.3.refs_0_), channel_id=1, source_target_pairs={{0,8},{8,0},{16,24},{24,16},{1,9},{9,1},{17,25},{25,17},{2,10},{10... | collective-permute-start | bytes 98312 | tf_op jit(solution)/shard_map/ppermute | solution.py:31
  72.4 9.5 %collective-permute-start.42 = (bf16[128,128]{1,0:T(8,128)(2,1)S(1)}, bf16[128,128]{1,0:T(8,128)(2,1)S(1)}, u32[]{:S(2)}, u32[]{:S(2)}) collective-permute-start(bf16[128,128]{1,0:T(8,128)(2,1)S(1)} %last.3.refs_0_), channel_id=1, source_target_pairs={{0,16},{8,24},{16,0},{24,8},{1,17},{9,25},{17,1},{25,9},{2,18},{10... | collective-permute-start | bytes 98312 | tf_op jit(solution)/shard_map/ppermute | solution.py:31
  74.6 7.4 %collective-permute-start.43 = (bf16[128,128]{1,0:T(8,128)(2,1)S(1)}, bf16[128,128]{1,0:T(8,128)(2,1)S(1)}, u32[]{:S(2)}, u32[]{:S(2)}) collective-permute-start(bf16[128,128]{1,0:T(8,128)(2,1)S(1)} %last.3.refs_0_), channel_id=1, source_target_pairs={{0,24},{8,16},{16,8},{24,0},{1,25},{9,17},{17,9},{25,1},{2,26},{10... | collective-permute-start | bytes 98312 | tf_op jit(solution)/shard_map/ppermute | solution.py:31
  77.5 6.8 %collective-permute-start.11 = (bf16[192,128]{1,0:T(8,128)(2,1)S(1)}, bf16[192,128]{1,0:T(8,128)(2,1)S(1)}, u32[]{:S(2)}, u32[]{:S(2)}) collective-permute-start(bf16[192,128]{1,0:T(8,128)(2,1)S(1)} %get-tuple-element.33), channel_id=1, source_target_pairs={{0,8},{8,0},{16,24},{24,16},{1,9},{9,1},{17,25},{25,17},{2,10},{10... | collective-permute-start | bytes 147464 | tf_op jit(solution)/shard_map/ppermute | solution.py:31
  77.5 6.7 %collective-permute-start.12 = (bf16[192,128]{1,0:T(8,128)(2,1)S(1)}, bf16[192,128]{1,0:T(8,128)(2,1)S(1)}, u32[]{:S(2)}, u32[]{:S(2)}) collective-permute-start(bf16[192,128]{1,0:T(8,128)(2,1)S(1)} %get-tuple-element.34), channel_id=1, source_target_pairs={{0,16},{8,24},{16,0},{24,8},{1,17},{9,25},{17,1},{25,9},{2,18},{10... | collective-permute-start | bytes 147464 | tf_op jit(solution)/shard_map/ppermute | solution.py:31
  82.8 6.9 %collective-permute-start.45 = (f32[128,128]{1,0:T(8,128)S(1)}, f32[128,128]{1,0:T(8,128)S(1)}, u32[]{:S(2)}, u32[]{:S(2)}) collective-permute-start(f32[128,128]{1,0:T(8,128)S(1)} %get-tuple-element.49.own_ref), channel_id=1, source_target_pairs={{0,2},{1,3},{2,0},{3,1},{4,6},{5,7},{6,4},{7,5},{8,10},{9,11},{10,... | collective-permute-start | bytes 196616 | tf_op jit(solution)/shard_map/ppermute | solution.py:31
  90.9 6.1 %collective-permute-start.20 = (bf16[192,128]{1,0:T(8,128)(2,1)S(1)}, bf16[192,128]{1,0:T(8,128)(2,1)S(1)}, u32[]{:S(2)}, u32[]{:S(2)}) collective-permute-start(bf16[192,128]{1,0:T(8,128)(2,1)S(1)} %last.2.refs_0_), channel_id=1, source_target_pairs={{0,7},{1,6},{2,5},{3,4},{4,3},{5,2},{6,1},{7,0},{8,15},{9,14},{10,... | collective-permute-start | bytes 147464 | tf_op jit(solution)/shard_map/ppermute | solution.py:31
  92.1 6.8 %collective-permute-start.46 = (f32[128,128]{1,0:T(8,128)S(1)}, f32[128,128]{1,0:T(8,128)S(1)}, u32[]{:S(2)}, u32[]{:S(2)}) collective-permute-start(f32[128,128]{1,0:T(8,128)S(1)} %get-tuple-element.49.own_ref), channel_id=1, source_target_pairs={{0,3},{1,2},{2,1},{3,0},{4,7},{5,6},{6,5},{7,4},{8,11},{9,10},{10,... | collective-permute-start | bytes 196616 | tf_op jit(solution)/shard_map/ppermute | solution.py:31
  94.2 7.5 %collective-permute-start.48 = (f32[128,128]{1,0:T(8,128)S(1)}, f32[128,128]{1,0:T(8,128)S(1)}, u32[]{:S(2)}, u32[]{:S(2)}) collective-permute-start(f32[128,128]{1,0:T(8,128)S(1)} %get-tuple-element.49.own_ref), channel_id=1, source_target_pairs={{0,5},{1,4},{2,7},{3,6},{4,1},{5,0},{6,3},{7,2},{8,13},{9,12},{10,... | collective-permute-start | bytes 196616 | tf_op jit(solution)/shard_map/ppermute | solution.py:31
  94.7 8.6 %collective-permute-start.49 = (f32[128,128]{1,0:T(8,128)S(1)}, f32[128,128]{1,0:T(8,128)S(1)}, u32[]{:S(2)}, u32[]{:S(2)}) collective-permute-start(f32[128,128]{1,0:T(8,128)S(1)} %get-tuple-element.49.own_ref), channel_id=1, source_target_pairs={{0,6},{1,7},{2,4},{3,5},{4,2},{5,3},{6,0},{7,1},{8,14},{9,15},{10,... | collective-permute-start | bytes 196616 | tf_op jit(solution)/shard_map/ppermute | solution.py:31
  97.0 6.3 %collective-permute-start.50 = (f32[128,128]{1,0:T(8,128)S(1)}, f32[128,128]{1,0:T(8,128)S(1)}, u32[]{:S(2)}, u32[]{:S(2)}) collective-permute-start(f32[128,128]{1,0:T(8,128)S(1)} %get-tuple-element.49.own_ref), channel_id=1, source_target_pairs={{0,7},{1,6},{2,5},{3,4},{4,3},{5,2},{6,1},{7,0},{8,15},{9,14},{10,... | collective-permute-start | bytes 196616 | tf_op jit(solution)/shard_map/ppermute | solution.py:31
  98.9 9.4 %collective-permute-start.21 = (f32[128,128]{1,0:T(8,128)S(1)}, f32[128,128]{1,0:T(8,128)S(1)}, u32[]{:S(2)}, u32[]{:S(2)}) collective-permute-start(f32[128,128]{1,0:T(8,128)S(1)} %get-tuple-element.37.own_ref), channel_id=1, source_target_pairs={{0,8},{8,0},{16,24},{24,16},{1,9},{9,1},{17,25},{25,17},{2,10},{10... | collective-permute-start | bytes 196616 | tf_op jit(solution)/shard_map/ppermute | solution.py:31
  99.0 9.3 %collective-permute-start.22 = (f32[128,128]{1,0:T(8,128)S(1)}, f32[128,128]{1,0:T(8,128)S(1)}, u32[]{:S(2)}, u32[]{:S(2)}) collective-permute-start(f32[128,128]{1,0:T(8,128)S(1)} %get-tuple-element.37.own_ref), channel_id=1, source_target_pairs={{0,16},{8,24},{16,0},{24,8},{1,17},{9,25},{17,1},{25,9},{2,18},{10... | collective-permute-start | bytes 196616 | tf_op jit(solution)/shard_map/ppermute | solution.py:31
  101.7 6.6 %collective-permute-start.23 = (f32[128,128]{1,0:T(8,128)S(1)}, f32[128,128]{1,0:T(8,128)S(1)}, u32[]{:S(2)}, u32[]{:S(2)}) collective-permute-start(f32[128,128]{1,0:T(8,128)S(1)} %get-tuple-element.37.own_ref), channel_id=1, source_target_pairs={{0,24},{8,16},{16,8},{24,0},{1,25},{9,17},{17,9},{25,1},{2,26},{10... | collective-permute-start | bytes 196616 | tf_op jit(solution)/shard_map/ppermute | solution.py:31
  (21 other events, 101.3 us)

commit v2 on v0

v2 whole, which is shorter than its diff:
```python
import functools
import math

import jax
import jax.numpy as jnp
from jax import lax
from jax.experimental import pallas as pl
from jax.experimental.pallas import tpu as pltpu
from jax.sharding import PartitionSpec as P

F32 = jnp.float32
BF16 = jnp.bfloat16
VMEM = pl.BlockSpec(memory_space=pltpu.VMEM)
SMEM = pl.BlockSpec(memory_space=pltpu.SMEM)
LIMIT = 24 * 1024 * 1024


def sds(shape, dtype):
    return jax.ShapeDtypeStruct(shape, dtype)


def params(**kw):
    return pltpu.CompilerParams(vmem_limit_bytes=LIMIT, **kw)


def cost(flops, nbytes):
    return pl.CostEstimate(flops=int(flops), bytes_accessed=int(nbytes), transcendentals=0)


def chunks_of(width):
    return width // max(1, width // 1024)


def sketch_of(feats_ref, weights, out_ref):
    width = feats_ref.shape[1]
    step = chunks_of(width)
    total = None
    for at in range(0, width, step):
        part = jnp.dot(
            feats_ref[:, at : at + step], weights(at, step), preferred_element_type=F32
        )
        total = part if total is None else total + part
    out_ref[...] = total.T.astype(BF16)


def text_sketch_kernel(order, me_ref, feats_ref, *refs):
    *parts, out_ref, probe = refs
    n = parts[0].shape[0]
    rows = parts[0].shape[1]
    for part, s in zip(parts, order):
        for i in range(n):
            col = 2 * i + (me_ref[0] % 2 ^ s)
            probe[pl.ds(pl.multiple_of(col * rows, rows), rows), :] = part[i]
    sketch_of(feats_ref, lambda at, step: probe[at : at + step, :], out_ref)


def image_sketch_kernel(me_ref, feats_ref, *refs):
    *parts, out_ref, probe = refs
    groups, n_row, rows, _ = parts[0].shape
    for s, part in enumerate(parts):
        core = me_ref[0] % 2 ^ s
        for g in range(groups):
            for r in range(n_row):
                at = (r * 2 * groups + 2 * g + core) * rows
                probe[pl.ds(pl.multiple_of(at, rows), rows), :] = part[g, r]
    sketch_of(feats_ref, lambda at, step: probe[at : at + step, :], out_ref)


def plain_sketch_kernel(me_ref, feats_ref, probe, out_ref):
    sketch_of(feats_ref, lambda at, step: probe[at : at + step, :], out_ref)


def sketch_call(kernel, me, feats, parts, scratch, name):
    pairs, width = feats.shape
    rank = parts[0].shape[-1]
    return pl.pallas_call(
        kernel,
        in_specs=[SMEM] + [VMEM] * (1 + len(parts)),
        out_specs=VMEM,
        out_shape=sds((rank, pairs), BF16),
        scratch_shapes=[pltpu.VMEM((width, rank), BF16)] * scratch,
        compiler_params=params(),
        cost_estimate=cost(2 * pairs * rank * width, 2 * pairs * width),
        name=name,
    )(me, feats, *parts)


def product_kernel(me_ref, sketch_ref, feats_ref, keep_ref, send_ref):
    core = me_ref[0] % 2
    blocks = keep_ref.shape[0]
    cols = feats_ref.shape[1] // blocks // 2

    @pl.loop(0, blocks)
    def _(i):
        for rel, ref in ((0, keep_ref), (1, send_ref)):
            at = pl.multiple_of((2 * i + (core ^ rel)) * cols, cols)
            out = jnp.dot(sketch_ref[...], feats_ref[:, pl.ds(at, cols)], preferred_element_type=F32)
            ref[i] = out.T.reshape(ref.shape[1:])


def product_call(me, sketch, feats, blocks, parts, name):
    pairs, width = feats.shape
    rank = sketch.shape[0]
    out = sds((blocks, parts, width // blocks // parts // 2, rank), F32)
    return pl.pallas_call(
        product_kernel,
        in_specs=[SMEM, VMEM, VMEM],
        out_specs=[VMEM, VMEM],
        out_shape=[out, out],
        compiler_params=params(),
        cost_estimate=cost(2 * pairs * rank * width, 2 * pairs * width),
        name=name,
    )(me, sketch, feats)


def plane_kernel(me_ref, ikeep, irecv, tkeep, trecv, iown, town, send):
    groups, n_row = send.shape[:2]
    rows = iown.shape[1]
    spot = me_ref[0] // 2
    for r in range(n_row):
        iown[r] = ikeep[r, spot] + irecv[r, spot]
        town[r] = tkeep[spot, r] + trecv[spot, r]
        for g in range(groups):
            send[g, r, :rows] = (ikeep[r, g] + irecv[r, g]).astype(BF16)
            send[g, r, rows:] = (tkeep[g, r] + trecv[g, r]).astype(BF16)


def plane_call(me, ikeep, irecv, tkeep, trecv):
    n_row, groups, irows, rank = ikeep.shape
    trows = tkeep.shape[2]
    return pl.pallas_call(
        plane_kernel,
        in_specs=[SMEM] + [VMEM] * 4,
        out_specs=[VMEM] * 3,
        out_shape=[
            sds((n_row, irows, rank), F32),
            sds((n_row, trows, rank), F32),
            sds((groups, n_row, irows + trows, rank), BF16),
        ],
        compiler_params=params(),
        cost_estimate=cost(ikeep.size, 12 * (ikeep.size + tkeep.size)),
        name="plane",
    )(me, ikeep, irecv, tkeep, trecv)


def depth_kernel(me_ref, iown, town, recv, ikeep, tkeep, send):
    groups, n_row = recv.shape[:2]
    rows = ikeep.shape[0]
    spot = me_ref[0] // 2

    def sums(r):
        image, text = iown[r], town[r]
        for s in range(1, groups):
            image = image + recv[spot ^ s, r, :rows].astype(F32)
            text = text + recv[spot ^ s, r, rows:].astype(F32)
        return image, text

    ikeep[...], tkeep[...] = sums(me_ref[1])
    for r in range(n_row):
        image, text = sums(r)
        send[r, :rows] = image.astype(BF16)
        send[r, rows:] = text.astype(BF16)


def depth_call(me, iown, town, recv):
    n_row, irows, rank = iown.shape
    trows = town.shape[1]
    return pl.pallas_call(
        depth_kernel,
        in_specs=[SMEM] + [VMEM] * 3,
        out_specs=[VMEM] * 3,
        out_shape=[
            sds((irows, rank), F32),
            sds((trows, rank), F32),
            sds((n_row, irows + trows, rank), BF16),
        ],
        compiler_params=params(),
        cost_estimate=cost(iown.size, 12 * (iown.size + town.size)),
        name="depth",
    )(me, iown, town, recv)


def last_kernel(me_ref, iown, town, recv, iout, tout):
    rows = iown.shape[0]
    image, text = iown[...], town[...]
    for s in range(1, recv.shape[0]):
        image = image + recv[me_ref[1] ^ s, :rows].astype(F32)
        text = text + recv[me_ref[1] ^ s, rows:].astype(F32)
    image, text = image.astype(BF16), text.astype(BF16)
    for i in range(iout.shape[0]):
        iout[i] = image
    for i in range(tout.shape[0]):
        tout[i] = text


def last_call(me, n_col, iown, town, recv):
    n_row = recv.shape[0]
    return pl.pallas_call(
        last_kernel,
        in_specs=[SMEM] + [VMEM] * 3,
        out_specs=[VMEM] * 2,
        out_shape=[sds((n_col,) + iown.shape, BF16), sds((n_row,) + town.shape, BF16)],
        compiler_params=params(),
        cost_estimate=cost(iown.size, 4 * n_col * iown.size),
        name="last",
    )(me, iown, town, recv)


def gram_kernel(panel_ref, out_ref):
    rank = out_ref.shape[-1]
    panel = panel_ref[...].reshape(-1, rank)
    gram = lax.dot_general(panel, panel, (((0,), (0,)), ((), ())), preferred_element_type=F32)
    for i in range(out_ref.shape[0]):
        out_ref[i] = gram


def gram_call(panel, copies):
    n, rows, rank = panel.shape
    return pl.pallas_call(
        gram_kernel,
        in_specs=[VMEM],
        out_specs=VMEM,
        out_shape=sds((copies, rank, rank), F32),
        compiler_params=params(),
        cost_estimate=cost(2 * n * rows * rank * rank, 4 * n * rows * rank),
        name="gram",
    )(panel)


def inverse_factor(gram):
    n = gram.shape[0]
    lane = lax.broadcasted_iota(jnp.int32, (8, n), 1)
    sub = lax.broadcasted_iota(jnp.int32, (8, n), 0)
    rows = [gram[8 * i : 8 * i + 8, :] for i in range(n // 8)]
    for b in range(n // 8):
        cols = [
            [jnp.broadcast_to(rows[i][:, 8 * b + j : 8 * b + j + 1], (8, n)) for i in range(b, n // 8)]
            for j in range(8)
        ]
        scale = jnp.ones((8, n), F32)
        for j in range(8):
            k = 8 * b + j
            pivot = jnp.broadcast_to(cols[j][0][j : j + 1, :], (8, n))
            inv = 1.0 / pivot
            scale = jnp.where(sub == j, pivot, scale)
            pivot_row = jnp.where(lane == k, 1.0, jnp.broadcast_to(rows[b][j : j + 1, :], (8, n)))
            below = sub > j
            mult = [c * inv for c in cols[j]]
            mult[0] = jnp.where(below, mult[0], 0.0)
            for jj in range(j + 1, 8):
                entry = jnp.broadcast_to(cols[jj][0][j : j + 1, :], (8, n))
                cols[jj] = [c - m * entry for c, m in zip(cols[jj], mult)]
            for i in range(b, n // 8):
                here = lane == k
                if i == b:
                    here = jnp.logical_and(here, below)
                rows[i] = jnp.where(here, 0.0, rows[i]) - mult[i - b] * pivot_row
            yield None
        unit = jnp.where(lane == sub + 8 * b, 1.0, jnp.where(lane < sub + 8 * b, rows[b], 0.0))
        rows[b] = unit * lax.rsqrt(scale)
        yield None
    yield jnp.concatenate(rows, axis=0)


def finish_kernel(widths, ipanel, igrams, tpanel, tgrams, iout, tout):
    def total(ref):
        value = ref[0]
        for i in range(1, ref.shape[0]):
            value = value + ref[i]
        return value

    inverses = None
    for inverses in zip(inverse_factor(total(igrams)), inverse_factor(total(tgrams))):
        pass
    dims = (((1,), (1,)), ((), ()))
    for inverse, width, panel_ref, out_ref in zip(inverses, widths, (ipanel, tpanel), (iout, tout)):
        inverse = inverse * math.sqrt(width)
        high = inverse.astype(BF16)
        low = (inverse - high.astype(F32)).astype(BF16)
        panel = panel_ref[...].reshape(out_ref.shape)
        out_ref[...] = lax.dot_general(panel, high, dims, preferred_element_type=F32) + lax.dot_general(
            panel, low, dims, preferred_element_type=F32
        )


def finish_call(widths, ipanel, igrams, tpanel, tgrams):
    rank = ipanel.shape[-1]
    outs = [sds((math.prod(p.shape[:-1]), rank), F32) for p in (ipanel, tpanel)]
    return pl.pallas_call(
        functools.partial(finish_kernel, widths),
        in_specs=[VMEM] * 4,
        out_specs=[VMEM] * 2,
        out_shape=outs,
        compiler_params=params(),
        cost_estimate=cost(10**10, 6 * ipanel.size),
        name="finish",
    )(ipanel, igrams, tpanel, tgrams)


def per_device(n_row, n_col, image_feats, text_feats, probe_image, probe_text):
    groups = n_col // 2
    rank = probe_text.shape[1]
    me = jnp.stack([lax.axis_index("col"), lax.axis_index("row")]).astype(jnp.int32)
    core_swap = lambda x: lax.ppermute(x, "col", [(i, i ^ 1) for i in range(n_col)])
    chips = [list(range(core, n_col, 2)) for core in range(2)]
    over_chips = lambda x: lax.all_to_all(x, "col", 0, 0, axis_index_groups=chips)
    over_col = lambda x: lax.all_to_all(x, "col", 0, 0)
    over_row = lambda x: lax.all_to_all(x, "row", 0, 0)
    copies = lambda x, n: jnp.broadcast_to(x[None], (n,) + x.shape)

    piece = probe_image.shape[0] // n_col
    text_part = over_chips(copies(probe_text, groups))
    text_parts = [text_part, core_swap(text_part)]
    if piece % 16 == 0:
        mine = lax.dynamic_slice_in_dim(probe_image, me[0] * piece, piece, 0)
        image_part = over_chips(copies(over_row(copies(mine, n_row)), groups))
        image_parts = [image_part, core_swap(image_part)]
        image_kernel, scratch = image_sketch_kernel, 1
    else:
        image_parts = [lax.all_gather(probe_image, "row", axis=0, tiled=True)]
        image_kernel, scratch = plain_sketch_kernel, 0

    text_kernel = functools.partial(text_sketch_kernel, (0, 1))
    sketch_text = sketch_call(text_kernel, me, text_feats, text_parts, 1, "sketch_text")
    ikeep, isend = product_call(me, sketch_text, image_feats, n_row, groups, "product_image")
    irecv = core_swap(isend)
    sketch_image = sketch_call(image_kernel, me, image_feats, image_parts, scratch, "sketch_image")
    tkeep, tsend = product_call(me, sketch_image, text_feats, groups, n_row, "product_text")
    trecv = core_swap(tsend)

    iown, town, send = plane_call(me, ikeep, irecv, tkeep, trecv)
    iown, town, send = depth_call(me, iown, town, over_chips(send))
    icopies, tcopies = last_call(me, n_col, iown, town, over_row(send))
    ipanel, tpanel = over_col(icopies), over_row(tcopies)
    ipanel = ipanel.reshape(groups, 2, -1, rank).transpose(1, 0, 2, 3).reshape(ipanel.shape)
    igrams = over_row(gram_call(ipanel, n_row))
    tgrams = over_col(gram_call(tpanel, n_col))
    widths = (image_feats.shape[1], text_feats.shape[1])
    return finish_call(widths, ipanel, igrams, tpanel, tgrams)


def solution(mesh):
    in_specs = (P(("row", "col"), None), P(("row", "col"), None), P("row", None), P("col", None))
    out_specs = (P("row", None), P("col", None))
    body = functools.partial(per_device, mesh.shape["row"], mesh.shape["col"])
    return jax.shard_map(body, mesh=mesh, in_specs=in_specs, out_specs=out_specs, check_vma=False)
```

time: 357 us -> 146 us (0.41)
  waiting for transfers between devices: 260 us -> 27.1 us
  blocking collectives: 0 us -> 76.2 us
  other arithmetic: 47.6 us -> 0.08 us
  matrix products: 32.7 us -> 0 us
  Pallas kernels: 0 us -> 21.8 us
  between operations: 14.2 us -> 0.79 us
  starting transfers between devices: 0.46 us -> 11.2 us
  local copies, waits for them, and re-layouts: 1.85 us -> 8.41 us
    reduce_scatter x2 -> x0, waiting for transfers between devices: 99.6 us -> none  [the longest x1 60.1 us: per_device(): lax.psum_scatter(lax.dot_general(columns, sketch_text, dims, preferred_el...]
    psum x3 -> x0, waiting for transfers between devices: 92.1 us -> none  [the longest x1 59.4 us: per_device(): image_panel = lax.psum(partial_panel, 'col')]
    all_to_all x0 -> x6, blocking collectives: none -> 76.2 us  [the longest x4 45.6 us: per_device(): over_row = lambda x: lax.all_to_all(x, 'row', 0, 0)]
    all_gather x2 -> x0, waiting for transfers between devices: 67 us -> none  [the longest x1 41.4 us: per_device(): lax.all_gather(probe_image, 'row', axis=0, tiled=True)]
    another operation x10 -> x1, other arithmetic: 45.9 us -> 0.07 us  [per_device(): jnp.stack([lax.axis_index('col'), lax.axis_index('row')]).astype(jnp.int32)]
    dot_general x4 -> x0, matrix products: 27 us -> none  [the longest x1 11.5 us: per_device(): lax.dot_general(columns, sketch_text, dims, preferred_element_type=jnp.fl...]
    all_to_all x0 -> x3, waiting for transfers between devices: none -> 24.5 us  [the longest x2 16.6 us: per_device(): over_col = lambda x: lax.all_to_all(x, 'col', 0, 0)]
    pallas_call x0 -> x10, Pallas kernels: none -> 21.8 us  [the longest x1 7.39 us: finish_call(): pl.pallas_call(functools.partial(finish_kernel, widths), in_specs=[VMEM]...]
  transfers between devices with their start and end apart: 7 -> 7, of which waited for: 7 -> 4; matrix products, arithmetic and copies ran while one was open for 11% -> 0% of each run, Pallas kernels for 0% -> 8%
where the time goes in v2:
time: 146 us
  blocking collectives  76.2 us (52%)
  waiting for transfers between devices  27.1 us (19%)
  Pallas kernels  21.8 us (15%)
  starting transfers between devices  11.2 us (8%)
  local copies, waits for them, and re-layouts  8.41 us (6%)
    all_to_all x4, blocking collectives, per_device(): over_row = lambda x: lax.all_to_all(x, 'row', 0, 0)  45.6 us
    all_to_all x2, blocking collectives, per_device(): lax.all_to_all(x, 'col', 0, 0, axis_index_groups=chips)  30.6 us
    all_to_all x2, waiting for transfers between devices, per_device(): over_col = lambda x: lax.all_to_all(x, 'col', 0, 0)  16.6 us
    all_to_all x1, waiting for transfers between devices, per_device(): lax.all_to_all(x, 'col', 0, 0, axis_index_groups=chips)  7.91 us
    pallas_call x1, Pallas kernels, finish_call(): pl.pallas_call(functools.partial(finish_kernel, widths), in_specs=[VMEM]...  7.39 us
    all_to_all x2, starting transfers between devices, per_device(): over_col = lambda x: lax.all_to_all(x, 'col', 0, 0)  6.95 us
    unnamed x12, local copies, waits for them, and re-layouts  6.35 us
    pallas_call x2, Pallas kernels, product_call(): pl.pallas_call(product_kernel, in_specs=[SMEM, VMEM, VMEM], out_specs=[VM...  5.37 us
  transfers between devices with their start and end apart: 7, of which 4 were waited for; matrix products, arithmetic and copies ran while one was open for 0% of the time, Pallas kernels for 8%

profile of v2, /device:TPU:0, one launch (start us, length us, event | category | flops | bytes accessed | tf_op | source)
XLA Modules:
  0.0 145.6 jit_solution(4860577389925384985)
XLA Ops:
  0.6 1.0 copy-done
  1.7 13.6 %all_to_all.45 = bf16[4,192,128]{2,1,0:T(8,128)(2,1)S(1)} all-to-all(bf16[4,192,128]{2,1,0:T(8,128)(2,1)S(1)} %broadcast_in_dim.7), channel_id=1, replica_groups=mesh['row'=4,'col'=8] {'row'}, dimensions={0} | all-to-all | bytes 393216 | tf_op jit(solution)/shard_map/all_to_all | solution.py:308
  15.3 1.0 broadcast_in_dim.6
  16.2 10.6 %all_to_all.46.refs_0_ = bf16[4,512,128]{2,1,0:T(8,128)(2,1)S(1)} all-to-all(bf16[4,512,128]{2,1,0:T(8,128)(2,1)S(1)} %broadcast_in_dim.6), channel_id=1, replica_groups={{0,2,4,6},{1,3,5,7},{8,10,12,14},{9,11,13,15},{16,18,20,22},{17,19,21,2..., dimensions={0} | all-to-all | bytes 1048576 | tf_op jit(solution)/shard_map/all_to_all | solution.py:306
  26.9 1.0 broadcast_in_dim.8
  27.9 3.5 %all-to-all-start.2 = ((bf16[4,4,192,128]{3,2,1,0:T(8,128)(2,1)}), bf16[4,4,192,128]{3,2,1,0:T(8,128)(2,1)S(1)}, u32[]{:S(2)}, u32[]{:S(2)}) async-start(bf16[4,4,192,128]{3,2,1,0:T(8,128)(2,1)} %broadcast_in_dim.8), calls=%async_computation.2 | async-start | bytes 1572864 | tf_op jit(solution)/shard_map/all_to_all | solution.py:306
  31.4 0.1 collective-permute-start
  31.5 7.9 %all-to-all-done.2.refs_0_ = bf16[4,4,192,128]{3,2,1,0:T(8,128)(2,1)S(1)} async-done(((bf16[4,4,192,128]{3,2,1,0:T(8,128)(2,1)}), bf16[4,4,192,128]{3,2,1,0:T(8,128)(2,1)S(1)}, u32[]{:S(2)}, u32[]{:S(2)}) %all-to-all-start.2) | async-done | bytes 786464 | tf_op jit(solution)/shard_map/all_to_all | solution.py:306
  39.4 0.1 pad_add_fusion.me_ref
  39.5 2.3 %copy-done.3 = bf16[576,4096]{1,0:T(8,128)(2,1)S(1)} copy-done((bf16[576,4096]{1,0:T(8,128)(2,1)S(1)}, bf16[576,4096]{1,0:T(8,128)(2,1)}, u32[]{:S(2)}) %copy-start.3) | copy-done | bytes 4718616
  41.8 2.1 %sketch_text.1.sketch_ref = bf16[128,576]{1,0:T(8,128)(2,1)S(1)} custom-call(s32[2]{0:T(128)S(1)} %pad_add_fusion.me_ref, bf16[576,4096]{1,0:T(8,128)(2,1)S(1)} %copy-done.3, bf16[4,512,128]{2,1,0:T(8,128)(2,1)S(1)} %all_to_all.46.refs_0_, bf16[4,512,128]{2,1,0:T(8,128)(2,1)S(1)} %collective-permute-done.refs_1_), custom_call_target="tpu_custom_call" | custom-call | flops 603979776 | bytes 4718592 | tf_op jit(solution)/shard_map/sketch_text/pallas_call | solution.py:76
  43.9 3.0 %copy-done.1 = bf16[576,6144]{1,0:T(8,128)(2,1)S(1)} copy-done((bf16[576,6144]{1,0:T(8,128)(2,1)S(1)}, bf16[576,6144]{1,0:T(8,128)(2,1)}, u32[]{:S(2)}) %copy-start.1) | copy-done | bytes 7077912
  46.9 2.9 %product_image.1 = (f32[4,4,192,128]{3,2,1,0:T(8,128)S(1)}, f32[4,4,192,128]{3,2,1,0:T(8,128)S(1)}) custom-call(s32[2]{0:T(128)S(1)} %pad_add_fusion.me_ref, bf16[128,576]{1,0:T(8,128)(2,1)S(1)} %sketch_text.1.sketch_ref, bf16[576,6144]{1,0:T(8,128)(2,1)S(1)} %copy-done.1), custom_call_target="tpu_custom_call" | custom-call | flops 905969664 | bytes 7077888 | tf_op jit(solution)/shard_map/product_image/pallas_call | solution.py:105
  49.9 0.6 collective-permute-start.1
  50.4 2.7 %sketch_image.1.sketch_ref = bf16[128,576]{1,0:T(8,128)(2,1)S(1)} custom-call(s32[2]{0:T(128)S(1)} %pad_add_fusion.me_ref, bf16[576,6144]{1,0:T(8,128)(2,1)S(1)} %copy-done.2, bf16[4,4,192,128]{3,2,1,0:T(8,128)(2,1)S(1)} %all-to-all-done.2.refs_0_, bf16[4,4,192,128]{3,2,1,0:T(8,128)(2,1)S(1)} %collective-permute-done.2.refs_1_), custom_call_target="tpu_custom_call" | custom-call | flops 905969664 | bytes 7077888 | tf_op jit(solution)/shard_map/sketch_image/pallas_call | solution.py:76
  53.2 2.5 %product_text.1 = (f32[4,4,128,128]{3,2,1,0:T(8,128)S(1)}, f32[4,4,128,128]{3,2,1,0:T(8,128)S(1)}) custom-call(s32[2]{0:T(128)S(1)} %pad_add_fusion.me_ref, bf16[128,576]{1,0:T(8,128)(2,1)S(1)} %sketch_image.1.sketch_ref, bf16[576,4096]{1,0:T(8,128)(2,1)S(1)} %bitcast.7), custom_call_target="tpu_custom_call" | custom-call | flops 603979776 | bytes 4718592 | tf_op jit(solution)/shard_map/product_text/pallas_call | solution.py:105
  55.7 0.1 collective-permute-start.3
  55.8 2.6 %collective-permute-done.3.trecv = f32[4,4,128,128]{3,2,1,0:T(8,128)S(1)} collective-permute-done((f32[4,4,128,128]{3,2,1,0:T(8,128)S(1)}, f32[4,4,128,128]{3,2,1,0:T(8,128)S(1)}, u32[]{:S(2)}, u32[]{:S(2)}) %collective-permute-start.3) | collective-permute-done | bytes 1048608 | tf_op jit(solution)/shard_map/ppermute | solution.py:304
  58.4 0.8 plane.1
  59.3 20.0 %all_to_all.47.recv = bf16[4,4,320,128]{3,2,1,0:T(8,128)(2,1)S(1)} all-to-all(bf16[4,4,320,128]{3,2,1,0:T(8,128)(2,1)S(1)} %get-tuple-element.20), channel_id=1, replica_groups={{0,2,4,6},{1,3,5,7},{8,10,12,14},{9,11,13,15},{16,18,20,22},{17,19,21,2..., dimensions={0} | all-to-all | bytes 2621440 | tf_op jit(solution)/shard_map/all_to_all | solution.py:306
  79.2 0.7 depth.1
  80.0 14.0 %all_to_all.48.recv = bf16[4,320,128]{2,1,0:T(8,128)(2,1)S(1)} all-to-all(bf16[4,320,128]{2,1,0:T(8,128)(2,1)S(1)} %get-tuple-element.23), channel_id=1, replica_groups=mesh['row'=4,'col'=8] {'row'}, dimensions={0} | all-to-all | bytes 655360 | tf_op jit(solution)/shard_map/all_to_all | solution.py:308
  93.9 1.3 last.1
  95.3 8.4 %all_to_all.49.panel_ref.tpanel = bf16[4,128,128]{2,1,0:T(8,128)(2,1)S(1)} all-to-all(bf16[4,128,128]{2,1,0:T(8,128)(2,1)S(1)} %get-tuple-element.25), channel_id=1, replica_groups=mesh['row'=4,'col'=8] {'row'}, dimensions={0} | all-to-all | bytes 262144 | tf_op jit(solution)/shard_map/all_to_all | solution.py:308
  103.7 3.5 %all-to-all-start.5 = ((bf16[8,192,128]{2,1,0:T(8,128)(2,1)}), bf16[8,192,128]{2,1,0:T(8,128)(2,1)S(1)}, u32[]{:S(2)}, u32[]{:S(2)}) async-start(bf16[8,192,128]{2,1,0:T(8,128)(2,1)} %get-tuple-element.24), calls=%async_computation.5 | async-start | bytes 786432 | tf_op jit(solution)/shard_map/all_to_all | solution.py:307
  107.2 1.0 gram.3
  108.2 7.2 %all-to-all-done.5 = bf16[8,192,128]{2,1,0:T(8,128)(2,1)S(1)} async-done(((bf16[8,192,128]{2,1,0:T(8,128)(2,1)}), bf16[8,192,128]{2,1,0:T(8,128)(2,1)S(1)}, u32[]{:S(2)}, u32[]{:S(2)}) %all-to-all-start.5) | async-done | bytes 393248 | tf_op jit(solution)/shard_map/all_to_all | solution.py:307
  115.4 3.5 %all-to-all-start.8 = ((f32[8,128,128]{2,1,0:T(8,128)}), f32[8,128,128]{2,1,0:T(8,128)S(1)}, u32[]{:S(2)}, u32[]{:S(2)}) async-start(f32[8,128,128]{2,1,0:T(8,128)} %gram.3), calls=%async_computation.8 | async-start | bytes 1048576 | tf_op jit(solution)/shard_map/all_to_all | solution.py:307
  119.0 0.3 gram.2
  119.3 9.3 %all-to-all-done.8.tgrams = f32[8,128,128]{2,1,0:T(8,128)S(1)} async-done(((f32[8,128,128]{2,1,0:T(8,128)}), f32[8,128,128]{2,1,0:T(8,128)S(1)}, u32[]{:S(2)}, u32[]{:S(2)}) %all-to-all-start.8) | async-done | bytes 524320 | tf_op jit(solution)/shard_map/all_to_all | solution.py:307
  128.6 9.6 %all_to_all.50.igrams = f32[4,128,128]{2,1,0:T(8,128)S(1)} all-to-all(f32[4,128,128]{2,1,0:T(8,128)S(1)} %gram.2), channel_id=1, replica_groups=mesh['row'=4,'col'=8] {'row'}, dimensions={0} | all-to-all | bytes 524288 | tf_op jit(solution)/shard_map/all_to_all | solution.py:308
  138.2 7.4 %finish.1 = (f32[1536,128]{1,0:T(8,128)}, f32[512,128]{1,0:T(8,128)}) custom-call(bf16[8,192,128]{2,1,0:T(8,128)(2,1)S(1)} %bitcast.9, f32[4,128,128]{2,1,0:T(8,128)S(1)} %all_to_all.50.igrams, bf16[4,128,128]{2,1,0:T(8,128)(2,1)S(1)} %all_to_all.49.panel_ref.tpanel, f32[8,128,128]{2,1,0:T(8,128)S(1)} %all-to-all-done.8.tgrams), custom_call_target="tpu_custom_call" | custom-call | flops 10000000000 | bytes 1179648 | tf_op jit(solution)/shard_map/finish/pallas_call | solution.py:289
  (17 shorter events, 0.1 us)
Async XLA Ops:
  0.6 1.0 copy-start
  27.9 11.5 %all-to-all-start.2 = ((bf16[4,4,192,128]{3,2,1,0:T(8,128)(2,1)}), bf16[4,4,192,128]{3,2,1,0:T(8,128)(2,1)S(1)}, u32[]{:S(2)}, u32[]{:S(2)}) async-start(bf16[4,4,192,128]{3,2,1,0:T(8,128)(2,1)} %broadcast_in_dim.8), calls=%async_computation.2 | async-start | bytes 1572864 | tf_op jit(solution)/shard_map/all_to_all | solution.py:306
  31.4 8.1 %collective-permute-start = (bf16[4,512,128]{2,1,0:T(8,128)(2,1)S(1)}, bf16[4,512,128]{2,1,0:T(8,128)(2,1)S(1)}, u32[]{:S(2)}, u32[]{:S(2)}) collective-permute-start(bf16[4,512,128]{2,1,0:T(8,128)(2,1)S(1)} %all_to_all.46.refs_0_), channel_id=1, source_target_pairs={{0,1},{1,0},{2,3},{3,2},{4,5},{5,4},{6,7},{7,6},{8,9},{9,8},{10,11... | collective-permute-start | bytes 1572872 | tf_op jit(solution)/shard_map/ppermute | solution.py:304
  39.4 11.0 %collective-permute-start.2 = (bf16[4,4,192,128]{3,2,1,0:T(8,128)(2,1)S(1)}, bf16[4,4,192,128]{3,2,1,0:T(8,128)(2,1)S(1)}, u32[]{:S(2)}, u32[]{:S(2)}) collective-permute-start(bf16[4,4,192,128]{3,2,1,0:T(8,128)(2,1)S(1)} %all-to-all-done.2.refs_0_), channel_id=1, source_target_pairs={{0,1},{1,0},{2,3},{3,2},{4,5},{5,4},{6,7},{7,6},{8,9},{9,8},{10,11... | collective-permute-start | bytes 2359304 | tf_op jit(solution)/shard_map/ppermute | solution.py:304
  39.5 2.3 %copy-start.3 = (bf16[576,4096]{1,0:T(8,128)(2,1)S(1)}, bf16[576,4096]{1,0:T(8,128)(2,1)}, u32[]{:S(2)}) copy-start(bf16[576,4096]{1,0:T(8,128)(2,1)} %feats_ref.7) | copy-start | bytes 14155780
  43.9 3.0 %copy-start.1 = (bf16[576,6144]{1,0:T(8,128)(2,1)S(1)}, bf16[576,6144]{1,0:T(8,128)(2,1)}, u32[]{:S(2)}) copy-start(bf16[576,6144]{1,0:T(8,128)(2,1)} %feats_ref.6) | copy-start | bytes 21233668
  46.9 3.5 %copy-start.2 = (bf16[576,6144]{1,0:T(8,128)(2,1)S(1)}, bf16[576,6144]{1,0:T(8,128)(2,1)}, u32[]{:S(2)}) copy-start(bf16[576,6144]{1,0:T(8,128)(2,1)} %feats_ref.6) | copy-start | bytes 21233668
  46.9 6.2 %slice-start = ((s8[4718592]{0:T(1024)(128)(4,1)}), s8[4194304]{0:T(1024)(128)(4,1)S(1)}, s32[]{:S(2)}) async-start(s8[4718592]{0:T(1024)(128)(4,1)} %bitcast.6), calls=%async_computation.9 | async-start | bytes 8388608
  49.9 3.3 %slice-start.1 = ((s8[4718592]{0:T(1024)(128)(4,1)}), s8[524288]{0:T(1024)(128)(4,1)S(1)}, s32[]{:S(2)}) async-start(s8[4718592]{0:T(1024)(128)(4,1)} %bitcast.6), calls=%async_computation.10 | async-start | bytes 1048576
  49.9 5.9 %collective-permute-start.1 = (f32[4,4,192,128]{3,2,1,0:T(8,128)S(1)}, f32[4,4,192,128]{3,2,1,0:T(8,128)S(1)}, u32[]{:S(2)}, u32[]{:S(2)}) collective-permute-start(f32[4,4,192,128]{3,2,1,0:T(8,128)S(1)} %get-tuple-element.15), channel_id=1, source_target_pairs={{0,1},{1,0},{2,3},{3,2},{4,5},{5,4},{6,7},{7,6},{8,9},{9,8},{10,11... | collective-permute-start | bytes 4718600 | tf_op jit(solution)/shard_map/ppermute | solution.py:304
  55.7 2.7 %collective-permute-start.3 = (f32[4,4,128,128]{3,2,1,0:T(8,128)S(1)}, f32[4,4,128,128]{3,2,1,0:T(8,128)S(1)}, u32[]{:S(2)}, u32[]{:S(2)}) collective-permute-start(f32[4,4,128,128]{3,2,1,0:T(8,128)S(1)} %get-tuple-element.17), channel_id=1, source_target_pairs={{0,1},{1,0},{2,3},{3,2},{4,5},{5,4},{6,7},{7,6},{8,9},{9,8},{10,11... | collective-permute-start | bytes 3145736 | tf_op jit(solution)/shard_map/ppermute | solution.py:304
  103.7 11.7 %all-to-all-start.5 = ((bf16[8,192,128]{2,1,0:T(8,128)(2,1)}), bf16[8,192,128]{2,1,0:T(8,128)(2,1)S(1)}, u32[]{:S(2)}, u32[]{:S(2)}) async-start(bf16[8,192,128]{2,1,0:T(8,128)(2,1)} %get-tuple-element.24), calls=%async_computation.5 | async-start | bytes 786432 | tf_op jit(solution)/shard_map/all_to_all | solution.py:307
  115.4 13.2 %all-to-all-start.8 = ((f32[8,128,128]{2,1,0:T(8,128)}), f32[8,128,128]{2,1,0:T(8,128)S(1)}, u32[]{:S(2)}, u32[]{:S(2)}) async-start(f32[8,128,128]{2,1,0:T(8,128)} %gram.3), calls=%async_computation.8 | async-start | bytes 1048576 | tf_op jit(solution)/shard_map/all_to_all | solution.py:307

commit v3 on v0

v3 whole, which is shorter than its diff:
```python
import functools
import math

import jax
import jax.numpy as jnp
from jax import lax
from jax.experimental import pallas as pl
from jax.experimental.pallas import tpu as pltpu
from jax.sharding import PartitionSpec as P

F32 = jnp.float32
BF16 = jnp.bfloat16
VMEM = pl.BlockSpec(memory_space=pltpu.VMEM)
SMEM = pl.BlockSpec(memory_space=pltpu.SMEM)
LIMIT = 24 * 1024 * 1024


def sds(shape, dtype):
    return jax.ShapeDtypeStruct(shape, dtype)


def params(**kw):
    return pltpu.CompilerParams(vmem_limit_bytes=LIMIT, **kw)


def cost(flops, nbytes):
    return pl.CostEstimate(flops=int(flops), bytes_accessed=int(nbytes), transcendentals=0)


def text_sketch_kernel(order, me_ref, feats_ref, *refs):
    *parts, out_ref = refs
    total = None
    for part, s in zip(parts, order):
        rows = part.shape[0]
        at = pl.multiple_of((me_ref[0] ^ s) * rows, rows)
        term = jnp.dot(feats_ref[:, pl.ds(at, rows)], part[...], preferred_element_type=F32)
        total = term if total is None else total + term
    out_ref[...] = total.T.astype(BF16)


def image_sketch_kernel(order, me_ref, feats_ref, own_ref, *refs):
    *parts, out_ref = refs
    rows = own_ref.shape[0]
    half = rows // 2
    at = pl.multiple_of(me_ref[1] * rows, rows)
    total = jnp.dot(feats_ref[:, pl.ds(at, rows)], own_ref[...], preferred_element_type=F32)
    for part, (t, c) in zip(parts, order):
        at = (me_ref[1] ^ t) * rows + (me_ref[0] % 2 ^ c) * half
        at = pl.multiple_of(at, half)
        total = total + jnp.dot(feats_ref[:, pl.ds(at, half)], part[...], preferred_element_type=F32)
    out_ref[...] = total.T.astype(BF16)


def sketch_call(kernel, order, me, feats, parts, name):
    pairs, width = feats.shape
    rank = parts[0].shape[-1]
    return pl.pallas_call(
        functools.partial(kernel, order),
        in_specs=[SMEM] + [VMEM] * (1 + len(parts)),
        out_specs=VMEM,
        out_shape=sds((rank, pairs), BF16),
        compiler_params=params(),
        cost_estimate=cost(2 * pairs * rank * width, 2 * pairs * width),
        name=name,
    )(me, feats, *parts)


def product_kernel(me_ref, sketch_ref, feats_ref, keep_ref, send_ref):
    core = me_ref[0] % 2
    blocks = keep_ref.shape[0]
    cols = feats_ref.shape[1] // blocks // 2

    @pl.loop(0, blocks)
    def _(i):
        for rel, ref in ((0, keep_ref), (1, send_ref)):
            at = pl.multiple_of((2 * i + (core ^ rel)) * cols, cols)
            out = jnp.dot(sketch_ref[...], feats_ref[:, pl.ds(at, cols)], preferred_element_type=F32)
            ref[i] = out.T.reshape(ref.shape[1:])


def product_call(me, sketch, feats, blocks, parts, name):
    pairs, width = feats.shape
    rank = sketch.shape[0]
    out = sds((blocks, parts, width // blocks // parts // 2, rank), F32)
    return pl.pallas_call(
        product_kernel,
        in_specs=[SMEM, VMEM, VMEM],
        out_specs=[VMEM, VMEM],
        out_shape=[out, out],
        compiler_params=params(),
        cost_estimate=cost(2 * pairs * rank * width, 2 * pairs * width),
        name=name,
    )(me, sketch, feats)


def sums_kernel(which, axis, shifts, n, me_ref, *refs):
    terms, (own_ref, *sends) = refs[:n], refs[n:]
    spot = me_ref[1] if which == "row" else me_ref[0] // 2

    def total(i):
        at = (slice(None),) * axis + (i,)
        value = terms[0][at]
        for term in terms[1:]:
            value = value + term[at].astype(F32)
        return value

    own_ref[...] = total(spot)
    for s, ref in zip(shifts, sends):
        ref[...] = total(spot ^ s).astype(BF16)


def sums_call(which, axis, shifts, me, terms, name):
    shape = list(terms[0].shape)
    size = terms[0].size
    del shape[axis]
    return pl.pallas_call(
        functools.partial(sums_kernel, which, axis, shifts, len(terms)),
        in_specs=[SMEM] + [VMEM] * len(terms),
        out_specs=[VMEM] * (1 + len(shifts)),
        out_shape=[sds(shape, F32)] + [sds(shape, BF16)] * len(shifts),
        compiler_params=params(),
        cost_estimate=cost(size, 4 * size * len(terms)),
        name=name,
    )(me, *terms)


def last_kernel(own_ref, *refs):
    *recv, out_ref = refs
    value = own_ref[...]
    for ref in recv:
        value = value + ref[...].astype(F32)
    out_ref[...] = value.astype(out_ref.dtype)


def last_call(own, recv, dtype, name):
    return pl.pallas_call(
        last_kernel,
        in_specs=[VMEM] * (1 + len(recv)),
        out_specs=VMEM,
        out_shape=sds(own.shape, dtype),
        compiler_params=params(),
        cost_estimate=cost(own.size, 12 * own.size),
        name=name,
    )(own, *recv)


def gram_kernel(which, order, me_ref, *refs):
    parts, (panel_ref, gram_ref) = refs[: len(order)], refs[len(order) :]
    for s, part in zip(order, parts):
        if which == "row":
            panel_ref[me_ref[1] ^ s] = part[...]
        else:
            spot = me_ref[0] ^ s
            panel_ref[spot % 2 * (len(order) // 2) + spot // 2] = part[...]
    panel = panel_ref[...].reshape(-1, gram_ref.shape[0])
    gram_ref[...] = lax.dot_general(
        panel, panel, (((0,), (0,)), ((), ())), preferred_element_type=F32
    )


def gram_call(which, order, me, parts, name):
    n = len(parts)
    rows, rank = parts[0].shape
    return pl.pallas_call(
        functools.partial(gram_kernel, which, order),
        in_specs=[SMEM] + [VMEM] * n,
        out_specs=[VMEM, VMEM],
        out_shape=[sds((n, rows, rank), BF16), sds((rank, rank), F32)],
        compiler_params=params(),
        cost_estimate=cost(2 * n * rows * rank * rank, 4 * n * rows * rank),
        name=name,
    )(me, *parts)


def inverse_factor(gram):
    n = gram.shape[0]
    lane = lax.broadcasted_iota(jnp.int32, (8, n), 1)
    sub = lax.broadcasted_iota(jnp.int32, (8, n), 0)
    rows = [gram[8 * i : 8 * i + 8, :] for i in range(n // 8)]
    for b in range(n // 8):
        cols = [
            [jnp.broadcast_to(rows[i][:, 8 * b + j : 8 * b + j + 1], (8, n)) for i in range(b, n // 8)]
            for j in range(8)
        ]
        scale = jnp.ones((8, n), F32)
        for j in range(8):
            k = 8 * b + j
            pivot = jnp.broadcast_to(cols[j][0][j : j + 1, :], (8, n))
            inv = 1.0 / pivot
            scale = jnp.where(sub == j, pivot, scale)
            pivot_row = jnp.where(lane == k, 1.0, jnp.broadcast_to(rows[b][j : j + 1, :], (8, n)))
            below = sub > j
            mult = [c * inv for c in cols[j]]
            mult[0] = jnp.where(below, mult[0], 0.0)
            for jj in range(j + 1, 8):
                entry = jnp.broadcast_to(cols[jj][0][j : j + 1, :], (8, n))
                cols[jj] = [c - m * entry for c, m in zip(cols[jj], mult)]
            for i in range(b, n // 8):
                here = lane == k
                if i == b:
                    here = jnp.logical_and(here, below)
                rows[i] = jnp.where(here, 0.0, rows[i]) - mult[i - b] * pivot_row
            yield None
        unit = jnp.where(lane == sub + 8 * b, 1.0, jnp.where(lane < sub + 8 * b, rows[b], 0.0))
        rows[b] = unit * lax.rsqrt(scale)
        yield None
    yield jnp.concatenate(rows, axis=0)


def finish_kernel(widths, n_image, ipanel, tpanel, *refs):
    *grams, iout, tout = refs

    def total(refs):
        value = refs[0][...]
        for ref in refs[1:]:
            value = value + ref[...]
        return value

    inverses = None
    for inverses in zip(inverse_factor(total(grams[:n_image])), inverse_factor(total(grams[n_image:]))):
        pass
    dims = (((1,), (1,)), ((), ()))
    for inverse, width, panel_ref, out_ref in zip(inverses, widths, (ipanel, tpanel), (iout, tout)):
        inverse = inverse * math.sqrt(width)
        high = inverse.astype(BF16)
        low = (inverse - high.astype(F32)).astype(BF16)
        panel = panel_ref[...].reshape(out_ref.shape)
        out_ref[...] = lax.dot_general(panel, high, dims, preferred_element_type=F32) + lax.dot_general(
            panel, low, dims, preferred_element_type=F32
        )


def finish_call(widths, ipanel, igrams, tpanel, tgrams):
    rank = ipanel.shape[-1]
    outs = [sds((math.prod(p.shape[:-1]), rank), F32) for p in (ipanel, tpanel)]
    return pl.pallas_call(
        functools.partial(finish_kernel, widths, len(igrams)),
        in_specs=[VMEM] * (2 + len(igrams) + len(tgrams)),
        out_specs=[VMEM] * 2,
        out_shape=outs,
        compiler_params=params(),
        cost_estimate=cost(10**10, 6 * ipanel.size),
        name="finish",
    )(ipanel, tpanel, *igrams, *tgrams)


def per_device(n_row, n_col, image_feats, text_feats, probe_image, probe_text):
    groups = n_col // 2
    me = jnp.stack([lax.axis_index("col"), lax.axis_index("row")]).astype(jnp.int32)
    col_swap = lambda x, s: lax.ppermute(x, "col", [(i, i ^ s) for i in range(n_col)])
    row_swap = lambda x, s: lax.ppermute(x, "row", [(i, i ^ s) for i in range(n_row)])
    chips, depths = list(range(1, groups)), list(range(1, n_row))
    over_chips = lambda xs: [col_swap(x, 2 * s) for x, s in zip(xs, chips)]
    over_depth = lambda xs: [row_swap(x, t) for x, t in zip(xs, depths)]

    def over_plane(x):
        got = {0: x}
        for s, block in zip(chips, over_chips([x] * len(chips))):
            got[2 * s] = block
        for s in list(got):
            got[s ^ 1] = col_swap(got[s], 1)
        return got

    half = probe_image.shape[0] // 2
    mine = lax.dynamic_slice_in_dim(probe_image, me[0] % 2 * half, half, 0)
    text_parts = over_plane(probe_text)
    image_parts = {}
    for t, block in zip(depths, over_depth([mine] * len(depths))):
        image_parts[t, 0] = block
        image_parts[t, 1] = col_swap(block, 1)

    sketch_text = sketch_call(
        text_sketch_kernel, list(text_parts), me, text_feats, list(text_parts.values()), "sketch_text"
    )
    keep, send = product_call(me, sketch_text, image_feats, n_row, groups, "product_image")
    own, *sends = sums_call("col", 1, chips, me, [keep, col_swap(send, 1)], "image_cores")
    own, *sends = sums_call("row", 0, depths, me, [own] + over_chips(sends), "image_plane")
    mine = last_call(own, over_depth(sends), BF16, "image_depth")
    parts = over_plane(mine)
    ipanel, gram = gram_call("col", list(parts), me, list(parts.values()), "image_gram")
    igrams = [gram] + over_depth([gram] * len(depths))

    sketch_image = sketch_call(
        image_sketch_kernel,
        list(image_parts),
        me,
        image_feats,
        [probe_image] + list(image_parts.values()),
        "sketch_image",
    )
    keep, send = product_call(me, sketch_image, text_feats, groups, n_row, "product_text")
    own, *sends = sums_call("row", 1, depths, me, [keep, col_swap(send, 1)], "text_cores")
    own, *sends = sums_call("col", 0, chips, me, [own] + over_depth(sends), "text_depth")
    mine = last_call(own, over_chips(sends), BF16, "text_plane")
    parts = [mine] + over_depth([mine] * len(depths))
    tpanel, gram = gram_call("row", [0] + depths, me, parts, "text_gram")
    gram = last_call(gram, [col_swap(gram, 1)], F32, "text_gram_cores")
    tgrams = [gram] + over_chips([gram] * len(chips))

    widths = (image_feats.shape[1], text_feats.shape[1])
    return finish_call(widths, ipanel, igrams, tpanel, tgrams)


def solution(mesh):
    in_specs = (P(("row", "col"), None), P(("row", "col"), None), P("row", None), P("col", None))
    out_specs = (P("row", None), P("col", None))
    body = functools.partial(per_device, mesh.shape["row"], mesh.shape["col"])
    return jax.shard_map(body, mesh=mesh, in_specs=in_specs, out_specs=out_specs, check_vma=False)
```

time: 357 us -> 109 us (0.31)
  waiting for transfers between devices: 260 us -> 33.3 us
  other arithmetic: 47.6 us -> 0.08 us
  starting transfers between devices: 0.46 us -> 46 us
  matrix products: 32.7 us -> 0 us
  Pallas kernels: 0 us -> 21.7 us
  between operations: 14.2 us -> 0.84 us
  local copies, waits for them, and re-layouts: 1.85 us -> 7.2 us
    reduce_scatter x2 -> x0, waiting for transfers between devices: 99.6 us -> none  [the longest x1 60.1 us: per_device(): lax.psum_scatter(lax.dot_general(columns, sketch_text, dims, preferred_el...]
    psum x3 -> x0, waiting for transfers between devices: 92.1 us -> none  [the longest x1 59.4 us: per_device(): image_panel = lax.psum(partial_panel, 'col')]
    all_gather x2 -> x0, waiting for transfers between devices: 67 us -> none  [the longest x1 41.4 us: per_device(): lax.all_gather(probe_image, 'row', axis=0, tiled=True)]
    ppermute x0 -> x44, starting transfers between devices: none -> 46 us  [the longest x15 24 us: per_device(): lax.ppermute(x, 'row', [(i, i ^ s) for i in range(n_row)])]
    another operation x10 -> x1, other arithmetic: 45.9 us -> 0.07 us  [per_device(): jnp.stack([lax.axis_index('col'), lax.axis_index('row')]).astype(jnp.int32)]
    ppermute x0 -> x44, waiting for transfers between devices: none -> 33.3 us  [the longest x29 17 us: per_device(): lax.ppermute(x, 'col', [(i, i ^ s) for i in range(n_col)])]
    dot_general x4 -> x0, matrix products: 27 us -> none  [the longest x1 11.5 us: per_device(): lax.dot_general(columns, sketch_text, dims, preferred_element_type=jnp.fl...]
    pallas_call x0 -> x14, Pallas kernels: none -> 21.7 us  [the longest x1 7.39 us: finish_call(): pl.pallas_call(functools.partial(finish_kernel, widths, len(igrams)), in_...]
  transfers between devices with their start and end apart: 7 -> 44, of which waited for: 7 -> 16; matrix products, arithmetic and copies ran while one was open for 11% -> 1% of each run, Pallas kernels for 0% -> 13%
where the time goes in v3:
time: 109 us
  starting transfers between devices  46 us (42%)
  waiting for transfers between devices  33.3 us (31%)
  Pallas kernels  21.7 us (20%)
  local copies, waits for them, and re-layouts  7.2 us (7%)
    ppermute x15, starting transfers between devices, per_device(): lax.ppermute(x, 'row', [(i, i ^ s) for i in range(n_row)])  24 us
    ppermute x29, starting transfers between devices, per_device(): lax.ppermute(x, 'col', [(i, i ^ s) for i in range(n_col)])  22.1 us
    ppermute x29, waiting for transfers between devices, per_device(): lax.ppermute(x, 'col', [(i, i ^ s) for i in range(n_col)])  17 us
    ppermute x15, waiting for transfers between devices, per_device(): lax.ppermute(x, 'row', [(i, i ^ s) for i in range(n_row)])  16.3 us
    pallas_call x1, Pallas kernels, finish_call(): pl.pallas_call(functools.partial(finish_kernel, widths, len(igrams)), in_...  7.39 us
    unnamed x14, local copies, waits for them, and re-layouts  6.26 us
    pallas_call x2, Pallas kernels, product_call(): pl.pallas_call(product_kernel, in_specs=[SMEM, VMEM, VMEM], out_specs=[VM...  5.35 us
    pallas_call x2, Pallas kernels, sketch_call(): pl.pallas_call(functools.partial(kernel, order), in_specs=[SMEM] + [VMEM]...  4.64 us
  transfers between devices with their start and end apart: 44, of which 16 were waited for; matrix products, arithmetic and copies ran while one was open for 1% of the time, Pallas kernels for 13%

profile of v3, /device:TPU:0, one launch (start us, length us, event | category | flops | bytes accessed | tf_op | source)
XLA Modules:
  0.0 109.1 jit_solution(13232647606780583009)
XLA Ops:
  0.6 3.0 %collective-permute-start = (bf16[512,128]{1,0:T(8,128)(2,1)}, bf16[512,128]{1,0:T(8,128)(2,1)S(1)}, u32[]{:S(2)}, u32[]{:S(2)}) collective-permute-start(bf16[512,128]{1,0:T(8,128)(2,1)} %refs_0_.1), channel_id=1, source_target_pairs={{0,2},{1,3},{2,0},{3,1},{4,6},{5,7},{6,4},{7,5},{8,10},{9,11},{10,... | collective-permute-start | bytes 393224 | tf_op jit(solution)/shard_map/ppermute | solution.py:250
  3.6 1.5 %collective-permute-start.1 = (bf16[512,128]{1,0:T(8,128)(2,1)}, bf16[512,128]{1,0:T(8,128)(2,1)S(1)}, u32[]{:S(2)}, u32[]{:S(2)}) collective-permute-start(bf16[512,128]{1,0:T(8,128)(2,1)} %refs_0_.1), channel_id=1, source_target_pairs={{0,4},{1,5},{2,6},{3,7},{4,0},{5,1},{6,2},{7,3},{8,12},{9,13},{10,... | collective-permute-start | bytes 393224 | tf_op jit(solution)/shard_map/ppermute | solution.py:250
  5.2 2.7 %collective-permute-done.refs_1_ = bf16[512,128]{1,0:T(8,128)(2,1)S(1)} collective-permute-done((bf16[512,128]{1,0:T(8,128)(2,1)}, bf16[512,128]{1,0:T(8,128)(2,1)S(1)}, u32[]{:S(2)}, u32[]{:S(2)}) %collective-permute-start) | collective-permute-done | bytes 131104 | tf_op jit(solution)/shard_map/ppermute | solution.py:250
  7.9 3.8 %collective-permute-done.1.refs_2_ = bf16[512,128]{1,0:T(8,128)(2,1)S(1)} collective-permute-done((bf16[512,128]{1,0:T(8,128)(2,1)}, bf16[512,128]{1,0:T(8,128)(2,1)S(1)}, u32[]{:S(2)}, u32[]{:S(2)}) %collective-permute-start.1) | collective-permute-done | bytes 131104 | tf_op jit(solution)/shard_map/ppermute | solution.py:250
  13.1 1.6 %collective-permute-start.21 = (bf16[768,128]{1,0:T(8,128)(2,1)S(1)}, bf16[768,128]{1,0:T(8,128)(2,1)S(1)}, u32[]{:S(2)}, u32[]{:S(2)}) collective-permute-start(bf16[768,128]{1,0:T(8,128)(2,1)S(1)} %constant_dynamic-slice_fusion), channel_id=1, source_target_pairs={{0,8},{8,0},{16,24},{24,16},{1,9},{9,1},{17,25},{25,17},{2,10},{10... | collective-permute-start | bytes 589832 | tf_op jit(solution)/shard_map/ppermute | solution.py:251
  14.8 2.6 %collective-permute-start.23 = (bf16[768,128]{1,0:T(8,128)(2,1)S(1)}, bf16[768,128]{1,0:T(8,128)(2,1)S(1)}, u32[]{:S(2)}, u32[]{:S(2)}) collective-permute-start(bf16[768,128]{1,0:T(8,128)(2,1)S(1)} %constant_dynamic-slice_fusion), channel_id=1, source_target_pairs={{0,16},{8,24},{16,0},{24,8},{1,17},{9,25},{17,1},{25,9},{2,18},{10... | collective-permute-start | bytes 589832 | tf_op jit(solution)/shard_map/ppermute | solution.py:251
  17.6 2.3 %copy-done.2 = bf16[576,4096]{1,0:T(8,128)(2,1)S(1)} copy-done((bf16[576,4096]{1,0:T(8,128)(2,1)S(1)}, bf16[576,4096]{1,0:T(8,128)(2,1)}, u32[]{:S(2)}) %copy-start.2) | copy-done | bytes 4718616
  20.9 2.0 %sketch_text.1.sketch_ref = bf16[128,576]{1,0:T(8,128)(2,1)S(1)} custom-call(s32[2]{0:T(128)S(1)} %pad_add_fusion.me_ref, bf16[576,4096]{1,0:T(8,128)(2,1)S(1)} %copy-done.2, bf16[512,128]{1,0:T(8,128)(2,1)S(1)} %copy-done.4, bf16[512,128]{1,0:T(8,128)(2,1)S(1)} %collective-permute-done.refs_1_, bf16[512,128]{1,0:T(8,128)(2,1)S(1)} %collective-permute-done.1.refs_2_, ...), custom_call_target="tpu_custom_call" | custom-call | flops 603979776 | bytes 4718592 | tf_op jit(solution)/shard_map/sketch_text/pallas_call | solution.py:57
  22.9 3.0 %copy-done = bf16[576,6144]{1,0:T(8,128)(2,1)S(1)} copy-done((bf16[576,6144]{1,0:T(8,128)(2,1)S(1)}, bf16[576,6144]{1,0:T(8,128)(2,1)}, u32[]{:S(2)}) %copy-start) | copy-done | bytes 7077912
  25.9 2.9 %product_image.1 = (f32[4,4,192,128]{3,2,1,0:T(8,128)S(1)}, f32[4,4,192,128]{3,2,1,0:T(8,128)S(1)}) custom-call(s32[2]{0:T(128)S(1)} %pad_add_fusion.me_ref, bf16[128,576]{1,0:T(8,128)(2,1)S(1)} %sketch_text.1.sketch_ref, bf16[576,6144]{1,0:T(8,128)(2,1)S(1)} %copy-done), custom_call_target="tpu_custom_call" | custom-call | flops 905969664 | bytes 7077888 | tf_op jit(solution)/shard_map/product_image/pallas_call | solution.py:85
  29.4 2.5 %collective-permute-done.23.refs_2_ = bf16[768,128]{1,0:T(8,128)(2,1)S(1)} collective-permute-done((bf16[768,128]{1,0:T(8,128)(2,1)S(1)}, bf16[768,128]{1,0:T(8,128)(2,1)S(1)}, u32[]{:S(2)}, u32[]{:S(2)}) %collective-permute-start.23) | collective-permute-done | bytes 196640 | tf_op jit(solution)/shard_map/ppermute | solution.py:251
  33.7 2.6 %sketch_image.1.sketch_ref = bf16[128,576]{1,0:T(8,128)(2,1)S(1)} custom-call(s32[2]{0:T(128)S(1)} %pad_add_fusion.me_ref, bf16[576,6144]{1,0:T(8,128)(2,1)S(1)} %copy-done.1, bf16[1536,128]{1,0:T(8,128)(2,1)S(1)} %copy-done.3, bf16[768,128]{1,0:T(8,128)(2,1)S(1)} %collective-permute-done.21.refs_0_, bf16[768,128]{1,0:T(8,128)(2,1)S(1)} %collective-permute-done.22.refs_1_, ...), custom_call_target="tpu_custom_call" | custom-call | flops 905969664 | bytes 7077888 | tf_op jit(solution)/shard_map/sketch_image/pallas_call | solution.py:57
  36.3 2.4 %product_text.1 = (f32[4,4,128,128]{3,2,1,0:T(8,128)S(1)}, f32[4,4,128,128]{3,2,1,0:T(8,128)S(1)}) custom-call(s32[2]{0:T(128)S(1)} %pad_add_fusion.me_ref, bf16[128,576]{1,0:T(8,128)(2,1)S(1)} %sketch_image.1.sketch_ref, bf16[576,4096]{1,0:T(8,128)(2,1)S(1)} %bitcast.3), custom_call_target="tpu_custom_call" | custom-call | flops 603979776 | bytes 4718592 | tf_op jit(solution)/shard_map/product_text/pallas_call | solution.py:85
  39.1 2.4 %collective-permute-done.27.refs_1_ = f32[4,4,128,128]{3,2,1,0:T(8,128)S(1)} collective-permute-done((f32[4,4,128,128]{3,2,1,0:T(8,128)S(1)}, f32[4,4,128,128]{3,2,1,0:T(8,128)S(1)}, u32[]{:S(2)}, u32[]{:S(2)}) %collective-permute-start.27) | collective-permute-done | bytes 1048608 | tf_op jit(solution)/shard_map/ppermute | solution.py:250
  42.1 3.3 %collective-permute-start.28 = (bf16[4,128,128]{2,1,0:T(8,128)(2,1)S(1)}, bf16[4,128,128]{2,1,0:T(8,128)(2,1)S(1)}, u32[]{:S(2)}, u32[]{:S(2)}) collective-permute-start(bf16[4,128,128]{2,1,0:T(8,128)(2,1)S(1)} %get-tuple-element.40), channel_id=1, source_target_pairs={{0,8},{8,0},{16,24},{24,16},{1,9},{9,1},{17,25},{25,17},{2,10},{10... | collective-permute-start | bytes 393224 | tf_op jit(solution)/shard_map/ppermute | solution.py:251
  51.2 1.5 %collective-permute-start.10 = (bf16[4,192,128]{2,1,0:T(8,128)(2,1)S(1)}, bf16[4,192,128]{2,1,0:T(8,128)(2,1)S(1)}, u32[]{:S(2)}, u32[]{:S(2)}) collective-permute-start(bf16[4,192,128]{2,1,0:T(8,128)(2,1)S(1)} %get-tuple-element.31), channel_id=1, source_target_pairs={{0,6},{1,7},{2,4},{3,5},{4,2},{5,3},{6,0},{7,1},{8,14},{9,15},{10,... | collective-permute-start | bytes 589832 | tf_op jit(solution)/shard_map/ppermute | solution.py:250
  52.7 5.7 %collective-permute-done.29.refs_2_ = bf16[4,128,128]{2,1,0:T(8,128)(2,1)S(1)} collective-permute-done((bf16[4,128,128]{2,1,0:T(8,128)(2,1)S(1)}, bf16[4,128,128]{2,1,0:T(8,128)(2,1)S(1)}, u32[]{:S(2)}, u32[]{:S(2)}) %collective-permute-start.29) | collective-permute-done | bytes 131104 | tf_op jit(solution)/shard_map/ppermute | solution.py:251
  61.1 1.9 %collective-permute-done.31.refs_0_ = bf16[128,128]{1,0:T(8,128)(2,1)S(1)} collective-permute-done((bf16[128,128]{1,0:T(8,128)(2,1)S(1)}, bf16[128,128]{1,0:T(8,128)(2,1)S(1)}, u32[]{:S(2)}, u32[]{:S(2)}) %collective-permute-start.31) | collective-permute-done | bytes 32800 | tf_op jit(solution)/shard_map/ppermute | solution.py:250
  63.0 1.5 %collective-permute-start.33 = (bf16[128,128]{1,0:T(8,128)(2,1)S(1)}, bf16[128,128]{1,0:T(8,128)(2,1)S(1)}, u32[]{:S(2)}, u32[]{:S(2)}) collective-permute-start(bf16[128,128]{1,0:T(8,128)(2,1)S(1)} %get-tuple-element.46), channel_id=1, source_target_pairs={{0,6},{1,7},{2,4},{3,5},{4,2},{5,3},{6,0},{7,1},{8,14},{9,15},{10,... | collective-permute-start | bytes 98312 | tf_op jit(solution)/shard_map/ppermute | solution.py:250
  64.5 3.3 %collective-permute-done.33.refs_2_ = bf16[128,128]{1,0:T(8,128)(2,1)S(1)} collective-permute-done((bf16[128,128]{1,0:T(8,128)(2,1)S(1)}, bf16[128,128]{1,0:T(8,128)(2,1)S(1)}, u32[]{:S(2)}, u32[]{:S(2)}) %collective-permute-start.33) | collective-permute-done | bytes 32800 | tf_op jit(solution)/shard_map/ppermute | solution.py:250
  67.8 2.4 %collective-permute-start.34 = (bf16[128,128]{1,0:T(8,128)(2,1)S(1)}, bf16[128,128]{1,0:T(8,128)(2,1)S(1)}, u32[]{:S(2)}, u32[]{:S(2)}) collective-permute-start(bf16[128,128]{1,0:T(8,128)(2,1)S(1)} %text_plane.1.refs_0_), channel_id=1, source_target_pairs={{0,8},{8,0},{16,24},{24,16},{1,9},{9,1},{17,25},{25,17},{2,10},{10... | collective-permute-start | bytes 98312 | tf_op jit(solution)/shard_map/ppermute | solution.py:251
  71.2 1.4 %collective-permute-start.36 = (bf16[128,128]{1,0:T(8,128)(2,1)S(1)}, bf16[128,128]{1,0:T(8,128)(2,1)S(1)}, u32[]{:S(2)}, u32[]{:S(2)}) collective-permute-start(bf16[128,128]{1,0:T(8,128)(2,1)S(1)} %text_plane.1.refs_0_), channel_id=1, source_target_pairs={{0,24},{8,16},{16,8},{24,0},{1,25},{9,17},{17,9},{25,1},{2,26},{10... | collective-permute-start | bytes 98312 | tf_op jit(solution)/shard_map/ppermute | solution.py:251
  74.4 1.9 %collective-permute-start.12 = (bf16[192,128]{1,0:T(8,128)(2,1)S(1)}, bf16[192,128]{1,0:T(8,128)(2,1)S(1)}, u32[]{:S(2)}, u32[]{:S(2)}) collective-permute-start(bf16[192,128]{1,0:T(8,128)(2,1)S(1)} %get-tuple-element.34), channel_id=1, source_target_pairs={{0,16},{8,24},{16,0},{24,8},{1,17},{9,25},{17,1},{25,9},{2,18},{10... | collective-permute-start | bytes 147464 | tf_op jit(solution)/shard_map/ppermute | solution.py:251
  76.3 1.4 %collective-permute-start.13 = (bf16[192,128]{1,0:T(8,128)(2,1)S(1)}, bf16[192,128]{1,0:T(8,128)(2,1)S(1)}, u32[]{:S(2)}, u32[]{:S(2)}) collective-permute-start(bf16[192,128]{1,0:T(8,128)(2,1)S(1)} %get-tuple-element.35), channel_id=1, source_target_pairs={{0,24},{8,16},{16,8},{24,0},{1,25},{9,17},{17,9},{25,1},{2,26},{10... | collective-permute-start | bytes 147464 | tf_op jit(solution)/shard_map/ppermute | solution.py:251
  79.9 2.3 %collective-permute-done.13.refs_2_ = bf16[192,128]{1,0:T(8,128)(2,1)S(1)} collective-permute-done((bf16[192,128]{1,0:T(8,128)(2,1)S(1)}, bf16[192,128]{1,0:T(8,128)(2,1)S(1)}, u32[]{:S(2)}, u32[]{:S(2)}) %collective-permute-start.13) | collective-permute-done | bytes 49184 | tf_op jit(solution)/shard_map/ppermute | solution.py:251
  84.4 1.4 %collective-permute-start.16 = (bf16[192,128]{1,0:T(8,128)(2,1)S(1)}, bf16[192,128]{1,0:T(8,128)(2,1)S(1)}, u32[]{:S(2)}, u32[]{:S(2)}) collective-permute-start(bf16[192,128]{1,0:T(8,128)(2,1)S(1)} %image_depth.1.refs_0_), channel_id=1, source_target_pairs={{0,6},{1,7},{2,4},{3,5},{4,2},{5,3},{6,0},{7,1},{8,14},{9,15},{10,... | collective-permute-start | bytes 147464 | tf_op jit(solution)/shard_map/ppermute | solution.py:250
  87.7 1.7 %collective-permute-done.16.refs_3_ = bf16[192,128]{1,0:T(8,128)(2,1)S(1)} collective-permute-done((bf16[192,128]{1,0:T(8,128)(2,1)S(1)}, bf16[192,128]{1,0:T(8,128)(2,1)S(1)}, u32[]{:S(2)}, u32[]{:S(2)}) %collective-permute-start.16) | collective-permute-done | bytes 49184 | tf_op jit(solution)/shard_map/ppermute | solution.py:250
  90.6 1.8 %collective-permute-start.43 = (f32[128,128]{1,0:T(8,128)S(1)}, f32[128,128]{1,0:T(8,128)S(1)}, u32[]{:S(2)}, u32[]{:S(2)}) collective-permute-start(f32[128,128]{1,0:T(8,128)S(1)} %text_gram_cores.1.refs_4_), channel_id=1, source_target_pairs={{0,6},{1,7},{2,4},{3,5},{4,2},{5,3},{6,0},{7,1},{8,14},{9,15},{10,... | collective-permute-start | bytes 196616 | tf_op jit(solution)/shard_map/ppermute | solution.py:250
  93.3 1.9 %collective-permute-start.38 = (f32[128,128]{1,0:T(8,128)S(1)}, f32[128,128]{1,0:T(8,128)S(1)}, u32[]{:S(2)}, u32[]{:S(2)}) collective-permute-start(f32[128,128]{1,0:T(8,128)S(1)} %get-tuple-element.48.refs_0_), channel_id=1, source_target_pairs={{0,16},{8,24},{16,0},{24,8},{1,17},{9,25},{17,1},{25,9},{2,18},{10... | collective-permute-start | bytes 196616 | tf_op jit(solution)/shard_map/ppermute | solution.py:251
  95.3 2.4 %collective-permute-start.39 = (f32[128,128]{1,0:T(8,128)S(1)}, f32[128,128]{1,0:T(8,128)S(1)}, u32[]{:S(2)}, u32[]{:S(2)}) collective-permute-start(f32[128,128]{1,0:T(8,128)S(1)} %get-tuple-element.48.refs_0_), channel_id=1, source_target_pairs={{0,24},{8,16},{16,8},{24,0},{1,25},{9,17},{17,9},{25,1},{2,26},{10... | collective-permute-start | bytes 196616 | tf_op jit(solution)/shard_map/ppermute | solution.py:251
  98.3 3.4 %collective-permute-done.38.refs_2_ = f32[128,128]{1,0:T(8,128)S(1)} collective-permute-done((f32[128,128]{1,0:T(8,128)S(1)}, f32[128,128]{1,0:T(8,128)S(1)}, u32[]{:S(2)}, u32[]{:S(2)}) %collective-permute-start.38) | collective-permute-done | bytes 65568 | tf_op jit(solution)/shard_map/ppermute | solution.py:251
  101.7 7.4 %finish.1 = (f32[1536,128]{1,0:T(8,128)}, f32[512,128]{1,0:T(8,128)}) custom-call(bf16[8,192,128]{2,1,0:T(8,128)(2,1)S(1)} %get-tuple-element.36.ipanel, bf16[4,128,128]{2,1,0:T(8,128)(2,1)S(1)} %get-tuple-element.47.tpanel, f32[128,128]{1,0:T(8,128)S(1)} %get-tuple-element.48.refs_0_, f32[128,128]{1,0:T(8,128)S(1)} %collective-permute-done.37.refs_1_, ...), custom_call_target="tpu_custom_call" | custom-call | flops 10000000000 | bytes 1179648 | tf_op jit(solution)/shard_map/finish/pallas_call | solution.py:236
  (87 shorter events, 26.2 us)
Async XLA Ops:
  0.6 7.2 %collective-permute-start = (bf16[512,128]{1,0:T(8,128)(2,1)}, bf16[512,128]{1,0:T(8,128)(2,1)S(1)}, u32[]{:S(2)}, u32[]{:S(2)}) collective-permute-start(bf16[512,128]{1,0:T(8,128)(2,1)} %refs_0_.1), channel_id=1, source_target_pairs={{0,2},{1,3},{2,0},{3,1},{4,6},{5,7},{6,4},{7,5},{8,10},{9,11},{10,... | collective-permute-start | bytes 393224 | tf_op jit(solution)/shard_map/ppermute | solution.py:250
  3.6 8.0 %collective-permute-start.1 = (bf16[512,128]{1,0:T(8,128)(2,1)}, bf16[512,128]{1,0:T(8,128)(2,1)S(1)}, u32[]{:S(2)}, u32[]{:S(2)}) collective-permute-start(bf16[512,128]{1,0:T(8,128)(2,1)} %refs_0_.1), channel_id=1, source_target_pairs={{0,4},{1,5},{2,6},{3,7},{4,0},{5,1},{6,2},{7,3},{8,12},{9,13},{10,... | collective-permute-start | bytes 393224 | tf_op jit(solution)/shard_map/ppermute | solution.py:250
  5.2 6.5 %collective-permute-start.2 = (bf16[512,128]{1,0:T(8,128)(2,1)}, bf16[512,128]{1,0:T(8,128)(2,1)S(1)}, u32[]{:S(2)}, u32[]{:S(2)}) collective-permute-start(bf16[512,128]{1,0:T(8,128)(2,1)} %refs_0_.1), channel_id=1, source_target_pairs={{0,6},{1,7},{2,4},{3,5},{4,2},{5,3},{6,0},{7,1},{8,14},{9,15},{10,... | collective-permute-start | bytes 393224 | tf_op jit(solution)/shard_map/ppermute | solution.py:250
  5.2 9.6 %collective-permute-start.3 = (bf16[512,128]{1,0:T(8,128)(2,1)}, bf16[512,128]{1,0:T(8,128)(2,1)S(1)}, u32[]{:S(2)}, u32[]{:S(2)}) collective-permute-start(bf16[512,128]{1,0:T(8,128)(2,1)} %refs_0_.1), channel_id=1, source_target_pairs={{0,1},{1,0},{2,3},{3,2},{4,5},{5,4},{6,7},{7,6},{8,9},{9,8},{10,11... | collective-permute-start | bytes 393224 | tf_op jit(solution)/shard_map/ppermute | solution.py:250
  7.9 9.5 %collective-permute-start.4 = (bf16[512,128]{1,0:T(8,128)(2,1)S(1)}, bf16[512,128]{1,0:T(8,128)(2,1)S(1)}, u32[]{:S(2)}, u32[]{:S(2)}) collective-permute-start(bf16[512,128]{1,0:T(8,128)(2,1)S(1)} %collective-permute-done.refs_1_), channel_id=1, source_target_pairs={{0,1},{1,0},{2,3},{3,2},{4,5},{5,4},{6,7},{7,6},{8,9},{9,8},{10,11... | collective-permute-start | bytes 393224 | tf_op jit(solution)/shard_map/ppermute | solution.py:250
  11.6 6.0 %collective-permute-start.5 = (bf16[512,128]{1,0:T(8,128)(2,1)S(1)}, bf16[512,128]{1,0:T(8,128)(2,1)S(1)}, u32[]{:S(2)}, u32[]{:S(2)}) collective-permute-start(bf16[512,128]{1,0:T(8,128)(2,1)S(1)} %collective-permute-done.1.refs_2_), channel_id=1, source_target_pairs={{0,1},{1,0},{2,3},{3,2},{4,5},{5,4},{6,7},{7,6},{8,9},{9,8},{10,11... | collective-permute-start | bytes 393224 | tf_op jit(solution)/shard_map/ppermute | solution.py:250
  11.6 6.0 %collective-permute-start.6 = (bf16[512,128]{1,0:T(8,128)(2,1)S(1)}, bf16[512,128]{1,0:T(8,128)(2,1)S(1)}, u32[]{:S(2)}, u32[]{:S(2)}) collective-permute-start(bf16[512,128]{1,0:T(8,128)(2,1)S(1)} %collective-permute-done.2.refs_3_), channel_id=1, source_target_pairs={{0,1},{1,0},{2,3},{3,2},{4,5},{5,4},{6,7},{7,6},{8,9},{9,8},{10,11... | collective-permute-start | bytes 393224 | tf_op jit(solution)/shard_map/ppermute | solution.py:250
  13.1 15.8 %collective-permute-start.21 = (bf16[768,128]{1,0:T(8,128)(2,1)S(1)}, bf16[768,128]{1,0:T(8,128)(2,1)S(1)}, u32[]{:S(2)}, u32[]{:S(2)}) collective-permute-start(bf16[768,128]{1,0:T(8,128)(2,1)S(1)} %constant_dynamic-slice_fusion), channel_id=1, source_target_pairs={{0,8},{8,0},{16,24},{24,16},{1,9},{9,1},{17,25},{25,17},{2,10},{10... | collective-permute-start | bytes 589832 | tf_op jit(solution)/shard_map/ppermute | solution.py:251
  14.8 17.1 %collective-permute-start.23 = (bf16[768,128]{1,0:T(8,128)(2,1)S(1)}, bf16[768,128]{1,0:T(8,128)(2,1)S(1)}, u32[]{:S(2)}, u32[]{:S(2)}) collective-permute-start(bf16[768,128]{1,0:T(8,128)(2,1)S(1)} %constant_dynamic-slice_fusion), channel_id=1, source_target_pairs={{0,16},{8,24},{16,0},{24,8},{1,17},{9,25},{17,1},{25,9},{2,18},{10... | collective-permute-start | bytes 589832 | tf_op jit(solution)/shard_map/ppermute | solution.py:251
  17.4 14.5 %collective-permute-start.25 = (bf16[768,128]{1,0:T(8,128)(2,1)S(1)}, bf16[768,128]{1,0:T(8,128)(2,1)S(1)}, u32[]{:S(2)}, u32[]{:S(2)}) collective-permute-start(bf16[768,128]{1,0:T(8,128)(2,1)S(1)} %constant_dynamic-slice_fusion), channel_id=1, source_target_pairs={{0,24},{8,16},{16,8},{24,0},{1,25},{9,17},{17,9},{25,1},{2,26},{10... | collective-permute-start | bytes 589832 | tf_op jit(solution)/shard_map/ppermute | solution.py:251
  28.8 19.1 %collective-permute-start.7 = (f32[4,4,192,128]{3,2,1,0:T(8,128)S(1)}, f32[4,4,192,128]{3,2,1,0:T(8,128)S(1)}, u32[]{:S(2)}, u32[]{:S(2)}) collective-permute-start(f32[4,4,192,128]{3,2,1,0:T(8,128)S(1)} %get-tuple-element.27), channel_id=1, source_target_pairs={{0,1},{1,0},{2,3},{3,2},{4,5},{5,4},{6,7},{7,6},{8,9},{9,8},{10,11... | collective-permute-start | bytes 4718600 | tf_op jit(solution)/shard_map/ppermute | solution.py:250
  42.1 9.0 %collective-permute-start.28 = (bf16[4,128,128]{2,1,0:T(8,128)(2,1)S(1)}, bf16[4,128,128]{2,1,0:T(8,128)(2,1)S(1)}, u32[]{:S(2)}, u32[]{:S(2)}) collective-permute-start(bf16[4,128,128]{2,1,0:T(8,128)(2,1)S(1)} %get-tuple-element.40), channel_id=1, source_target_pairs={{0,8},{8,0},{16,24},{24,16},{1,9},{9,1},{17,25},{25,17},{2,10},{10... | collective-permute-start | bytes 393224 | tf_op jit(solution)/shard_map/ppermute | solution.py:251
  45.5 12.9 %collective-permute-start.29 = (bf16[4,128,128]{2,1,0:T(8,128)(2,1)S(1)}, bf16[4,128,128]{2,1,0:T(8,128)(2,1)S(1)}, u32[]{:S(2)}, u32[]{:S(2)}) collective-permute-start(bf16[4,128,128]{2,1,0:T(8,128)(2,1)S(1)} %get-tuple-element.41), channel_id=1, source_target_pairs={{0,16},{8,24},{16,0},{24,8},{1,17},{9,25},{17,1},{25,9},{2,18},{10... | collective-permute-start | bytes 393224 | tf_op jit(solution)/shard_map/ppermute | solution.py:251
  46.6 11.8 %collective-permute-start.30 = (bf16[4,128,128]{2,1,0:T(8,128)(2,1)S(1)}, bf16[4,128,128]{2,1,0:T(8,128)(2,1)S(1)}, u32[]{:S(2)}, u32[]{:S(2)}) collective-permute-start(bf16[4,128,128]{2,1,0:T(8,128)(2,1)S(1)} %get-tuple-element.42), channel_id=1, source_target_pairs={{0,24},{8,16},{16,8},{24,0},{1,25},{9,17},{17,9},{25,1},{2,26},{10... | collective-permute-start | bytes 393224 | tf_op jit(solution)/shard_map/ppermute | solution.py:251
  48.7 22.6 %collective-permute-start.8 = (bf16[4,192,128]{2,1,0:T(8,128)(2,1)S(1)}, bf16[4,192,128]{2,1,0:T(8,128)(2,1)S(1)}, u32[]{:S(2)}, u32[]{:S(2)}) collective-permute-start(bf16[4,192,128]{2,1,0:T(8,128)(2,1)S(1)} %get-tuple-element.29), channel_id=1, source_target_pairs={{0,2},{1,3},{2,0},{3,1},{4,6},{5,7},{6,4},{7,5},{8,10},{9,11},{10,... | collective-permute-start | bytes 589832 | tf_op jit(solution)/shard_map/ppermute | solution.py:250
  49.9 22.7 %collective-permute-start.9 = (bf16[4,192,128]{2,1,0:T(8,128)(2,1)S(1)}, bf16[4,192,128]{2,1,0:T(8,128)(2,1)S(1)}, u32[]{:S(2)}, u32[]{:S(2)}) collective-permute-start(bf16[4,192,128]{2,1,0:T(8,128)(2,1)S(1)} %get-tuple-element.30), channel_id=1, source_target_pairs={{0,4},{1,5},{2,6},{3,7},{4,0},{5,1},{6,2},{7,3},{8,12},{9,13},{10,... | collective-permute-start | bytes 589832 | tf_op jit(solution)/shard_map/ppermute | solution.py:250
  51.2 21.5 %collective-permute-start.10 = (bf16[4,192,128]{2,1,0:T(8,128)(2,1)S(1)}, bf16[4,192,128]{2,1,0:T(8,128)(2,1)S(1)}, u32[]{:S(2)}, u32[]{:S(2)}) collective-permute-start(bf16[4,192,128]{2,1,0:T(8,128)(2,1)S(1)} %get-tuple-element.31), channel_id=1, source_target_pairs={{0,6},{1,7},{2,4},{3,5},{4,2},{5,3},{6,0},{7,1},{8,14},{9,15},{10,... | collective-permute-start | bytes 589832 | tf_op jit(solution)/shard_map/ppermute | solution.py:250
  67.8 8.5 %collective-permute-start.34 = (bf16[128,128]{1,0:T(8,128)(2,1)S(1)}, bf16[128,128]{1,0:T(8,128)(2,1)S(1)}, u32[]{:S(2)}, u32[]{:S(2)}) collective-permute-start(bf16[128,128]{1,0:T(8,128)(2,1)S(1)} %text_plane.1.refs_0_), channel_id=1, source_target_pairs={{0,8},{8,0},{16,24},{24,16},{1,9},{9,1},{17,25},{25,17},{2,10},{10... | collective-permute-start | bytes 98312 | tf_op jit(solution)/shard_map/ppermute | solution.py:251
  70.2 7.5 %collective-permute-start.35 = (bf16[128,128]{1,0:T(8,128)(2,1)S(1)}, bf16[128,128]{1,0:T(8,128)(2,1)S(1)}, u32[]{:S(2)}, u32[]{:S(2)}) collective-permute-start(bf16[128,128]{1,0:T(8,128)(2,1)S(1)} %text_plane.1.refs_0_), channel_id=1, source_target_pairs={{0,16},{8,24},{16,0},{24,8},{1,17},{9,25},{17,1},{25,9},{2,18},{10... | collective-permute-start | bytes 98312 | tf_op jit(solution)/shard_map/ppermute | solution.py:251
  71.2 6.5 %collective-permute-start.36 = (bf16[128,128]{1,0:T(8,128)(2,1)S(1)}, bf16[128,128]{1,0:T(8,128)(2,1)S(1)}, u32[]{:S(2)}, u32[]{:S(2)}) collective-permute-start(bf16[128,128]{1,0:T(8,128)(2,1)S(1)} %text_plane.1.refs_0_), channel_id=1, source_target_pairs={{0,24},{8,16},{16,8},{24,0},{1,25},{9,17},{17,9},{25,1},{2,26},{10... | collective-permute-start | bytes 98312 | tf_op jit(solution)/shard_map/ppermute | solution.py:251
  73.3 5.3 %collective-permute-start.11 = (bf16[192,128]{1,0:T(8,128)(2,1)S(1)}, bf16[192,128]{1,0:T(8,128)(2,1)S(1)}, u32[]{:S(2)}, u32[]{:S(2)}) collective-permute-start(bf16[192,128]{1,0:T(8,128)(2,1)S(1)} %get-tuple-element.33), channel_id=1, source_target_pairs={{0,8},{8,0},{16,24},{24,16},{1,9},{9,1},{17,25},{25,17},{2,10},{10... | collective-permute-start | bytes 147464 | tf_op jit(solution)/shard_map/ppermute | solution.py:251
  74.4 5.5 %collective-permute-start.12 = (bf16[192,128]{1,0:T(8,128)(2,1)S(1)}, bf16[192,128]{1,0:T(8,128)(2,1)S(1)}, u32[]{:S(2)}, u32[]{:S(2)}) collective-permute-start(bf16[192,128]{1,0:T(8,128)(2,1)S(1)} %get-tuple-element.34), channel_id=1, source_target_pairs={{0,16},{8,24},{16,0},{24,8},{1,17},{9,25},{17,1},{25,9},{2,18},{10... | collective-permute-start | bytes 147464 | tf_op jit(solution)/shard_map/ppermute | solution.py:251
  76.3 5.9 %collective-permute-start.13 = (bf16[192,128]{1,0:T(8,128)(2,1)S(1)}, bf16[192,128]{1,0:T(8,128)(2,1)S(1)}, u32[]{:S(2)}, u32[]{:S(2)}) collective-permute-start(bf16[192,128]{1,0:T(8,128)(2,1)S(1)} %get-tuple-element.35), channel_id=1, source_target_pairs={{0,24},{8,16},{16,8},{24,0},{1,25},{9,17},{17,9},{25,1},{2,26},{10... | collective-permute-start | bytes 147464 | tf_op jit(solution)/shard_map/ppermute | solution.py:251
  78.5 7.3 %collective-permute-start.40 = (f32[128,128]{1,0:T(8,128)S(1)}, f32[128,128]{1,0:T(8,128)S(1)}, u32[]{:S(2)}, u32[]{:S(2)}) collective-permute-start(f32[128,128]{1,0:T(8,128)S(1)} %get-tuple-element.49.own_ref), channel_id=1, source_target_pairs={{0,1},{1,0},{2,3},{3,2},{4,5},{5,4},{6,7},{7,6},{8,9},{9,8},{10,11... | collective-permute-start | bytes 196616 | tf_op jit(solution)/shard_map/ppermute | solution.py:250
  82.2 4.9 %collective-permute-start.14 = (bf16[192,128]{1,0:T(8,128)(2,1)S(1)}, bf16[192,128]{1,0:T(8,128)(2,1)S(1)}, u32[]{:S(2)}, u32[]{:S(2)}) collective-permute-start(bf16[192,128]{1,0:T(8,128)(2,1)S(1)} %image_depth.1.refs_0_), channel_id=1, source_target_pairs={{0,2},{1,3},{2,0},{3,1},{4,6},{5,7},{6,4},{7,5},{8,10},{9,11},{10,... | collective-permute-start | bytes 147464 | tf_op jit(solution)/shard_map/ppermute | solution.py:250
  84.4 5.0 %collective-permute-start.16 = (bf16[192,128]{1,0:T(8,128)(2,1)S(1)}, bf16[192,128]{1,0:T(8,128)(2,1)S(1)}, u32[]{:S(2)}, u32[]{:S(2)}) collective-permute-start(bf16[192,128]{1,0:T(8,128)(2,1)S(1)} %image_depth.1.refs_0_), channel_id=1, source_target_pairs={{0,6},{1,7},{2,4},{3,5},{4,2},{5,3},{6,0},{7,1},{8,14},{9,15},{10,... | collective-permute-start | bytes 147464 | tf_op jit(solution)/shard_map/ppermute | solution.py:250
  85.8 9.4 %collective-permute-start.41 = (f32[128,128]{1,0:T(8,128)S(1)}, f32[128,128]{1,0:T(8,128)S(1)}, u32[]{:S(2)}, u32[]{:S(2)}) collective-permute-start(f32[128,128]{1,0:T(8,128)S(1)} %text_gram_cores.1.refs_4_), channel_id=1, source_target_pairs={{0,2},{1,3},{2,0},{3,1},{4,6},{5,7},{6,4},{7,5},{8,10},{9,11},{10,... | collective-permute-start | bytes 196616 | tf_op jit(solution)/shard_map/ppermute | solution.py:250
  89.4 8.3 %collective-permute-start.42 = (f32[128,128]{1,0:T(8,128)S(1)}, f32[128,128]{1,0:T(8,128)S(1)}, u32[]{:S(2)}, u32[]{:S(2)}) collective-permute-start(f32[128,128]{1,0:T(8,128)S(1)} %text_gram_cores.1.refs_4_), channel_id=1, source_target_pairs={{0,4},{1,5},{2,6},{3,7},{4,0},{5,1},{6,2},{7,3},{8,12},{9,13},{10,... | collective-permute-start | bytes 196616 | tf_op jit(solution)/shard_map/ppermute | solution.py:250
  90.6 7.1 %collective-permute-start.43 = (f32[128,128]{1,0:T(8,128)S(1)}, f32[128,128]{1,0:T(8,128)S(1)}, u32[]{:S(2)}, u32[]{:S(2)}) collective-permute-start(f32[128,128]{1,0:T(8,128)S(1)} %text_gram_cores.1.refs_4_), channel_id=1, source_target_pairs={{0,6},{1,7},{2,4},{3,5},{4,2},{5,3},{6,0},{7,1},{8,14},{9,15},{10,... | collective-permute-start | bytes 196616 | tf_op jit(solution)/shard_map/ppermute | solution.py:250
  93.2 5.1 %collective-permute-start.37 = (f32[128,128]{1,0:T(8,128)S(1)}, f32[128,128]{1,0:T(8,128)S(1)}, u32[]{:S(2)}, u32[]{:S(2)}) collective-permute-start(f32[128,128]{1,0:T(8,128)S(1)} %get-tuple-element.48.refs_0_), channel_id=1, source_target_pairs={{0,8},{8,0},{16,24},{24,16},{1,9},{9,1},{17,25},{25,17},{2,10},{10... | collective-permute-start | bytes 196616 | tf_op jit(solution)/shard_map/ppermute | solution.py:251
  93.3 8.4 %collective-permute-start.38 = (f32[128,128]{1,0:T(8,128)S(1)}, f32[128,128]{1,0:T(8,128)S(1)}, u32[]{:S(2)}, u32[]{:S(2)}) collective-permute-start(f32[128,128]{1,0:T(8,128)S(1)} %get-tuple-element.48.refs_0_), channel_id=1, source_target_pairs={{0,16},{8,24},{16,0},{24,8},{1,17},{9,25},{17,1},{25,9},{2,18},{10... | collective-permute-start | bytes 196616 | tf_op jit(solution)/shard_map/ppermute | solution.py:251
  95.3 6.5 %collective-permute-start.39 = (f32[128,128]{1,0:T(8,128)S(1)}, f32[128,128]{1,0:T(8,128)S(1)}, u32[]{:S(2)}, u32[]{:S(2)}) collective-permute-start(f32[128,128]{1,0:T(8,128)S(1)} %get-tuple-element.48.refs_0_), channel_id=1, source_target_pairs={{0,24},{8,16},{16,8},{24,0},{1,25},{9,17},{17,9},{25,1},{2,26},{10... | collective-permute-start | bytes 196616 | tf_op jit(solution)/shard_map/ppermute | solution.py:251
  (19 other events, 84.7 us)

commit v4 on v3

--- a/solution.py
+++ b/solution.py
@@ -12,7 +12,7 @@
 BF16 = jnp.bfloat16
 VMEM = pl.BlockSpec(memory_space=pltpu.VMEM)
 SMEM = pl.BlockSpec(memory_space=pltpu.SMEM)
-LIMIT = 24 * 1024 * 1024
+LIMIT = 32 * 1024 * 1024
 
 
 def sds(shape, dtype):
@@ -27,70 +27,74 @@
     return pl.CostEstimate(flops=int(flops), bytes_accessed=int(nbytes), transcendentals=0)
 
 
-def text_sketch_kernel(order, me_ref, feats_ref, *refs):
-    *parts, out_ref = refs
+def panel_kernel(shifts, n_out, me_ref, a_hbm, b_hbm, *refs):
+    n = len(shifts)
+    parts, (keep_ref, send_ref, a_ref, b_ref, a_sem, b_sem) = refs[:n], refs[n:]
+    core = me_ref[0] % 2
+    depth = parts[0].shape[0]
+    cols = b_ref.shape[1] // n_out // 2
+
+    def column(i):
+        if n == 1:
+            return 0
+        return pl.multiple_of((me_ref[0] ^ shifts[i]) * depth, depth)
+
+    def copies():
+        out = []
+        pieces = max(1, depth // 1024)
+        for i in range(n):
+            for j in range(pieces):
+                at = pl.ds(column(i) + j * (depth // pieces), depth // pieces)
+                out.append(pltpu.make_async_copy(a_hbm.at[:, at], a_ref.at[:, at], a_sem.at[i * pieces + j]))
+        wide = b_ref.shape[1] // n_out
+        for i in range(n_out):
+            at = pl.ds(i * wide, wide)
+            out.append(pltpu.make_async_copy(b_hbm.at[:, at], b_ref.at[:, at], b_sem.at[i]))
+        return out
+
+    moves = copies()
+    for move in moves:
+        move.start()
     total = None
-    for part, s in zip(parts, order):
-        rows = part.shape[0]
-        at = pl.multiple_of((me_ref[0] ^ s) * rows, rows)
-        term = jnp.dot(feats_ref[:, pl.ds(at, rows)], part[...], preferred_element_type=F32)
-        total = term if total is None else total + term
-    out_ref[...] = total.T.astype(BF16)
-
-
-def image_sketch_kernel(order, me_ref, feats_ref, own_ref, *refs):
-    *parts, out_ref = refs
-    rows = own_ref.shape[0]
-    half = rows // 2
-    at = pl.multiple_of(me_ref[1] * rows, rows)
-    total = jnp.dot(feats_ref[:, pl.ds(at, rows)], own_ref[...], preferred_element_type=F32)
-    for part, (t, c) in zip(parts, order):
-        at = (me_ref[1] ^ t) * rows + (me_ref[0] % 2 ^ c) * half
-        at = pl.multiple_of(at, half)
-        total = total + jnp.dot(feats_ref[:, pl.ds(at, half)], part[...], preferred_element_type=F32)
-    out_ref[...] = total.T.astype(BF16)
-
-
-def sketch_call(kernel, order, me, feats, parts, name):
-    pairs, width = feats.shape
-    rank = parts[0].shape[-1]
-    return pl.pallas_call(
-        functools.partial(kernel, order),
-        in_specs=[SMEM] + [VMEM] * (1 + len(parts)),
-        out_specs=VMEM,
-        out_shape=sds((rank, pairs), BF16),
-        compiler_params=params(),
-        cost_estimate=cost(2 * pairs * rank * width, 2 * pairs * width),
-        name=name,
-    )(me, feats, *parts)
-
-
-def product_kernel(me_ref, sketch_ref, feats_ref, keep_ref, send_ref):
-    core = me_ref[0] % 2
-    blocks = keep_ref.shape[0]
-    cols = feats_ref.shape[1] // blocks // 2
-
-    @pl.loop(0, blocks)
-    def _(i):
+    pieces = max(1, depth // 1024)
+    step = depth // pieces
+    for i in range(n):
+        for j in range(pieces):
+            moves[i * pieces + j].wait()
+            at = pl.ds(column(i) + j * step, step)
+            weights = parts[i][j * step : j * step + step, :]
+            term = jnp.dot(a_ref[:, at], weights, preferred_element_type=F32)
+            total = term if total is None else total + term
+    sketch = total.T.astype(BF16)
+    for i in range(n_out):
+        moves[n * pieces + i].wait()
         for rel, ref in ((0, keep_ref), (1, send_ref)):
             at = pl.multiple_of((2 * i + (core ^ rel)) * cols, cols)
-            out = jnp.dot(sketch_ref[...], feats_ref[:, pl.ds(at, cols)], preferred_element_type=F32)
+            out = jnp.dot(sketch, b_ref[:, pl.ds(at, cols)], preferred_element_type=F32)
             ref[i] = out.T.reshape(ref.shape[1:])
 
 
-def product_call(me, sketch, feats, blocks, parts, name):
-    pairs, width = feats.shape
-    rank = sketch.shape[0]
-    out = sds((blocks, parts, width // blocks // parts // 2, rank), F32)
-    return pl.pallas_call(
-        product_kernel,
-        in_specs=[SMEM, VMEM, VMEM],
+def panel_call(me, a, b, parts, shifts, blocks, pieces, name):
+    pairs, width = b.shape
+    rank = parts[0].shape[-1]
+    out = sds((blocks, pieces, width // blocks // pieces // 2, rank), F32)
+    n_copies = len(parts) * max(1, parts[0].shape[0] // 1024)
+    anywhere = pl.BlockSpec(memory_space=pl.ANY)
+    return pl.pallas_call(
+        functools.partial(panel_kernel, shifts, blocks),
+        in_specs=[SMEM, anywhere, anywhere] + [VMEM] * len(parts),
         out_specs=[VMEM, VMEM],
         out_shape=[out, out],
-        compiler_params=params(),
-        cost_estimate=cost(2 * pairs * rank * width, 2 * pairs * width),
+        scratch_shapes=[
+            pltpu.VMEM(a.shape, BF16),
+            pltpu.VMEM(b.shape, BF16),
+            pltpu.SemaphoreType.DMA((n_copies,)),
+            pltpu.SemaphoreType.DMA((blocks,)),
+        ],
+        compiler_params=params(),
+        cost_estimate=cost(2 * pairs * rank * (width + a.shape[1]), 2 * pairs * (width + a.shape[1])),
         name=name,
-    )(me, sketch, feats)
+    )(me, a, b, *parts)
 
 
 def sums_kernel(which, axis, shifts, n, me_ref, *refs):
@@ -170,6 +174,34 @@
         cost_estimate=cost(2 * n * rows * rank * rank, 4 * n * rows * rank),
         name=name,
     )(me, *parts)
+
+
+def tree_sum(values):
+    while len(values) > 1:
+        values = [x + y for x, y in zip(values[::2], values[1::2])]
+    return values[0]
+
+
+def text_gram_kernel(*refs):
+    *parts, panel_ref, gram_ref = refs
+    panel = tree_sum([part[...].astype(F32) for part in parts]).astype(BF16)
+    panel_ref[0] = panel
+    gram_ref[...] = lax.dot_general(
+        panel, panel, (((0,), (0,)), ((), ())), preferred_element_type=F32
+    )
+
+
+def text_gram_call(parts):
+    rows, rank = parts[0].shape
+    return pl.pallas_call(
+        text_gram_kernel,
+        in_specs=[VMEM] * len(parts),
+        out_specs=[VMEM, VMEM],
+        out_shape=[sds((1, rows, rank), BF16), sds((rank, rank), F32)],
+        compiler_params=params(),
+        cost_estimate=cost(2 * rows * rank * rank, 4 * rows * rank),
+        name="text_gram",
+    )(*parts)
 
 
 def inverse_factor(gram):
@@ -261,18 +293,19 @@
             got[s ^ 1] = col_swap(got[s], 1)
         return got
 
-    half = probe_image.shape[0] // 2
-    mine = lax.dynamic_slice_in_dim(probe_image, me[0] % 2 * half, half, 0)
     text_parts = over_plane(probe_text)
-    image_parts = {}
-    for t, block in zip(depths, over_depth([mine] * len(depths))):
-        image_parts[t, 0] = block
-        image_parts[t, 1] = col_swap(block, 1)
-
-    sketch_text = sketch_call(
-        text_sketch_kernel, list(text_parts), me, text_feats, list(text_parts.values()), "sketch_text"
+    image_whole = lax.all_gather(probe_image, "row", axis=0, tiled=True)
+
+    keep, send = panel_call(
+        me,
+        text_feats,
+        image_feats,
+        list(text_parts.values()),
+        list(text_parts),
+        n_row,
+        groups,
+        "image_panel",
     )
-    keep, send = product_call(me, sketch_text, image_feats, n_row, groups, "product_image")
     own, *sends = sums_call("col", 1, chips, me, [keep, col_swap(send, 1)], "image_cores")
     own, *sends = sums_call("row", 0, depths, me, [own] + over_chips(sends), "image_plane")
     mine = last_call(own, over_depth(sends), BF16, "image_depth")
@@ -280,20 +313,13 @@
     ipanel, gram = gram_call("col", list(parts), me, list(parts.values()), "image_gram")
     igrams = [gram] + over_depth([gram] * len(depths))
 
-    sketch_image = sketch_call(
-        image_sketch_kernel,
-        list(image_parts),
-        me,
-        image_feats,
-        [probe_image] + list(image_parts.values()),
-        "sketch_image",
+    keep, send = panel_call(
+        me, image_feats, text_feats, [image_whole], [0], groups, 1, "text_panel"
     )
-    keep, send = product_call(me, sketch_image, text_feats, groups, n_row, "product_text")
-    own, *sends = sums_call("row", 1, depths, me, [keep, col_swap(send, 1)], "text_cores")
-    own, *sends = sums_call("col", 0, chips, me, [own] + over_depth(sends), "text_depth")
-    mine = last_call(own, over_chips(sends), BF16, "text_plane")
-    parts = [mine] + over_depth([mine] * len(depths))
-    tpanel, gram = gram_call("row", [0] + depths, me, parts, "text_gram")
+    own, *sends = sums_call("col", 0, chips, me, [keep, col_swap(send, 1)], "text_cores")
+    own, sends = own[0], [x[0] for x in sends]
+    mine = last_call(own, [x for x in over_chips(sends)], BF16, "text_plane")
+    tpanel, gram = text_gram_call([mine] + over_depth([mine] * len(depths)))
     gram = last_call(gram, [col_swap(gram, 1)], F32, "text_gram_cores")
     tgrams = [gram] + over_chips([gram] * len(chips))
 

time: 109 us -> 127 us (1.17)
  between operations: 0.84 us -> 14.1 us
  starting transfers between devices: 46 us -> 36.1 us
  Pallas kernels: 21.7 us -> 29.2 us
  local copies, waits for them, and re-layouts: 7.2 us -> 13 us
    ppermute x15 -> x9, waiting for transfers between devices: 16.3 us -> 3.17 us  [per_device(): lax.ppermute(x, 'row', [(i, i ^ s) for i in range(n_row)])]
    all_gather x0 -> x1, waiting for transfers between devices: none -> 12.7 us  [per_device(): image_whole = lax.all_gather(probe_image, 'row', axis=0, tiled=True)]
    ppermute x15 -> x9, starting transfers between devices: 24 us -> 13.8 us  [per_device(): lax.ppermute(x, 'row', [(i, i ^ s) for i in range(n_row)])]
    pallas_call x4 -> x3, Pallas kernels: 9.98 us -> 18.8 us  [the longest x2 18.5 us: panel_call(): pl.pallas_call(functools.partial(panel_kernel, shifts, blocks), in_specs=...]
    unnamed x14 -> x12, local copies, waits for them, and re-layouts: 6.26 us -> 13 us
    ppermute x29 -> x26, waiting for transfers between devices: 17 us -> 17.7 us  [per_device(): lax.ppermute(x, 'col', [(i, i ^ s) for i in range(n_col)])]
    pallas_call x4 -> x3, Pallas kernels: 2.57 us -> 1.97 us  [sums_call(): pl.pallas_call(functools.partial(sums_kernel, which, axis, shifts, len(te...]
    ppermute x29 -> x26, starting transfers between devices: 22.1 us -> 22.3 us  [per_device(): lax.ppermute(x, 'col', [(i, i ^ s) for i in range(n_col)])]
  transfers between devices with their start and end apart: 44 -> 36, of which waited for: 16 -> 15; matrix products, arithmetic and copies ran while one was open for 1% -> 0% of each run, Pallas kernels for 13% -> 17%
where the time goes in v4:
time: 127 us
  starting transfers between devices  36.1 us (28%)
  waiting for transfers between devices  34.2 us (27%)
  Pallas kernels  29.2 us (23%)
  between operations  14.1 us (11%)
  local copies, waits for them, and re-layouts  13 us (10%)
    ppermute x26, starting transfers between devices, per_device(): lax.ppermute(x, 'col', [(i, i ^ s) for i in range(n_col)])  22.3 us
    pallas_call x2, Pallas kernels, panel_call(): pl.pallas_call(functools.partial(panel_kernel, shifts, blocks), in_specs=...  18.5 us
    ppermute x26, waiting for transfers between devices, per_device(): lax.ppermute(x, 'col', [(i, i ^ s) for i in range(n_col)])  17.7 us
    ppermute x9, starting transfers between devices, per_device(): lax.ppermute(x, 'row', [(i, i ^ s) for i in range(n_row)])  13.8 us
    unnamed x12, local copies, waits for them, and re-layouts  13 us
    all_gather x1, waiting for transfers between devices, per_device(): image_whole = lax.all_gather(probe_image, 'row', axis=0, tiled=True)  12.7 us
    pallas_call x1, Pallas kernels, finish_call(): pl.pallas_call(functools.partial(finish_kernel, widths, len(igrams)), in_...  7.39 us
    ppermute x9, waiting for transfers between devices, per_device(): lax.ppermute(x, 'row', [(i, i ^ s) for i in range(n_row)])  3.17 us
  transfers between devices with their start and end apart: 36, of which 15 were waited for; matrix products, arithmetic and copies ran while one was open for 0% of the time, Pallas kernels for 17%

profile of v4, /device:TPU:0, one launch (start us, length us, event | category | flops | bytes accessed | tf_op | source)
XLA Modules:
  0.0 126.7 jit_solution(14790301138379088508)
XLA Ops:
  7.9 3.0 %collective-permute-start = (bf16[512,128]{1,0:T(8,128)(2,1)}, bf16[512,128]{1,0:T(8,128)(2,1)S(1)}, u32[]{:S(2)}, u32[]{:S(2)}) collective-permute-start(bf16[512,128]{1,0:T(8,128)(2,1)} %refs_0_.1), channel_id=1, source_target_pairs={{0,2},{1,3},{2,0},{3,1},{4,6},{5,7},{6,4},{7,5},{8,10},{9,11},{10,... | collective-permute-start | bytes 393224 | tf_op jit(solution)/shard_map/ppermute | solution.py:282
  10.9 1.5 %collective-permute-start.1 = (bf16[512,128]{1,0:T(8,128)(2,1)}, bf16[512,128]{1,0:T(8,128)(2,1)S(1)}, u32[]{:S(2)}, u32[]{:S(2)}) collective-permute-start(bf16[512,128]{1,0:T(8,128)(2,1)} %refs_0_.1), channel_id=1, source_target_pairs={{0,4},{1,5},{2,6},{3,7},{4,0},{5,1},{6,2},{7,3},{8,12},{9,13},{10,... | collective-permute-start | bytes 393224 | tf_op jit(solution)/shard_map/ppermute | solution.py:282
  12.4 2.7 %collective-permute-done.refs_1_ = bf16[512,128]{1,0:T(8,128)(2,1)S(1)} collective-permute-done((bf16[512,128]{1,0:T(8,128)(2,1)}, bf16[512,128]{1,0:T(8,128)(2,1)S(1)}, u32[]{:S(2)}, u32[]{:S(2)}) %collective-permute-start) | collective-permute-done | bytes 131104 | tf_op jit(solution)/shard_map/ppermute | solution.py:282
  15.1 3.8 %collective-permute-done.1.refs_2_ = bf16[512,128]{1,0:T(8,128)(2,1)S(1)} collective-permute-done((bf16[512,128]{1,0:T(8,128)(2,1)}, bf16[512,128]{1,0:T(8,128)(2,1)S(1)}, u32[]{:S(2)}, u32[]{:S(2)}) %collective-permute-start.1) | collective-permute-done | bytes 131104 | tf_op jit(solution)/shard_map/ppermute | solution.py:282
  20.4 3.0 %copy-done = bf16[576,6144]{1,0:T(8,128)(2,1)S(1)} copy-done((bf16[576,6144]{1,0:T(8,128)(2,1)S(1)}, bf16[576,6144]{1,0:T(8,128)(2,1)}, u32[]{:S(2)}) %copy-start) | copy-done | bytes 7077912
  23.5 2.3 %copy-done.2 = bf16[576,4096]{1,0:T(8,128)(2,1)S(1)} copy-done((bf16[576,4096]{1,0:T(8,128)(2,1)S(1)}, bf16[576,4096]{1,0:T(8,128)(2,1)}, u32[]{:S(2)}) %copy-start.2) | copy-done | bytes 4718616
  26.7 9.6 %image_panel.1 = (f32[4,4,192,128]{3,2,1,0:T(8,128)S(1)}, f32[4,4,192,128]{3,2,1,0:T(8,128)}) custom-call(s32[2]{0:T(128)S(1)} %pad_add_fusion.me_ref, bf16[576,4096]{1,0:T(8,128)(2,1)S(1)} %copy-done.2, bf16[576,6144]{1,0:T(8,128)(2,1)S(1)} %copy-done, bf16[512,128]{1,0:T(8,128)(2,1)S(1)} %copy-done.5, bf16[512,128]{1,0:T(8,128)(2,1)S(1)} %collective-permute-done.refs_1_, ...), custom_call_target="tpu_custom_call" | custom-call | flops 1509949440 | bytes 11796480 | tf_op jit(solution)/shard_map/image_panel/pallas_call | solution.py:83
  36.7 12.7 %all-gather.2.cloned.1.call-done.refs_0_ = bf16[6144,128]{1,0:T(8,128)(2,1)} async-done(((bf16[1536,128]{1,0:T(8,128)(2,1)}), bf16[6144,128]{1,0:T(8,128)(2,1)}) %all-gather.2.cloned.1.call-update) | async-done | bytes 1572880 | tf_op jit(solution)/shard_map/all_gather | solution.py:297
  49.4 3.0 %copy-done.1 = bf16[576,6144]{1,0:T(8,128)(2,1)S(1)} copy-done((bf16[576,6144]{1,0:T(8,128)(2,1)S(1)}, bf16[576,6144]{1,0:T(8,128)(2,1)}, u32[]{:S(2)}) %copy-start.1) | copy-done | bytes 7077912
  52.4 2.3 %copy-done.3 = bf16[576,4096]{1,0:T(8,128)(2,1)S(1)} copy-done((bf16[576,4096]{1,0:T(8,128)(2,1)S(1)}, bf16[576,4096]{1,0:T(8,128)(2,1)}, u32[]{:S(2)}) %copy-start.3) | copy-done | bytes 4718616
  54.7 1.4 %copy-done.4 = bf16[6144,128]{1,0:T(8,128)(2,1)S(1)} copy-done((bf16[6144,128]{1,0:T(8,128)(2,1)S(1)}, bf16[6144,128]{1,0:T(8,128)(2,1)}, u32[]{:S(2)}) %copy-start.4) | copy-done | bytes 1572888
  56.1 8.9 %text_panel.1 = (f32[4,1,512,128]{3,2,1,0:T(8,128)S(1)}, f32[4,1,512,128]{3,2,1,0:T(8,128)S(1)}) custom-call(s32[2]{0:T(128)S(1)} %pad_add_fusion.me_ref, bf16[576,6144]{1,0:T(8,128)(2,1)S(1)} %copy-done.1, bf16[576,4096]{1,0:T(8,128)(2,1)S(1)} %copy-done.3, bf16[6144,128]{1,0:T(8,128)(2,1)S(1)} %copy-done.4), custom_call_target="tpu_custom_call" | custom-call | flops 1509949440 | bytes 11796480 | tf_op jit(solution)/shard_map/text_panel/pallas_call | solution.py:83
  65.9 1.5 %collective-permute-start.8 = (bf16[4,192,128]{2,1,0:T(8,128)(2,1)S(1)}, bf16[4,192,128]{2,1,0:T(8,128)(2,1)S(1)}, u32[]{:S(2)}, u32[]{:S(2)}) collective-permute-start(bf16[4,192,128]{2,1,0:T(8,128)(2,1)S(1)} %get-tuple-element.25), channel_id=1, source_target_pairs={{0,2},{1,3},{2,0},{3,1},{4,6},{5,7},{6,4},{7,5},{8,10},{9,11},{10,... | collective-permute-start | bytes 589832 | tf_op jit(solution)/shard_map/ppermute | solution.py:282
  67.4 1.5 %collective-permute-start.9 = (bf16[4,192,128]{2,1,0:T(8,128)(2,1)S(1)}, bf16[4,192,128]{2,1,0:T(8,128)(2,1)S(1)}, u32[]{:S(2)}, u32[]{:S(2)}) collective-permute-start(bf16[4,192,128]{2,1,0:T(8,128)(2,1)S(1)} %get-tuple-element.26), channel_id=1, source_target_pairs={{0,4},{1,5},{2,6},{3,7},{4,0},{5,1},{6,2},{7,3},{8,12},{9,13},{10,... | collective-permute-start | bytes 589832 | tf_op jit(solution)/shard_map/ppermute | solution.py:282
  70.1 1.5 %collective-permute-start.22 = (bf16[512,128]{1,0:T(8,128)(2,1)S(1)}, bf16[512,128]{1,0:T(8,128)(2,1)S(1)}, u32[]{:S(2)}, u32[]{:S(2)}) collective-permute-start(bf16[512,128]{1,0:T(8,128)(2,1)S(1)} %bitcast.9), channel_id=1, source_target_pairs={{0,2},{1,3},{2,0},{3,1},{4,6},{5,7},{6,4},{7,5},{8,10},{9,11},{10,... | collective-permute-start | bytes 393224 | tf_op jit(solution)/shard_map/ppermute | solution.py:282
  71.6 1.5 %collective-permute-start.23 = (bf16[512,128]{1,0:T(8,128)(2,1)S(1)}, bf16[512,128]{1,0:T(8,128)(2,1)S(1)}, u32[]{:S(2)}, u32[]{:S(2)}) collective-permute-start(bf16[512,128]{1,0:T(8,128)(2,1)S(1)} %bitcast.8), channel_id=1, source_target_pairs={{0,4},{1,5},{2,6},{3,7},{4,0},{5,1},{6,2},{7,3},{8,12},{9,13},{10,... | collective-permute-start | bytes 393224 | tf_op jit(solution)/shard_map/ppermute | solution.py:282
  73.6 2.4 %collective-permute-start.24 = (bf16[512,128]{1,0:T(8,128)(2,1)S(1)}, bf16[512,128]{1,0:T(8,128)(2,1)S(1)}, u32[]{:S(2)}, u32[]{:S(2)}) collective-permute-start(bf16[512,128]{1,0:T(8,128)(2,1)S(1)} %bitcast.7), channel_id=1, source_target_pairs={{0,6},{1,7},{2,4},{3,5},{4,2},{5,3},{6,0},{7,1},{8,14},{9,15},{10,... | collective-permute-start | bytes 393224 | tf_op jit(solution)/shard_map/ppermute | solution.py:282
  76.0 3.4 %collective-permute-done.9.refs_2_ = bf16[4,192,128]{2,1,0:T(8,128)(2,1)S(1)} collective-permute-done((bf16[4,192,128]{2,1,0:T(8,128)(2,1)S(1)}, bf16[4,192,128]{2,1,0:T(8,128)(2,1)S(1)}, u32[]{:S(2)}, u32[]{:S(2)}) %collective-permute-start.9) | collective-permute-done | bytes 196640 | tf_op jit(solution)/shard_map/ppermute | solution.py:282
  80.5 1.4 %collective-permute-start.12 = (bf16[192,128]{1,0:T(8,128)(2,1)S(1)}, bf16[192,128]{1,0:T(8,128)(2,1)S(1)}, u32[]{:S(2)}, u32[]{:S(2)}) collective-permute-start(bf16[192,128]{1,0:T(8,128)(2,1)S(1)} %get-tuple-element.30), channel_id=1, source_target_pairs={{0,16},{8,24},{16,0},{24,8},{1,17},{9,25},{17,1},{25,9},{2,18},{10... | collective-permute-start | bytes 147464 | tf_op jit(solution)/shard_map/ppermute | solution.py:283
  81.9 2.6 %collective-permute-start.13 = (bf16[192,128]{1,0:T(8,128)(2,1)S(1)}, bf16[192,128]{1,0:T(8,128)(2,1)S(1)}, u32[]{:S(2)}, u32[]{:S(2)}) collective-permute-start(bf16[192,128]{1,0:T(8,128)(2,1)S(1)} %get-tuple-element.31), channel_id=1, source_target_pairs={{0,24},{8,16},{16,8},{24,0},{1,25},{9,17},{17,9},{25,1},{2,26},{10... | collective-permute-start | bytes 147464 | tf_op jit(solution)/shard_map/ppermute | solution.py:283
  84.8 1.6 %collective-permute-start.26 = (bf16[512,128]{1,0:T(8,128)(2,1)S(1)}, bf16[512,128]{1,0:T(8,128)(2,1)S(1)}, u32[]{:S(2)}, u32[]{:S(2)}) collective-permute-start(bf16[512,128]{1,0:T(8,128)(2,1)S(1)} %text_plane.1.refs_0_), channel_id=1, source_target_pairs={{0,16},{8,24},{16,0},{24,8},{1,17},{9,25},{17,1},{25,9},{2,18},{10... | collective-permute-start | bytes 393224 | tf_op jit(solution)/shard_map/ppermute | solution.py:283
  86.4 2.0 %collective-permute-done.13.refs_2_ = bf16[192,128]{1,0:T(8,128)(2,1)S(1)} collective-permute-done((bf16[192,128]{1,0:T(8,128)(2,1)S(1)}, bf16[192,128]{1,0:T(8,128)(2,1)S(1)}, u32[]{:S(2)}, u32[]{:S(2)}) %collective-permute-start.13) | collective-permute-done | bytes 49184 | tf_op jit(solution)/shard_map/ppermute | solution.py:283
  88.9 3.0 %collective-permute-start.27 = (bf16[512,128]{1,0:T(8,128)(2,1)S(1)}, bf16[512,128]{1,0:T(8,128)(2,1)S(1)}, u32[]{:S(2)}, u32[]{:S(2)}) collective-permute-start(bf16[512,128]{1,0:T(8,128)(2,1)S(1)} %text_plane.1.refs_0_), channel_id=1, source_target_pairs={{0,24},{8,16},{16,8},{24,0},{1,25},{9,17},{17,9},{25,1},{2,26},{10... | collective-permute-start | bytes 393224 | tf_op jit(solution)/shard_map/ppermute | solution.py:283
  93.1 1.5 %collective-permute-start.16 = (bf16[192,128]{1,0:T(8,128)(2,1)S(1)}, bf16[192,128]{1,0:T(8,128)(2,1)S(1)}, u32[]{:S(2)}, u32[]{:S(2)}) collective-permute-start(bf16[192,128]{1,0:T(8,128)(2,1)S(1)} %image_depth.1.refs_0_), channel_id=1, source_target_pairs={{0,6},{1,7},{2,4},{3,5},{4,2},{5,3},{6,0},{7,1},{8,14},{9,15},{10,... | collective-permute-start | bytes 147464 | tf_op jit(solution)/shard_map/ppermute | solution.py:282
  94.6 1.4 %collective-permute-done.15.refs_2_ = bf16[192,128]{1,0:T(8,128)(2,1)S(1)} collective-permute-done((bf16[192,128]{1,0:T(8,128)(2,1)S(1)}, bf16[192,128]{1,0:T(8,128)(2,1)S(1)}, u32[]{:S(2)}, u32[]{:S(2)}) %collective-permute-start.15) | collective-permute-done | bytes 49184 | tf_op jit(solution)/shard_map/ppermute | solution.py:282
  95.9 2.1 %collective-permute-done.16.refs_3_ = bf16[192,128]{1,0:T(8,128)(2,1)S(1)} collective-permute-done((bf16[192,128]{1,0:T(8,128)(2,1)S(1)}, bf16[192,128]{1,0:T(8,128)(2,1)S(1)}, u32[]{:S(2)}, u32[]{:S(2)}) %collective-permute-start.16) | collective-permute-done | bytes 49184 | tf_op jit(solution)/shard_map/ppermute | solution.py:282
  101.1 2.6 %collective-permute-start.29 = (f32[128,128]{1,0:T(8,128)S(1)}, f32[128,128]{1,0:T(8,128)S(1)}, u32[]{:S(2)}, u32[]{:S(2)}) collective-permute-start(f32[128,128]{1,0:T(8,128)S(1)} %get-tuple-element.40.refs_0_), channel_id=1, source_target_pairs={{0,16},{8,24},{16,0},{24,8},{1,17},{9,25},{17,1},{25,9},{2,18},{10... | collective-permute-start | bytes 196616 | tf_op jit(solution)/shard_map/ppermute | solution.py:283
  103.8 1.4 %collective-permute-start.30 = (f32[128,128]{1,0:T(8,128)S(1)}, f32[128,128]{1,0:T(8,128)S(1)}, u32[]{:S(2)}, u32[]{:S(2)}) collective-permute-start(f32[128,128]{1,0:T(8,128)S(1)} %get-tuple-element.40.refs_0_), channel_id=1, source_target_pairs={{0,24},{8,16},{16,8},{24,0},{1,25},{9,17},{17,9},{25,1},{2,26},{10... | collective-permute-start | bytes 196616 | tf_op jit(solution)/shard_map/ppermute | solution.py:283
  105.2 1.6 %collective-permute-start.32 = (f32[128,128]{1,0:T(8,128)S(1)}, f32[128,128]{1,0:T(8,128)S(1)}, u32[]{:S(2)}, u32[]{:S(2)}) collective-permute-start(f32[128,128]{1,0:T(8,128)S(1)} %text_gram_cores.1.refs_4_), channel_id=1, source_target_pairs={{0,2},{1,3},{2,0},{3,1},{4,6},{5,7},{6,4},{7,5},{8,10},{9,11},{10,... | collective-permute-start | bytes 196616 | tf_op jit(solution)/shard_map/ppermute | solution.py:282
  107.3 1.5 %collective-permute-start.34 = (f32[128,128]{1,0:T(8,128)S(1)}, f32[128,128]{1,0:T(8,128)S(1)}, u32[]{:S(2)}, u32[]{:S(2)}) collective-permute-start(f32[128,128]{1,0:T(8,128)S(1)} %text_gram_cores.1.refs_4_), channel_id=1, source_target_pairs={{0,6},{1,7},{2,4},{3,5},{4,2},{5,3},{6,0},{7,1},{8,14},{9,15},{10,... | collective-permute-start | bytes 196616 | tf_op jit(solution)/shard_map/ppermute | solution.py:282
  109.9 1.4 %collective-permute-done.33.refs_6_ = f32[128,128]{1,0:T(8,128)S(1)} collective-permute-done((f32[128,128]{1,0:T(8,128)S(1)}, f32[128,128]{1,0:T(8,128)S(1)}, u32[]{:S(2)}, u32[]{:S(2)}) %collective-permute-start.33) | collective-permute-done | bytes 65568 | tf_op jit(solution)/shard_map/ppermute | solution.py:282
  112.5 7.4 %finish.1 = (f32[1536,128]{1,0:T(8,128)}, f32[512,128]{1,0:T(8,128)}) custom-call(bf16[8,192,128]{2,1,0:T(8,128)(2,1)S(1)} %get-tuple-element.32.ipanel, bf16[1,512,128]{2,1,0:T(8,128)(2,1)S(1)} %get-tuple-element.39.tpanel, f32[128,128]{1,0:T(8,128)S(1)} %get-tuple-element.40.refs_0_, f32[128,128]{1,0:T(8,128)S(1)} %collective-permute-done.28.refs_1_, ...), custom_call_target="tpu_custom_call" | custom-call | flops 10000000000 | bytes 1179648 | tf_op jit(solution)/shard_map/finish/pallas_call | solution.py:268
  (65 shorter events, 15.3 us)
Async XLA Ops:
  7.2 42.2 %all-gather.2.cloned.1.call-start = ((), (), s32[]{:S(2)}) async-start(), calls=%async_computation | async-start | bytes 1966080 | tf_op jit(solution)/shard_map/all_gather | solution.py:297
  7.9 7.2 %collective-permute-start = (bf16[512,128]{1,0:T(8,128)(2,1)}, bf16[512,128]{1,0:T(8,128)(2,1)S(1)}, u32[]{:S(2)}, u32[]{:S(2)}) collective-permute-start(bf16[512,128]{1,0:T(8,128)(2,1)} %refs_0_.1), channel_id=1, source_target_pairs={{0,2},{1,3},{2,0},{3,1},{4,6},{5,7},{6,4},{7,5},{8,10},{9,11},{10,... | collective-permute-start | bytes 393224 | tf_op jit(solution)/shard_map/ppermute | solution.py:282
  10.9 8.0 %collective-permute-start.1 = (bf16[512,128]{1,0:T(8,128)(2,1)}, bf16[512,128]{1,0:T(8,128)(2,1)S(1)}, u32[]{:S(2)}, u32[]{:S(2)}) collective-permute-start(bf16[512,128]{1,0:T(8,128)(2,1)} %refs_0_.1), channel_id=1, source_target_pairs={{0,4},{1,5},{2,6},{3,7},{4,0},{5,1},{6,2},{7,3},{8,12},{9,13},{10,... | collective-permute-start | bytes 393224 | tf_op jit(solution)/shard_map/ppermute | solution.py:282
  12.4 6.5 %collective-permute-start.2 = (bf16[512,128]{1,0:T(8,128)(2,1)}, bf16[512,128]{1,0:T(8,128)(2,1)S(1)}, u32[]{:S(2)}, u32[]{:S(2)}) collective-permute-start(bf16[512,128]{1,0:T(8,128)(2,1)} %refs_0_.1), channel_id=1, source_target_pairs={{0,6},{1,7},{2,4},{3,5},{4,2},{5,3},{6,0},{7,1},{8,14},{9,15},{10,... | collective-permute-start | bytes 393224 | tf_op jit(solution)/shard_map/ppermute | solution.py:282
  12.4 7.0 %collective-permute-start.3 = (bf16[512,128]{1,0:T(8,128)(2,1)}, bf16[512,128]{1,0:T(8,128)(2,1)S(1)}, u32[]{:S(2)}, u32[]{:S(2)}) collective-permute-start(bf16[512,128]{1,0:T(8,128)(2,1)} %refs_0_.1), channel_id=1, source_target_pairs={{0,1},{1,0},{2,3},{3,2},{4,5},{5,4},{6,7},{7,6},{8,9},{9,8},{10,11... | collective-permute-start | bytes 393224 | tf_op jit(solution)/shard_map/ppermute | solution.py:282
  15.1 4.4 %collective-permute-start.4 = (bf16[512,128]{1,0:T(8,128)(2,1)S(1)}, bf16[512,128]{1,0:T(8,128)(2,1)S(1)}, u32[]{:S(2)}, u32[]{:S(2)}) collective-permute-start(bf16[512,128]{1,0:T(8,128)(2,1)S(1)} %collective-permute-done.refs_1_), channel_id=1, source_target_pairs={{0,1},{1,0},{2,3},{3,2},{4,5},{5,4},{6,7},{7,6},{8,9},{9,8},{10,11... | collective-permute-start | bytes 393224 | tf_op jit(solution)/shard_map/ppermute | solution.py:282
  18.9 1.5 %collective-permute-start.6 = (bf16[512,128]{1,0:T(8,128)(2,1)S(1)}, bf16[512,128]{1,0:T(8,128)(2,1)S(1)}, u32[]{:S(2)}, u32[]{:S(2)}) collective-permute-start(bf16[512,128]{1,0:T(8,128)(2,1)S(1)} %collective-permute-done.2.refs_3_), channel_id=1, source_target_pairs={{0,1},{1,0},{2,3},{3,2},{4,5},{5,4},{6,7},{7,6},{8,9},{9,8},{10,11... | collective-permute-start | bytes 393224 | tf_op jit(solution)/shard_map/ppermute | solution.py:282
  36.3 28.8 %collective-permute-start.7 = (f32[4,4,192,128]{3,2,1,0:T(8,128)}, f32[4,4,192,128]{3,2,1,0:T(8,128)S(1)}, u32[]{:S(2)}, u32[]{:S(2)}) collective-permute-start(f32[4,4,192,128]{3,2,1,0:T(8,128)} %get-tuple-element.23), channel_id=1, source_target_pairs={{0,1},{1,0},{2,3},{3,2},{4,5},{5,4},{6,7},{7,6},{8,9},{9,8},{10,11... | collective-permute-start | bytes 4718600 | tf_op jit(solution)/shard_map/ppermute | solution.py:282
  65.1 4.4 %collective-permute-start.21 = (f32[4,1,512,128]{3,2,1,0:T(8,128)S(1)}, f32[4,1,512,128]{3,2,1,0:T(8,128)S(1)}, u32[]{:S(2)}, u32[]{:S(2)}) collective-permute-start(f32[4,1,512,128]{3,2,1,0:T(8,128)S(1)} %get-tuple-element.34), channel_id=1, source_target_pairs={{0,1},{1,0},{2,3},{3,2},{4,5},{5,4},{6,7},{7,6},{8,9},{9,8},{10,11... | collective-permute-start | bytes 3145736 | tf_op jit(solution)/shard_map/ppermute | solution.py:282
  65.9 7.8 %collective-permute-start.8 = (bf16[4,192,128]{2,1,0:T(8,128)(2,1)S(1)}, bf16[4,192,128]{2,1,0:T(8,128)(2,1)S(1)}, u32[]{:S(2)}, u32[]{:S(2)}) collective-permute-start(bf16[4,192,128]{2,1,0:T(8,128)(2,1)S(1)} %get-tuple-element.25), channel_id=1, source_target_pairs={{0,2},{1,3},{2,0},{3,1},{4,6},{5,7},{6,4},{7,5},{8,10},{9,11},{10,... | collective-permute-start | bytes 589832 | tf_op jit(solution)/shard_map/ppermute | solution.py:282
  67.4 12.0 %collective-permute-start.9 = (bf16[4,192,128]{2,1,0:T(8,128)(2,1)S(1)}, bf16[4,192,128]{2,1,0:T(8,128)(2,1)S(1)}, u32[]{:S(2)}, u32[]{:S(2)}) collective-permute-start(bf16[4,192,128]{2,1,0:T(8,128)(2,1)S(1)} %get-tuple-element.26), channel_id=1, source_target_pairs={{0,4},{1,5},{2,6},{3,7},{4,0},{5,1},{6,2},{7,3},{8,12},{9,13},{10,... | collective-permute-start | bytes 589832 | tf_op jit(solution)/shard_map/ppermute | solution.py:282
  68.9 10.5 %collective-permute-start.10 = (bf16[4,192,128]{2,1,0:T(8,128)(2,1)S(1)}, bf16[4,192,128]{2,1,0:T(8,128)(2,1)S(1)}, u32[]{:S(2)}, u32[]{:S(2)}) collective-permute-start(bf16[4,192,128]{2,1,0:T(8,128)(2,1)S(1)} %get-tuple-element.27), channel_id=1, source_target_pairs={{0,6},{1,7},{2,4},{3,5},{4,2},{5,3},{6,0},{7,1},{8,14},{9,15},{10,... | collective-permute-start | bytes 589832 | tf_op jit(solution)/shard_map/ppermute | solution.py:282
  70.1 11.8 %collective-permute-start.22 = (bf16[512,128]{1,0:T(8,128)(2,1)S(1)}, bf16[512,128]{1,0:T(8,128)(2,1)S(1)}, u32[]{:S(2)}, u32[]{:S(2)}) collective-permute-start(bf16[512,128]{1,0:T(8,128)(2,1)S(1)} %bitcast.9), channel_id=1, source_target_pairs={{0,2},{1,3},{2,0},{3,1},{4,6},{5,7},{6,4},{7,5},{8,10},{9,11},{10,... | collective-permute-start | bytes 393224 | tf_op jit(solution)/shard_map/ppermute | solution.py:282
  71.6 12.8 %collective-permute-start.23 = (bf16[512,128]{1,0:T(8,128)(2,1)S(1)}, bf16[512,128]{1,0:T(8,128)(2,1)S(1)}, u32[]{:S(2)}, u32[]{:S(2)}) collective-permute-start(bf16[512,128]{1,0:T(8,128)(2,1)S(1)} %bitcast.8), channel_id=1, source_target_pairs={{0,4},{1,5},{2,6},{3,7},{4,0},{5,1},{6,2},{7,3},{8,12},{9,13},{10,... | collective-permute-start | bytes 393224 | tf_op jit(solution)/shard_map/ppermute | solution.py:282
  73.6 10.8 %collective-permute-start.24 = (bf16[512,128]{1,0:T(8,128)(2,1)S(1)}, bf16[512,128]{1,0:T(8,128)(2,1)S(1)}, u32[]{:S(2)}, u32[]{:S(2)}) collective-permute-start(bf16[512,128]{1,0:T(8,128)(2,1)S(1)} %bitcast.7), channel_id=1, source_target_pairs={{0,6},{1,7},{2,4},{3,5},{4,2},{5,3},{6,0},{7,1},{8,14},{9,15},{10,... | collective-permute-start | bytes 393224 | tf_op jit(solution)/shard_map/ppermute | solution.py:282
  80.0 6.4 %collective-permute-start.11 = (bf16[192,128]{1,0:T(8,128)(2,1)S(1)}, bf16[192,128]{1,0:T(8,128)(2,1)S(1)}, u32[]{:S(2)}, u32[]{:S(2)}) collective-permute-start(bf16[192,128]{1,0:T(8,128)(2,1)S(1)} %get-tuple-element.29), channel_id=1, source_target_pairs={{0,8},{8,0},{16,24},{24,16},{1,9},{9,1},{17,25},{25,17},{2,10},{10... | collective-permute-start | bytes 147464 | tf_op jit(solution)/shard_map/ppermute | solution.py:283
  80.5 5.9 %collective-permute-start.12 = (bf16[192,128]{1,0:T(8,128)(2,1)S(1)}, bf16[192,128]{1,0:T(8,128)(2,1)S(1)}, u32[]{:S(2)}, u32[]{:S(2)}) collective-permute-start(bf16[192,128]{1,0:T(8,128)(2,1)S(1)} %get-tuple-element.30), channel_id=1, source_target_pairs={{0,16},{8,24},{16,0},{24,8},{1,17},{9,25},{17,1},{25,9},{2,18},{10... | collective-permute-start | bytes 147464 | tf_op jit(solution)/shard_map/ppermute | solution.py:283
  81.9 6.5 %collective-permute-start.13 = (bf16[192,128]{1,0:T(8,128)(2,1)S(1)}, bf16[192,128]{1,0:T(8,128)(2,1)S(1)}, u32[]{:S(2)}, u32[]{:S(2)}) collective-permute-start(bf16[192,128]{1,0:T(8,128)(2,1)S(1)} %get-tuple-element.31), channel_id=1, source_target_pairs={{0,24},{8,16},{16,8},{24,0},{1,25},{9,17},{17,9},{25,1},{2,26},{10... | collective-permute-start | bytes 147464 | tf_op jit(solution)/shard_map/ppermute | solution.py:283
  84.5 13.6 %collective-permute-start.25 = (bf16[512,128]{1,0:T(8,128)(2,1)S(1)}, bf16[512,128]{1,0:T(8,128)(2,1)S(1)}, u32[]{:S(2)}, u32[]{:S(2)}) collective-permute-start(bf16[512,128]{1,0:T(8,128)(2,1)S(1)} %text_plane.1.refs_0_), channel_id=1, source_target_pairs={{0,8},{8,0},{16,24},{24,16},{1,9},{9,1},{17,25},{25,17},{2,10},{10... | collective-permute-start | bytes 393224 | tf_op jit(solution)/shard_map/ppermute | solution.py:283
  84.8 13.8 %collective-permute-start.26 = (bf16[512,128]{1,0:T(8,128)(2,1)S(1)}, bf16[512,128]{1,0:T(8,128)(2,1)S(1)}, u32[]{:S(2)}, u32[]{:S(2)}) collective-permute-start(bf16[512,128]{1,0:T(8,128)(2,1)S(1)} %text_plane.1.refs_0_), channel_id=1, source_target_pairs={{0,16},{8,24},{16,0},{24,8},{1,17},{9,25},{17,1},{25,9},{2,18},{10... | collective-permute-start | bytes 393224 | tf_op jit(solution)/shard_map/ppermute | solution.py:283
  88.4 4.7 %collective-permute-start.14 = (bf16[192,128]{1,0:T(8,128)(2,1)S(1)}, bf16[192,128]{1,0:T(8,128)(2,1)S(1)}, u32[]{:S(2)}, u32[]{:S(2)}) collective-permute-start(bf16[192,128]{1,0:T(8,128)(2,1)S(1)} %image_depth.1.refs_0_), channel_id=1, source_target_pairs={{0,2},{1,3},{2,0},{3,1},{4,6},{5,7},{6,4},{7,5},{8,10},{9,11},{10,... | collective-permute-start | bytes 147464 | tf_op jit(solution)/shard_map/ppermute | solution.py:282
  88.9 9.8 %collective-permute-start.27 = (bf16[512,128]{1,0:T(8,128)(2,1)S(1)}, bf16[512,128]{1,0:T(8,128)(2,1)S(1)}, u32[]{:S(2)}, u32[]{:S(2)}) collective-permute-start(bf16[512,128]{1,0:T(8,128)(2,1)S(1)} %text_plane.1.refs_0_), channel_id=1, source_target_pairs={{0,24},{8,16},{16,8},{24,0},{1,25},{9,17},{17,9},{25,1},{2,26},{10... | collective-permute-start | bytes 393224 | tf_op jit(solution)/shard_map/ppermute | solution.py:283
  91.8 4.1 %collective-permute-start.15 = (bf16[192,128]{1,0:T(8,128)(2,1)S(1)}, bf16[192,128]{1,0:T(8,128)(2,1)S(1)}, u32[]{:S(2)}, u32[]{:S(2)}) collective-permute-start(bf16[192,128]{1,0:T(8,128)(2,1)S(1)} %image_depth.1.refs_0_), channel_id=1, source_target_pairs={{0,4},{1,5},{2,6},{3,7},{4,0},{5,1},{6,2},{7,3},{8,12},{9,13},{10,... | collective-permute-start | bytes 147464 | tf_op jit(solution)/shard_map/ppermute | solution.py:282
  93.1 5.0 %collective-permute-start.16 = (bf16[192,128]{1,0:T(8,128)(2,1)S(1)}, bf16[192,128]{1,0:T(8,128)(2,1)S(1)}, u32[]{:S(2)}, u32[]{:S(2)}) collective-permute-start(bf16[192,128]{1,0:T(8,128)(2,1)S(1)} %image_depth.1.refs_0_), channel_id=1, source_target_pairs={{0,6},{1,7},{2,4},{3,5},{4,2},{5,3},{6,0},{7,1},{8,14},{9,15},{10,... | collective-permute-start | bytes 147464 | tf_op jit(solution)/shard_map/ppermute | solution.py:282
  95.9 3.5 %collective-permute-start.17 = (bf16[192,128]{1,0:T(8,128)(2,1)S(1)}, bf16[192,128]{1,0:T(8,128)(2,1)S(1)}, u32[]{:S(2)}, u32[]{:S(2)}) collective-permute-start(bf16[192,128]{1,0:T(8,128)(2,1)S(1)} %image_depth.1.refs_0_), channel_id=1, source_target_pairs={{0,1},{1,0},{2,3},{3,2},{4,5},{5,4},{6,7},{7,6},{8,9},{9,8},{10,11... | collective-permute-start | bytes 147464 | tf_op jit(solution)/shard_map/ppermute | solution.py:282
  98.9 6.2 %collective-permute-start.31 = (f32[128,128]{1,0:T(8,128)S(1)}, f32[128,128]{1,0:T(8,128)S(1)}, u32[]{:S(2)}, u32[]{:S(2)}) collective-permute-start(f32[128,128]{1,0:T(8,128)S(1)} %get-tuple-element.41.own_ref), channel_id=1, source_target_pairs={{0,1},{1,0},{2,3},{3,2},{4,5},{5,4},{6,7},{7,6},{8,9},{9,8},{10,11... | collective-permute-start | bytes 196616 | tf_op jit(solution)/shard_map/ppermute | solution.py:282
  100.7 6.6 %collective-permute-start.28 = (f32[128,128]{1,0:T(8,128)S(1)}, f32[128,128]{1,0:T(8,128)S(1)}, u32[]{:S(2)}, u32[]{:S(2)}) collective-permute-start(f32[128,128]{1,0:T(8,128)S(1)} %get-tuple-element.40.refs_0_), channel_id=1, source_target_pairs={{0,8},{8,0},{16,24},{24,16},{1,9},{9,1},{17,25},{25,17},{2,10},{10... | collective-permute-start | bytes 196616 | tf_op jit(solution)/shard_map/ppermute | solution.py:283
  101.1 7.8 %collective-permute-start.29 = (f32[128,128]{1,0:T(8,128)S(1)}, f32[128,128]{1,0:T(8,128)S(1)}, u32[]{:S(2)}, u32[]{:S(2)}) collective-permute-start(f32[128,128]{1,0:T(8,128)S(1)} %get-tuple-element.40.refs_0_), channel_id=1, source_target_pairs={{0,16},{8,24},{16,0},{24,8},{1,17},{9,25},{17,1},{25,9},{2,18},{10... | collective-permute-start | bytes 196616 | tf_op jit(solution)/shard_map/ppermute | solution.py:283
  103.8 6.2 %collective-permute-start.30 = (f32[128,128]{1,0:T(8,128)S(1)}, f32[128,128]{1,0:T(8,128)S(1)}, u32[]{:S(2)}, u32[]{:S(2)}) collective-permute-start(f32[128,128]{1,0:T(8,128)S(1)} %get-tuple-element.40.refs_0_), channel_id=1, source_target_pairs={{0,24},{8,16},{16,8},{24,0},{1,25},{9,17},{17,9},{25,1},{2,26},{10... | collective-permute-start | bytes 196616 | tf_op jit(solution)/shard_map/ppermute | solution.py:283
  105.2 4.7 %collective-permute-start.32 = (f32[128,128]{1,0:T(8,128)S(1)}, f32[128,128]{1,0:T(8,128)S(1)}, u32[]{:S(2)}, u32[]{:S(2)}) collective-permute-start(f32[128,128]{1,0:T(8,128)S(1)} %text_gram_cores.1.refs_4_), channel_id=1, source_target_pairs={{0,2},{1,3},{2,0},{3,1},{4,6},{5,7},{6,4},{7,5},{8,10},{9,11},{10,... | collective-permute-start | bytes 196616 | tf_op jit(solution)/shard_map/ppermute | solution.py:282
  106.8 4.6 %collective-permute-start.33 = (f32[128,128]{1,0:T(8,128)S(1)}, f32[128,128]{1,0:T(8,128)S(1)}, u32[]{:S(2)}, u32[]{:S(2)}) collective-permute-start(f32[128,128]{1,0:T(8,128)S(1)} %text_gram_cores.1.refs_4_), channel_id=1, source_target_pairs={{0,4},{1,5},{2,6},{3,7},{4,0},{5,1},{6,2},{7,3},{8,12},{9,13},{10,... | collective-permute-start | bytes 196616 | tf_op jit(solution)/shard_map/ppermute | solution.py:282
  107.3 5.2 %collective-permute-start.34 = (f32[128,128]{1,0:T(8,128)S(1)}, f32[128,128]{1,0:T(8,128)S(1)}, u32[]{:S(2)}, u32[]{:S(2)}) collective-permute-start(f32[128,128]{1,0:T(8,128)S(1)} %text_gram_cores.1.refs_4_), channel_id=1, source_target_pairs={{0,6},{1,7},{2,4},{3,5},{4,2},{5,3},{6,0},{7,1},{8,14},{9,15},{10,... | collective-permute-start | bytes 196616 | tf_op jit(solution)/shard_map/ppermute | solution.py:282
  (10 other events, 18.4 us)
Sparse Core Ops, SparseCore 0:
  9.6 39.7 all-gather.1

commit v5 on v4

--- a/solution.py
+++ b/solution.py
@@ -13,6 +13,7 @@
 VMEM = pl.BlockSpec(memory_space=pltpu.VMEM)
 SMEM = pl.BlockSpec(memory_space=pltpu.SMEM)
 LIMIT = 32 * 1024 * 1024
+PANEL_LIMIT = 46 * 1024 * 1024
 
 
 def sds(shape, dtype):
@@ -27,71 +28,70 @@
     return pl.CostEstimate(flops=int(flops), bytes_accessed=int(nbytes), transcendentals=0)
 
 
-def panel_kernel(shifts, n_out, me_ref, a_hbm, b_hbm, *refs):
-    n = len(shifts)
+def text_columns(shifts, depth):
+    return lambda me_ref: [pl.multiple_of((me_ref[0] ^ s) * depth, depth) for s in shifts]
+
+
+def image_columns(order, depth):
+    def columns(me_ref):
+        core = me_ref[0] % 2
+        out = []
+        for even, odd, half in order:
+            at = (me_ref[1] ^ (even + core * (odd - even))) * depth
+            if half is not None:
+                at = pl.multiple_of(at + (core ^ half) * (depth // 2), depth // 2)
+            else:
+                at = pl.multiple_of(at, depth)
+            out.append(at)
+        return out
+
+    return columns
+
+
+def panel_kernel(columns, n, n_out, me_ref, a_hbm, b_hbm, *refs):
     parts, (keep_ref, send_ref, a_ref, b_ref, a_sem, b_sem) = refs[:n], refs[n:]
     core = me_ref[0] % 2
-    depth = parts[0].shape[0]
     cols = b_ref.shape[1] // n_out // 2
-
-    def column(i):
-        if n == 1:
-            return 0
-        return pl.multiple_of((me_ref[0] ^ shifts[i]) * depth, depth)
-
-    def copies():
-        out = []
-        pieces = max(1, depth // 1024)
-        for i in range(n):
-            for j in range(pieces):
-                at = pl.ds(column(i) + j * (depth // pieces), depth // pieces)
-                out.append(pltpu.make_async_copy(a_hbm.at[:, at], a_ref.at[:, at], a_sem.at[i * pieces + j]))
-        wide = b_ref.shape[1] // n_out
-        for i in range(n_out):
-            at = pl.ds(i * wide, wide)
-            out.append(pltpu.make_async_copy(b_hbm.at[:, at], b_ref.at[:, at], b_sem.at[i]))
-        return out
-
-    moves = copies()
+    moves = []
+    spans = [pl.ds(at, part.shape[0]) for at, part in zip(columns(me_ref), parts)]
+    for i, span in enumerate(spans):
+        moves.append(pltpu.make_async_copy(a_hbm.at[:, span], a_ref.at[:, span], a_sem.at[i]))
+    for i in range(n_out):
+        span = pl.ds(2 * i * cols, 2 * cols)
+        moves.append(pltpu.make_async_copy(b_hbm.at[:, span], b_ref.at[:, span], b_sem.at[i]))
     for move in moves:
         move.start()
     total = None
-    pieces = max(1, depth // 1024)
-    step = depth // pieces
-    for i in range(n):
-        for j in range(pieces):
-            moves[i * pieces + j].wait()
-            at = pl.ds(column(i) + j * step, step)
-            weights = parts[i][j * step : j * step + step, :]
-            term = jnp.dot(a_ref[:, at], weights, preferred_element_type=F32)
-            total = term if total is None else total + term
+    for i, span in enumerate(spans):
+        moves[i].wait()
+        term = jnp.dot(a_ref[:, span], parts[i][...], preferred_element_type=F32)
+        total = term if total is None else total + term
     sketch = total.T.astype(BF16)
     for i in range(n_out):
-        moves[n * pieces + i].wait()
+        moves[n + i].wait()
         for rel, ref in ((0, keep_ref), (1, send_ref)):
             at = pl.multiple_of((2 * i + (core ^ rel)) * cols, cols)
             out = jnp.dot(sketch, b_ref[:, pl.ds(at, cols)], preferred_element_type=F32)
             ref[i] = out.T.reshape(ref.shape[1:])
 
 
-def panel_call(me, a, b, parts, shifts, blocks, pieces, name):
+def panel_call(me, a, b, parts, columns, blocks, pieces, name):
     pairs, width = b.shape
     rank = parts[0].shape[-1]
     out = sds((blocks, pieces, width // blocks // pieces // 2, rank), F32)
-    n_copies = len(parts) * max(1, parts[0].shape[0] // 1024)
-    anywhere = pl.BlockSpec(memory_space=pl.ANY)
-    return pl.pallas_call(
-        functools.partial(panel_kernel, shifts, blocks),
-        in_specs=[SMEM, anywhere, anywhere] + [VMEM] * len(parts),
+    hbm = pl.BlockSpec(memory_space=pltpu.HBM)
+    return pl.pallas_call(
+        functools.partial(panel_kernel, columns, len(parts), blocks),
+        in_specs=[SMEM, hbm, hbm] + [VMEM] * len(parts),
         out_specs=[VMEM, VMEM],
         out_shape=[out, out],
         scratch_shapes=[
             pltpu.VMEM(a.shape, BF16),
             pltpu.VMEM(b.shape, BF16),
-            pltpu.SemaphoreType.DMA((n_copies,)),
+            pltpu.SemaphoreType.DMA((len(parts),)),
             pltpu.SemaphoreType.DMA((blocks,)),
         ],
-        compiler_params=params(),
+        compiler_params=pltpu.CompilerParams(vmem_limit_bytes=PANEL_LIMIT),
         cost_estimate=cost(2 * pairs * rank * (width + a.shape[1]), 2 * pairs * (width + a.shape[1])),
         name=name,
     )(me, a, b, *parts)
@@ -293,29 +293,45 @@
             got[s ^ 1] = col_swap(got[s], 1)
         return got
 
+    def split_swap(x, even, odd):
+        pairs = []
+        for r in range(n_row):
+            for c in range(n_col):
+                pairs.append((r * n_col + c, (r ^ (odd if c % 2 else even)) * n_col + c))
+        return lax.ppermute(x, ("row", "col"), pairs)
+
+    fetched = [(t, t + 1, split_swap(probe_image, t, t + 1)) for t in depths[:-1:2]]
     text_parts = over_plane(probe_text)
-    image_whole = lax.all_gather(probe_image, "row", axis=0, tiled=True)
-
+    first, *blocks = lax.optimization_barrier((me, *[block for _, _, block in fetched]))
+    half = probe_image.shape[0] // 2
+    last = depths[-1]
+    mine = row_swap(lax.dynamic_slice_in_dim(probe_image, me[0] % 2 * half, half, 0), last)
+    image_order = [(0, 0, None)]
+    image_parts = [probe_image]
+    for (even, odd, _), block in zip(fetched, blocks):
+        image_order += [(even, odd, None), (odd, even, None)]
+        image_parts += [block, col_swap(block, 1)]
+    image_order += [(last, last, 0), (last, last, 1)]
+
+    columns = text_columns(list(text_parts), probe_text.shape[0])
     keep, send = panel_call(
-        me,
-        text_feats,
-        image_feats,
-        list(text_parts.values()),
-        list(text_parts),
-        n_row,
-        groups,
-        "image_panel",
+        first, text_feats, image_feats, list(text_parts.values()), columns, n_row, groups, "image_panel"
     )
     own, *sends = sums_call("col", 1, chips, me, [keep, col_swap(send, 1)], "image_cores")
-    own, *sends = sums_call("row", 0, depths, me, [own] + over_chips(sends), "image_plane")
+    own, mine = lax.optimization_barrier((own, mine))
+    image_parts += [mine, col_swap(mine, 1)]
+    received = over_chips(sends)
+    columns = image_columns(image_order, probe_image.shape[0])
+    keep, send = panel_call(
+        me, image_feats, text_feats, image_parts, columns, groups, 1, "text_panel"
+    )
+    send, *received = lax.optimization_barrier((send, *received))
+    own, *sends = sums_call("row", 0, depths, me, [own] + received, "image_plane")
     mine = last_call(own, over_depth(sends), BF16, "image_depth")
     parts = over_plane(mine)
     ipanel, gram = gram_call("col", list(parts), me, list(parts.values()), "image_gram")
     igrams = [gram] + over_depth([gram] * len(depths))
 
-    keep, send = panel_call(
-        me, image_feats, text_feats, [image_whole], [0], groups, 1, "text_panel"
-    )
     own, *sends = sums_call("col", 0, chips, me, [keep, col_swap(send, 1)], "text_cores")
     own, sends = own[0], [x[0] for x in sends]
     mine = last_call(own, [x for x in over_chips(sends)], BF16, "text_plane")

time: 127 us -> 98.5 us (0.78)
  between operations: 14.1 us -> 0.78 us
  local copies, waits for them, and re-layouts: 13 us -> 0.93 us
  waiting for transfers between devices: 34.2 us -> 23.7 us
  starting transfers between devices: 36.1 us -> 43 us
    all_gather x1 -> x0, waiting for transfers between devices: 12.7 us -> none  [per_device(): image_whole = lax.all_gather(probe_image, 'row', axis=0, tiled=True)]
    unnamed x12 -> x8, local copies, waits for them, and re-layouts: 13 us -> 0.92 us
    ppermute x9 -> x10, starting transfers between devices: 13.8 us -> 18.7 us  [per_device(): lax.ppermute(x, 'row', [(i, i ^ s) for i in range(n_row)])]
    ppermute x9 -> x10, waiting for transfers between devices: 3.17 us -> 7.01 us  [per_device(): lax.ppermute(x, 'row', [(i, i ^ s) for i in range(n_row)])]
    ppermute x0 -> x1, starting transfers between devices: none -> 3.09 us  [split_swap(): return lax.ppermute(x, ('row', 'col'), pairs)]
    ppermute x26 -> x28, starting transfers between devices: 22.3 us -> 21.3 us  [per_device(): lax.ppermute(x, 'col', [(i, i ^ s) for i in range(n_col)])]
    ppermute x26 -> x28, waiting for transfers between devices: 17.7 us -> 16.7 us  [per_device(): lax.ppermute(x, 'col', [(i, i ^ s) for i in range(n_col)])]
  transfers between devices with their start and end apart: 36 -> 39, of which waited for: 15 -> 14; matrix products, arithmetic and copies ran while one was open for 0% -> 0% of each run, Pallas kernels for 17% -> 12%
where the time goes in v5:
time: 98.5 us; the launch traced here: 98.4 us
  starting transfers between devices  43 us (44%)
  Pallas kernels  29.8 us (30%)
  waiting for transfers between devices  23.7 us (24%)
    ppermute x28, starting transfers between devices, per_device(): lax.ppermute(x, 'col', [(i, i ^ s) for i in range(n_col)])  21.3 us
    pallas_call x2, Pallas kernels, panel_call(): pl.pallas_call(functools.partial(panel_kernel, columns, len(parts), block...  19 us
    ppermute x10, starting transfers between devices, per_device(): lax.ppermute(x, 'row', [(i, i ^ s) for i in range(n_row)])  18.7 us
    ppermute x28, waiting for transfers between devices, per_device(): lax.ppermute(x, 'col', [(i, i ^ s) for i in range(n_col)])  16.7 us
    pallas_call x1, Pallas kernels, finish_call(): pl.pallas_call(functools.partial(finish_kernel, widths, len(igrams)), in_...  7.57 us
    ppermute x10, waiting for transfers between devices, per_device(): lax.ppermute(x, 'row', [(i, i ^ s) for i in range(n_row)])  7.01 us
    ppermute x1, starting transfers between devices, split_swap(): return lax.ppermute(x, ('row', 'col'), pairs)  3.09 us
    pallas_call x3, Pallas kernels, sums_call(): pl.pallas_call(functools.partial(sums_kernel, which, axis, shifts, len(te...  1.98 us
  transfers between devices with their start and end apart: 39, of which 14 were waited for; matrix products, arithmetic and copies ran while one was open for 0% of the time, Pallas kernels for 12%

profile of v5, /device:TPU:0, one launch (start us, length us, event | category | flops | bytes accessed | tf_op | source)
XLA Modules:
  0.0 98.4 jit_solution(2790680388466470061)
XLA Ops:
  0.6 3.1 %collective-permute-start = (bf16[1536,128]{1,0:T(8,128)(2,1)}, bf16[1536,128]{1,0:T(8,128)(2,1)S(1)}, u32[]{:S(2)}, u32[]{:S(2)}) collective-permute-start(bf16[1536,128]{1,0:T(8,128)(2,1)} %refs_0_.3), channel_id=1, source_target_pairs={{0,8},{1,17},{2,10},{3,19},{4,12},{5,21},{6,14},{7,23},{8,0},{9,25... | collective-permute-start | bytes 1179656 | tf_op jit(solution)/shard_map/ppermute | solution.py:301
  3.7 1.5 %collective-permute-start.1 = (bf16[512,128]{1,0:T(8,128)(2,1)}, bf16[512,128]{1,0:T(8,128)(2,1)S(1)}, u32[]{:S(2)}, u32[]{:S(2)}) collective-permute-start(bf16[512,128]{1,0:T(8,128)(2,1)} %refs_0_.2), channel_id=1, source_target_pairs={{0,2},{1,3},{2,0},{3,1},{4,6},{5,7},{6,4},{7,5},{8,10},{9,11},{10,... | collective-permute-start | bytes 393224 | tf_op jit(solution)/shard_map/ppermute | solution.py:282
  5.2 1.5 %collective-permute-start.2 = (bf16[512,128]{1,0:T(8,128)(2,1)}, bf16[512,128]{1,0:T(8,128)(2,1)S(1)}, u32[]{:S(2)}, u32[]{:S(2)}) collective-permute-start(bf16[512,128]{1,0:T(8,128)(2,1)} %refs_0_.2), channel_id=1, source_target_pairs={{0,4},{1,5},{2,6},{3,7},{4,0},{5,1},{6,2},{7,3},{8,12},{9,13},{10,... | collective-permute-start | bytes 393224 | tf_op jit(solution)/shard_map/ppermute | solution.py:282
  7.2 3.0 %collective-permute-done.1.refs_1_ = bf16[512,128]{1,0:T(8,128)(2,1)S(1)} collective-permute-done((bf16[512,128]{1,0:T(8,128)(2,1)}, bf16[512,128]{1,0:T(8,128)(2,1)S(1)}, u32[]{:S(2)}, u32[]{:S(2)}) %collective-permute-start.1) | collective-permute-done | bytes 131104 | tf_op jit(solution)/shard_map/ppermute | solution.py:282
  10.2 3.7 %collective-permute-done.2.refs_2_ = bf16[512,128]{1,0:T(8,128)(2,1)S(1)} collective-permute-done((bf16[512,128]{1,0:T(8,128)(2,1)}, bf16[512,128]{1,0:T(8,128)(2,1)S(1)}, u32[]{:S(2)}, u32[]{:S(2)}) %collective-permute-start.2) | collective-permute-done | bytes 131104 | tf_op jit(solution)/shard_map/ppermute | solution.py:282
  15.5 0.9 copy-done.3
  16.4 9.8 %image_panel.1 = (f32[4,4,192,128]{3,2,1,0:T(8,128)S(1)}, f32[4,4,192,128]{3,2,1,0:T(8,128)}) custom-call(s32[2]{0:T(128)S(1)} %pad_add_fusion.me_ref, bf16[576,4096]{1,0:T(8,128)(2,1)} %b_hbm.3, bf16[576,6144]{1,0:T(8,128)(2,1)} %a_hbm.3, bf16[512,128]{1,0:T(8,128)(2,1)S(1)} %copy-done.3, bf16[512,128]{1,0:T(8,128)(2,1)S(1)} %collective-permute-done.1.refs_1_, ...), custom_call_target="tpu_custom_call" | custom-call | flops 1509949440 | bytes 11796480 | tf_op jit(solution)/shard_map/image_panel/pallas_call | solution.py:83
  26.6 2.9 %collective-permute-start.9 = (bf16[768,128]{1,0:T(8,128)(2,1)S(1)}, bf16[768,128]{1,0:T(8,128)(2,1)S(1)}, u32[]{:S(2)}, u32[]{:S(2)}) collective-permute-start(bf16[768,128]{1,0:T(8,128)(2,1)S(1)} %constant_dynamic-slice_fusion), channel_id=1, source_target_pairs={{0,24},{8,16},{16,8},{24,0},{1,25},{9,17},{17,9},{25,1},{2,26},{10... | collective-permute-start | bytes 589832 | tf_op jit(solution)/shard_map/ppermute | solution.py:283
  30.6 5.0 %collective-permute-done.9.refs_3_ = bf16[768,128]{1,0:T(8,128)(2,1)S(1)} collective-permute-done((bf16[768,128]{1,0:T(8,128)(2,1)S(1)}, bf16[768,128]{1,0:T(8,128)(2,1)S(1)}, u32[]{:S(2)}, u32[]{:S(2)}) %collective-permute-start.9) | collective-permute-done | bytes 196640 | tf_op jit(solution)/shard_map/ppermute | solution.py:283
  35.6 1.1 %collective-permute-start.12 = (bf16[4,192,128]{2,1,0:T(8,128)(2,1)S(1)}, bf16[4,192,128]{2,1,0:T(8,128)(2,1)S(1)}, u32[]{:S(2)}, u32[]{:S(2)}) collective-permute-start(bf16[4,192,128]{2,1,0:T(8,128)(2,1)S(1)} %get-tuple-element.38), channel_id=1, source_target_pairs={{0,2},{1,3},{2,0},{3,1},{4,6},{5,7},{6,4},{7,5},{8,10},{9,11},{10,... | collective-permute-start | bytes 589832 | tf_op jit(solution)/shard_map/ppermute | solution.py:282
  36.6 1.5 %collective-permute-start.13 = (bf16[4,192,128]{2,1,0:T(8,128)(2,1)S(1)}, bf16[4,192,128]{2,1,0:T(8,128)(2,1)S(1)}, u32[]{:S(2)}, u32[]{:S(2)}) collective-permute-start(bf16[4,192,128]{2,1,0:T(8,128)(2,1)S(1)} %get-tuple-element.39), channel_id=1, source_target_pairs={{0,4},{1,5},{2,6},{3,7},{4,0},{5,1},{6,2},{7,3},{8,12},{9,13},{10,... | collective-permute-start | bytes 589832 | tf_op jit(solution)/shard_map/ppermute | solution.py:282
  39.1 9.2 %text_panel.1 = (f32[4,1,512,128]{3,2,1,0:T(8,128)S(1)}, f32[4,1,512,128]{3,2,1,0:T(8,128)S(1)}) custom-call(s32[2]{0:T(128)S(1)} %pad_add_fusion.me_ref, bf16[576,6144]{1,0:T(8,128)(2,1)} %a_hbm.3, bf16[576,4096]{1,0:T(8,128)(2,1)} %b_hbm.3, bf16[1536,128]{1,0:T(8,128)(2,1)S(1)} %copy-done, bf16[1536,128]{1,0:T(8,128)(2,1)S(1)} %copy-done.2, ...), custom_call_target="tpu_custom_call" | custom-call | flops 1509949440 | bytes 11796480 | tf_op jit(solution)/shard_map/text_panel/pallas_call | solution.py:83
  48.4 2.6 %collective-permute-done.25.refs_1_ = f32[4,1,512,128]{3,2,1,0:T(8,128)S(1)} collective-permute-done((f32[4,1,512,128]{3,2,1,0:T(8,128)S(1)}, f32[4,1,512,128]{3,2,1,0:T(8,128)S(1)}, u32[]{:S(2)}, u32[]{:S(2)}) %collective-permute-start.25) | collective-permute-done | bytes 1048608 | tf_op jit(solution)/shard_map/ppermute | solution.py:282
  51.7 1.1 %collective-permute-start.26 = (bf16[512,128]{1,0:T(8,128)(2,1)S(1)}, bf16[512,128]{1,0:T(8,128)(2,1)S(1)}, u32[]{:S(2)}, u32[]{:S(2)}) collective-permute-start(bf16[512,128]{1,0:T(8,128)(2,1)S(1)} %bitcast.9), channel_id=1, source_target_pairs={{0,2},{1,3},{2,0},{3,1},{4,6},{5,7},{6,4},{7,5},{8,10},{9,11},{10,... | collective-permute-start | bytes 393224 | tf_op jit(solution)/shard_map/ppermute | solution.py:282
  52.8 1.5 %collective-permute-start.27 = (bf16[512,128]{1,0:T(8,128)(2,1)S(1)}, bf16[512,128]{1,0:T(8,128)(2,1)S(1)}, u32[]{:S(2)}, u32[]{:S(2)}) collective-permute-start(bf16[512,128]{1,0:T(8,128)(2,1)S(1)} %bitcast.8), channel_id=1, source_target_pairs={{0,4},{1,5},{2,6},{3,7},{4,0},{5,1},{6,2},{7,3},{8,12},{9,13},{10,... | collective-permute-start | bytes 393224 | tf_op jit(solution)/shard_map/ppermute | solution.py:282
  55.9 3.5 %collective-permute-start.15 = (bf16[192,128]{1,0:T(8,128)(2,1)S(1)}, bf16[192,128]{1,0:T(8,128)(2,1)S(1)}, u32[]{:S(2)}, u32[]{:S(2)}) collective-permute-start(bf16[192,128]{1,0:T(8,128)(2,1)S(1)} %get-tuple-element.45), channel_id=1, source_target_pairs={{0,8},{8,0},{16,24},{24,16},{1,9},{9,1},{17,25},{25,17},{2,10},{10... | collective-permute-start | bytes 147464 | tf_op jit(solution)/shard_map/ppermute | solution.py:283
  59.6 2.1 %collective-permute-start.17 = (bf16[192,128]{1,0:T(8,128)(2,1)S(1)}, bf16[192,128]{1,0:T(8,128)(2,1)S(1)}, u32[]{:S(2)}, u32[]{:S(2)}) collective-permute-start(bf16[192,128]{1,0:T(8,128)(2,1)S(1)} %get-tuple-element.47), channel_id=1, source_target_pairs={{0,24},{8,16},{16,8},{24,0},{1,25},{9,17},{17,9},{25,1},{2,26},{10... | collective-permute-start | bytes 147464 | tf_op jit(solution)/shard_map/ppermute | solution.py:283
  61.8 3.0 %collective-permute-start.29 = (bf16[512,128]{1,0:T(8,128)(2,1)S(1)}, bf16[512,128]{1,0:T(8,128)(2,1)S(1)}, u32[]{:S(2)}, u32[]{:S(2)}) collective-permute-start(bf16[512,128]{1,0:T(8,128)(2,1)S(1)} %text_plane.1.refs_0_), channel_id=1, source_target_pairs={{0,8},{8,0},{16,24},{24,16},{1,9},{9,1},{17,25},{25,17},{2,10},{10... | collective-permute-start | bytes 393224 | tf_op jit(solution)/shard_map/ppermute | solution.py:283
  65.7 1.6 %collective-permute-start.18 = (bf16[192,128]{1,0:T(8,128)(2,1)S(1)}, bf16[192,128]{1,0:T(8,128)(2,1)S(1)}, u32[]{:S(2)}, u32[]{:S(2)}) collective-permute-start(bf16[192,128]{1,0:T(8,128)(2,1)S(1)} %image_depth.1.refs_0_), channel_id=1, source_target_pairs={{0,2},{1,3},{2,0},{3,1},{4,6},{5,7},{6,4},{7,5},{8,10},{9,11},{10,... | collective-permute-start | bytes 147464 | tf_op jit(solution)/shard_map/ppermute | solution.py:282
  67.3 2.2 %collective-permute-start.31 = (bf16[512,128]{1,0:T(8,128)(2,1)S(1)}, bf16[512,128]{1,0:T(8,128)(2,1)S(1)}, u32[]{:S(2)}, u32[]{:S(2)}) collective-permute-start(bf16[512,128]{1,0:T(8,128)(2,1)S(1)} %text_plane.1.refs_0_), channel_id=1, source_target_pairs={{0,24},{8,16},{16,8},{24,0},{1,25},{9,17},{17,9},{25,1},{2,26},{10... | collective-permute-start | bytes 393224 | tf_op jit(solution)/shard_map/ppermute | solution.py:283
  69.4 1.8 %collective-permute-start.19 = (bf16[192,128]{1,0:T(8,128)(2,1)S(1)}, bf16[192,128]{1,0:T(8,128)(2,1)S(1)}, u32[]{:S(2)}, u32[]{:S(2)}) collective-permute-start(bf16[192,128]{1,0:T(8,128)(2,1)S(1)} %image_depth.1.refs_0_), channel_id=1, source_target_pairs={{0,4},{1,5},{2,6},{3,7},{4,0},{5,1},{6,2},{7,3},{8,12},{9,13},{10,... | collective-permute-start | bytes 147464 | tf_op jit(solution)/shard_map/ppermute | solution.py:282
  71.2 1.6 %collective-permute-start.20 = (bf16[192,128]{1,0:T(8,128)(2,1)S(1)}, bf16[192,128]{1,0:T(8,128)(2,1)S(1)}, u32[]{:S(2)}, u32[]{:S(2)}) collective-permute-start(bf16[192,128]{1,0:T(8,128)(2,1)S(1)} %image_depth.1.refs_0_), channel_id=1, source_target_pairs={{0,6},{1,7},{2,4},{3,5},{4,2},{5,3},{6,0},{7,1},{8,14},{9,15},{10,... | collective-permute-start | bytes 147464 | tf_op jit(solution)/shard_map/ppermute | solution.py:282
  73.5 2.7 %collective-permute-done.20.refs_3_ = bf16[192,128]{1,0:T(8,128)(2,1)S(1)} collective-permute-done((bf16[192,128]{1,0:T(8,128)(2,1)S(1)}, bf16[192,128]{1,0:T(8,128)(2,1)S(1)}, u32[]{:S(2)}, u32[]{:S(2)}) %collective-permute-start.20) | collective-permute-done | bytes 49184 | tf_op jit(solution)/shard_map/ppermute | solution.py:282
  78.8 1.3 %collective-permute-start.32 = (f32[128,128]{1,0:T(8,128)S(1)}, f32[128,128]{1,0:T(8,128)S(1)}, u32[]{:S(2)}, u32[]{:S(2)}) collective-permute-start(f32[128,128]{1,0:T(8,128)S(1)} %get-tuple-element.56.refs_0_), channel_id=1, source_target_pairs={{0,8},{8,0},{16,24},{24,16},{1,9},{9,1},{17,25},{25,17},{2,10},{10... | collective-permute-start | bytes 196616 | tf_op jit(solution)/shard_map/ppermute | solution.py:283
  80.1 1.1 %collective-permute-start.33 = (f32[128,128]{1,0:T(8,128)S(1)}, f32[128,128]{1,0:T(8,128)S(1)}, u32[]{:S(2)}, u32[]{:S(2)}) collective-permute-start(f32[128,128]{1,0:T(8,128)S(1)} %get-tuple-element.56.refs_0_), channel_id=1, source_target_pairs={{0,16},{8,24},{16,0},{24,8},{1,17},{9,25},{17,1},{25,9},{2,18},{10... | collective-permute-start | bytes 196616 | tf_op jit(solution)/shard_map/ppermute | solution.py:283
  81.1 2.1 %collective-permute-start.34 = (f32[128,128]{1,0:T(8,128)S(1)}, f32[128,128]{1,0:T(8,128)S(1)}, u32[]{:S(2)}, u32[]{:S(2)}) collective-permute-start(f32[128,128]{1,0:T(8,128)S(1)} %get-tuple-element.56.refs_0_), channel_id=1, source_target_pairs={{0,24},{8,16},{16,8},{24,0},{1,25},{9,17},{17,9},{25,1},{2,26},{10... | collective-permute-start | bytes 196616 | tf_op jit(solution)/shard_map/ppermute | solution.py:283
  83.3 1.5 %collective-permute-start.36 = (f32[128,128]{1,0:T(8,128)S(1)}, f32[128,128]{1,0:T(8,128)S(1)}, u32[]{:S(2)}, u32[]{:S(2)}) collective-permute-start(f32[128,128]{1,0:T(8,128)S(1)} %text_gram_cores.1.refs_4_), channel_id=1, source_target_pairs={{0,2},{1,3},{2,0},{3,1},{4,6},{5,7},{6,4},{7,5},{8,10},{9,11},{10,... | collective-permute-start | bytes 196616 | tf_op jit(solution)/shard_map/ppermute | solution.py:282
  85.6 1.2 %collective-permute-start.38 = (f32[128,128]{1,0:T(8,128)S(1)}, f32[128,128]{1,0:T(8,128)S(1)}, u32[]{:S(2)}, u32[]{:S(2)}) collective-permute-start(f32[128,128]{1,0:T(8,128)S(1)} %text_gram_cores.1.refs_4_), channel_id=1, source_target_pairs={{0,6},{1,7},{2,4},{3,5},{4,2},{5,3},{6,0},{7,1},{8,14},{9,15},{10,... | collective-permute-start | bytes 196616 | tf_op jit(solution)/shard_map/ppermute | solution.py:282
  86.8 1.5 %collective-permute-done.33.refs_2_ = f32[128,128]{1,0:T(8,128)S(1)} collective-permute-done((f32[128,128]{1,0:T(8,128)S(1)}, f32[128,128]{1,0:T(8,128)S(1)}, u32[]{:S(2)}, u32[]{:S(2)}) %collective-permute-start.33) | collective-permute-done | bytes 65568 | tf_op jit(solution)/shard_map/ppermute | solution.py:283
  88.3 1.2 %collective-permute-done.37.refs_6_ = f32[128,128]{1,0:T(8,128)S(1)} collective-permute-done((f32[128,128]{1,0:T(8,128)S(1)}, f32[128,128]{1,0:T(8,128)S(1)}, u32[]{:S(2)}, u32[]{:S(2)}) %collective-permute-start.37) | collective-permute-done | bytes 65568 | tf_op jit(solution)/shard_map/ppermute | solution.py:282
  89.5 1.3 %collective-permute-done.38.refs_7_ = f32[128,128]{1,0:T(8,128)S(1)} collective-permute-done((f32[128,128]{1,0:T(8,128)S(1)}, f32[128,128]{1,0:T(8,128)S(1)}, u32[]{:S(2)}, u32[]{:S(2)}) %collective-permute-start.38) | collective-permute-done | bytes 65568 | tf_op jit(solution)/shard_map/ppermute | solution.py:282
  90.8 7.6 %finish.1 = (f32[1536,128]{1,0:T(8,128)}, f32[512,128]{1,0:T(8,128)}) custom-call(bf16[8,192,128]{2,1,0:T(8,128)(2,1)S(1)} %get-tuple-element.48.ipanel, bf16[1,512,128]{2,1,0:T(8,128)(2,1)S(1)} %get-tuple-element.55.tpanel, f32[128,128]{1,0:T(8,128)S(1)} %get-tuple-element.56.refs_0_, f32[128,128]{1,0:T(8,128)S(1)} %collective-permute-done.32.refs_1_, ...), custom_call_target="tpu_custom_call" | custom-call | flops 10000000000 | bytes 1179648 | tf_op jit(solution)/shard_map/finish/pallas_call | solution.py:268
  (67 shorter events, 12.1 us)
Async XLA Ops:
  0.6 13.9 %collective-permute-start = (bf16[1536,128]{1,0:T(8,128)(2,1)}, bf16[1536,128]{1,0:T(8,128)(2,1)S(1)}, u32[]{:S(2)}, u32[]{:S(2)}) collective-permute-start(bf16[1536,128]{1,0:T(8,128)(2,1)} %refs_0_.3), channel_id=1, source_target_pairs={{0,8},{1,17},{2,10},{3,19},{4,12},{5,21},{6,14},{7,23},{8,0},{9,25... | collective-permute-start | bytes 1179656 | tf_op jit(solution)/shard_map/ppermute | solution.py:301
  3.7 6.5 %collective-permute-start.1 = (bf16[512,128]{1,0:T(8,128)(2,1)}, bf16[512,128]{1,0:T(8,128)(2,1)S(1)}, u32[]{:S(2)}, u32[]{:S(2)}) collective-permute-start(bf16[512,128]{1,0:T(8,128)(2,1)} %refs_0_.2), channel_id=1, source_target_pairs={{0,2},{1,3},{2,0},{3,1},{4,6},{5,7},{6,4},{7,5},{8,10},{9,11},{10,... | collective-permute-start | bytes 393224 | tf_op jit(solution)/shard_map/ppermute | solution.py:282
  5.2 8.7 %collective-permute-start.2 = (bf16[512,128]{1,0:T(8,128)(2,1)}, bf16[512,128]{1,0:T(8,128)(2,1)S(1)}, u32[]{:S(2)}, u32[]{:S(2)}) collective-permute-start(bf16[512,128]{1,0:T(8,128)(2,1)} %refs_0_.2), channel_id=1, source_target_pairs={{0,4},{1,5},{2,6},{3,7},{4,0},{5,1},{6,2},{7,3},{8,12},{9,13},{10,... | collective-permute-start | bytes 393224 | tf_op jit(solution)/shard_map/ppermute | solution.py:282
  6.7 7.2 %collective-permute-start.3 = (bf16[512,128]{1,0:T(8,128)(2,1)}, bf16[512,128]{1,0:T(8,128)(2,1)S(1)}, u32[]{:S(2)}, u32[]{:S(2)}) collective-permute-start(bf16[512,128]{1,0:T(8,128)(2,1)} %refs_0_.2), channel_id=1, source_target_pairs={{0,6},{1,7},{2,4},{3,5},{4,2},{5,3},{6,0},{7,1},{8,14},{9,15},{10,... | collective-permute-start | bytes 393224 | tf_op jit(solution)/shard_map/ppermute | solution.py:282
  7.2 7.3 %collective-permute-start.4 = (bf16[512,128]{1,0:T(8,128)(2,1)}, bf16[512,128]{1,0:T(8,128)(2,1)S(1)}, u32[]{:S(2)}, u32[]{:S(2)}) collective-permute-start(bf16[512,128]{1,0:T(8,128)(2,1)} %refs_0_.2), channel_id=1, source_target_pairs={{0,1},{1,0},{2,3},{3,2},{4,5},{5,4},{6,7},{7,6},{8,9},{9,8},{10,11... | collective-permute-start | bytes 393224 | tf_op jit(solution)/shard_map/ppermute | solution.py:282
  10.2 4.3 %collective-permute-start.5 = (bf16[512,128]{1,0:T(8,128)(2,1)S(1)}, bf16[512,128]{1,0:T(8,128)(2,1)S(1)}, u32[]{:S(2)}, u32[]{:S(2)}) collective-permute-start(bf16[512,128]{1,0:T(8,128)(2,1)S(1)} %collective-permute-done.1.refs_1_), channel_id=1, source_target_pairs={{0,1},{1,0},{2,3},{3,2},{4,5},{5,4},{6,7},{7,6},{8,9},{9,8},{10,11... | collective-permute-start | bytes 393224 | tf_op jit(solution)/shard_map/ppermute | solution.py:282
  26.2 3.7 %collective-permute-start.8 = (f32[4,4,192,128]{3,2,1,0:T(8,128)}, f32[4,4,192,128]{3,2,1,0:T(8,128)S(1)}, u32[]{:S(2)}, u32[]{:S(2)}) collective-permute-start(f32[4,4,192,128]{3,2,1,0:T(8,128)} %get-tuple-element.32), channel_id=1, source_target_pairs={{0,1},{1,0},{2,3},{3,2},{4,5},{5,4},{6,7},{7,6},{8,9},{9,8},{10,11... | collective-permute-start | bytes 4718600 | tf_op jit(solution)/shard_map/ppermute | solution.py:282
  26.6 9.0 %collective-permute-start.9 = (bf16[768,128]{1,0:T(8,128)(2,1)S(1)}, bf16[768,128]{1,0:T(8,128)(2,1)S(1)}, u32[]{:S(2)}, u32[]{:S(2)}) collective-permute-start(bf16[768,128]{1,0:T(8,128)(2,1)S(1)} %constant_dynamic-slice_fusion), channel_id=1, source_target_pairs={{0,24},{8,16},{16,8},{24,0},{1,25},{9,17},{17,9},{25,1},{2,26},{10... | collective-permute-start | bytes 589832 | tf_op jit(solution)/shard_map/ppermute | solution.py:283
  29.5 9.5 %collective-permute-start.10 = (bf16[1536,128]{1,0:T(8,128)(2,1)}, bf16[1536,128]{1,0:T(8,128)(2,1)S(1)}, u32[]{:S(2)}, u32[]{:S(2)}) collective-permute-start(bf16[1536,128]{1,0:T(8,128)(2,1)} %copy-done.1), channel_id=1, source_target_pairs={{0,1},{1,0},{2,3},{3,2},{4,5},{5,4},{6,7},{7,6},{8,9},{9,8},{10,11... | collective-permute-start | bytes 1179656 | tf_op jit(solution)/shard_map/ppermute | solution.py:282
  35.6 12.7 %collective-permute-start.12 = (bf16[4,192,128]{2,1,0:T(8,128)(2,1)S(1)}, bf16[4,192,128]{2,1,0:T(8,128)(2,1)S(1)}, u32[]{:S(2)}, u32[]{:S(2)}) collective-permute-start(bf16[4,192,128]{2,1,0:T(8,128)(2,1)S(1)} %get-tuple-element.38), channel_id=1, source_target_pairs={{0,2},{1,3},{2,0},{3,1},{4,6},{5,7},{6,4},{7,5},{8,10},{9,11},{10,... | collective-permute-start | bytes 589832 | tf_op jit(solution)/shard_map/ppermute | solution.py:282
  36.6 11.6 %collective-permute-start.13 = (bf16[4,192,128]{2,1,0:T(8,128)(2,1)S(1)}, bf16[4,192,128]{2,1,0:T(8,128)(2,1)S(1)}, u32[]{:S(2)}, u32[]{:S(2)}) collective-permute-start(bf16[4,192,128]{2,1,0:T(8,128)(2,1)S(1)} %get-tuple-element.39), channel_id=1, source_target_pairs={{0,4},{1,5},{2,6},{3,7},{4,0},{5,1},{6,2},{7,3},{8,12},{9,13},{10,... | collective-permute-start | bytes 589832 | tf_op jit(solution)/shard_map/ppermute | solution.py:282
  38.2 10.1 %collective-permute-start.14 = (bf16[4,192,128]{2,1,0:T(8,128)(2,1)S(1)}, bf16[4,192,128]{2,1,0:T(8,128)(2,1)S(1)}, u32[]{:S(2)}, u32[]{:S(2)}) collective-permute-start(bf16[4,192,128]{2,1,0:T(8,128)(2,1)S(1)} %get-tuple-element.40), channel_id=1, source_target_pairs={{0,6},{1,7},{2,4},{3,5},{4,2},{5,3},{6,0},{7,1},{8,14},{9,15},{10,... | collective-permute-start | bytes 589832 | tf_op jit(solution)/shard_map/ppermute | solution.py:282
  51.7 7.9 %collective-permute-start.26 = (bf16[512,128]{1,0:T(8,128)(2,1)S(1)}, bf16[512,128]{1,0:T(8,128)(2,1)S(1)}, u32[]{:S(2)}, u32[]{:S(2)}) collective-permute-start(bf16[512,128]{1,0:T(8,128)(2,1)S(1)} %bitcast.9), channel_id=1, source_target_pairs={{0,2},{1,3},{2,0},{3,1},{4,6},{5,7},{6,4},{7,5},{8,10},{9,11},{10,... | collective-permute-start | bytes 393224 | tf_op jit(solution)/shard_map/ppermute | solution.py:282
  52.8 9.0 %collective-permute-start.27 = (bf16[512,128]{1,0:T(8,128)(2,1)S(1)}, bf16[512,128]{1,0:T(8,128)(2,1)S(1)}, u32[]{:S(2)}, u32[]{:S(2)}) collective-permute-start(bf16[512,128]{1,0:T(8,128)(2,1)S(1)} %bitcast.8), channel_id=1, source_target_pairs={{0,4},{1,5},{2,6},{3,7},{4,0},{5,1},{6,2},{7,3},{8,12},{9,13},{10,... | collective-permute-start | bytes 393224 | tf_op jit(solution)/shard_map/ppermute | solution.py:282
  54.3 7.4 %collective-permute-start.28 = (bf16[512,128]{1,0:T(8,128)(2,1)S(1)}, bf16[512,128]{1,0:T(8,128)(2,1)S(1)}, u32[]{:S(2)}, u32[]{:S(2)}) collective-permute-start(bf16[512,128]{1,0:T(8,128)(2,1)S(1)} %bitcast.7), channel_id=1, source_target_pairs={{0,6},{1,7},{2,4},{3,5},{4,2},{5,3},{6,0},{7,1},{8,14},{9,15},{10,... | collective-permute-start | bytes 393224 | tf_op jit(solution)/shard_map/ppermute | solution.py:282
  55.9 9.2 %collective-permute-start.15 = (bf16[192,128]{1,0:T(8,128)(2,1)S(1)}, bf16[192,128]{1,0:T(8,128)(2,1)S(1)}, u32[]{:S(2)}, u32[]{:S(2)}) collective-permute-start(bf16[192,128]{1,0:T(8,128)(2,1)S(1)} %get-tuple-element.45), channel_id=1, source_target_pairs={{0,8},{8,0},{16,24},{24,16},{1,9},{9,1},{17,25},{25,17},{2,10},{10... | collective-permute-start | bytes 147464 | tf_op jit(solution)/shard_map/ppermute | solution.py:283
  59.3 5.8 %collective-permute-start.16 = (bf16[192,128]{1,0:T(8,128)(2,1)S(1)}, bf16[192,128]{1,0:T(8,128)(2,1)S(1)}, u32[]{:S(2)}, u32[]{:S(2)}) collective-permute-start(bf16[192,128]{1,0:T(8,128)(2,1)S(1)} %get-tuple-element.46), channel_id=1, source_target_pairs={{0,16},{8,24},{16,0},{24,8},{1,17},{9,25},{17,1},{25,9},{2,18},{10... | collective-permute-start | bytes 147464 | tf_op jit(solution)/shard_map/ppermute | solution.py:283
  59.6 6.0 %collective-permute-start.17 = (bf16[192,128]{1,0:T(8,128)(2,1)S(1)}, bf16[192,128]{1,0:T(8,128)(2,1)S(1)}, u32[]{:S(2)}, u32[]{:S(2)}) collective-permute-start(bf16[192,128]{1,0:T(8,128)(2,1)S(1)} %get-tuple-element.47), channel_id=1, source_target_pairs={{0,24},{8,16},{16,8},{24,0},{1,25},{9,17},{17,9},{25,1},{2,26},{10... | collective-permute-start | bytes 147464 | tf_op jit(solution)/shard_map/ppermute | solution.py:283
  61.8 14.3 %collective-permute-start.29 = (bf16[512,128]{1,0:T(8,128)(2,1)S(1)}, bf16[512,128]{1,0:T(8,128)(2,1)S(1)}, u32[]{:S(2)}, u32[]{:S(2)}) collective-permute-start(bf16[512,128]{1,0:T(8,128)(2,1)S(1)} %text_plane.1.refs_0_), channel_id=1, source_target_pairs={{0,8},{8,0},{16,24},{24,16},{1,9},{9,1},{17,25},{25,17},{2,10},{10... | collective-permute-start | bytes 393224 | tf_op jit(solution)/shard_map/ppermute | solution.py:283
  64.8 11.8 %collective-permute-start.30 = (bf16[512,128]{1,0:T(8,128)(2,1)S(1)}, bf16[512,128]{1,0:T(8,128)(2,1)S(1)}, u32[]{:S(2)}, u32[]{:S(2)}) collective-permute-start(bf16[512,128]{1,0:T(8,128)(2,1)S(1)} %text_plane.1.refs_0_), channel_id=1, source_target_pairs={{0,16},{8,24},{16,0},{24,8},{1,17},{9,25},{17,1},{25,9},{2,18},{10... | collective-permute-start | bytes 393224 | tf_op jit(solution)/shard_map/ppermute | solution.py:283
  65.7 5.5 %collective-permute-start.18 = (bf16[192,128]{1,0:T(8,128)(2,1)S(1)}, bf16[192,128]{1,0:T(8,128)(2,1)S(1)}, u32[]{:S(2)}, u32[]{:S(2)}) collective-permute-start(bf16[192,128]{1,0:T(8,128)(2,1)S(1)} %image_depth.1.refs_0_), channel_id=1, source_target_pairs={{0,2},{1,3},{2,0},{3,1},{4,6},{5,7},{6,4},{7,5},{8,10},{9,11},{10,... | collective-permute-start | bytes 147464 | tf_op jit(solution)/shard_map/ppermute | solution.py:282
  67.3 9.5 %collective-permute-start.31 = (bf16[512,128]{1,0:T(8,128)(2,1)S(1)}, bf16[512,128]{1,0:T(8,128)(2,1)S(1)}, u32[]{:S(2)}, u32[]{:S(2)}) collective-permute-start(bf16[512,128]{1,0:T(8,128)(2,1)S(1)} %text_plane.1.refs_0_), channel_id=1, source_target_pairs={{0,24},{8,16},{16,8},{24,0},{1,25},{9,17},{17,9},{25,1},{2,26},{10... | collective-permute-start | bytes 393224 | tf_op jit(solution)/shard_map/ppermute | solution.py:283
  69.4 4.1 %collective-permute-start.19 = (bf16[192,128]{1,0:T(8,128)(2,1)S(1)}, bf16[192,128]{1,0:T(8,128)(2,1)S(1)}, u32[]{:S(2)}, u32[]{:S(2)}) collective-permute-start(bf16[192,128]{1,0:T(8,128)(2,1)S(1)} %image_depth.1.refs_0_), channel_id=1, source_target_pairs={{0,4},{1,5},{2,6},{3,7},{4,0},{5,1},{6,2},{7,3},{8,12},{9,13},{10,... | collective-permute-start | bytes 147464 | tf_op jit(solution)/shard_map/ppermute | solution.py:282
  71.2 5.0 %collective-permute-start.20 = (bf16[192,128]{1,0:T(8,128)(2,1)S(1)}, bf16[192,128]{1,0:T(8,128)(2,1)S(1)}, u32[]{:S(2)}, u32[]{:S(2)}) collective-permute-start(bf16[192,128]{1,0:T(8,128)(2,1)S(1)} %image_depth.1.refs_0_), channel_id=1, source_target_pairs={{0,6},{1,7},{2,4},{3,5},{4,2},{5,3},{6,0},{7,1},{8,14},{9,15},{10,... | collective-permute-start | bytes 147464 | tf_op jit(solution)/shard_map/ppermute | solution.py:282
  73.5 4.0 %collective-permute-start.21 = (bf16[192,128]{1,0:T(8,128)(2,1)S(1)}, bf16[192,128]{1,0:T(8,128)(2,1)S(1)}, u32[]{:S(2)}, u32[]{:S(2)}) collective-permute-start(bf16[192,128]{1,0:T(8,128)(2,1)S(1)} %image_depth.1.refs_0_), channel_id=1, source_target_pairs={{0,1},{1,0},{2,3},{3,2},{4,5},{5,4},{6,7},{7,6},{8,9},{9,8},{10,11... | collective-permute-start | bytes 147464 | tf_op jit(solution)/shard_map/ppermute | solution.py:282
  77.0 6.2 %collective-permute-start.35 = (f32[128,128]{1,0:T(8,128)S(1)}, f32[128,128]{1,0:T(8,128)S(1)}, u32[]{:S(2)}, u32[]{:S(2)}) collective-permute-start(f32[128,128]{1,0:T(8,128)S(1)} %get-tuple-element.57.own_ref), channel_id=1, source_target_pairs={{0,1},{1,0},{2,3},{3,2},{4,5},{5,4},{6,7},{7,6},{8,9},{9,8},{10,11... | collective-permute-start | bytes 196616 | tf_op jit(solution)/shard_map/ppermute | solution.py:282
  78.8 6.8 %collective-permute-start.32 = (f32[128,128]{1,0:T(8,128)S(1)}, f32[128,128]{1,0:T(8,128)S(1)}, u32[]{:S(2)}, u32[]{:S(2)}) collective-permute-start(f32[128,128]{1,0:T(8,128)S(1)} %get-tuple-element.56.refs_0_), channel_id=1, source_target_pairs={{0,8},{8,0},{16,24},{24,16},{1,9},{9,1},{17,25},{25,17},{2,10},{10... | collective-permute-start | bytes 196616 | tf_op jit(solution)/shard_map/ppermute | solution.py:283
  80.1 8.2 %collective-permute-start.33 = (f32[128,128]{1,0:T(8,128)S(1)}, f32[128,128]{1,0:T(8,128)S(1)}, u32[]{:S(2)}, u32[]{:S(2)}) collective-permute-start(f32[128,128]{1,0:T(8,128)S(1)} %get-tuple-element.56.refs_0_), channel_id=1, source_target_pairs={{0,16},{8,24},{16,0},{24,8},{1,17},{9,25},{17,1},{25,9},{2,18},{10... | collective-permute-start | bytes 196616 | tf_op jit(solution)/shard_map/ppermute | solution.py:283
  81.1 7.2 %collective-permute-start.34 = (f32[128,128]{1,0:T(8,128)S(1)}, f32[128,128]{1,0:T(8,128)S(1)}, u32[]{:S(2)}, u32[]{:S(2)}) collective-permute-start(f32[128,128]{1,0:T(8,128)S(1)} %get-tuple-element.56.refs_0_), channel_id=1, source_target_pairs={{0,24},{8,16},{16,8},{24,0},{1,25},{9,17},{17,9},{25,1},{2,26},{10... | collective-permute-start | bytes 196616 | tf_op jit(solution)/shard_map/ppermute | solution.py:283
  83.3 5.0 %collective-permute-start.36 = (f32[128,128]{1,0:T(8,128)S(1)}, f32[128,128]{1,0:T(8,128)S(1)}, u32[]{:S(2)}, u32[]{:S(2)}) collective-permute-start(f32[128,128]{1,0:T(8,128)S(1)} %text_gram_cores.1.refs_4_), channel_id=1, source_target_pairs={{0,2},{1,3},{2,0},{3,1},{4,6},{5,7},{6,4},{7,5},{8,10},{9,11},{10,... | collective-permute-start | bytes 196616 | tf_op jit(solution)/shard_map/ppermute | solution.py:282
  84.7 4.8 %collective-permute-start.37 = (f32[128,128]{1,0:T(8,128)S(1)}, f32[128,128]{1,0:T(8,128)S(1)}, u32[]{:S(2)}, u32[]{:S(2)}) collective-permute-start(f32[128,128]{1,0:T(8,128)S(1)} %text_gram_cores.1.refs_4_), channel_id=1, source_target_pairs={{0,4},{1,5},{2,6},{3,7},{4,0},{5,1},{6,2},{7,3},{8,12},{9,13},{10,... | collective-permute-start | bytes 196616 | tf_op jit(solution)/shard_map/ppermute | solution.py:282
  85.6 5.2 %collective-permute-start.38 = (f32[128,128]{1,0:T(8,128)S(1)}, f32[128,128]{1,0:T(8,128)S(1)}, u32[]{:S(2)}, u32[]{:S(2)}) collective-permute-start(f32[128,128]{1,0:T(8,128)S(1)} %text_gram_cores.1.refs_4_), channel_id=1, source_target_pairs={{0,6},{1,7},{2,4},{3,5},{4,2},{5,3},{6,0},{7,1},{8,14},{9,15},{10,... | collective-permute-start | bytes 196616 | tf_op jit(solution)/shard_map/ppermute | solution.py:282
  (11 other events, 36.0 us)

commit v6 on v5

--- a/solution.py
+++ b/solution.py
@@ -12,8 +12,8 @@
 BF16 = jnp.bfloat16
 VMEM = pl.BlockSpec(memory_space=pltpu.VMEM)
 SMEM = pl.BlockSpec(memory_space=pltpu.SMEM)
-LIMIT = 32 * 1024 * 1024
-PANEL_LIMIT = 46 * 1024 * 1024
+LIMIT = 16 * 1024 * 1024
+LOAD_LIMITS = (42, 46)
 
 
 def sds(shape, dtype):
@@ -48,27 +48,36 @@
     return columns
 
 
-def panel_kernel(columns, n, n_out, me_ref, a_hbm, b_hbm, *refs):
-    parts, (keep_ref, send_ref, a_ref, b_ref, a_sem, b_sem) = refs[:n], refs[n:]
+def load_kernel(hbm_ref, out_ref, sem):
+    move = pltpu.make_async_copy(hbm_ref, out_ref, sem)
+    move.start()
+    move.wait()
+
+
+def load_call(x, limit):
+    return pl.pallas_call(
+        load_kernel,
+        in_specs=[pl.BlockSpec(memory_space=pltpu.HBM)],
+        out_specs=VMEM,
+        out_shape=sds(x.shape, x.dtype),
+        scratch_shapes=[pltpu.SemaphoreType.DMA],
+        compiler_params=pltpu.CompilerParams(vmem_limit_bytes=limit * 1024 * 1024),
+        cost_estimate=cost(1, 4 * x.size),
+        name="load",
+    )(x)
+
+
+def panel_kernel(columns, n, n_out, me_ref, a_ref, b_ref, *refs):
+    parts, (keep_ref, send_ref) = refs[:n], refs[n:]
     core = me_ref[0] % 2
     cols = b_ref.shape[1] // n_out // 2
-    moves = []
-    spans = [pl.ds(at, part.shape[0]) for at, part in zip(columns(me_ref), parts)]
-    for i, span in enumerate(spans):
-        moves.append(pltpu.make_async_copy(a_hbm.at[:, span], a_ref.at[:, span], a_sem.at[i]))
-    for i in range(n_out):
-        span = pl.ds(2 * i * cols, 2 * cols)
-        moves.append(pltpu.make_async_copy(b_hbm.at[:, span], b_ref.at[:, span], b_sem.at[i]))
-    for move in moves:
-        move.start()
     total = None
-    for i, span in enumerate(spans):
-        moves[i].wait()
-        term = jnp.dot(a_ref[:, span], parts[i][...], preferred_element_type=F32)
+    for at, part in zip(columns(me_ref), parts):
+        span = pl.ds(at, part.shape[0])
+        term = jnp.dot(a_ref[:, span], part[...], preferred_element_type=F32)
         total = term if total is None else total + term
     sketch = total.T.astype(BF16)
     for i in range(n_out):
-        moves[n + i].wait()
         for rel, ref in ((0, keep_ref), (1, send_ref)):
             at = pl.multiple_of((2 * i + (core ^ rel)) * cols, cols)
             out = jnp.dot(sketch, b_ref[:, pl.ds(at, cols)], preferred_element_type=F32)
@@ -79,19 +88,12 @@
     pairs, width = b.shape
     rank = parts[0].shape[-1]
     out = sds((blocks, pieces, width // blocks // pieces // 2, rank), F32)
-    hbm = pl.BlockSpec(memory_space=pltpu.HBM)
     return pl.pallas_call(
         functools.partial(panel_kernel, columns, len(parts), blocks),
-        in_specs=[SMEM, hbm, hbm] + [VMEM] * len(parts),
+        in_specs=[SMEM] + [VMEM] * (2 + len(parts)),
         out_specs=[VMEM, VMEM],
         out_shape=[out, out],
-        scratch_shapes=[
-            pltpu.VMEM(a.shape, BF16),
-            pltpu.VMEM(b.shape, BF16),
-            pltpu.SemaphoreType.DMA((len(parts),)),
-            pltpu.SemaphoreType.DMA((blocks,)),
-        ],
-        compiler_params=pltpu.CompilerParams(vmem_limit_bytes=PANEL_LIMIT),
+        compiler_params=params(),
         cost_estimate=cost(2 * pairs * rank * (width + a.shape[1]), 2 * pairs * (width + a.shape[1])),
         name=name,
     )(me, a, b, *parts)
@@ -204,37 +206,55 @@
     )(*parts)
 
 
+def reciprocal(x):
+    guess = pl.reciprocal(x, approx=True)
+    guess = guess * (2.0 - x * guess)
+    return guess * (2.0 - x * guess)
+
+
 def inverse_factor(gram):
     n = gram.shape[0]
+    blocks = n // 8
     lane = lax.broadcasted_iota(jnp.int32, (8, n), 1)
     sub = lax.broadcasted_iota(jnp.int32, (8, n), 0)
-    rows = [gram[8 * i : 8 * i + 8, :] for i in range(n // 8)]
-    for b in range(n // 8):
-        cols = [
-            [jnp.broadcast_to(rows[i][:, 8 * b + j : 8 * b + j + 1], (8, n)) for i in range(b, n // 8)]
-            for j in range(8)
-        ]
-        scale = jnp.ones((8, n), F32)
+    rows = [gram[8 * i : 8 * i + 8, :] for i in range(blocks)]
+
+    def column(x, k):
+        return jnp.broadcast_to(x[:, k : k + 1], (8, n))
+
+    def row(x, j):
+        return jnp.broadcast_to(x[j : j + 1, :], (8, n))
+
+    for b in range(blocks):
+        first = 8 * b
+        diag = [column(rows[b], first + j) for j in range(8)]
+        below = [[column(rows[i], first + j) for j in range(8)] for i in range(b + 1, blocks)]
+        lower = full = rows[b]
+        pivots = scales = jnp.ones((8, n), F32)
         for j in range(8):
-            k = 8 * b + j
-            pivot = jnp.broadcast_to(cols[j][0][j : j + 1, :], (8, n))
-            inv = 1.0 / pivot
-            scale = jnp.where(sub == j, pivot, scale)
-            pivot_row = jnp.where(lane == k, 1.0, jnp.broadcast_to(rows[b][j : j + 1, :], (8, n)))
-            below = sub > j
-            mult = [c * inv for c in cols[j]]
-            mult[0] = jnp.where(below, mult[0], 0.0)
+            k = first + j
+            pivot = row(diag[j], j)
+            inv = reciprocal(pivot)
+            others = jnp.where(sub == j, 0.0, diag[j] * inv)
+            pivot_row = jnp.where(lane == k, 1.0, row(lower, j))
             for jj in range(j + 1, 8):
-                entry = jnp.broadcast_to(cols[jj][0][j : j + 1, :], (8, n))
-                cols[jj] = [c - m * entry for c, m in zip(cols[jj], mult)]
-            for i in range(b, n // 8):
-                here = lane == k
-                if i == b:
-                    here = jnp.logical_and(here, below)
-                rows[i] = jnp.where(here, 0.0, rows[i]) - mult[i - b] * pivot_row
+                diag[jj] = diag[jj] - others * row(diag[jj], j)
+            full = jnp.where(lane == k, jnp.where(sub == j, 1.0, 0.0), full) - others * pivot_row
+            lower = jnp.where(sub > j, full, lower)
+            pivots = jnp.where(sub == j, pivot, pivots)
+            scales = jnp.where(sub == j, inv, scales)
             yield None
-        unit = jnp.where(lane == sub + 8 * b, 1.0, jnp.where(lane < sub + 8 * b, rows[b], 0.0))
-        rows[b] = unit * lax.rsqrt(scale)
+        full = full * scales
+        solved = [row(full, j) for j in range(8)]
+        inside = jnp.logical_and(lane >= first, lane < first + 8)
+        for i in range(b + 1, blocks):
+            terms = [c * z for c, z in zip(below[i - b - 1], solved)]
+            while len(terms) > 1:
+                terms = [x + y for x, y in zip(terms[::2], terms[1::2])]
+            rows[i] = jnp.where(inside, 0.0, rows[i]) - terms[0]
+        diagonal = sub + first
+        unit = jnp.where(lane == diagonal, 1.0, jnp.where(lane < diagonal, lower, 0.0))
+        rows[b] = unit * lax.rsqrt(pivots)
         yield None
     yield jnp.concatenate(rows, axis=0)
 
@@ -285,9 +305,9 @@
     over_chips = lambda xs: [col_swap(x, 2 * s) for x, s in zip(xs, chips)]
     over_depth = lambda xs: [row_swap(x, t) for x, t in zip(xs, depths)]
 
-    def over_plane(x):
+    def over_plane(x, received=None):
         got = {0: x}
-        for s, block in zip(chips, over_chips([x] * len(chips))):
+        for s, block in zip(chips, received or over_chips([x] * len(chips))):
             got[2 * s] = block
         for s in list(got):
             got[s ^ 1] = col_swap(got[s], 1)
@@ -301,7 +321,12 @@
         return lax.ppermute(x, ("row", "col"), pairs)
 
     fetched = [(t, t + 1, split_swap(probe_image, t, t + 1)) for t in depths[:-1:2]]
-    text_parts = over_plane(probe_text)
+    text_feats = load_call(text_feats, LOAD_LIMITS[0])
+    image_feats = load_call(image_feats, LOAD_LIMITS[1])
+    text_feats, image_feats, *received = lax.optimization_barrier(
+        (text_feats, image_feats, *over_chips([probe_text] * len(chips)))
+    )
+    text_parts = over_plane(probe_text, received)
     first, *blocks = lax.optimization_barrier((me, *[block for _, _, block in fetched]))
     half = probe_image.shape[0] // 2
     last = depths[-1]
@@ -327,12 +352,13 @@
     )
     send, *received = lax.optimization_barrier((send, *received))
     own, *sends = sums_call("row", 0, depths, me, [own] + received, "image_plane")
+    text_recv, own = lax.optimization_barrier((col_swap(send, 1), own))
     mine = last_call(own, over_depth(sends), BF16, "image_depth")
     parts = over_plane(mine)
     ipanel, gram = gram_call("col", list(parts), me, list(parts.values()), "image_gram")
     igrams = [gram] + over_depth([gram] * len(depths))
 
-    own, *sends = sums_call("col", 0, chips, me, [keep, col_swap(send, 1)], "text_cores")
+    own, *sends = sums_call("col", 0, chips, me, [keep, text_recv], "text_cores")
     own, sends = own[0], [x[0] for x in sends]
     mine = last_call(own, [x for x in over_chips(sends)], BF16, "text_plane")
     tpanel, gram = text_gram_call([mine] + over_depth([mine] * len(depths)))

time: 98.5 us -> 106 us (1.076)
  local copies, waits for them, and re-layouts: 0.93 us -> 16.6 us
  waiting for transfers between devices: 23.7 us -> 16.6 us
  Pallas kernels: 29.8 us -> 27.1 us
  starting transfers between devices: 43 us -> 44.2 us
    unnamed x8 -> x22, local copies, waits for them, and re-layouts: 0.92 us -> 16.6 us
    ppermute x28, waiting for transfers between devices: 16.7 us -> 9.16 us  [per_device(): lax.ppermute(x, 'col', [(i, i ^ s) for i in range(n_col)])]
    pallas_call x2, Pallas kernels: 19 us -> 12 us  [panel_call(): pl.pallas_call(functools.partial(panel_kernel, columns, len(parts), block...]
    pallas_call x0 -> x2, Pallas kernels: none -> 3.37 us  [load_call(): pl.pallas_call(load_kernel, in_specs=[pl.BlockSpec(memory_space=pltpu.HBM...]
  transfers between devices with their start and end apart: 39 -> 39, of which waited for: 14 -> 13; matrix products, arithmetic and copies ran while one was open for 0% -> 0% of each run, Pallas kernels for 12% -> 11%
where the time goes in v6:
time: 106 us; the launch traced here: 105 us
  starting transfers between devices  44.2 us (42%)
  Pallas kernels  27.1 us (26%)
  local copies, waits for them, and re-layouts  16.6 us (16%)
  waiting for transfers between devices  16.6 us (16%)
    ppermute x28, starting transfers between devices, per_device(): lax.ppermute(x, 'col', [(i, i ^ s) for i in range(n_col)])  21.6 us
    ppermute x10, starting transfers between devices, per_device(): lax.ppermute(x, 'row', [(i, i ^ s) for i in range(n_row)])  19.5 us
    unnamed x22, local copies, waits for them, and re-layouts  16.6 us
    pallas_call x2, Pallas kernels, panel_call(): pl.pallas_call(functools.partial(panel_kernel, columns, len(parts), block...  12 us
    ppermute x28, waiting for transfers between devices, per_device(): lax.ppermute(x, 'col', [(i, i ^ s) for i in range(n_col)])  9.16 us
    pallas_call x1, Pallas kernels, finish_call(): pl.pallas_call(functools.partial(finish_kernel, widths, len(igrams)), in_...  8.44 us
    ppermute x10, waiting for transfers between devices, per_device(): lax.ppermute(x, 'row', [(i, i ^ s) for i in range(n_row)])  7.39 us
    pallas_call x2, Pallas kernels, load_call(): pl.pallas_call(load_kernel, in_specs=[pl.BlockSpec(memory_space=pltpu.HBM...  3.37 us
  transfers between devices with their start and end apart: 39, of which 13 were waited for; matrix products, arithmetic and copies ran while one was open for 0% of the time, Pallas kernels for 11%

profile of v6, /device:TPU:0, one launch (start us, length us, event | category | flops | bytes accessed | tf_op | source)
XLA Modules:
  0.0 105.4 jit_solution(901245360019036815)
XLA Ops:
  0.6 3.1 %collective-permute-start.3 = (bf16[1536,128]{1,0:T(8,128)(2,1)}, bf16[1536,128]{1,0:T(8,128)(2,1)S(1)}, u32[]{:S(2)}, u32[]{:S(2)}) collective-permute-start(bf16[1536,128]{1,0:T(8,128)(2,1)} %refs_0_.3), channel_id=1, source_target_pairs={{0,8},{1,17},{2,10},{3,19},{4,12},{5,21},{6,14},{7,23},{8,0},{9,25... | collective-permute-start | bytes 1179656 | tf_op jit(solution)/shard_map/ppermute | solution.py:321
  3.7 1.5 %collective-permute-start = (bf16[512,128]{1,0:T(8,128)(2,1)}, bf16[512,128]{1,0:T(8,128)(2,1)S(1)}, u32[]{:S(2)}, u32[]{:S(2)}) collective-permute-start(bf16[512,128]{1,0:T(8,128)(2,1)} %refs_0_.2), channel_id=1, source_target_pairs={{0,2},{1,3},{2,0},{3,1},{4,6},{5,7},{6,4},{7,5},{8,10},{9,11},{10,... | collective-permute-start | bytes 393224 | tf_op jit(solution)/shard_map/ppermute | solution.py:302
  5.2 1.5 %collective-permute-start.1 = (bf16[512,128]{1,0:T(8,128)(2,1)}, bf16[512,128]{1,0:T(8,128)(2,1)S(1)}, u32[]{:S(2)}, u32[]{:S(2)}) collective-permute-start(bf16[512,128]{1,0:T(8,128)(2,1)} %refs_0_.2), channel_id=1, source_target_pairs={{0,4},{1,5},{2,6},{3,7},{4,0},{5,1},{6,2},{7,3},{8,12},{9,13},{10,... | collective-permute-start | bytes 393224 | tf_op jit(solution)/shard_map/ppermute | solution.py:302
  7.2 3.0 %load.3.b_ref.a_ref = bf16[576,6144]{1,0:T(8,128)(2,1)S(1)} custom-call(bf16[576,6144]{1,0:T(8,128)(2,1)} %hbm_ref.3), custom_call_target="tpu_custom_call" | custom-call | flops 1 | bytes 14155776 | tf_op jit(solution)/shard_map/load/pallas_call | solution.py:58
  10.3 2.8 %copy-done = bf16[576,6144]{1,0:T(8,128)(2,1)} copy-done((bf16[576,6144]{1,0:T(8,128)(2,1)}, bf16[576,6144]{1,0:T(8,128)(2,1)S(1)}, u32[]{:S(2)}) %copy-start) | copy-done | bytes 7077912
  13.4 2.1 %copy-done.3 = bf16[576,4096]{1,0:T(8,128)(2,1)} copy-done((bf16[576,4096]{1,0:T(8,128)(2,1)}, bf16[576,4096]{1,0:T(8,128)(2,1)S(1)}, u32[]{:S(2)}) %copy-start.3) | copy-done | bytes 4718616
  17.7 3.0 %copy-done.1 = bf16[576,6144]{1,0:T(8,128)(2,1)S(1)} copy-done((bf16[576,6144]{1,0:T(8,128)(2,1)S(1)}, bf16[576,6144]{1,0:T(8,128)(2,1)}, u32[]{:S(2)}) %copy-start.1) | copy-done | bytes 7077912
  20.7 2.3 %copy-done.4 = bf16[576,4096]{1,0:T(8,128)(2,1)S(1)} copy-done((bf16[576,4096]{1,0:T(8,128)(2,1)S(1)}, bf16[576,4096]{1,0:T(8,128)(2,1)}, u32[]{:S(2)}) %copy-start.4) | copy-done | bytes 4718616
  23.0 6.9 %image_panel.1 = (f32[4,4,192,128]{3,2,1,0:T(8,128)S(1)}, f32[4,4,192,128]{3,2,1,0:T(8,128)}) custom-call(s32[2]{0:T(128)S(1)} %pad_add_fusion.me_ref, bf16[576,4096]{1,0:T(8,128)(2,1)S(1)} %copy-done.4, bf16[576,6144]{1,0:T(8,128)(2,1)S(1)} %copy-done.1, bf16[512,128]{1,0:T(8,128)(2,1)S(1)} %copy-done.10, ...), custom_call_target="tpu_custom_call" | custom-call | flops 1509949440 | bytes 11796480 | tf_op jit(solution)/shard_map/image_panel/pallas_call | solution.py:91
  30.3 2.5 %collective-permute-start.10 = (bf16[768,128]{1,0:T(8,128)(2,1)S(1)}, bf16[768,128]{1,0:T(8,128)(2,1)S(1)}, u32[]{:S(2)}, u32[]{:S(2)}) collective-permute-start(bf16[768,128]{1,0:T(8,128)(2,1)S(1)} %constant_dynamic-slice_fusion), channel_id=1, source_target_pairs={{0,24},{8,16},{16,8},{24,0},{1,25},{9,17},{17,9},{25,1},{2,26},{10... | collective-permute-start | bytes 589832 | tf_op jit(solution)/shard_map/ppermute | solution.py:303
  34.3 5.0 %collective-permute-done.10.refs_3_ = bf16[768,128]{1,0:T(8,128)(2,1)S(1)} collective-permute-done((bf16[768,128]{1,0:T(8,128)(2,1)S(1)}, bf16[768,128]{1,0:T(8,128)(2,1)S(1)}, u32[]{:S(2)}, u32[]{:S(2)}) %collective-permute-start.10) | collective-permute-done | bytes 196640 | tf_op jit(solution)/shard_map/ppermute | solution.py:303
  39.2 1.5 %collective-permute-start.12 = (bf16[4,192,128]{2,1,0:T(8,128)(2,1)S(1)}, bf16[4,192,128]{2,1,0:T(8,128)(2,1)S(1)}, u32[]{:S(2)}, u32[]{:S(2)}) collective-permute-start(bf16[4,192,128]{2,1,0:T(8,128)(2,1)S(1)} %get-tuple-element.49), channel_id=1, source_target_pairs={{0,2},{1,3},{2,0},{3,1},{4,6},{5,7},{6,4},{7,5},{8,10},{9,11},{10,... | collective-permute-start | bytes 589832 | tf_op jit(solution)/shard_map/ppermute | solution.py:302
  40.7 1.5 %collective-permute-start.13 = (bf16[4,192,128]{2,1,0:T(8,128)(2,1)S(1)}, bf16[4,192,128]{2,1,0:T(8,128)(2,1)S(1)}, u32[]{:S(2)}, u32[]{:S(2)}) collective-permute-start(bf16[4,192,128]{2,1,0:T(8,128)(2,1)S(1)} %get-tuple-element.50), channel_id=1, source_target_pairs={{0,4},{1,5},{2,6},{3,7},{4,0},{5,1},{6,2},{7,3},{8,12},{9,13},{10,... | collective-permute-start | bytes 589832 | tf_op jit(solution)/shard_map/ppermute | solution.py:302
  42.7 3.0 %copy-done.2 = bf16[576,6144]{1,0:T(8,128)(2,1)S(1)} copy-done((bf16[576,6144]{1,0:T(8,128)(2,1)S(1)}, bf16[576,6144]{1,0:T(8,128)(2,1)}, u32[]{:S(2)}) %copy-start.2) | copy-done | bytes 7077912
  45.8 2.3 %copy-done.5 = bf16[576,4096]{1,0:T(8,128)(2,1)S(1)} copy-done((bf16[576,4096]{1,0:T(8,128)(2,1)S(1)}, bf16[576,4096]{1,0:T(8,128)(2,1)}, u32[]{:S(2)}) %copy-start.5) | copy-done | bytes 4718616
  49.1 5.1 %text_panel.1 = (f32[4,1,512,128]{3,2,1,0:T(8,128)S(1)}, f32[4,1,512,128]{3,2,1,0:T(8,128)S(1)}) custom-call(s32[2]{0:T(128)S(1)} %pad_add_fusion.me_ref, bf16[576,6144]{1,0:T(8,128)(2,1)S(1)} %copy-done.2, bf16[576,4096]{1,0:T(8,128)(2,1)S(1)} %copy-done.5, bf16[1536,128]{1,0:T(8,128)(2,1)S(1)} %copy-done.7, bf16[1536,128]{1,0:T(8,128)(2,1)S(1)} %copy-done.9, ...), custom_call_target="tpu_custom_call" | custom-call | flops 1509949440 | bytes 11796480 | tf_op jit(solution)/shard_map/text_panel/pallas_call | solution.py:91
  55.0 2.0 %collective-permute-done.15.refs_1_ = f32[4,1,512,128]{3,2,1,0:T(8,128)S(1)} collective-permute-done((f32[4,1,512,128]{3,2,1,0:T(8,128)S(1)}, f32[4,1,512,128]{3,2,1,0:T(8,128)S(1)}, u32[]{:S(2)}, u32[]{:S(2)}) %collective-permute-start.15) | collective-permute-done | bytes 1048608 | tf_op jit(solution)/shard_map/ppermute | solution.py:302
  57.6 1.6 %collective-permute-start.26 = (bf16[512,128]{1,0:T(8,128)(2,1)S(1)}, bf16[512,128]{1,0:T(8,128)(2,1)S(1)}, u32[]{:S(2)}, u32[]{:S(2)}) collective-permute-start(bf16[512,128]{1,0:T(8,128)(2,1)S(1)} %bitcast.9), channel_id=1, source_target_pairs={{0,2},{1,3},{2,0},{3,1},{4,6},{5,7},{6,4},{7,5},{8,10},{9,11},{10,... | collective-permute-start | bytes 393224 | tf_op jit(solution)/shard_map/ppermute | solution.py:302
  59.2 1.5 %collective-permute-start.27 = (bf16[512,128]{1,0:T(8,128)(2,1)S(1)}, bf16[512,128]{1,0:T(8,128)(2,1)S(1)}, u32[]{:S(2)}, u32[]{:S(2)}) collective-permute-start(bf16[512,128]{1,0:T(8,128)(2,1)S(1)} %bitcast.8), channel_id=1, source_target_pairs={{0,4},{1,5},{2,6},{3,7},{4,0},{5,1},{6,2},{7,3},{8,12},{9,13},{10,... | collective-permute-start | bytes 393224 | tf_op jit(solution)/shard_map/ppermute | solution.py:302
  61.2 3.7 %collective-permute-start.16 = (bf16[192,128]{1,0:T(8,128)(2,1)S(1)}, bf16[192,128]{1,0:T(8,128)(2,1)S(1)}, u32[]{:S(2)}, u32[]{:S(2)}) collective-permute-start(bf16[192,128]{1,0:T(8,128)(2,1)S(1)} %get-tuple-element.59), channel_id=1, source_target_pairs={{0,8},{8,0},{16,24},{24,16},{1,9},{9,1},{17,25},{25,17},{2,10},{10... | collective-permute-start | bytes 147464 | tf_op jit(solution)/shard_map/ppermute | solution.py:303
  66.1 1.5 %collective-permute-start.18 = (bf16[192,128]{1,0:T(8,128)(2,1)S(1)}, bf16[192,128]{1,0:T(8,128)(2,1)S(1)}, u32[]{:S(2)}, u32[]{:S(2)}) collective-permute-start(bf16[192,128]{1,0:T(8,128)(2,1)S(1)} %get-tuple-element.61), channel_id=1, source_target_pairs={{0,24},{8,16},{16,8},{24,0},{1,25},{9,17},{17,9},{25,1},{2,26},{10... | collective-permute-start | bytes 147464 | tf_op jit(solution)/shard_map/ppermute | solution.py:303
  67.6 3.5 %collective-permute-start.29 = (bf16[512,128]{1,0:T(8,128)(2,1)S(1)}, bf16[512,128]{1,0:T(8,128)(2,1)S(1)}, u32[]{:S(2)}, u32[]{:S(2)}) collective-permute-start(bf16[512,128]{1,0:T(8,128)(2,1)S(1)} %text_plane.1.refs_0_), channel_id=1, source_target_pairs={{0,8},{8,0},{16,24},{24,16},{1,9},{9,1},{17,25},{25,17},{2,10},{10... | collective-permute-start | bytes 393224 | tf_op jit(solution)/shard_map/ppermute | solution.py:303
  73.7 1.4 %collective-permute-start.31 = (bf16[512,128]{1,0:T(8,128)(2,1)S(1)}, bf16[512,128]{1,0:T(8,128)(2,1)S(1)}, u32[]{:S(2)}, u32[]{:S(2)}) collective-permute-start(bf16[512,128]{1,0:T(8,128)(2,1)S(1)} %text_plane.1.refs_0_), channel_id=1, source_target_pairs={{0,24},{8,16},{16,8},{24,0},{1,25},{9,17},{17,9},{25,1},{2,26},{10... | collective-permute-start | bytes 393224 | tf_op jit(solution)/shard_map/ppermute | solution.py:303
  75.2 1.6 %collective-permute-start.20 = (bf16[192,128]{1,0:T(8,128)(2,1)S(1)}, bf16[192,128]{1,0:T(8,128)(2,1)S(1)}, u32[]{:S(2)}, u32[]{:S(2)}) collective-permute-start(bf16[192,128]{1,0:T(8,128)(2,1)S(1)} %image_depth.1.refs_0_), channel_id=1, source_target_pairs={{0,4},{1,5},{2,6},{3,7},{4,0},{5,1},{6,2},{7,3},{8,12},{9,13},{10,... | collective-permute-start | bytes 147464 | tf_op jit(solution)/shard_map/ppermute | solution.py:302
  76.8 2.0 %collective-permute-start.21 = (bf16[192,128]{1,0:T(8,128)(2,1)S(1)}, bf16[192,128]{1,0:T(8,128)(2,1)S(1)}, u32[]{:S(2)}, u32[]{:S(2)}) collective-permute-start(bf16[192,128]{1,0:T(8,128)(2,1)S(1)} %image_depth.1.refs_0_), channel_id=1, source_target_pairs={{0,6},{1,7},{2,4},{3,5},{4,2},{5,3},{6,0},{7,1},{8,14},{9,15},{10,... | collective-permute-start | bytes 147464 | tf_op jit(solution)/shard_map/ppermute | solution.py:302
  79.3 2.5 %collective-permute-done.21.refs_3_ = bf16[192,128]{1,0:T(8,128)(2,1)S(1)} collective-permute-done((bf16[192,128]{1,0:T(8,128)(2,1)S(1)}, bf16[192,128]{1,0:T(8,128)(2,1)S(1)}, u32[]{:S(2)}, u32[]{:S(2)}) %collective-permute-start.21) | collective-permute-done | bytes 49184 | tf_op jit(solution)/shard_map/ppermute | solution.py:302
  85.0 1.5 %collective-permute-start.32 = (f32[128,128]{1,0:T(8,128)S(1)}, f32[128,128]{1,0:T(8,128)S(1)}, u32[]{:S(2)}, u32[]{:S(2)}) collective-permute-start(f32[128,128]{1,0:T(8,128)S(1)} %get-tuple-element.70.refs_0_), channel_id=1, source_target_pairs={{0,8},{8,0},{16,24},{24,16},{1,9},{9,1},{17,25},{25,17},{2,10},{10... | collective-permute-start | bytes 196616 | tf_op jit(solution)/shard_map/ppermute | solution.py:303
  86.5 1.6 %collective-permute-start.33 = (f32[128,128]{1,0:T(8,128)S(1)}, f32[128,128]{1,0:T(8,128)S(1)}, u32[]{:S(2)}, u32[]{:S(2)}) collective-permute-start(f32[128,128]{1,0:T(8,128)S(1)} %get-tuple-element.70.refs_0_), channel_id=1, source_target_pairs={{0,16},{8,24},{16,0},{24,8},{1,17},{9,25},{17,1},{25,9},{2,18},{10... | collective-permute-start | bytes 196616 | tf_op jit(solution)/shard_map/ppermute | solution.py:303
  88.1 1.4 %collective-permute-start.34 = (f32[128,128]{1,0:T(8,128)S(1)}, f32[128,128]{1,0:T(8,128)S(1)}, u32[]{:S(2)}, u32[]{:S(2)}) collective-permute-start(f32[128,128]{1,0:T(8,128)S(1)} %get-tuple-element.70.refs_0_), channel_id=1, source_target_pairs={{0,24},{8,16},{16,8},{24,0},{1,25},{9,17},{17,9},{25,1},{2,26},{10... | collective-permute-start | bytes 196616 | tf_op jit(solution)/shard_map/ppermute | solution.py:303
  89.4 2.0 %collective-permute-start.36 = (f32[128,128]{1,0:T(8,128)S(1)}, f32[128,128]{1,0:T(8,128)S(1)}, u32[]{:S(2)}, u32[]{:S(2)}) collective-permute-start(f32[128,128]{1,0:T(8,128)S(1)} %text_gram_cores.1.refs_4_), channel_id=1, source_target_pairs={{0,2},{1,3},{2,0},{3,1},{4,6},{5,7},{6,4},{7,5},{8,10},{9,11},{10,... | collective-permute-start | bytes 196616 | tf_op jit(solution)/shard_map/ppermute | solution.py:302
  93.0 1.9 %collective-permute-done.33.refs_2_ = f32[128,128]{1,0:T(8,128)S(1)} collective-permute-done((f32[128,128]{1,0:T(8,128)S(1)}, f32[128,128]{1,0:T(8,128)S(1)}, u32[]{:S(2)}, u32[]{:S(2)}) %collective-permute-start.33) | collective-permute-done | bytes 65568 | tf_op jit(solution)/shard_map/ppermute | solution.py:303
  96.9 8.4 %finish.1 = (f32[1536,128]{1,0:T(8,128)}, f32[512,128]{1,0:T(8,128)}) custom-call(bf16[8,192,128]{2,1,0:T(8,128)(2,1)S(1)} %get-tuple-element.62.ipanel, bf16[1,512,128]{2,1,0:T(8,128)(2,1)S(1)} %get-tuple-element.69.tpanel, f32[128,128]{1,0:T(8,128)S(1)} %get-tuple-element.70.refs_0_, f32[128,128]{1,0:T(8,128)S(1)} %collective-permute-done.32.refs_1_, ...), custom_call_target="tpu_custom_call" | custom-call | flops 10000000000 | bytes 1179648 | tf_op jit(solution)/shard_map/finish/pallas_call | solution.py:288
  (83 shorter events, 19.2 us)
Async XLA Ops:
  0.6 16.1 %collective-permute-start.3 = (bf16[1536,128]{1,0:T(8,128)(2,1)}, bf16[1536,128]{1,0:T(8,128)(2,1)S(1)}, u32[]{:S(2)}, u32[]{:S(2)}) collective-permute-start(bf16[1536,128]{1,0:T(8,128)(2,1)} %refs_0_.3), channel_id=1, source_target_pairs={{0,8},{1,17},{2,10},{3,19},{4,12},{5,21},{6,14},{7,23},{8,0},{9,25... | collective-permute-start | bytes 1179656 | tf_op jit(solution)/shard_map/ppermute | solution.py:321
  3.7 11.8 %collective-permute-start = (bf16[512,128]{1,0:T(8,128)(2,1)}, bf16[512,128]{1,0:T(8,128)(2,1)S(1)}, u32[]{:S(2)}, u32[]{:S(2)}) collective-permute-start(bf16[512,128]{1,0:T(8,128)(2,1)} %refs_0_.2), channel_id=1, source_target_pairs={{0,2},{1,3},{2,0},{3,1},{4,6},{5,7},{6,4},{7,5},{8,10},{9,11},{10,... | collective-permute-start | bytes 393224 | tf_op jit(solution)/shard_map/ppermute | solution.py:302
  5.2 10.3 %collective-permute-start.1 = (bf16[512,128]{1,0:T(8,128)(2,1)}, bf16[512,128]{1,0:T(8,128)(2,1)S(1)}, u32[]{:S(2)}, u32[]{:S(2)}) collective-permute-start(bf16[512,128]{1,0:T(8,128)(2,1)} %refs_0_.2), channel_id=1, source_target_pairs={{0,4},{1,5},{2,6},{3,7},{4,0},{5,1},{6,2},{7,3},{8,12},{9,13},{10,... | collective-permute-start | bytes 393224 | tf_op jit(solution)/shard_map/ppermute | solution.py:302
  6.7 8.8 %collective-permute-start.2 = (bf16[512,128]{1,0:T(8,128)(2,1)}, bf16[512,128]{1,0:T(8,128)(2,1)S(1)}, u32[]{:S(2)}, u32[]{:S(2)}) collective-permute-start(bf16[512,128]{1,0:T(8,128)(2,1)} %refs_0_.2), channel_id=1, source_target_pairs={{0,6},{1,7},{2,4},{3,5},{4,2},{5,3},{6,0},{7,1},{8,14},{9,15},{10,... | collective-permute-start | bytes 393224 | tf_op jit(solution)/shard_map/ppermute | solution.py:302
  7.2 9.5 %collective-permute-start.5 = (bf16[512,128]{1,0:T(8,128)(2,1)}, bf16[512,128]{1,0:T(8,128)(2,1)S(1)}, u32[]{:S(2)}, u32[]{:S(2)}) collective-permute-start(bf16[512,128]{1,0:T(8,128)(2,1)} %refs_0_.2), channel_id=1, source_target_pairs={{0,1},{1,0},{2,3},{3,2},{4,5},{5,4},{6,7},{7,6},{8,9},{9,8},{10,11... | collective-permute-start | bytes 393224 | tf_op jit(solution)/shard_map/ppermute | solution.py:302
  29.9 3.6 %collective-permute-start.9 = (f32[4,4,192,128]{3,2,1,0:T(8,128)}, f32[4,4,192,128]{3,2,1,0:T(8,128)S(1)}, u32[]{:S(2)}, u32[]{:S(2)}) collective-permute-start(f32[4,4,192,128]{3,2,1,0:T(8,128)} %get-tuple-element.45), channel_id=1, source_target_pairs={{0,1},{1,0},{2,3},{3,2},{4,5},{5,4},{6,7},{7,6},{8,9},{9,8},{10,11... | collective-permute-start | bytes 4718600 | tf_op jit(solution)/shard_map/ppermute | solution.py:302
  30.3 9.0 %collective-permute-start.10 = (bf16[768,128]{1,0:T(8,128)(2,1)S(1)}, bf16[768,128]{1,0:T(8,128)(2,1)S(1)}, u32[]{:S(2)}, u32[]{:S(2)}) collective-permute-start(bf16[768,128]{1,0:T(8,128)(2,1)S(1)} %constant_dynamic-slice_fusion), channel_id=1, source_target_pairs={{0,24},{8,16},{16,8},{24,0},{1,25},{9,17},{17,9},{25,1},{2,26},{10... | collective-permute-start | bytes 589832 | tf_op jit(solution)/shard_map/ppermute | solution.py:303
  32.8 9.9 %collective-permute-start.4 = (bf16[1536,128]{1,0:T(8,128)(2,1)}, bf16[1536,128]{1,0:T(8,128)(2,1)S(1)}, u32[]{:S(2)}, u32[]{:S(2)}) collective-permute-start(bf16[1536,128]{1,0:T(8,128)(2,1)} %copy-done.8), channel_id=1, source_target_pairs={{0,1},{1,0},{2,3},{3,2},{4,5},{5,4},{6,7},{7,6},{8,9},{9,8},{10,11... | collective-permute-start | bytes 1179656 | tf_op jit(solution)/shard_map/ppermute | solution.py:302
  39.2 3.5 %collective-permute-start.11 = (bf16[768,128]{1,0:T(8,128)(2,1)S(1)}, bf16[768,128]{1,0:T(8,128)(2,1)S(1)}, u32[]{:S(2)}, u32[]{:S(2)}) collective-permute-start(bf16[768,128]{1,0:T(8,128)(2,1)S(1)} %collective-permute-done.10.refs_3_), channel_id=1, source_target_pairs={{0,1},{1,0},{2,3},{3,2},{4,5},{5,4},{6,7},{7,6},{8,9},{9,8},{10,11... | collective-permute-start | bytes 589832 | tf_op jit(solution)/shard_map/ppermute | solution.py:302
  39.2 15.0 %collective-permute-start.12 = (bf16[4,192,128]{2,1,0:T(8,128)(2,1)S(1)}, bf16[4,192,128]{2,1,0:T(8,128)(2,1)S(1)}, u32[]{:S(2)}, u32[]{:S(2)}) collective-permute-start(bf16[4,192,128]{2,1,0:T(8,128)(2,1)S(1)} %get-tuple-element.49), channel_id=1, source_target_pairs={{0,2},{1,3},{2,0},{3,1},{4,6},{5,7},{6,4},{7,5},{8,10},{9,11},{10,... | collective-permute-start | bytes 589832 | tf_op jit(solution)/shard_map/ppermute | solution.py:302
  40.7 13.5 %collective-permute-start.13 = (bf16[4,192,128]{2,1,0:T(8,128)(2,1)S(1)}, bf16[4,192,128]{2,1,0:T(8,128)(2,1)S(1)}, u32[]{:S(2)}, u32[]{:S(2)}) collective-permute-start(bf16[4,192,128]{2,1,0:T(8,128)(2,1)S(1)} %get-tuple-element.50), channel_id=1, source_target_pairs={{0,4},{1,5},{2,6},{3,7},{4,0},{5,1},{6,2},{7,3},{8,12},{9,13},{10,... | collective-permute-start | bytes 589832 | tf_op jit(solution)/shard_map/ppermute | solution.py:302
  42.3 12.0 %collective-permute-start.14 = (bf16[4,192,128]{2,1,0:T(8,128)(2,1)S(1)}, bf16[4,192,128]{2,1,0:T(8,128)(2,1)S(1)}, u32[]{:S(2)}, u32[]{:S(2)}) collective-permute-start(bf16[4,192,128]{2,1,0:T(8,128)(2,1)S(1)} %get-tuple-element.51), channel_id=1, source_target_pairs={{0,6},{1,7},{2,4},{3,5},{4,2},{5,3},{6,0},{7,1},{8,14},{9,15},{10,... | collective-permute-start | bytes 589832 | tf_op jit(solution)/shard_map/ppermute | solution.py:302
  57.6 8.5 %collective-permute-start.26 = (bf16[512,128]{1,0:T(8,128)(2,1)S(1)}, bf16[512,128]{1,0:T(8,128)(2,1)S(1)}, u32[]{:S(2)}, u32[]{:S(2)}) collective-permute-start(bf16[512,128]{1,0:T(8,128)(2,1)S(1)} %bitcast.9), channel_id=1, source_target_pairs={{0,2},{1,3},{2,0},{3,1},{4,6},{5,7},{6,4},{7,5},{8,10},{9,11},{10,... | collective-permute-start | bytes 393224 | tf_op jit(solution)/shard_map/ppermute | solution.py:302
  59.2 8.4 %collective-permute-start.27 = (bf16[512,128]{1,0:T(8,128)(2,1)S(1)}, bf16[512,128]{1,0:T(8,128)(2,1)S(1)}, u32[]{:S(2)}, u32[]{:S(2)}) collective-permute-start(bf16[512,128]{1,0:T(8,128)(2,1)S(1)} %bitcast.8), channel_id=1, source_target_pairs={{0,4},{1,5},{2,6},{3,7},{4,0},{5,1},{6,2},{7,3},{8,12},{9,13},{10,... | collective-permute-start | bytes 393224 | tf_op jit(solution)/shard_map/ppermute | solution.py:302
  60.7 6.8 %collective-permute-start.28 = (bf16[512,128]{1,0:T(8,128)(2,1)S(1)}, bf16[512,128]{1,0:T(8,128)(2,1)S(1)}, u32[]{:S(2)}, u32[]{:S(2)}) collective-permute-start(bf16[512,128]{1,0:T(8,128)(2,1)S(1)} %bitcast.7), channel_id=1, source_target_pairs={{0,6},{1,7},{2,4},{3,5},{4,2},{5,3},{6,0},{7,1},{8,14},{9,15},{10,... | collective-permute-start | bytes 393224 | tf_op jit(solution)/shard_map/ppermute | solution.py:302
  61.2 11.2 %collective-permute-start.16 = (bf16[192,128]{1,0:T(8,128)(2,1)S(1)}, bf16[192,128]{1,0:T(8,128)(2,1)S(1)}, u32[]{:S(2)}, u32[]{:S(2)}) collective-permute-start(bf16[192,128]{1,0:T(8,128)(2,1)S(1)} %get-tuple-element.59), channel_id=1, source_target_pairs={{0,8},{8,0},{16,24},{24,16},{1,9},{9,1},{17,25},{25,17},{2,10},{10... | collective-permute-start | bytes 147464 | tf_op jit(solution)/shard_map/ppermute | solution.py:303
  64.9 7.5 %collective-permute-start.17 = (bf16[192,128]{1,0:T(8,128)(2,1)S(1)}, bf16[192,128]{1,0:T(8,128)(2,1)S(1)}, u32[]{:S(2)}, u32[]{:S(2)}) collective-permute-start(bf16[192,128]{1,0:T(8,128)(2,1)S(1)} %get-tuple-element.60), channel_id=1, source_target_pairs={{0,16},{8,24},{16,0},{24,8},{1,17},{9,25},{17,1},{25,9},{2,18},{10... | collective-permute-start | bytes 147464 | tf_op jit(solution)/shard_map/ppermute | solution.py:303
  66.1 6.3 %collective-permute-start.18 = (bf16[192,128]{1,0:T(8,128)(2,1)S(1)}, bf16[192,128]{1,0:T(8,128)(2,1)S(1)}, u32[]{:S(2)}, u32[]{:S(2)}) collective-permute-start(bf16[192,128]{1,0:T(8,128)(2,1)S(1)} %get-tuple-element.61), channel_id=1, source_target_pairs={{0,24},{8,16},{16,8},{24,0},{1,25},{9,17},{17,9},{25,1},{2,26},{10... | collective-permute-start | bytes 147464 | tf_op jit(solution)/shard_map/ppermute | solution.py:303
  67.6 14.2 %collective-permute-start.29 = (bf16[512,128]{1,0:T(8,128)(2,1)S(1)}, bf16[512,128]{1,0:T(8,128)(2,1)S(1)}, u32[]{:S(2)}, u32[]{:S(2)}) collective-permute-start(bf16[512,128]{1,0:T(8,128)(2,1)S(1)} %text_plane.1.refs_0_), channel_id=1, source_target_pairs={{0,8},{8,0},{16,24},{24,16},{1,9},{9,1},{17,25},{25,17},{2,10},{10... | collective-permute-start | bytes 393224 | tf_op jit(solution)/shard_map/ppermute | solution.py:303
  71.1 11.7 %collective-permute-start.30 = (bf16[512,128]{1,0:T(8,128)(2,1)S(1)}, bf16[512,128]{1,0:T(8,128)(2,1)S(1)}, u32[]{:S(2)}, u32[]{:S(2)}) collective-permute-start(bf16[512,128]{1,0:T(8,128)(2,1)S(1)} %text_plane.1.refs_0_), channel_id=1, source_target_pairs={{0,16},{8,24},{16,0},{24,8},{1,17},{9,25},{17,1},{25,9},{2,18},{10... | collective-permute-start | bytes 393224 | tf_op jit(solution)/shard_map/ppermute | solution.py:303
  72.4 4.4 %collective-permute-start.19 = (bf16[192,128]{1,0:T(8,128)(2,1)S(1)}, bf16[192,128]{1,0:T(8,128)(2,1)S(1)}, u32[]{:S(2)}, u32[]{:S(2)}) collective-permute-start(bf16[192,128]{1,0:T(8,128)(2,1)S(1)} %image_depth.1.refs_0_), channel_id=1, source_target_pairs={{0,2},{1,3},{2,0},{3,1},{4,6},{5,7},{6,4},{7,5},{8,10},{9,11},{10,... | collective-permute-start | bytes 147464 | tf_op jit(solution)/shard_map/ppermute | solution.py:302
  73.7 9.1 %collective-permute-start.31 = (bf16[512,128]{1,0:T(8,128)(2,1)S(1)}, bf16[512,128]{1,0:T(8,128)(2,1)S(1)}, u32[]{:S(2)}, u32[]{:S(2)}) collective-permute-start(bf16[512,128]{1,0:T(8,128)(2,1)S(1)} %text_plane.1.refs_0_), channel_id=1, source_target_pairs={{0,24},{8,16},{16,8},{24,0},{1,25},{9,17},{17,9},{25,1},{2,26},{10... | collective-permute-start | bytes 393224 | tf_op jit(solution)/shard_map/ppermute | solution.py:303
  75.2 4.1 %collective-permute-start.20 = (bf16[192,128]{1,0:T(8,128)(2,1)S(1)}, bf16[192,128]{1,0:T(8,128)(2,1)S(1)}, u32[]{:S(2)}, u32[]{:S(2)}) collective-permute-start(bf16[192,128]{1,0:T(8,128)(2,1)S(1)} %image_depth.1.refs_0_), channel_id=1, source_target_pairs={{0,4},{1,5},{2,6},{3,7},{4,0},{5,1},{6,2},{7,3},{8,12},{9,13},{10,... | collective-permute-start | bytes 147464 | tf_op jit(solution)/shard_map/ppermute | solution.py:302
  76.8 5.0 %collective-permute-start.21 = (bf16[192,128]{1,0:T(8,128)(2,1)S(1)}, bf16[192,128]{1,0:T(8,128)(2,1)S(1)}, u32[]{:S(2)}, u32[]{:S(2)}) collective-permute-start(bf16[192,128]{1,0:T(8,128)(2,1)S(1)} %image_depth.1.refs_0_), channel_id=1, source_target_pairs={{0,6},{1,7},{2,4},{3,5},{4,2},{5,3},{6,0},{7,1},{8,14},{9,15},{10,... | collective-permute-start | bytes 147464 | tf_op jit(solution)/shard_map/ppermute | solution.py:302
  79.3 4.4 %collective-permute-start.22 = (bf16[192,128]{1,0:T(8,128)(2,1)S(1)}, bf16[192,128]{1,0:T(8,128)(2,1)S(1)}, u32[]{:S(2)}, u32[]{:S(2)}) collective-permute-start(bf16[192,128]{1,0:T(8,128)(2,1)S(1)} %image_depth.1.refs_0_), channel_id=1, source_target_pairs={{0,1},{1,0},{2,3},{3,2},{4,5},{5,4},{6,7},{7,6},{8,9},{9,8},{10,11... | collective-permute-start | bytes 147464 | tf_op jit(solution)/shard_map/ppermute | solution.py:302
  83.1 6.3 %collective-permute-start.35 = (f32[128,128]{1,0:T(8,128)S(1)}, f32[128,128]{1,0:T(8,128)S(1)}, u32[]{:S(2)}, u32[]{:S(2)}) collective-permute-start(f32[128,128]{1,0:T(8,128)S(1)} %get-tuple-element.71.own_ref), channel_id=1, source_target_pairs={{0,1},{1,0},{2,3},{3,2},{4,5},{5,4},{6,7},{7,6},{8,9},{9,8},{10,11... | collective-permute-start | bytes 196616 | tf_op jit(solution)/shard_map/ppermute | solution.py:302
  85.0 6.8 %collective-permute-start.32 = (f32[128,128]{1,0:T(8,128)S(1)}, f32[128,128]{1,0:T(8,128)S(1)}, u32[]{:S(2)}, u32[]{:S(2)}) collective-permute-start(f32[128,128]{1,0:T(8,128)S(1)} %get-tuple-element.70.refs_0_), channel_id=1, source_target_pairs={{0,8},{8,0},{16,24},{24,16},{1,9},{9,1},{17,25},{25,17},{2,10},{10... | collective-permute-start | bytes 196616 | tf_op jit(solution)/shard_map/ppermute | solution.py:303
  86.5 8.4 %collective-permute-start.33 = (f32[128,128]{1,0:T(8,128)S(1)}, f32[128,128]{1,0:T(8,128)S(1)}, u32[]{:S(2)}, u32[]{:S(2)}) collective-permute-start(f32[128,128]{1,0:T(8,128)S(1)} %get-tuple-element.70.refs_0_), channel_id=1, source_target_pairs={{0,16},{8,24},{16,0},{24,8},{1,17},{9,25},{17,1},{25,9},{2,18},{10... | collective-permute-start | bytes 196616 | tf_op jit(solution)/shard_map/ppermute | solution.py:303
  88.1 6.8 %collective-permute-start.34 = (f32[128,128]{1,0:T(8,128)S(1)}, f32[128,128]{1,0:T(8,128)S(1)}, u32[]{:S(2)}, u32[]{:S(2)}) collective-permute-start(f32[128,128]{1,0:T(8,128)S(1)} %get-tuple-element.70.refs_0_), channel_id=1, source_target_pairs={{0,24},{8,16},{16,8},{24,0},{1,25},{9,17},{17,9},{25,1},{2,26},{10... | collective-permute-start | bytes 196616 | tf_op jit(solution)/shard_map/ppermute | solution.py:303
  89.4 5.4 %collective-permute-start.36 = (f32[128,128]{1,0:T(8,128)S(1)}, f32[128,128]{1,0:T(8,128)S(1)}, u32[]{:S(2)}, u32[]{:S(2)}) collective-permute-start(f32[128,128]{1,0:T(8,128)S(1)} %text_gram_cores.1.refs_4_), channel_id=1, source_target_pairs={{0,2},{1,3},{2,0},{3,1},{4,6},{5,7},{6,4},{7,5},{8,10},{9,11},{10,... | collective-permute-start | bytes 196616 | tf_op jit(solution)/shard_map/ppermute | solution.py:302
  91.4 4.4 %collective-permute-start.37 = (f32[128,128]{1,0:T(8,128)S(1)}, f32[128,128]{1,0:T(8,128)S(1)}, u32[]{:S(2)}, u32[]{:S(2)}) collective-permute-start(f32[128,128]{1,0:T(8,128)S(1)} %text_gram_cores.1.refs_4_), channel_id=1, source_target_pairs={{0,4},{1,5},{2,6},{3,7},{4,0},{5,1},{6,2},{7,3},{8,12},{9,13},{10,... | collective-permute-start | bytes 196616 | tf_op jit(solution)/shard_map/ppermute | solution.py:302
  91.8 5.2 %collective-permute-start.38 = (f32[128,128]{1,0:T(8,128)S(1)}, f32[128,128]{1,0:T(8,128)S(1)}, u32[]{:S(2)}, u32[]{:S(2)}) collective-permute-start(f32[128,128]{1,0:T(8,128)S(1)} %text_gram_cores.1.refs_4_), channel_id=1, source_target_pairs={{0,6},{1,7},{2,4},{3,5},{4,2},{5,3},{6,0},{7,1},{8,14},{9,15},{10,... | collective-permute-start | bytes 196616 | tf_op jit(solution)/shard_map/ppermute | solution.py:302
  (18 other events, 53.8 us)

commit v7 on v6

--- a/solution.py
+++ b/solution.py
@@ -13,7 +13,7 @@
 VMEM = pl.BlockSpec(memory_space=pltpu.VMEM)
 SMEM = pl.BlockSpec(memory_space=pltpu.SMEM)
 LIMIT = 16 * 1024 * 1024
-LOAD_LIMITS = (42, 46)
+LOAD_LIMITS = (4, 4)
 
 
 def sds(shape, dtype):
@@ -206,55 +206,37 @@
     )(*parts)
 
 
-def reciprocal(x):
-    guess = pl.reciprocal(x, approx=True)
-    guess = guess * (2.0 - x * guess)
-    return guess * (2.0 - x * guess)
-
-
 def inverse_factor(gram):
     n = gram.shape[0]
-    blocks = n // 8
     lane = lax.broadcasted_iota(jnp.int32, (8, n), 1)
     sub = lax.broadcasted_iota(jnp.int32, (8, n), 0)
-    rows = [gram[8 * i : 8 * i + 8, :] for i in range(blocks)]
-
-    def column(x, k):
-        return jnp.broadcast_to(x[:, k : k + 1], (8, n))
-
-    def row(x, j):
-        return jnp.broadcast_to(x[j : j + 1, :], (8, n))
-
-    for b in range(blocks):
-        first = 8 * b
-        diag = [column(rows[b], first + j) for j in range(8)]
-        below = [[column(rows[i], first + j) for j in range(8)] for i in range(b + 1, blocks)]
-        lower = full = rows[b]
-        pivots = scales = jnp.ones((8, n), F32)
+    rows = [gram[8 * i : 8 * i + 8, :] for i in range(n // 8)]
+    for b in range(n // 8):
+        cols = [
+            [jnp.broadcast_to(rows[i][:, 8 * b + j : 8 * b + j + 1], (8, n)) for i in range(b, n // 8)]
+            for j in range(8)
+        ]
+        scale = jnp.ones((8, n), F32)
         for j in range(8):
-            k = first + j
-            pivot = row(diag[j], j)
-            inv = reciprocal(pivot)
-            others = jnp.where(sub == j, 0.0, diag[j] * inv)
-            pivot_row = jnp.where(lane == k, 1.0, row(lower, j))
+            k = 8 * b + j
+            pivot = jnp.broadcast_to(cols[j][0][j : j + 1, :], (8, n))
+            inv = 1.0 / pivot
+            scale = jnp.where(sub == j, pivot, scale)
+            pivot_row = jnp.where(lane == k, 1.0, jnp.broadcast_to(rows[b][j : j + 1, :], (8, n)))
+            below = sub > j
+            mult = [c * inv for c in cols[j]]
+            mult[0] = jnp.where(below, mult[0], 0.0)
             for jj in range(j + 1, 8):
-                diag[jj] = diag[jj] - others * row(diag[jj], j)
-            full = jnp.where(lane == k, jnp.where(sub == j, 1.0, 0.0), full) - others * pivot_row
-            lower = jnp.where(sub > j, full, lower)
-            pivots = jnp.where(sub == j, pivot, pivots)
-            scales = jnp.where(sub == j, inv, scales)
+                entry = jnp.broadcast_to(cols[jj][0][j : j + 1, :], (8, n))
+                cols[jj] = [c - m * entry for c, m in zip(cols[jj], mult)]
+            for i in range(b, n // 8):
+                here = lane == k
+                if i == b:
+                    here = jnp.logical_and(here, below)
+                rows[i] = jnp.where(here, 0.0, rows[i]) - mult[i - b] * pivot_row
             yield None
-        full = full * scales
-        solved = [row(full, j) for j in range(8)]
-        inside = jnp.logical_and(lane >= first, lane < first + 8)
-        for i in range(b + 1, blocks):
-            terms = [c * z for c, z in zip(below[i - b - 1], solved)]
-            while len(terms) > 1:
-                terms = [x + y for x, y in zip(terms[::2], terms[1::2])]
-            rows[i] = jnp.where(inside, 0.0, rows[i]) - terms[0]
-        diagonal = sub + first
-        unit = jnp.where(lane == diagonal, 1.0, jnp.where(lane < diagonal, lower, 0.0))
-        rows[b] = unit * lax.rsqrt(pivots)
+        unit = jnp.where(lane == sub + 8 * b, 1.0, jnp.where(lane < sub + 8 * b, rows[b], 0.0))
+        rows[b] = unit * lax.rsqrt(scale)
         yield None
     yield jnp.concatenate(rows, axis=0)
 
@@ -343,9 +325,9 @@
         first, text_feats, image_feats, list(text_parts.values()), columns, n_row, groups, "image_panel"
     )
     own, *sends = sums_call("col", 1, chips, me, [keep, col_swap(send, 1)], "image_cores")
-    own, mine = lax.optimization_barrier((own, mine))
+    received = over_chips(sends)
+    mine, *received = lax.optimization_barrier((mine, *received))
     image_parts += [mine, col_swap(mine, 1)]
-    received = over_chips(sends)
     columns = image_columns(image_order, probe_image.shape[0])
     keep, send = panel_call(
         me, image_feats, text_feats, image_parts, columns, groups, 1, "text_panel"

time: 106 us -> 110 us (1.038)
  waiting for transfers between devices: 16.6 us -> 22.8 us
  local copies, waits for them, and re-layouts: 16.6 us -> 21 us
  Pallas kernels: 27.1 us -> 23.7 us
  starting transfers between devices: 44.2 us -> 41.2 us
    ppermute x28, waiting for transfers between devices: 9.16 us -> 19.1 us  [per_device(): lax.ppermute(x, 'col', [(i, i ^ s) for i in range(n_col)])]
    unnamed x22 -> x24, local copies, waits for them, and re-layouts: 16.6 us -> 21 us
    ppermute x10, waiting for transfers between devices: 7.39 us -> 3.67 us  [per_device(): lax.ppermute(x, 'row', [(i, i ^ s) for i in range(n_row)])]
    pallas_call x2, Pallas kernels: 3.37 us -> 0.8 us  [load_call(): pl.pallas_call(load_kernel, in_specs=[pl.BlockSpec(memory_space=pltpu.HBM...]
    ppermute x10, starting transfers between devices: 19.5 us -> 18 us  [per_device(): lax.ppermute(x, 'row', [(i, i ^ s) for i in range(n_row)])]
    ppermute x28, starting transfers between devices: 21.6 us -> 20.1 us  [per_device(): lax.ppermute(x, 'col', [(i, i ^ s) for i in range(n_col)])]
  transfers between devices with their start and end apart: 39 -> 39, of which waited for: 13 -> 17; matrix products, arithmetic and copies ran while one was open for 0% -> 0% of each run, Pallas kernels for 11% -> 3%
where the time goes in v7:
time: 110 us; the launch traced here: 109 us
  starting transfers between devices  41.2 us (37%)
  Pallas kernels  23.7 us (22%)
  waiting for transfers between devices  22.8 us (21%)
  local copies, waits for them, and re-layouts  21 us (19%)
    unnamed x24, local copies, waits for them, and re-layouts  21 us
    ppermute x28, starting transfers between devices, per_device(): lax.ppermute(x, 'col', [(i, i ^ s) for i in range(n_col)])  20.1 us
    ppermute x28, waiting for transfers between devices, per_device(): lax.ppermute(x, 'col', [(i, i ^ s) for i in range(n_col)])  19.1 us
    ppermute x10, starting transfers between devices, per_device(): lax.ppermute(x, 'row', [(i, i ^ s) for i in range(n_row)])  18 us
    pallas_call x2, Pallas kernels, panel_call(): pl.pallas_call(functools.partial(panel_kernel, columns, len(parts), block...  12 us
    pallas_call x1, Pallas kernels, finish_call(): pl.pallas_call(functools.partial(finish_kernel, widths, len(igrams)), in_...  7.57 us
    ppermute x10, waiting for transfers between devices, per_device(): lax.ppermute(x, 'row', [(i, i ^ s) for i in range(n_row)])  3.67 us
    ppermute x1, starting transfers between devices, split_swap(): return lax.ppermute(x, ('row', 'col'), pairs)  3.09 us
  transfers between devices with their start and end apart: 39, of which 17 were waited for; matrix products, arithmetic and copies ran while one was open for 0% of the time, Pallas kernels for 3%

profile of v7, /device:TPU:0, one launch (start us, length us, event | category | flops | bytes accessed | tf_op | source)
XLA Modules:
  0.0 109.4 jit_solution(9983415130334663353)
XLA Ops:
  0.6 3.1 %collective-permute-start.3 = (bf16[1536,128]{1,0:T(8,128)(2,1)}, bf16[1536,128]{1,0:T(8,128)(2,1)S(1)}, u32[]{:S(2)}, u32[]{:S(2)}) collective-permute-start(bf16[1536,128]{1,0:T(8,128)(2,1)} %refs_0_.3), channel_id=1, source_target_pairs={{0,8},{1,17},{2,10},{3,19},{4,12},{5,21},{6,14},{7,23},{8,0},{9,25... | collective-permute-start | bytes 1179656 | tf_op jit(solution)/shard_map/ppermute | solution.py:303
  3.7 1.5 %collective-permute-start = (bf16[512,128]{1,0:T(8,128)(2,1)}, bf16[512,128]{1,0:T(8,128)(2,1)S(1)}, u32[]{:S(2)}, u32[]{:S(2)}) collective-permute-start(bf16[512,128]{1,0:T(8,128)(2,1)} %refs_0_.2), channel_id=1, source_target_pairs={{0,2},{1,3},{2,0},{3,1},{4,6},{5,7},{6,4},{7,5},{8,10},{9,11},{10,... | collective-permute-start | bytes 393224 | tf_op jit(solution)/shard_map/ppermute | solution.py:284
  5.2 1.5 %collective-permute-start.1 = (bf16[512,128]{1,0:T(8,128)(2,1)}, bf16[512,128]{1,0:T(8,128)(2,1)S(1)}, u32[]{:S(2)}, u32[]{:S(2)}) collective-permute-start(bf16[512,128]{1,0:T(8,128)(2,1)} %refs_0_.2), channel_id=1, source_target_pairs={{0,4},{1,5},{2,6},{3,7},{4,0},{5,1},{6,2},{7,3},{8,12},{9,13},{10,... | collective-permute-start | bytes 393224 | tf_op jit(solution)/shard_map/ppermute | solution.py:284
  7.2 3.0 %copy-done.6 = bf16[576,6144]{1,0:T(8,128)(2,1)S(1)} copy-done((bf16[576,6144]{1,0:T(8,128)(2,1)S(1)}, bf16[576,6144]{1,0:T(8,128)(2,1)}, u32[]{:S(2)}) %copy-start.6) | copy-done | bytes 7077912
  10.7 3.5 %copy-done = bf16[576,6144]{1,0:T(8,128)(2,1)} copy-done((bf16[576,6144]{1,0:T(8,128)(2,1)}, bf16[576,6144]{1,0:T(8,128)(2,1)S(1)}, u32[]{:S(2)}) %copy-start) | copy-done | bytes 7077912
  15.2 2.1 %copy-done.3 = bf16[576,4096]{1,0:T(8,128)(2,1)} copy-done((bf16[576,4096]{1,0:T(8,128)(2,1)}, bf16[576,4096]{1,0:T(8,128)(2,1)S(1)}, u32[]{:S(2)}) %copy-start.3) | copy-done | bytes 4718616
  19.4 3.0 %copy-done.1 = bf16[576,6144]{1,0:T(8,128)(2,1)S(1)} copy-done((bf16[576,6144]{1,0:T(8,128)(2,1)S(1)}, bf16[576,6144]{1,0:T(8,128)(2,1)}, u32[]{:S(2)}) %copy-start.1) | copy-done | bytes 7077912
  22.5 2.3 %copy-done.4 = bf16[576,4096]{1,0:T(8,128)(2,1)S(1)} copy-done((bf16[576,4096]{1,0:T(8,128)(2,1)S(1)}, bf16[576,4096]{1,0:T(8,128)(2,1)}, u32[]{:S(2)}) %copy-start.4) | copy-done | bytes 4718616
  24.8 6.9 %image_panel.1 = (f32[4,4,192,128]{3,2,1,0:T(8,128)S(1)}, f32[4,4,192,128]{3,2,1,0:T(8,128)}) custom-call(s32[2]{0:T(128)S(1)} %pad_add_fusion.me_ref, bf16[576,4096]{1,0:T(8,128)(2,1)S(1)} %copy-done.4, bf16[576,6144]{1,0:T(8,128)(2,1)S(1)} %copy-done.1, bf16[512,128]{1,0:T(8,128)(2,1)S(1)} %copy-done.11, ...), custom_call_target="tpu_custom_call" | custom-call | flops 1509949440 | bytes 11796480 | tf_op jit(solution)/shard_map/image_panel/pallas_call | solution.py:91
  32.0 2.5 %collective-permute-start.5 = (bf16[768,128]{1,0:T(8,128)(2,1)S(1)}, bf16[768,128]{1,0:T(8,128)(2,1)S(1)}, u32[]{:S(2)}, u32[]{:S(2)}) collective-permute-start(bf16[768,128]{1,0:T(8,128)(2,1)S(1)} %constant_dynamic-slice_fusion), channel_id=1, source_target_pairs={{0,24},{8,16},{16,8},{24,0},{1,25},{9,17},{17,9},{25,1},{2,26},{10... | collective-permute-start | bytes 589832 | tf_op jit(solution)/shard_map/ppermute | solution.py:285
  36.0 1.6 %collective-permute-start.11 = (bf16[4,192,128]{2,1,0:T(8,128)(2,1)S(1)}, bf16[4,192,128]{2,1,0:T(8,128)(2,1)S(1)}, u32[]{:S(2)}, u32[]{:S(2)}) collective-permute-start(bf16[4,192,128]{2,1,0:T(8,128)(2,1)S(1)} %get-tuple-element.48), channel_id=1, source_target_pairs={{0,2},{1,3},{2,0},{3,1},{4,6},{5,7},{6,4},{7,5},{8,10},{9,11},{10,... | collective-permute-start | bytes 589832 | tf_op jit(solution)/shard_map/ppermute | solution.py:284
  37.6 1.5 %collective-permute-start.12 = (bf16[4,192,128]{2,1,0:T(8,128)(2,1)S(1)}, bf16[4,192,128]{2,1,0:T(8,128)(2,1)S(1)}, u32[]{:S(2)}, u32[]{:S(2)}) collective-permute-start(bf16[4,192,128]{2,1,0:T(8,128)(2,1)S(1)} %get-tuple-element.49), channel_id=1, source_target_pairs={{0,4},{1,5},{2,6},{3,7},{4,0},{5,1},{6,2},{7,3},{8,12},{9,13},{10,... | collective-permute-start | bytes 589832 | tf_op jit(solution)/shard_map/ppermute | solution.py:284
  39.6 1.4 %collective-permute-done.5.refs_3_ = bf16[768,128]{1,0:T(8,128)(2,1)S(1)} collective-permute-done((bf16[768,128]{1,0:T(8,128)(2,1)S(1)}, bf16[768,128]{1,0:T(8,128)(2,1)S(1)}, u32[]{:S(2)}, u32[]{:S(2)}) %collective-permute-start.5) | collective-permute-done | bytes 196640 | tf_op jit(solution)/shard_map/ppermute | solution.py:285
  41.0 2.8 %collective-permute-done.11.refs_1_ = bf16[4,192,128]{2,1,0:T(8,128)(2,1)S(1)} collective-permute-done((bf16[4,192,128]{2,1,0:T(8,128)(2,1)S(1)}, bf16[4,192,128]{2,1,0:T(8,128)(2,1)S(1)}, u32[]{:S(2)}, u32[]{:S(2)}) %collective-permute-start.11) | collective-permute-done | bytes 196640 | tf_op jit(solution)/shard_map/ppermute | solution.py:284
  43.8 4.8 %collective-permute-done.12.refs_2_ = bf16[4,192,128]{2,1,0:T(8,128)(2,1)S(1)} collective-permute-done((bf16[4,192,128]{2,1,0:T(8,128)(2,1)S(1)}, bf16[4,192,128]{2,1,0:T(8,128)(2,1)S(1)}, u32[]{:S(2)}, u32[]{:S(2)}) %collective-permute-start.12) | collective-permute-done | bytes 196640 | tf_op jit(solution)/shard_map/ppermute | solution.py:284
  48.7 1.4 %collective-permute-done.14.refs_4_ = bf16[768,128]{1,0:T(8,128)(2,1)S(1)} collective-permute-done((bf16[768,128]{1,0:T(8,128)(2,1)S(1)}, bf16[768,128]{1,0:T(8,128)(2,1)S(1)}, u32[]{:S(2)}, u32[]{:S(2)}) %collective-permute-start.14) | collective-permute-done | bytes 196640 | tf_op jit(solution)/shard_map/ppermute | solution.py:284
  50.1 3.0 %copy-done.2 = bf16[576,6144]{1,0:T(8,128)(2,1)S(1)} copy-done((bf16[576,6144]{1,0:T(8,128)(2,1)S(1)}, bf16[576,6144]{1,0:T(8,128)(2,1)}, u32[]{:S(2)}) %copy-start.2) | copy-done | bytes 7077912
  53.1 2.3 %copy-done.5 = bf16[576,4096]{1,0:T(8,128)(2,1)S(1)} copy-done((bf16[576,4096]{1,0:T(8,128)(2,1)S(1)}, bf16[576,4096]{1,0:T(8,128)(2,1)}, u32[]{:S(2)}) %copy-start.5) | copy-done | bytes 4718616
  56.4 5.1 %text_panel.1 = (f32[4,1,512,128]{3,2,1,0:T(8,128)S(1)}, f32[4,1,512,128]{3,2,1,0:T(8,128)S(1)}) custom-call(s32[2]{0:T(128)S(1)} %pad_add_fusion.me_ref, bf16[576,6144]{1,0:T(8,128)(2,1)S(1)} %copy-done.2, bf16[576,4096]{1,0:T(8,128)(2,1)S(1)} %copy-done.5, bf16[1536,128]{1,0:T(8,128)(2,1)S(1)} %copy-done.8, bf16[1536,128]{1,0:T(8,128)(2,1)S(1)} %copy-done.10, ...), custom_call_target="tpu_custom_call" | custom-call | flops 1509949440 | bytes 11796480 | tf_op jit(solution)/shard_map/text_panel/pallas_call | solution.py:91
  62.4 1.9 %collective-permute-done.15.refs_1_ = f32[4,1,512,128]{3,2,1,0:T(8,128)S(1)} collective-permute-done((f32[4,1,512,128]{3,2,1,0:T(8,128)S(1)}, f32[4,1,512,128]{3,2,1,0:T(8,128)S(1)}, u32[]{:S(2)}, u32[]{:S(2)}) %collective-permute-start.15) | collective-permute-done | bytes 1048608 | tf_op jit(solution)/shard_map/ppermute | solution.py:284
  67.1 1.4 %collective-permute-start.28 = (bf16[512,128]{1,0:T(8,128)(2,1)S(1)}, bf16[512,128]{1,0:T(8,128)(2,1)S(1)}, u32[]{:S(2)}, u32[]{:S(2)}) collective-permute-start(bf16[512,128]{1,0:T(8,128)(2,1)S(1)} %bitcast.7), channel_id=1, source_target_pairs={{0,6},{1,7},{2,4},{3,5},{4,2},{5,3},{6,0},{7,1},{8,14},{9,15},{10,... | collective-permute-start | bytes 393224 | tf_op jit(solution)/shard_map/ppermute | solution.py:284
  69.5 2.1 %collective-permute-start.17 = (bf16[192,128]{1,0:T(8,128)(2,1)S(1)}, bf16[192,128]{1,0:T(8,128)(2,1)S(1)}, u32[]{:S(2)}, u32[]{:S(2)}) collective-permute-start(bf16[192,128]{1,0:T(8,128)(2,1)S(1)} %get-tuple-element.64), channel_id=1, source_target_pairs={{0,16},{8,24},{16,0},{24,8},{1,17},{9,25},{17,1},{25,9},{2,18},{10... | collective-permute-start | bytes 147464 | tf_op jit(solution)/shard_map/ppermute | solution.py:285
  71.5 2.1 %collective-permute-start.18 = (bf16[192,128]{1,0:T(8,128)(2,1)S(1)}, bf16[192,128]{1,0:T(8,128)(2,1)S(1)}, u32[]{:S(2)}, u32[]{:S(2)}) collective-permute-start(bf16[192,128]{1,0:T(8,128)(2,1)S(1)} %get-tuple-element.65), channel_id=1, source_target_pairs={{0,24},{8,16},{16,8},{24,0},{1,25},{9,17},{17,9},{25,1},{2,26},{10... | collective-permute-start | bytes 147464 | tf_op jit(solution)/shard_map/ppermute | solution.py:285
  75.4 2.1 %collective-permute-start.30 = (bf16[512,128]{1,0:T(8,128)(2,1)S(1)}, bf16[512,128]{1,0:T(8,128)(2,1)S(1)}, u32[]{:S(2)}, u32[]{:S(2)}) collective-permute-start(bf16[512,128]{1,0:T(8,128)(2,1)S(1)} %text_plane.1.refs_0_), channel_id=1, source_target_pairs={{0,16},{8,24},{16,0},{24,8},{1,17},{9,25},{17,1},{25,9},{2,18},{10... | collective-permute-start | bytes 393224 | tf_op jit(solution)/shard_map/ppermute | solution.py:285
  78.9 2.8 %collective-permute-start.31 = (bf16[512,128]{1,0:T(8,128)(2,1)S(1)}, bf16[512,128]{1,0:T(8,128)(2,1)S(1)}, u32[]{:S(2)}, u32[]{:S(2)}) collective-permute-start(bf16[512,128]{1,0:T(8,128)(2,1)S(1)} %text_plane.1.refs_0_), channel_id=1, source_target_pairs={{0,24},{8,16},{16,8},{24,0},{1,25},{9,17},{17,9},{25,1},{2,26},{10... | collective-permute-start | bytes 393224 | tf_op jit(solution)/shard_map/ppermute | solution.py:285
  82.0 1.6 %collective-permute-start.21 = (bf16[192,128]{1,0:T(8,128)(2,1)S(1)}, bf16[192,128]{1,0:T(8,128)(2,1)S(1)}, u32[]{:S(2)}, u32[]{:S(2)}) collective-permute-start(bf16[192,128]{1,0:T(8,128)(2,1)S(1)} %image_depth.1.refs_0_), channel_id=1, source_target_pairs={{0,6},{1,7},{2,4},{3,5},{4,2},{5,3},{6,0},{7,1},{8,14},{9,15},{10,... | collective-permute-start | bytes 147464 | tf_op jit(solution)/shard_map/ppermute | solution.py:284
  83.5 2.2 %collective-permute-done.20.refs_2_ = bf16[192,128]{1,0:T(8,128)(2,1)S(1)} collective-permute-done((bf16[192,128]{1,0:T(8,128)(2,1)S(1)}, bf16[192,128]{1,0:T(8,128)(2,1)S(1)}, u32[]{:S(2)}, u32[]{:S(2)}) %collective-permute-start.20) | collective-permute-done | bytes 49184 | tf_op jit(solution)/shard_map/ppermute | solution.py:284
  91.6 1.7 %collective-permute-start.33 = (f32[128,128]{1,0:T(8,128)S(1)}, f32[128,128]{1,0:T(8,128)S(1)}, u32[]{:S(2)}, u32[]{:S(2)}) collective-permute-start(f32[128,128]{1,0:T(8,128)S(1)} %get-tuple-element.74.refs_0_), channel_id=1, source_target_pairs={{0,16},{8,24},{16,0},{24,8},{1,17},{9,25},{17,1},{25,9},{2,18},{10... | collective-permute-start | bytes 196616 | tf_op jit(solution)/shard_map/ppermute | solution.py:285
  93.3 1.5 %collective-permute-start.34 = (f32[128,128]{1,0:T(8,128)S(1)}, f32[128,128]{1,0:T(8,128)S(1)}, u32[]{:S(2)}, u32[]{:S(2)}) collective-permute-start(f32[128,128]{1,0:T(8,128)S(1)} %get-tuple-element.74.refs_0_), channel_id=1, source_target_pairs={{0,24},{8,16},{16,8},{24,0},{1,25},{9,17},{17,9},{25,1},{2,26},{10... | collective-permute-start | bytes 196616 | tf_op jit(solution)/shard_map/ppermute | solution.py:285
  96.7 1.7 %collective-permute-start.38 = (f32[128,128]{1,0:T(8,128)S(1)}, f32[128,128]{1,0:T(8,128)S(1)}, u32[]{:S(2)}, u32[]{:S(2)}) collective-permute-start(f32[128,128]{1,0:T(8,128)S(1)} %text_gram_cores.1.refs_4_), channel_id=1, source_target_pairs={{0,6},{1,7},{2,4},{3,5},{4,2},{5,3},{6,0},{7,1},{8,14},{9,15},{10,... | collective-permute-start | bytes 196616 | tf_op jit(solution)/shard_map/ppermute | solution.py:284
  98.4 1.4 %collective-permute-done.33.refs_2_ = f32[128,128]{1,0:T(8,128)S(1)} collective-permute-done((f32[128,128]{1,0:T(8,128)S(1)}, f32[128,128]{1,0:T(8,128)S(1)}, u32[]{:S(2)}, u32[]{:S(2)}) %collective-permute-start.33) | collective-permute-done | bytes 65568 | tf_op jit(solution)/shard_map/ppermute | solution.py:285
  101.8 7.6 %finish.1 = (f32[1536,128]{1,0:T(8,128)}, f32[512,128]{1,0:T(8,128)}) custom-call(bf16[8,192,128]{2,1,0:T(8,128)(2,1)S(1)} %get-tuple-element.66.ipanel, bf16[1,512,128]{2,1,0:T(8,128)(2,1)S(1)} %get-tuple-element.73.tpanel, f32[128,128]{1,0:T(8,128)S(1)} %get-tuple-element.74.refs_0_, f32[128,128]{1,0:T(8,128)S(1)} %collective-permute-done.32.refs_1_, ...), custom_call_target="tpu_custom_call" | custom-call | flops 10000000000 | bytes 1179648 | tf_op jit(solution)/shard_map/finish/pallas_call | solution.py:270
  (85 shorter events, 25.0 us)
Async XLA Ops:
  0.6 17.9 %collective-permute-start.3 = (bf16[1536,128]{1,0:T(8,128)(2,1)}, bf16[1536,128]{1,0:T(8,128)(2,1)S(1)}, u32[]{:S(2)}, u32[]{:S(2)}) collective-permute-start(bf16[1536,128]{1,0:T(8,128)(2,1)} %refs_0_.3), channel_id=1, source_target_pairs={{0,8},{1,17},{2,10},{3,19},{4,12},{5,21},{6,14},{7,23},{8,0},{9,25... | collective-permute-start | bytes 1179656 | tf_op jit(solution)/shard_map/ppermute | solution.py:303
  3.7 13.6 %collective-permute-start = (bf16[512,128]{1,0:T(8,128)(2,1)}, bf16[512,128]{1,0:T(8,128)(2,1)S(1)}, u32[]{:S(2)}, u32[]{:S(2)}) collective-permute-start(bf16[512,128]{1,0:T(8,128)(2,1)} %refs_0_.2), channel_id=1, source_target_pairs={{0,2},{1,3},{2,0},{3,1},{4,6},{5,7},{6,4},{7,5},{8,10},{9,11},{10,... | collective-permute-start | bytes 393224 | tf_op jit(solution)/shard_map/ppermute | solution.py:284
  5.2 12.1 %collective-permute-start.1 = (bf16[512,128]{1,0:T(8,128)(2,1)}, bf16[512,128]{1,0:T(8,128)(2,1)S(1)}, u32[]{:S(2)}, u32[]{:S(2)}) collective-permute-start(bf16[512,128]{1,0:T(8,128)(2,1)} %refs_0_.2), channel_id=1, source_target_pairs={{0,4},{1,5},{2,6},{3,7},{4,0},{5,1},{6,2},{7,3},{8,12},{9,13},{10,... | collective-permute-start | bytes 393224 | tf_op jit(solution)/shard_map/ppermute | solution.py:284
  6.7 10.6 %collective-permute-start.2 = (bf16[512,128]{1,0:T(8,128)(2,1)}, bf16[512,128]{1,0:T(8,128)(2,1)S(1)}, u32[]{:S(2)}, u32[]{:S(2)}) collective-permute-start(bf16[512,128]{1,0:T(8,128)(2,1)} %refs_0_.2), channel_id=1, source_target_pairs={{0,6},{1,7},{2,4},{3,5},{4,2},{5,3},{6,0},{7,1},{8,14},{9,15},{10,... | collective-permute-start | bytes 393224 | tf_op jit(solution)/shard_map/ppermute | solution.py:284
  7.2 11.3 %collective-permute-start.6 = (bf16[512,128]{1,0:T(8,128)(2,1)}, bf16[512,128]{1,0:T(8,128)(2,1)S(1)}, u32[]{:S(2)}, u32[]{:S(2)}) collective-permute-start(bf16[512,128]{1,0:T(8,128)(2,1)} %refs_0_.2), channel_id=1, source_target_pairs={{0,1},{1,0},{2,3},{3,2},{4,5},{5,4},{6,7},{7,6},{8,9},{9,8},{10,11... | collective-permute-start | bytes 393224 | tf_op jit(solution)/shard_map/ppermute | solution.py:284
  31.7 3.6 %collective-permute-start.10 = (f32[4,4,192,128]{3,2,1,0:T(8,128)}, f32[4,4,192,128]{3,2,1,0:T(8,128)S(1)}, u32[]{:S(2)}, u32[]{:S(2)}) collective-permute-start(f32[4,4,192,128]{3,2,1,0:T(8,128)} %get-tuple-element.47), channel_id=1, source_target_pairs={{0,1},{1,0},{2,3},{3,2},{4,5},{5,4},{6,7},{7,6},{8,9},{9,8},{10,11... | collective-permute-start | bytes 4718600 | tf_op jit(solution)/shard_map/ppermute | solution.py:284
  32.0 9.0 %collective-permute-start.5 = (bf16[768,128]{1,0:T(8,128)(2,1)S(1)}, bf16[768,128]{1,0:T(8,128)(2,1)S(1)}, u32[]{:S(2)}, u32[]{:S(2)}) collective-permute-start(bf16[768,128]{1,0:T(8,128)(2,1)S(1)} %constant_dynamic-slice_fusion), channel_id=1, source_target_pairs={{0,24},{8,16},{16,8},{24,0},{1,25},{9,17},{17,9},{25,1},{2,26},{10... | collective-permute-start | bytes 589832 | tf_op jit(solution)/shard_map/ppermute | solution.py:285
  36.0 7.8 %collective-permute-start.11 = (bf16[4,192,128]{2,1,0:T(8,128)(2,1)S(1)}, bf16[4,192,128]{2,1,0:T(8,128)(2,1)S(1)}, u32[]{:S(2)}, u32[]{:S(2)}) collective-permute-start(bf16[4,192,128]{2,1,0:T(8,128)(2,1)S(1)} %get-tuple-element.48), channel_id=1, source_target_pairs={{0,2},{1,3},{2,0},{3,1},{4,6},{5,7},{6,4},{7,5},{8,10},{9,11},{10,... | collective-permute-start | bytes 589832 | tf_op jit(solution)/shard_map/ppermute | solution.py:284
  37.6 11.1 %collective-permute-start.12 = (bf16[4,192,128]{2,1,0:T(8,128)(2,1)S(1)}, bf16[4,192,128]{2,1,0:T(8,128)(2,1)S(1)}, u32[]{:S(2)}, u32[]{:S(2)}) collective-permute-start(bf16[4,192,128]{2,1,0:T(8,128)(2,1)S(1)} %get-tuple-element.49), channel_id=1, source_target_pairs={{0,4},{1,5},{2,6},{3,7},{4,0},{5,1},{6,2},{7,3},{8,12},{9,13},{10,... | collective-permute-start | bytes 589832 | tf_op jit(solution)/shard_map/ppermute | solution.py:284
  39.1 9.5 %collective-permute-start.13 = (bf16[4,192,128]{2,1,0:T(8,128)(2,1)S(1)}, bf16[4,192,128]{2,1,0:T(8,128)(2,1)S(1)}, u32[]{:S(2)}, u32[]{:S(2)}) collective-permute-start(bf16[4,192,128]{2,1,0:T(8,128)(2,1)S(1)} %get-tuple-element.50), channel_id=1, source_target_pairs={{0,6},{1,7},{2,4},{3,5},{4,2},{5,3},{6,0},{7,1},{8,14},{9,15},{10,... | collective-permute-start | bytes 589832 | tf_op jit(solution)/shard_map/ppermute | solution.py:284
  39.6 9.1 %collective-permute-start.4 = (bf16[1536,128]{1,0:T(8,128)(2,1)}, bf16[1536,128]{1,0:T(8,128)(2,1)S(1)}, u32[]{:S(2)}, u32[]{:S(2)}) collective-permute-start(bf16[1536,128]{1,0:T(8,128)(2,1)} %copy-done.9), channel_id=1, source_target_pairs={{0,1},{1,0},{2,3},{3,2},{4,5},{5,4},{6,7},{7,6},{8,9},{9,8},{10,11... | collective-permute-start | bytes 1179656 | tf_op jit(solution)/shard_map/ppermute | solution.py:284
  61.6 2.7 %collective-permute-start.15 = (f32[4,1,512,128]{3,2,1,0:T(8,128)S(1)}, f32[4,1,512,128]{3,2,1,0:T(8,128)S(1)}, u32[]{:S(2)}, u32[]{:S(2)}) collective-permute-start(f32[4,1,512,128]{3,2,1,0:T(8,128)S(1)} %get-tuple-element.56), channel_id=1, source_target_pairs={{0,1},{1,0},{2,3},{3,2},{4,5},{5,4},{6,7},{7,6},{8,9},{9,8},{10,11... | collective-permute-start | bytes 3145736 | tf_op jit(solution)/shard_map/ppermute | solution.py:284
  65.0 6.6 %collective-permute-start.26 = (bf16[512,128]{1,0:T(8,128)(2,1)S(1)}, bf16[512,128]{1,0:T(8,128)(2,1)S(1)}, u32[]{:S(2)}, u32[]{:S(2)}) collective-permute-start(bf16[512,128]{1,0:T(8,128)(2,1)S(1)} %bitcast.9), channel_id=1, source_target_pairs={{0,2},{1,3},{2,0},{3,1},{4,6},{5,7},{6,4},{7,5},{8,10},{9,11},{10,... | collective-permute-start | bytes 393224 | tf_op jit(solution)/shard_map/ppermute | solution.py:284
  66.2 7.4 %collective-permute-start.27 = (bf16[512,128]{1,0:T(8,128)(2,1)S(1)}, bf16[512,128]{1,0:T(8,128)(2,1)S(1)}, u32[]{:S(2)}, u32[]{:S(2)}) collective-permute-start(bf16[512,128]{1,0:T(8,128)(2,1)S(1)} %bitcast.8), channel_id=1, source_target_pairs={{0,4},{1,5},{2,6},{3,7},{4,0},{5,1},{6,2},{7,3},{8,12},{9,13},{10,... | collective-permute-start | bytes 393224 | tf_op jit(solution)/shard_map/ppermute | solution.py:284
  67.1 7.2 %collective-permute-start.28 = (bf16[512,128]{1,0:T(8,128)(2,1)S(1)}, bf16[512,128]{1,0:T(8,128)(2,1)S(1)}, u32[]{:S(2)}, u32[]{:S(2)}) collective-permute-start(bf16[512,128]{1,0:T(8,128)(2,1)S(1)} %bitcast.7), channel_id=1, source_target_pairs={{0,6},{1,7},{2,4},{3,5},{4,2},{5,3},{6,0},{7,1},{8,14},{9,15},{10,... | collective-permute-start | bytes 393224 | tf_op jit(solution)/shard_map/ppermute | solution.py:284
  68.5 9.0 %collective-permute-start.16 = (bf16[192,128]{1,0:T(8,128)(2,1)S(1)}, bf16[192,128]{1,0:T(8,128)(2,1)S(1)}, u32[]{:S(2)}, u32[]{:S(2)}) collective-permute-start(bf16[192,128]{1,0:T(8,128)(2,1)S(1)} %get-tuple-element.63), channel_id=1, source_target_pairs={{0,8},{8,0},{16,24},{24,16},{1,9},{9,1},{17,25},{25,17},{2,10},{10... | collective-permute-start | bytes 147464 | tf_op jit(solution)/shard_map/ppermute | solution.py:285
  69.5 8.0 %collective-permute-start.17 = (bf16[192,128]{1,0:T(8,128)(2,1)S(1)}, bf16[192,128]{1,0:T(8,128)(2,1)S(1)}, u32[]{:S(2)}, u32[]{:S(2)}) collective-permute-start(bf16[192,128]{1,0:T(8,128)(2,1)S(1)} %get-tuple-element.64), channel_id=1, source_target_pairs={{0,16},{8,24},{16,0},{24,8},{1,17},{9,25},{17,1},{25,9},{2,18},{10... | collective-permute-start | bytes 147464 | tf_op jit(solution)/shard_map/ppermute | solution.py:285
  71.5 6.0 %collective-permute-start.18 = (bf16[192,128]{1,0:T(8,128)(2,1)S(1)}, bf16[192,128]{1,0:T(8,128)(2,1)S(1)}, u32[]{:S(2)}, u32[]{:S(2)}) collective-permute-start(bf16[192,128]{1,0:T(8,128)(2,1)S(1)} %get-tuple-element.65), channel_id=1, source_target_pairs={{0,24},{8,16},{16,8},{24,0},{1,25},{9,17},{17,9},{25,1},{2,26},{10... | collective-permute-start | bytes 147464 | tf_op jit(solution)/shard_map/ppermute | solution.py:285
  74.4 12.6 %collective-permute-start.29 = (bf16[512,128]{1,0:T(8,128)(2,1)S(1)}, bf16[512,128]{1,0:T(8,128)(2,1)S(1)}, u32[]{:S(2)}, u32[]{:S(2)}) collective-permute-start(bf16[512,128]{1,0:T(8,128)(2,1)S(1)} %text_plane.1.refs_0_), channel_id=1, source_target_pairs={{0,8},{8,0},{16,24},{24,16},{1,9},{9,1},{17,25},{25,17},{2,10},{10... | collective-permute-start | bytes 393224 | tf_op jit(solution)/shard_map/ppermute | solution.py:285
  75.4 12.8 %collective-permute-start.30 = (bf16[512,128]{1,0:T(8,128)(2,1)S(1)}, bf16[512,128]{1,0:T(8,128)(2,1)S(1)}, u32[]{:S(2)}, u32[]{:S(2)}) collective-permute-start(bf16[512,128]{1,0:T(8,128)(2,1)S(1)} %text_plane.1.refs_0_), channel_id=1, source_target_pairs={{0,16},{8,24},{16,0},{24,8},{1,17},{9,25},{17,1},{25,9},{2,18},{10... | collective-permute-start | bytes 393224 | tf_op jit(solution)/shard_map/ppermute | solution.py:285
  77.6 4.4 %collective-permute-start.19 = (bf16[192,128]{1,0:T(8,128)(2,1)S(1)}, bf16[192,128]{1,0:T(8,128)(2,1)S(1)}, u32[]{:S(2)}, u32[]{:S(2)}) collective-permute-start(bf16[192,128]{1,0:T(8,128)(2,1)S(1)} %image_depth.1.refs_0_), channel_id=1, source_target_pairs={{0,2},{1,3},{2,0},{3,1},{4,6},{5,7},{6,4},{7,5},{8,10},{9,11},{10,... | collective-permute-start | bytes 147464 | tf_op jit(solution)/shard_map/ppermute | solution.py:284
  78.9 9.3 %collective-permute-start.31 = (bf16[512,128]{1,0:T(8,128)(2,1)S(1)}, bf16[512,128]{1,0:T(8,128)(2,1)S(1)}, u32[]{:S(2)}, u32[]{:S(2)}) collective-permute-start(bf16[512,128]{1,0:T(8,128)(2,1)S(1)} %text_plane.1.refs_0_), channel_id=1, source_target_pairs={{0,24},{8,16},{16,8},{24,0},{1,25},{9,17},{17,9},{25,1},{2,26},{10... | collective-permute-start | bytes 393224 | tf_op jit(solution)/shard_map/ppermute | solution.py:285
  81.7 4.1 %collective-permute-start.20 = (bf16[192,128]{1,0:T(8,128)(2,1)S(1)}, bf16[192,128]{1,0:T(8,128)(2,1)S(1)}, u32[]{:S(2)}, u32[]{:S(2)}) collective-permute-start(bf16[192,128]{1,0:T(8,128)(2,1)S(1)} %image_depth.1.refs_0_), channel_id=1, source_target_pairs={{0,4},{1,5},{2,6},{3,7},{4,0},{5,1},{6,2},{7,3},{8,12},{9,13},{10,... | collective-permute-start | bytes 147464 | tf_op jit(solution)/shard_map/ppermute | solution.py:284
  82.0 5.0 %collective-permute-start.21 = (bf16[192,128]{1,0:T(8,128)(2,1)S(1)}, bf16[192,128]{1,0:T(8,128)(2,1)S(1)}, u32[]{:S(2)}, u32[]{:S(2)}) collective-permute-start(bf16[192,128]{1,0:T(8,128)(2,1)S(1)} %image_depth.1.refs_0_), channel_id=1, source_target_pairs={{0,6},{1,7},{2,4},{3,5},{4,2},{5,3},{6,0},{7,1},{8,14},{9,15},{10,... | collective-permute-start | bytes 147464 | tf_op jit(solution)/shard_map/ppermute | solution.py:284
  85.8 3.3 %collective-permute-start.22 = (bf16[192,128]{1,0:T(8,128)(2,1)S(1)}, bf16[192,128]{1,0:T(8,128)(2,1)S(1)}, u32[]{:S(2)}, u32[]{:S(2)}) collective-permute-start(bf16[192,128]{1,0:T(8,128)(2,1)S(1)} %image_depth.1.refs_0_), channel_id=1, source_target_pairs={{0,1},{1,0},{2,3},{3,2},{4,5},{5,4},{6,7},{7,6},{8,9},{9,8},{10,11... | collective-permute-start | bytes 147464 | tf_op jit(solution)/shard_map/ppermute | solution.py:284
  88.5 6.3 %collective-permute-start.35 = (f32[128,128]{1,0:T(8,128)S(1)}, f32[128,128]{1,0:T(8,128)S(1)}, u32[]{:S(2)}, u32[]{:S(2)}) collective-permute-start(f32[128,128]{1,0:T(8,128)S(1)} %get-tuple-element.75.own_ref), channel_id=1, source_target_pairs={{0,1},{1,0},{2,3},{3,2},{4,5},{5,4},{6,7},{7,6},{8,9},{9,8},{10,11... | collective-permute-start | bytes 196616 | tf_op jit(solution)/shard_map/ppermute | solution.py:284
  90.3 6.3 %collective-permute-start.32 = (f32[128,128]{1,0:T(8,128)S(1)}, f32[128,128]{1,0:T(8,128)S(1)}, u32[]{:S(2)}, u32[]{:S(2)}) collective-permute-start(f32[128,128]{1,0:T(8,128)S(1)} %get-tuple-element.74.refs_0_), channel_id=1, source_target_pairs={{0,8},{8,0},{16,24},{24,16},{1,9},{9,1},{17,25},{25,17},{2,10},{10... | collective-permute-start | bytes 196616 | tf_op jit(solution)/shard_map/ppermute | solution.py:285
  91.6 8.3 %collective-permute-start.33 = (f32[128,128]{1,0:T(8,128)S(1)}, f32[128,128]{1,0:T(8,128)S(1)}, u32[]{:S(2)}, u32[]{:S(2)}) collective-permute-start(f32[128,128]{1,0:T(8,128)S(1)} %get-tuple-element.74.refs_0_), channel_id=1, source_target_pairs={{0,16},{8,24},{16,0},{24,8},{1,17},{9,25},{17,1},{25,9},{2,18},{10... | collective-permute-start | bytes 196616 | tf_op jit(solution)/shard_map/ppermute | solution.py:285
  93.3 6.6 %collective-permute-start.34 = (f32[128,128]{1,0:T(8,128)S(1)}, f32[128,128]{1,0:T(8,128)S(1)}, u32[]{:S(2)}, u32[]{:S(2)}) collective-permute-start(f32[128,128]{1,0:T(8,128)S(1)} %get-tuple-element.74.refs_0_), channel_id=1, source_target_pairs={{0,24},{8,16},{16,8},{24,0},{1,25},{9,17},{17,9},{25,1},{2,26},{10... | collective-permute-start | bytes 196616 | tf_op jit(solution)/shard_map/ppermute | solution.py:285
  94.8 5.0 %collective-permute-start.36 = (f32[128,128]{1,0:T(8,128)S(1)}, f32[128,128]{1,0:T(8,128)S(1)}, u32[]{:S(2)}, u32[]{:S(2)}) collective-permute-start(f32[128,128]{1,0:T(8,128)S(1)} %text_gram_cores.1.refs_4_), channel_id=1, source_target_pairs={{0,2},{1,3},{2,0},{3,1},{4,6},{5,7},{6,4},{7,5},{8,10},{9,11},{10,... | collective-permute-start | bytes 196616 | tf_op jit(solution)/shard_map/ppermute | solution.py:284
  96.1 4.6 %collective-permute-start.37 = (f32[128,128]{1,0:T(8,128)S(1)}, f32[128,128]{1,0:T(8,128)S(1)}, u32[]{:S(2)}, u32[]{:S(2)}) collective-permute-start(f32[128,128]{1,0:T(8,128)S(1)} %text_gram_cores.1.refs_4_), channel_id=1, source_target_pairs={{0,4},{1,5},{2,6},{3,7},{4,0},{5,1},{6,2},{7,3},{8,12},{9,13},{10,... | collective-permute-start | bytes 196616 | tf_op jit(solution)/shard_map/ppermute | solution.py:284
  96.7 5.2 %collective-permute-start.38 = (f32[128,128]{1,0:T(8,128)S(1)}, f32[128,128]{1,0:T(8,128)S(1)}, u32[]{:S(2)}, u32[]{:S(2)}) collective-permute-start(f32[128,128]{1,0:T(8,128)S(1)} %text_gram_cores.1.refs_4_), channel_id=1, source_target_pairs={{0,6},{1,7},{2,4},{3,5},{4,2},{5,3},{6,0},{7,1},{8,14},{9,15},{10,... | collective-permute-start | bytes 196616 | tf_op jit(solution)/shard_map/ppermute | solution.py:284
  (19 other events, 48.8 us)

commit v8 on v5

--- a/solution.py
+++ b/solution.py
@@ -28,12 +28,12 @@
     return pl.CostEstimate(flops=int(flops), bytes_accessed=int(nbytes), transcendentals=0)
 
 
-def text_columns(shifts, depth):
+def text_rows(shifts, depth):
     return lambda me_ref: [pl.multiple_of((me_ref[0] ^ s) * depth, depth) for s in shifts]
 
 
-def image_columns(order, depth):
-    def columns(me_ref):
+def image_rows(order, depth):
+    def rows(me_ref):
         core = me_ref[0] % 2
         out = []
         for even, odd, half in order:
@@ -45,50 +45,55 @@
             out.append(at)
         return out
 
-    return columns
-
-
-def panel_kernel(columns, n, n_out, me_ref, a_hbm, b_hbm, *refs):
-    parts, (keep_ref, send_ref, a_ref, b_ref, a_sem, b_sem) = refs[:n], refs[n:]
+    return rows
+
+
+def panel_kernel(rows, n, n_in, n_out, me_ref, a_hbm, b_hbm, *refs):
+    parts, (keep_ref, send_ref, a_ref, b_ref, probe, a_sem, b_sem) = refs[:n], refs[n:]
     core = me_ref[0] % 2
+    tall = a_ref.shape[0] // n_in
     cols = b_ref.shape[1] // n_out // 2
     moves = []
-    spans = [pl.ds(at, part.shape[0]) for at, part in zip(columns(me_ref), parts)]
-    for i, span in enumerate(spans):
-        moves.append(pltpu.make_async_copy(a_hbm.at[:, span], a_ref.at[:, span], a_sem.at[i]))
+    for i in range(n_in):
+        span = pl.ds(i * tall, tall)
+        moves.append(pltpu.make_async_copy(a_hbm.at[span], a_ref.at[span], a_sem.at[i]))
     for i in range(n_out):
         span = pl.ds(2 * i * cols, 2 * cols)
         moves.append(pltpu.make_async_copy(b_hbm.at[:, span], b_ref.at[:, span], b_sem.at[i]))
     for move in moves:
         move.start()
-    total = None
-    for i, span in enumerate(spans):
+    for at, part in zip(rows(me_ref), parts):
+        probe[pl.ds(at, part.shape[0]), :] = part[...]
+    sketches = []
+    for i in range(n_in):
         moves[i].wait()
-        term = jnp.dot(a_ref[:, span], parts[i][...], preferred_element_type=F32)
-        total = term if total is None else total + term
-    sketch = total.T.astype(BF16)
+        chunk = a_ref[i * tall : i * tall + tall, :]
+        sketches.append(jnp.dot(chunk, probe[...], preferred_element_type=F32))
+    sketch = jnp.concatenate(sketches, axis=0).T.astype(BF16)
     for i in range(n_out):
-        moves[n + i].wait()
+        moves[n_in + i].wait()
         for rel, ref in ((0, keep_ref), (1, send_ref)):
             at = pl.multiple_of((2 * i + (core ^ rel)) * cols, cols)
             out = jnp.dot(sketch, b_ref[:, pl.ds(at, cols)], preferred_element_type=F32)
             ref[i] = out.T.reshape(ref.shape[1:])
 
 
-def panel_call(me, a, b, parts, columns, blocks, pieces, name):
+def panel_call(me, a, b, parts, rows, blocks, pieces, name):
     pairs, width = b.shape
     rank = parts[0].shape[-1]
     out = sds((blocks, pieces, width // blocks // pieces // 2, rank), F32)
     hbm = pl.BlockSpec(memory_space=pltpu.HBM)
-    return pl.pallas_call(
-        functools.partial(panel_kernel, columns, len(parts), blocks),
+    n_in = 3 if pairs % 48 == 0 else 1
+    return pl.pallas_call(
+        functools.partial(panel_kernel, rows, len(parts), n_in, blocks),
         in_specs=[SMEM, hbm, hbm] + [VMEM] * len(parts),
         out_specs=[VMEM, VMEM],
         out_shape=[out, out],
         scratch_shapes=[
             pltpu.VMEM(a.shape, BF16),
             pltpu.VMEM(b.shape, BF16),
-            pltpu.SemaphoreType.DMA((len(parts),)),
+            pltpu.VMEM((a.shape[1], rank), BF16),
+            pltpu.SemaphoreType.DMA((n_in,)),
             pltpu.SemaphoreType.DMA((blocks,)),
         ],
         compiler_params=pltpu.CompilerParams(vmem_limit_bytes=PANEL_LIMIT),
@@ -218,7 +223,8 @@
         for j in range(8):
             k = 8 * b + j
             pivot = jnp.broadcast_to(cols[j][0][j : j + 1, :], (8, n))
-            inv = 1.0 / pivot
+            guess = pl.reciprocal(pivot, approx=True)
+            inv = guess * (2.0 - pivot * guess)
             scale = jnp.where(sub == j, pivot, scale)
             pivot_row = jnp.where(lane == k, 1.0, jnp.broadcast_to(rows[b][j : j + 1, :], (8, n)))
             below = sub > j
@@ -313,28 +319,29 @@
         image_parts += [block, col_swap(block, 1)]
     image_order += [(last, last, 0), (last, last, 1)]
 
-    columns = text_columns(list(text_parts), probe_text.shape[0])
+    columns = text_rows(list(text_parts), probe_text.shape[0])
     keep, send = panel_call(
         first, text_feats, image_feats, list(text_parts.values()), columns, n_row, groups, "image_panel"
     )
-    own, *sends = sums_call("col", 1, chips, me, [keep, col_swap(send, 1)], "image_cores")
-    own, mine = lax.optimization_barrier((own, mine))
+    send, mine = lax.optimization_barrier((send, mine))
     image_parts += [mine, col_swap(mine, 1)]
-    received = over_chips(sends)
-    columns = image_columns(image_order, probe_image.shape[0])
-    keep, send = panel_call(
-        me, image_feats, text_feats, image_parts, columns, groups, 1, "text_panel"
-    )
-    send, *received = lax.optimization_barrier((send, *received))
-    own, *sends = sums_call("row", 0, depths, me, [own] + received, "image_plane")
+    own, *image_sends = sums_call("col", 1, chips, me, [keep, col_swap(send, 1)], "image_cores")
+    own, *sends = sums_call("row", 0, depths, me, [own] + over_chips(image_sends), "image_plane")
+    after_plane = sends[0]
     mine = last_call(own, over_depth(sends), BF16, "image_depth")
     parts = over_plane(mine)
     ipanel, gram = gram_call("col", list(parts), me, list(parts.values()), "image_gram")
     igrams = [gram] + over_depth([gram] * len(depths))
 
-    own, *sends = sums_call("col", 0, chips, me, [keep, col_swap(send, 1)], "text_cores")
+    columns = image_rows(image_order, probe_image.shape[0])
+    keep, send = panel_call(
+        me, image_feats, text_feats, image_parts, columns, groups, 1, "text_panel"
+    )
+    swapped, _ = lax.optimization_barrier((col_swap(send, 1), image_sends[0]))
+    own, *sends = sums_call("col", 0, chips, me, [keep, swapped], "text_cores")
     own, sends = own[0], [x[0] for x in sends]
-    mine = last_call(own, [x for x in over_chips(sends)], BF16, "text_plane")
+    own, _ = lax.optimization_barrier((own, after_plane))
+    mine = last_call(own, over_chips(sends), BF16, "text_plane")
     tpanel, gram = text_gram_call([mine] + over_depth([mine] * len(depths)))
     gram = last_call(gram, [col_swap(gram, 1)], F32, "text_gram_cores")
     tgrams = [gram] + over_chips([gram] * len(chips))

time: 98.5 us -> 92.4 us (0.938)
  Pallas kernels: 29.8 us -> 24 us
    pallas_call x2, Pallas kernels: 19 us -> 13 us  [panel_call(): pl.pallas_call(functools.partial(panel_kernel, rows, len(parts), n_in, bl...]
    ppermute x10, waiting for transfers between devices: 7.01 us -> 2.8 us  [per_device(): lax.ppermute(x, 'row', [(i, i ^ s) for i in range(n_row)])]
    ppermute x28, waiting for transfers between devices: 16.7 us -> 20.5 us  [per_device(): lax.ppermute(x, 'col', [(i, i ^ s) for i in range(n_col)])]
    ppermute x10, starting transfers between devices: 18.7 us -> 16 us  [per_device(): lax.ppermute(x, 'row', [(i, i ^ s) for i in range(n_row)])]
    ppermute x28, starting transfers between devices: 21.3 us -> 23.1 us  [per_device(): lax.ppermute(x, 'col', [(i, i ^ s) for i in range(n_col)])]
  transfers between devices with their start and end apart: 39 -> 39, of which waited for: 14 -> 14; matrix products, arithmetic and copies ran while one was open for 0% -> 1% of each run, Pallas kernels for 12% -> 18%
where the time goes in v8:
time: 92.4 us; the launch traced here: 92.3 us
  starting transfers between devices  42.2 us (46%)
  Pallas kernels  24 us (26%)
  waiting for transfers between devices  23.3 us (25%)
  local copies, waits for them, and re-layouts  1.89 us (2%)
    ppermute x28, starting transfers between devices, per_device(): lax.ppermute(x, 'col', [(i, i ^ s) for i in range(n_col)])  23.1 us
    ppermute x28, waiting for transfers between devices, per_device(): lax.ppermute(x, 'col', [(i, i ^ s) for i in range(n_col)])  20.5 us
    ppermute x10, starting transfers between devices, per_device(): lax.ppermute(x, 'row', [(i, i ^ s) for i in range(n_row)])  16 us
    pallas_call x2, Pallas kernels, panel_call(): pl.pallas_call(functools.partial(panel_kernel, rows, len(parts), n_in, bl...  13 us
    pallas_call x1, Pallas kernels, finish_call(): pl.pallas_call(functools.partial(finish_kernel, widths, len(igrams)), in_...  7.76 us
    ppermute x1, starting transfers between devices, split_swap(): return lax.ppermute(x, ('row', 'col'), pairs)  3.09 us
    ppermute x10, waiting for transfers between devices, per_device(): lax.ppermute(x, 'row', [(i, i ^ s) for i in range(n_row)])  2.8 us
    pallas_call x3, Pallas kernels, sums_call(): pl.pallas_call(functools.partial(sums_kernel, which, axis, shifts, len(te...  1.97 us
  transfers between devices with their start and end apart: 39, of which 14 were waited for; matrix products, arithmetic and copies ran while one was open for 1% of the time, Pallas kernels for 18%

profile of v8, /device:TPU:0, one launch (start us, length us, event | category | flops | bytes accessed | tf_op | source)
XLA Modules:
  0.0 92.3 jit_solution(2381038702539738433)
XLA Ops:
  0.6 3.1 %collective-permute-start = (bf16[1536,128]{1,0:T(8,128)(2,1)}, bf16[1536,128]{1,0:T(8,128)(2,1)S(1)}, u32[]{:S(2)}, u32[]{:S(2)}) collective-permute-start(bf16[1536,128]{1,0:T(8,128)(2,1)} %refs_0_.3), channel_id=1, source_target_pairs={{0,8},{1,17},{2,10},{3,19},{4,12},{5,21},{6,14},{7,23},{8,0},{9,25... | collective-permute-start | bytes 1179656 | tf_op jit(solution)/shard_map/ppermute | solution.py:307
  3.7 1.5 %collective-permute-start.1 = (bf16[512,128]{1,0:T(8,128)(2,1)}, bf16[512,128]{1,0:T(8,128)(2,1)S(1)}, u32[]{:S(2)}, u32[]{:S(2)}) collective-permute-start(bf16[512,128]{1,0:T(8,128)(2,1)} %refs_0_.2), channel_id=1, source_target_pairs={{0,2},{1,3},{2,0},{3,1},{4,6},{5,7},{6,4},{7,5},{8,10},{9,11},{10,... | collective-permute-start | bytes 393224 | tf_op jit(solution)/shard_map/ppermute | solution.py:288
  5.2 1.5 %collective-permute-start.2 = (bf16[512,128]{1,0:T(8,128)(2,1)}, bf16[512,128]{1,0:T(8,128)(2,1)S(1)}, u32[]{:S(2)}, u32[]{:S(2)}) collective-permute-start(bf16[512,128]{1,0:T(8,128)(2,1)} %refs_0_.2), channel_id=1, source_target_pairs={{0,4},{1,5},{2,6},{3,7},{4,0},{5,1},{6,2},{7,3},{8,12},{9,13},{10,... | collective-permute-start | bytes 393224 | tf_op jit(solution)/shard_map/ppermute | solution.py:288
  7.2 3.0 %collective-permute-done.1.refs_1_ = bf16[512,128]{1,0:T(8,128)(2,1)S(1)} collective-permute-done((bf16[512,128]{1,0:T(8,128)(2,1)}, bf16[512,128]{1,0:T(8,128)(2,1)S(1)}, u32[]{:S(2)}, u32[]{:S(2)}) %collective-permute-start.1) | collective-permute-done | bytes 131104 | tf_op jit(solution)/shard_map/ppermute | solution.py:288
  10.2 3.7 %collective-permute-done.2.refs_2_ = bf16[512,128]{1,0:T(8,128)(2,1)S(1)} collective-permute-done((bf16[512,128]{1,0:T(8,128)(2,1)}, bf16[512,128]{1,0:T(8,128)(2,1)S(1)}, u32[]{:S(2)}, u32[]{:S(2)}) %collective-permute-start.2) | collective-permute-done | bytes 131104 | tf_op jit(solution)/shard_map/ppermute | solution.py:288
  15.4 2.4 %collective-permute-start.8 = (bf16[768,128]{1,0:T(8,128)(2,1)S(1)}, bf16[768,128]{1,0:T(8,128)(2,1)S(1)}, u32[]{:S(2)}, u32[]{:S(2)}) collective-permute-start(bf16[768,128]{1,0:T(8,128)(2,1)S(1)} %constant_dynamic-slice_fusion), channel_id=1, source_target_pairs={{0,24},{8,16},{16,8},{24,0},{1,25},{9,17},{17,9},{25,1},{2,26},{10... | collective-permute-start | bytes 589832 | tf_op jit(solution)/shard_map/ppermute | solution.py:289
  17.9 0.9 %copy-done.1 = bf16[512,128]{1,0:T(8,128)(2,1)S(1)} copy-done((bf16[512,128]{1,0:T(8,128)(2,1)S(1)}, bf16[512,128]{1,0:T(8,128)(2,1)}, u32[]{:S(2)}) %copy-start.1) | copy-done | bytes 131096
  18.9 6.1 %image_panel.1 = (f32[4,4,192,128]{3,2,1,0:T(8,128)S(1)}, f32[4,4,192,128]{3,2,1,0:T(8,128)S(1)}) custom-call(s32[2]{0:T(128)S(1)} %pad_add_fusion.me_ref, bf16[576,4096]{1,0:T(8,128)(2,1)} %b_hbm.3, bf16[576,6144]{1,0:T(8,128)(2,1)} %a_hbm.3, bf16[512,128]{1,0:T(8,128)(2,1)S(1)} %copy-done.1, bf16[512,128]{1,0:T(8,128)(2,1)S(1)} %collective-permute-done.1.refs_1_, ...), custom_call_target="tpu_custom_call" | custom-call | flops 1509949440 | bytes 11796480 | tf_op jit(solution)/shard_map/image_panel/pallas_call | solution.py:87
  25.7 3.7 %collective-permute-done.24.refs_4_ = bf16[768,128]{1,0:T(8,128)(2,1)S(1)} collective-permute-done((bf16[768,128]{1,0:T(8,128)(2,1)S(1)}, bf16[768,128]{1,0:T(8,128)(2,1)S(1)}, u32[]{:S(2)}, u32[]{:S(2)}) %collective-permute-start.24) | collective-permute-done | bytes 196640 | tf_op jit(solution)/shard_map/ppermute | solution.py:288
  29.4 6.9 %text_panel.1 = (f32[4,1,512,128]{3,2,1,0:T(8,128)S(1)}, f32[4,1,512,128]{3,2,1,0:T(8,128)S(1)}) custom-call(s32[2]{0:T(128)S(1)} %pad_add_fusion.me_ref, bf16[576,6144]{1,0:T(8,128)(2,1)} %a_hbm.3, bf16[576,4096]{1,0:T(8,128)(2,1)} %b_hbm.3, bf16[1536,128]{1,0:T(8,128)(2,1)S(1)} %copy-done, bf16[1536,128]{1,0:T(8,128)(2,1)S(1)} %collective-permute-done.refs_1_, ...), custom_call_target="tpu_custom_call" | custom-call | flops 1509949440 | bytes 11796480 | tf_op jit(solution)/shard_map/text_panel/pallas_call | solution.py:87
  37.2 1.6 %collective-permute-start.10 = (bf16[4,192,128]{2,1,0:T(8,128)(2,1)S(1)}, bf16[4,192,128]{2,1,0:T(8,128)(2,1)S(1)}, u32[]{:S(2)}, u32[]{:S(2)}) collective-permute-start(bf16[4,192,128]{2,1,0:T(8,128)(2,1)S(1)} %get-tuple-element.33), channel_id=1, source_target_pairs={{0,2},{1,3},{2,0},{3,1},{4,6},{5,7},{6,4},{7,5},{8,10},{9,11},{10,... | collective-permute-start | bytes 589832 | tf_op jit(solution)/shard_map/ppermute | solution.py:288
  38.7 1.5 %collective-permute-start.11 = (bf16[4,192,128]{2,1,0:T(8,128)(2,1)S(1)}, bf16[4,192,128]{2,1,0:T(8,128)(2,1)S(1)}, u32[]{:S(2)}, u32[]{:S(2)}) collective-permute-start(bf16[4,192,128]{2,1,0:T(8,128)(2,1)S(1)} %get-tuple-element.34), channel_id=1, source_target_pairs={{0,4},{1,5},{2,6},{3,7},{4,0},{5,1},{6,2},{7,3},{8,12},{9,13},{10,... | collective-permute-start | bytes 589832 | tf_op jit(solution)/shard_map/ppermute | solution.py:288
  41.4 1.5 %collective-permute-start.26 = (bf16[512,128]{1,0:T(8,128)(2,1)S(1)}, bf16[512,128]{1,0:T(8,128)(2,1)S(1)}, u32[]{:S(2)}, u32[]{:S(2)}) collective-permute-start(bf16[512,128]{1,0:T(8,128)(2,1)S(1)} %bitcast.9), channel_id=1, source_target_pairs={{0,2},{1,3},{2,0},{3,1},{4,6},{5,7},{6,4},{7,5},{8,10},{9,11},{10,... | collective-permute-start | bytes 393224 | tf_op jit(solution)/shard_map/ppermute | solution.py:288
  42.9 1.5 %collective-permute-start.27 = (bf16[512,128]{1,0:T(8,128)(2,1)S(1)}, bf16[512,128]{1,0:T(8,128)(2,1)S(1)}, u32[]{:S(2)}, u32[]{:S(2)}) collective-permute-start(bf16[512,128]{1,0:T(8,128)(2,1)S(1)} %bitcast.8), channel_id=1, source_target_pairs={{0,4},{1,5},{2,6},{3,7},{4,0},{5,1},{6,2},{7,3},{8,12},{9,13},{10,... | collective-permute-start | bytes 393224 | tf_op jit(solution)/shard_map/ppermute | solution.py:288
  45.0 2.4 %collective-permute-start.28 = (bf16[512,128]{1,0:T(8,128)(2,1)S(1)}, bf16[512,128]{1,0:T(8,128)(2,1)S(1)}, u32[]{:S(2)}, u32[]{:S(2)}) collective-permute-start(bf16[512,128]{1,0:T(8,128)(2,1)S(1)} %bitcast.7), channel_id=1, source_target_pairs={{0,6},{1,7},{2,4},{3,5},{4,2},{5,3},{6,0},{7,1},{8,14},{9,15},{10,... | collective-permute-start | bytes 393224 | tf_op jit(solution)/shard_map/ppermute | solution.py:288
  47.4 3.2 %collective-permute-done.11.refs_2_ = bf16[4,192,128]{2,1,0:T(8,128)(2,1)S(1)} collective-permute-done((bf16[4,192,128]{2,1,0:T(8,128)(2,1)S(1)}, bf16[4,192,128]{2,1,0:T(8,128)(2,1)S(1)}, u32[]{:S(2)}, u32[]{:S(2)}) %collective-permute-start.11) | collective-permute-done | bytes 196640 | tf_op jit(solution)/shard_map/ppermute | solution.py:288
  51.2 2.3 %collective-permute-start.13 = (bf16[192,128]{1,0:T(8,128)(2,1)S(1)}, bf16[192,128]{1,0:T(8,128)(2,1)S(1)}, u32[]{:S(2)}, u32[]{:S(2)}) collective-permute-start(bf16[192,128]{1,0:T(8,128)(2,1)S(1)} %get-tuple-element.37), channel_id=1, source_target_pairs={{0,8},{8,0},{16,24},{24,16},{1,9},{9,1},{17,25},{25,17},{2,10},{10... | collective-permute-start | bytes 147464 | tf_op jit(solution)/shard_map/ppermute | solution.py:289
  53.7 2.2 %collective-permute-start.15 = (bf16[192,128]{1,0:T(8,128)(2,1)S(1)}, bf16[192,128]{1,0:T(8,128)(2,1)S(1)}, u32[]{:S(2)}, u32[]{:S(2)}) collective-permute-start(bf16[192,128]{1,0:T(8,128)(2,1)S(1)} %get-tuple-element.39), channel_id=1, source_target_pairs={{0,24},{8,16},{16,8},{24,0},{1,25},{9,17},{17,9},{25,1},{2,26},{10... | collective-permute-start | bytes 147464 | tf_op jit(solution)/shard_map/ppermute | solution.py:289
  56.0 2.0 %collective-permute-start.29 = (bf16[512,128]{1,0:T(8,128)(2,1)S(1)}, bf16[512,128]{1,0:T(8,128)(2,1)S(1)}, u32[]{:S(2)}, u32[]{:S(2)}) collective-permute-start(bf16[512,128]{1,0:T(8,128)(2,1)S(1)} %text_plane.1.refs_0_), channel_id=1, source_target_pairs={{0,8},{8,0},{16,24},{24,16},{1,9},{9,1},{17,25},{25,17},{2,10},{10... | collective-permute-start | bytes 393224 | tf_op jit(solution)/shard_map/ppermute | solution.py:289
  58.7 1.1 %collective-permute-done.15.refs_2_ = bf16[192,128]{1,0:T(8,128)(2,1)S(1)} collective-permute-done((bf16[192,128]{1,0:T(8,128)(2,1)S(1)}, bf16[192,128]{1,0:T(8,128)(2,1)S(1)}, u32[]{:S(2)}, u32[]{:S(2)}) %collective-permute-start.15) | collective-permute-done | bytes 49184 | tf_op jit(solution)/shard_map/ppermute | solution.py:289
  59.9 1.0 %collective-permute-start.16 = (bf16[192,128]{1,0:T(8,128)(2,1)S(1)}, bf16[192,128]{1,0:T(8,128)(2,1)S(1)}, u32[]{:S(2)}, u32[]{:S(2)}) collective-permute-start(bf16[192,128]{1,0:T(8,128)(2,1)S(1)} %image_depth.1.refs_0_), channel_id=1, source_target_pairs={{0,2},{1,3},{2,0},{3,1},{4,6},{5,7},{6,4},{7,5},{8,10},{9,11},{10,... | collective-permute-start | bytes 147464 | tf_op jit(solution)/shard_map/ppermute | solution.py:288
  60.9 2.3 %collective-permute-start.31 = (bf16[512,128]{1,0:T(8,128)(2,1)S(1)}, bf16[512,128]{1,0:T(8,128)(2,1)S(1)}, u32[]{:S(2)}, u32[]{:S(2)}) collective-permute-start(bf16[512,128]{1,0:T(8,128)(2,1)S(1)} %text_plane.1.refs_0_), channel_id=1, source_target_pairs={{0,24},{8,16},{16,8},{24,0},{1,25},{9,17},{17,9},{25,1},{2,26},{10... | collective-permute-start | bytes 393224 | tf_op jit(solution)/shard_map/ppermute | solution.py:289
  63.2 1.9 %collective-permute-start.17 = (bf16[192,128]{1,0:T(8,128)(2,1)S(1)}, bf16[192,128]{1,0:T(8,128)(2,1)S(1)}, u32[]{:S(2)}, u32[]{:S(2)}) collective-permute-start(bf16[192,128]{1,0:T(8,128)(2,1)S(1)} %image_depth.1.refs_0_), channel_id=1, source_target_pairs={{0,4},{1,5},{2,6},{3,7},{4,0},{5,1},{6,2},{7,3},{8,12},{9,13},{10,... | collective-permute-start | bytes 147464 | tf_op jit(solution)/shard_map/ppermute | solution.py:288
  65.1 1.5 %collective-permute-start.18 = (bf16[192,128]{1,0:T(8,128)(2,1)S(1)}, bf16[192,128]{1,0:T(8,128)(2,1)S(1)}, u32[]{:S(2)}, u32[]{:S(2)}) collective-permute-start(bf16[192,128]{1,0:T(8,128)(2,1)S(1)} %image_depth.1.refs_0_), channel_id=1, source_target_pairs={{0,6},{1,7},{2,4},{3,5},{4,2},{5,3},{6,0},{7,1},{8,14},{9,15},{10,... | collective-permute-start | bytes 147464 | tf_op jit(solution)/shard_map/ppermute | solution.py:288
  67.3 2.8 %collective-permute-done.18.refs_3_ = bf16[192,128]{1,0:T(8,128)(2,1)S(1)} collective-permute-done((bf16[192,128]{1,0:T(8,128)(2,1)S(1)}, bf16[192,128]{1,0:T(8,128)(2,1)S(1)}, u32[]{:S(2)}, u32[]{:S(2)}) %collective-permute-start.18) | collective-permute-done | bytes 49184 | tf_op jit(solution)/shard_map/ppermute | solution.py:288
  72.7 1.2 %collective-permute-start.32 = (f32[128,128]{1,0:T(8,128)S(1)}, f32[128,128]{1,0:T(8,128)S(1)}, u32[]{:S(2)}, u32[]{:S(2)}) collective-permute-start(f32[128,128]{1,0:T(8,128)S(1)} %get-tuple-element.52.refs_0_), channel_id=1, source_target_pairs={{0,8},{8,0},{16,24},{24,16},{1,9},{9,1},{17,25},{25,17},{2,10},{10... | collective-permute-start | bytes 196616 | tf_op jit(solution)/shard_map/ppermute | solution.py:289
  74.8 2.4 %collective-permute-start.34 = (f32[128,128]{1,0:T(8,128)S(1)}, f32[128,128]{1,0:T(8,128)S(1)}, u32[]{:S(2)}, u32[]{:S(2)}) collective-permute-start(f32[128,128]{1,0:T(8,128)S(1)} %get-tuple-element.52.refs_0_), channel_id=1, source_target_pairs={{0,24},{8,16},{16,8},{24,0},{1,25},{9,17},{17,9},{25,1},{2,26},{10... | collective-permute-start | bytes 196616 | tf_op jit(solution)/shard_map/ppermute | solution.py:289
  78.1 1.2 %collective-permute-start.37 = (f32[128,128]{1,0:T(8,128)S(1)}, f32[128,128]{1,0:T(8,128)S(1)}, u32[]{:S(2)}, u32[]{:S(2)}) collective-permute-start(f32[128,128]{1,0:T(8,128)S(1)} %text_gram_cores.1.refs_4_), channel_id=1, source_target_pairs={{0,4},{1,5},{2,6},{3,7},{4,0},{5,1},{6,2},{7,3},{8,12},{9,13},{10,... | collective-permute-start | bytes 196616 | tf_op jit(solution)/shard_map/ppermute | solution.py:288
  79.3 1.4 %collective-permute-start.38 = (f32[128,128]{1,0:T(8,128)S(1)}, f32[128,128]{1,0:T(8,128)S(1)}, u32[]{:S(2)}, u32[]{:S(2)}) collective-permute-start(f32[128,128]{1,0:T(8,128)S(1)} %text_gram_cores.1.refs_4_), channel_id=1, source_target_pairs={{0,6},{1,7},{2,4},{3,5},{4,2},{5,3},{6,0},{7,1},{8,14},{9,15},{10,... | collective-permute-start | bytes 196616 | tf_op jit(solution)/shard_map/ppermute | solution.py:288
  80.8 1.2 %collective-permute-done.33.refs_2_ = f32[128,128]{1,0:T(8,128)S(1)} collective-permute-done((f32[128,128]{1,0:T(8,128)S(1)}, f32[128,128]{1,0:T(8,128)S(1)}, u32[]{:S(2)}, u32[]{:S(2)}) %collective-permute-start.33) | collective-permute-done | bytes 65568 | tf_op jit(solution)/shard_map/ppermute | solution.py:289
  83.0 1.5 %collective-permute-done.38.refs_7_ = f32[128,128]{1,0:T(8,128)S(1)} collective-permute-done((f32[128,128]{1,0:T(8,128)S(1)}, f32[128,128]{1,0:T(8,128)S(1)}, u32[]{:S(2)}, u32[]{:S(2)}) %collective-permute-start.38) | collective-permute-done | bytes 65568 | tf_op jit(solution)/shard_map/ppermute | solution.py:288
  84.5 7.8 %finish.1 = (f32[1536,128]{1,0:T(8,128)}, f32[512,128]{1,0:T(8,128)}) custom-call(bf16[8,192,128]{2,1,0:T(8,128)(2,1)S(1)} %get-tuple-element.40.ipanel, bf16[1,512,128]{2,1,0:T(8,128)(2,1)S(1)} %get-tuple-element.51.tpanel, f32[128,128]{1,0:T(8,128)S(1)} %get-tuple-element.52.refs_0_, f32[128,128]{1,0:T(8,128)S(1)} %collective-permute-done.32.refs_1_, ...), custom_call_target="tpu_custom_call" | custom-call | flops 10000000000 | bytes 1179648 | tf_op jit(solution)/shard_map/finish/pallas_call | solution.py:274
  (63 shorter events, 13.0 us)
Async XLA Ops:
  0.6 14.8 %collective-permute-start = (bf16[1536,128]{1,0:T(8,128)(2,1)}, bf16[1536,128]{1,0:T(8,128)(2,1)S(1)}, u32[]{:S(2)}, u32[]{:S(2)}) collective-permute-start(bf16[1536,128]{1,0:T(8,128)(2,1)} %refs_0_.3), channel_id=1, source_target_pairs={{0,8},{1,17},{2,10},{3,19},{4,12},{5,21},{6,14},{7,23},{8,0},{9,25... | collective-permute-start | bytes 1179656 | tf_op jit(solution)/shard_map/ppermute | solution.py:307
  3.7 6.5 %collective-permute-start.1 = (bf16[512,128]{1,0:T(8,128)(2,1)}, bf16[512,128]{1,0:T(8,128)(2,1)S(1)}, u32[]{:S(2)}, u32[]{:S(2)}) collective-permute-start(bf16[512,128]{1,0:T(8,128)(2,1)} %refs_0_.2), channel_id=1, source_target_pairs={{0,2},{1,3},{2,0},{3,1},{4,6},{5,7},{6,4},{7,5},{8,10},{9,11},{10,... | collective-permute-start | bytes 393224 | tf_op jit(solution)/shard_map/ppermute | solution.py:288
  5.2 8.7 %collective-permute-start.2 = (bf16[512,128]{1,0:T(8,128)(2,1)}, bf16[512,128]{1,0:T(8,128)(2,1)S(1)}, u32[]{:S(2)}, u32[]{:S(2)}) collective-permute-start(bf16[512,128]{1,0:T(8,128)(2,1)} %refs_0_.2), channel_id=1, source_target_pairs={{0,4},{1,5},{2,6},{3,7},{4,0},{5,1},{6,2},{7,3},{8,12},{9,13},{10,... | collective-permute-start | bytes 393224 | tf_op jit(solution)/shard_map/ppermute | solution.py:288
  6.7 7.2 %collective-permute-start.3 = (bf16[512,128]{1,0:T(8,128)(2,1)}, bf16[512,128]{1,0:T(8,128)(2,1)S(1)}, u32[]{:S(2)}, u32[]{:S(2)}) collective-permute-start(bf16[512,128]{1,0:T(8,128)(2,1)} %refs_0_.2), channel_id=1, source_target_pairs={{0,6},{1,7},{2,4},{3,5},{4,2},{5,3},{6,0},{7,1},{8,14},{9,15},{10,... | collective-permute-start | bytes 393224 | tf_op jit(solution)/shard_map/ppermute | solution.py:288
  7.2 10.7 %collective-permute-start.4 = (bf16[512,128]{1,0:T(8,128)(2,1)}, bf16[512,128]{1,0:T(8,128)(2,1)S(1)}, u32[]{:S(2)}, u32[]{:S(2)}) collective-permute-start(bf16[512,128]{1,0:T(8,128)(2,1)} %refs_0_.2), channel_id=1, source_target_pairs={{0,1},{1,0},{2,3},{3,2},{4,5},{5,4},{6,7},{7,6},{8,9},{9,8},{10,11... | collective-permute-start | bytes 393224 | tf_op jit(solution)/shard_map/ppermute | solution.py:288
  10.2 7.7 %collective-permute-start.5 = (bf16[512,128]{1,0:T(8,128)(2,1)S(1)}, bf16[512,128]{1,0:T(8,128)(2,1)S(1)}, u32[]{:S(2)}, u32[]{:S(2)}) collective-permute-start(bf16[512,128]{1,0:T(8,128)(2,1)S(1)} %collective-permute-done.1.refs_1_), channel_id=1, source_target_pairs={{0,1},{1,0},{2,3},{3,2},{4,5},{5,4},{6,7},{7,6},{8,9},{9,8},{10,11... | collective-permute-start | bytes 393224 | tf_op jit(solution)/shard_map/ppermute | solution.py:288
  15.4 9.6 %collective-permute-start.8 = (bf16[768,128]{1,0:T(8,128)(2,1)S(1)}, bf16[768,128]{1,0:T(8,128)(2,1)S(1)}, u32[]{:S(2)}, u32[]{:S(2)}) collective-permute-start(bf16[768,128]{1,0:T(8,128)(2,1)S(1)} %constant_dynamic-slice_fusion), channel_id=1, source_target_pairs={{0,24},{8,16},{16,8},{24,0},{1,25},{9,17},{17,9},{25,1},{2,26},{10... | collective-permute-start | bytes 589832 | tf_op jit(solution)/shard_map/ppermute | solution.py:289
  25.0 11.4 %collective-permute-start.9 = (f32[4,4,192,128]{3,2,1,0:T(8,128)S(1)}, f32[4,4,192,128]{3,2,1,0:T(8,128)S(1)}, u32[]{:S(2)}, u32[]{:S(2)}) collective-permute-start(f32[4,4,192,128]{3,2,1,0:T(8,128)S(1)} %get-tuple-element.31), channel_id=1, source_target_pairs={{0,1},{1,0},{2,3},{3,2},{4,5},{5,4},{6,7},{7,6},{8,9},{9,8},{10,11... | collective-permute-start | bytes 4718600 | tf_op jit(solution)/shard_map/ppermute | solution.py:288
  25.1 4.2 %collective-permute-start.23 = (bf16[1536,128]{1,0:T(8,128)(2,1)S(1)}, bf16[1536,128]{1,0:T(8,128)(2,1)S(1)}, u32[]{:S(2)}, u32[]{:S(2)}) collective-permute-start(bf16[1536,128]{1,0:T(8,128)(2,1)S(1)} %collective-permute-done.refs_1_), channel_id=1, source_target_pairs={{0,1},{1,0},{2,3},{3,2},{4,5},{5,4},{6,7},{7,6},{8,9},{9,8},{10,11... | collective-permute-start | bytes 1179656 | tf_op jit(solution)/shard_map/ppermute | solution.py:288
  36.3 4.5 %collective-permute-start.25 = (f32[4,1,512,128]{3,2,1,0:T(8,128)S(1)}, f32[4,1,512,128]{3,2,1,0:T(8,128)S(1)}, u32[]{:S(2)}, u32[]{:S(2)}) collective-permute-start(f32[4,1,512,128]{3,2,1,0:T(8,128)S(1)} %get-tuple-element.44), channel_id=1, source_target_pairs={{0,1},{1,0},{2,3},{3,2},{4,5},{5,4},{6,7},{7,6},{8,9},{9,8},{10,11... | collective-permute-start | bytes 3145736 | tf_op jit(solution)/shard_map/ppermute | solution.py:288
  37.2 7.8 %collective-permute-start.10 = (bf16[4,192,128]{2,1,0:T(8,128)(2,1)S(1)}, bf16[4,192,128]{2,1,0:T(8,128)(2,1)S(1)}, u32[]{:S(2)}, u32[]{:S(2)}) collective-permute-start(bf16[4,192,128]{2,1,0:T(8,128)(2,1)S(1)} %get-tuple-element.33), channel_id=1, source_target_pairs={{0,2},{1,3},{2,0},{3,1},{4,6},{5,7},{6,4},{7,5},{8,10},{9,11},{10,... | collective-permute-start | bytes 589832 | tf_op jit(solution)/shard_map/ppermute | solution.py:288
  38.7 11.9 %collective-permute-start.11 = (bf16[4,192,128]{2,1,0:T(8,128)(2,1)S(1)}, bf16[4,192,128]{2,1,0:T(8,128)(2,1)S(1)}, u32[]{:S(2)}, u32[]{:S(2)}) collective-permute-start(bf16[4,192,128]{2,1,0:T(8,128)(2,1)S(1)} %get-tuple-element.34), channel_id=1, source_target_pairs={{0,4},{1,5},{2,6},{3,7},{4,0},{5,1},{6,2},{7,3},{8,12},{9,13},{10,... | collective-permute-start | bytes 589832 | tf_op jit(solution)/shard_map/ppermute | solution.py:288
  40.3 10.3 %collective-permute-start.12 = (bf16[4,192,128]{2,1,0:T(8,128)(2,1)S(1)}, bf16[4,192,128]{2,1,0:T(8,128)(2,1)S(1)}, u32[]{:S(2)}, u32[]{:S(2)}) collective-permute-start(bf16[4,192,128]{2,1,0:T(8,128)(2,1)S(1)} %get-tuple-element.35), channel_id=1, source_target_pairs={{0,6},{1,7},{2,4},{3,5},{4,2},{5,3},{6,0},{7,1},{8,14},{9,15},{10,... | collective-permute-start | bytes 589832 | tf_op jit(solution)/shard_map/ppermute | solution.py:288
  41.4 12.3 %collective-permute-start.26 = (bf16[512,128]{1,0:T(8,128)(2,1)S(1)}, bf16[512,128]{1,0:T(8,128)(2,1)S(1)}, u32[]{:S(2)}, u32[]{:S(2)}) collective-permute-start(bf16[512,128]{1,0:T(8,128)(2,1)S(1)} %bitcast.9), channel_id=1, source_target_pairs={{0,2},{1,3},{2,0},{3,1},{4,6},{5,7},{6,4},{7,5},{8,10},{9,11},{10,... | collective-permute-start | bytes 393224 | tf_op jit(solution)/shard_map/ppermute | solution.py:288
  42.9 13.0 %collective-permute-start.27 = (bf16[512,128]{1,0:T(8,128)(2,1)S(1)}, bf16[512,128]{1,0:T(8,128)(2,1)S(1)}, u32[]{:S(2)}, u32[]{:S(2)}) collective-permute-start(bf16[512,128]{1,0:T(8,128)(2,1)S(1)} %bitcast.8), channel_id=1, source_target_pairs={{0,4},{1,5},{2,6},{3,7},{4,0},{5,1},{6,2},{7,3},{8,12},{9,13},{10,... | collective-permute-start | bytes 393224 | tf_op jit(solution)/shard_map/ppermute | solution.py:288
  45.0 11.0 %collective-permute-start.28 = (bf16[512,128]{1,0:T(8,128)(2,1)S(1)}, bf16[512,128]{1,0:T(8,128)(2,1)S(1)}, u32[]{:S(2)}, u32[]{:S(2)}) collective-permute-start(bf16[512,128]{1,0:T(8,128)(2,1)S(1)} %bitcast.7), channel_id=1, source_target_pairs={{0,6},{1,7},{2,4},{3,5},{4,2},{5,3},{6,0},{7,1},{8,14},{9,15},{10,... | collective-permute-start | bytes 393224 | tf_op jit(solution)/shard_map/ppermute | solution.py:288
  51.2 7.0 %collective-permute-start.13 = (bf16[192,128]{1,0:T(8,128)(2,1)S(1)}, bf16[192,128]{1,0:T(8,128)(2,1)S(1)}, u32[]{:S(2)}, u32[]{:S(2)}) collective-permute-start(bf16[192,128]{1,0:T(8,128)(2,1)S(1)} %get-tuple-element.37), channel_id=1, source_target_pairs={{0,8},{8,0},{16,24},{24,16},{1,9},{9,1},{17,25},{25,17},{2,10},{10... | collective-permute-start | bytes 147464 | tf_op jit(solution)/shard_map/ppermute | solution.py:289
  53.5 5.2 %collective-permute-start.14 = (bf16[192,128]{1,0:T(8,128)(2,1)S(1)}, bf16[192,128]{1,0:T(8,128)(2,1)S(1)}, u32[]{:S(2)}, u32[]{:S(2)}) collective-permute-start(bf16[192,128]{1,0:T(8,128)(2,1)S(1)} %get-tuple-element.38), channel_id=1, source_target_pairs={{0,16},{8,24},{16,0},{24,8},{1,17},{9,25},{17,1},{25,9},{2,18},{10... | collective-permute-start | bytes 147464 | tf_op jit(solution)/shard_map/ppermute | solution.py:289
  53.7 6.1 %collective-permute-start.15 = (bf16[192,128]{1,0:T(8,128)(2,1)S(1)}, bf16[192,128]{1,0:T(8,128)(2,1)S(1)}, u32[]{:S(2)}, u32[]{:S(2)}) collective-permute-start(bf16[192,128]{1,0:T(8,128)(2,1)S(1)} %get-tuple-element.39), channel_id=1, source_target_pairs={{0,24},{8,16},{16,8},{24,0},{1,25},{9,17},{17,9},{25,1},{2,26},{10... | collective-permute-start | bytes 147464 | tf_op jit(solution)/shard_map/ppermute | solution.py:289
  56.0 14.1 %collective-permute-start.29 = (bf16[512,128]{1,0:T(8,128)(2,1)S(1)}, bf16[512,128]{1,0:T(8,128)(2,1)S(1)}, u32[]{:S(2)}, u32[]{:S(2)}) collective-permute-start(bf16[512,128]{1,0:T(8,128)(2,1)S(1)} %text_plane.1.refs_0_), channel_id=1, source_target_pairs={{0,8},{8,0},{16,24},{24,16},{1,9},{9,1},{17,25},{25,17},{2,10},{10... | collective-permute-start | bytes 393224 | tf_op jit(solution)/shard_map/ppermute | solution.py:289
  58.0 12.6 %collective-permute-start.30 = (bf16[512,128]{1,0:T(8,128)(2,1)S(1)}, bf16[512,128]{1,0:T(8,128)(2,1)S(1)}, u32[]{:S(2)}, u32[]{:S(2)}) collective-permute-start(bf16[512,128]{1,0:T(8,128)(2,1)S(1)} %text_plane.1.refs_0_), channel_id=1, source_target_pairs={{0,16},{8,24},{16,0},{24,8},{1,17},{9,25},{17,1},{25,9},{2,18},{10... | collective-permute-start | bytes 393224 | tf_op jit(solution)/shard_map/ppermute | solution.py:289
  59.9 5.2 %collective-permute-start.16 = (bf16[192,128]{1,0:T(8,128)(2,1)S(1)}, bf16[192,128]{1,0:T(8,128)(2,1)S(1)}, u32[]{:S(2)}, u32[]{:S(2)}) collective-permute-start(bf16[192,128]{1,0:T(8,128)(2,1)S(1)} %image_depth.1.refs_0_), channel_id=1, source_target_pairs={{0,2},{1,3},{2,0},{3,1},{4,6},{5,7},{6,4},{7,5},{8,10},{9,11},{10,... | collective-permute-start | bytes 147464 | tf_op jit(solution)/shard_map/ppermute | solution.py:288
  60.9 9.8 %collective-permute-start.31 = (bf16[512,128]{1,0:T(8,128)(2,1)S(1)}, bf16[512,128]{1,0:T(8,128)(2,1)S(1)}, u32[]{:S(2)}, u32[]{:S(2)}) collective-permute-start(bf16[512,128]{1,0:T(8,128)(2,1)S(1)} %text_plane.1.refs_0_), channel_id=1, source_target_pairs={{0,24},{8,16},{16,8},{24,0},{1,25},{9,17},{17,9},{25,1},{2,26},{10... | collective-permute-start | bytes 393224 | tf_op jit(solution)/shard_map/ppermute | solution.py:289
  65.1 5.0 %collective-permute-start.18 = (bf16[192,128]{1,0:T(8,128)(2,1)S(1)}, bf16[192,128]{1,0:T(8,128)(2,1)S(1)}, u32[]{:S(2)}, u32[]{:S(2)}) collective-permute-start(bf16[192,128]{1,0:T(8,128)(2,1)S(1)} %image_depth.1.refs_0_), channel_id=1, source_target_pairs={{0,6},{1,7},{2,4},{3,5},{4,2},{5,3},{6,0},{7,1},{8,14},{9,15},{10,... | collective-permute-start | bytes 147464 | tf_op jit(solution)/shard_map/ppermute | solution.py:288
  67.3 4.2 %collective-permute-start.19 = (bf16[192,128]{1,0:T(8,128)(2,1)S(1)}, bf16[192,128]{1,0:T(8,128)(2,1)S(1)}, u32[]{:S(2)}, u32[]{:S(2)}) collective-permute-start(bf16[192,128]{1,0:T(8,128)(2,1)S(1)} %image_depth.1.refs_0_), channel_id=1, source_target_pairs={{0,1},{1,0},{2,3},{3,2},{4,5},{5,4},{6,7},{7,6},{8,9},{9,8},{10,11... | collective-permute-start | bytes 147464 | tf_op jit(solution)/shard_map/ppermute | solution.py:288
  70.9 6.3 %collective-permute-start.35 = (f32[128,128]{1,0:T(8,128)S(1)}, f32[128,128]{1,0:T(8,128)S(1)}, u32[]{:S(2)}, u32[]{:S(2)}) collective-permute-start(f32[128,128]{1,0:T(8,128)S(1)} %get-tuple-element.53.own_ref), channel_id=1, source_target_pairs={{0,1},{1,0},{2,3},{3,2},{4,5},{5,4},{6,7},{7,6},{8,9},{9,8},{10,11... | collective-permute-start | bytes 196616 | tf_op jit(solution)/shard_map/ppermute | solution.py:288
  72.7 6.6 %collective-permute-start.32 = (f32[128,128]{1,0:T(8,128)S(1)}, f32[128,128]{1,0:T(8,128)S(1)}, u32[]{:S(2)}, u32[]{:S(2)}) collective-permute-start(f32[128,128]{1,0:T(8,128)S(1)} %get-tuple-element.52.refs_0_), channel_id=1, source_target_pairs={{0,8},{8,0},{16,24},{24,16},{1,9},{9,1},{17,25},{25,17},{2,10},{10... | collective-permute-start | bytes 196616 | tf_op jit(solution)/shard_map/ppermute | solution.py:289
  73.9 8.0 %collective-permute-start.33 = (f32[128,128]{1,0:T(8,128)S(1)}, f32[128,128]{1,0:T(8,128)S(1)}, u32[]{:S(2)}, u32[]{:S(2)}) collective-permute-start(f32[128,128]{1,0:T(8,128)S(1)} %get-tuple-element.52.refs_0_), channel_id=1, source_target_pairs={{0,16},{8,24},{16,0},{24,8},{1,17},{9,25},{17,1},{25,9},{2,18},{10... | collective-permute-start | bytes 196616 | tf_op jit(solution)/shard_map/ppermute | solution.py:289
  74.8 7.2 %collective-permute-start.34 = (f32[128,128]{1,0:T(8,128)S(1)}, f32[128,128]{1,0:T(8,128)S(1)}, u32[]{:S(2)}, u32[]{:S(2)}) collective-permute-start(f32[128,128]{1,0:T(8,128)S(1)} %get-tuple-element.52.refs_0_), channel_id=1, source_target_pairs={{0,24},{8,16},{16,8},{24,0},{1,25},{9,17},{17,9},{25,1},{2,26},{10... | collective-permute-start | bytes 196616 | tf_op jit(solution)/shard_map/ppermute | solution.py:289
  77.2 4.9 %collective-permute-start.36 = (f32[128,128]{1,0:T(8,128)S(1)}, f32[128,128]{1,0:T(8,128)S(1)}, u32[]{:S(2)}, u32[]{:S(2)}) collective-permute-start(f32[128,128]{1,0:T(8,128)S(1)} %text_gram_cores.1.refs_4_), channel_id=1, source_target_pairs={{0,2},{1,3},{2,0},{3,1},{4,6},{5,7},{6,4},{7,5},{8,10},{9,11},{10,... | collective-permute-start | bytes 196616 | tf_op jit(solution)/shard_map/ppermute | solution.py:288
  78.1 4.9 %collective-permute-start.37 = (f32[128,128]{1,0:T(8,128)S(1)}, f32[128,128]{1,0:T(8,128)S(1)}, u32[]{:S(2)}, u32[]{:S(2)}) collective-permute-start(f32[128,128]{1,0:T(8,128)S(1)} %text_gram_cores.1.refs_4_), channel_id=1, source_target_pairs={{0,4},{1,5},{2,6},{3,7},{4,0},{5,1},{6,2},{7,3},{8,12},{9,13},{10,... | collective-permute-start | bytes 196616 | tf_op jit(solution)/shard_map/ppermute | solution.py:288
  79.3 5.2 %collective-permute-start.38 = (f32[128,128]{1,0:T(8,128)S(1)}, f32[128,128]{1,0:T(8,128)S(1)}, u32[]{:S(2)}, u32[]{:S(2)}) collective-permute-start(f32[128,128]{1,0:T(8,128)S(1)} %text_gram_cores.1.refs_4_), channel_id=1, source_target_pairs={{0,6},{1,7},{2,4},{3,5},{4,2},{5,3},{6,0},{7,1},{8,14},{9,15},{10,... | collective-permute-start | bytes 196616 | tf_op jit(solution)/shard_map/ppermute | solution.py:288
  (9 other events, 32.2 us)

commit v9 on v8

--- a/solution.py
+++ b/solution.py
@@ -49,7 +49,7 @@
 
 
 def panel_kernel(rows, n, n_in, n_out, me_ref, a_hbm, b_hbm, *refs):
-    parts, (keep_ref, send_ref, a_ref, b_ref, probe, a_sem, b_sem) = refs[:n], refs[n:]
+    parts, (keep_ref, send_ref, a_ref, b_ref, probe, a_sem, b_sem, own_sem) = refs[:n], refs[n:]
     core = me_ref[0] % 2
     tall = a_ref.shape[0] // n_in
     cols = b_ref.shape[1] // n_out // 2
@@ -60,10 +60,14 @@
     for i in range(n_out):
         span = pl.ds(2 * i * cols, 2 * cols)
         moves.append(pltpu.make_async_copy(b_hbm.at[:, span], b_ref.at[:, span], b_sem.at[i]))
+    places = rows(me_ref)
+    own = pltpu.make_async_copy(parts[0], probe.at[pl.ds(places[0], parts[0].shape[0])], own_sem)
+    own.start()
     for move in moves:
         move.start()
-    for at, part in zip(rows(me_ref), parts):
+    for at, part in zip(places[1:], parts[1:]):
         probe[pl.ds(at, part.shape[0]), :] = part[...]
+    own.wait()
     sketches = []
     for i in range(n_in):
         moves[i].wait()
@@ -86,7 +90,7 @@
     n_in = 3 if pairs % 48 == 0 else 1
     return pl.pallas_call(
         functools.partial(panel_kernel, rows, len(parts), n_in, blocks),
-        in_specs=[SMEM, hbm, hbm] + [VMEM] * len(parts),
+        in_specs=[SMEM, hbm, hbm, hbm] + [VMEM] * (len(parts) - 1),
         out_specs=[VMEM, VMEM],
         out_shape=[out, out],
         scratch_shapes=[
@@ -95,6 +99,7 @@
             pltpu.VMEM((a.shape[1], rank), BF16),
             pltpu.SemaphoreType.DMA((n_in,)),
             pltpu.SemaphoreType.DMA((blocks,)),
+            pltpu.SemaphoreType.DMA,
         ],
         compiler_params=pltpu.CompilerParams(vmem_limit_bytes=PANEL_LIMIT),
         cost_estimate=cost(2 * pairs * rank * (width + a.shape[1]), 2 * pairs * (width + a.shape[1])),
@@ -179,34 +184,6 @@
         cost_estimate=cost(2 * n * rows * rank * rank, 4 * n * rows * rank),
         name=name,
     )(me, *parts)
-
-
-def tree_sum(values):
-    while len(values) > 1:
-        values = [x + y for x, y in zip(values[::2], values[1::2])]
-    return values[0]
-
-
-def text_gram_kernel(*refs):
-    *parts, panel_ref, gram_ref = refs
-    panel = tree_sum([part[...].astype(F32) for part in parts]).astype(BF16)
-    panel_ref[0] = panel
-    gram_ref[...] = lax.dot_general(
-        panel, panel, (((0,), (0,)), ((), ())), preferred_element_type=F32
-    )
-
-
-def text_gram_call(parts):
-    rows, rank = parts[0].shape
-    return pl.pallas_call(
-        text_gram_kernel,
-        in_specs=[VMEM] * len(parts),
-        out_specs=[VMEM, VMEM],
-        out_shape=[sds((1, rows, rank), BF16), sds((rank, rank), F32)],
-        compiler_params=params(),
-        cost_estimate=cost(2 * rows * rank * rank, 4 * rows * rank),
-        name="text_gram",
-    )(*parts)
 
 
 def inverse_factor(gram):
@@ -291,9 +268,9 @@
     over_chips = lambda xs: [col_swap(x, 2 * s) for x, s in zip(xs, chips)]
     over_depth = lambda xs: [row_swap(x, t) for x, t in zip(xs, depths)]
 
-    def over_plane(x):
+    def over_plane(x, received=None):
         got = {0: x}
-        for s, block in zip(chips, over_chips([x] * len(chips))):
+        for s, block in zip(chips, received or over_chips([x] * len(chips))):
             got[2 * s] = block
         for s in list(got):
             got[s ^ 1] = col_swap(got[s], 1)
@@ -307,42 +284,50 @@
         return lax.ppermute(x, ("row", "col"), pairs)
 
     fetched = [(t, t + 1, split_swap(probe_image, t, t + 1)) for t in depths[:-1:2]]
-    text_parts = over_plane(probe_text)
+    half = probe_image.shape[0] // 2
+    mine = lax.dynamic_slice_in_dim(probe_image, me[0] % 2 * half, half, 0)
+    received = over_chips([probe_text] * len(chips))
+    mine, received[-1] = lax.optimization_barrier((mine, received[-1]))
+    text_parts = over_plane(probe_text, received)
     first, *blocks = lax.optimization_barrier((me, *[block for _, _, block in fetched]))
-    half = probe_image.shape[0] // 2
     last = depths[-1]
-    mine = row_swap(lax.dynamic_slice_in_dim(probe_image, me[0] % 2 * half, half, 0), last)
+    mine = row_swap(mine, last)
     image_order = [(0, 0, None)]
     image_parts = [probe_image]
-    for (even, odd, _), block in zip(fetched, blocks):
-        image_order += [(even, odd, None), (odd, even, None)]
-        image_parts += [block, col_swap(block, 1)]
-    image_order += [(last, last, 0), (last, last, 1)]
 
     columns = text_rows(list(text_parts), probe_text.shape[0])
     keep, send = panel_call(
         first, text_feats, image_feats, list(text_parts.values()), columns, n_row, groups, "image_panel"
     )
-    send, mine = lax.optimization_barrier((send, mine))
-    image_parts += [mine, col_swap(mine, 1)]
+    send, mine, *blocks = lax.optimization_barrier((send, mine, *blocks))
+    swapped = [col_swap(block, 1) for block in blocks]
+    send, other, *swapped = lax.optimization_barrier((send, col_swap(mine, 1), *swapped))
+    for (even, odd, _), block, twin in zip(fetched, blocks, swapped):
+        image_order += [(even, odd, None), (odd, even, None)]
+        image_parts += [block, twin]
+    image_order += [(last, last, 0), (last, last, 1)]
+    image_parts += [mine, other]
     own, *image_sends = sums_call("col", 1, chips, me, [keep, col_swap(send, 1)], "image_cores")
     own, *sends = sums_call("row", 0, depths, me, [own] + over_chips(image_sends), "image_plane")
     after_plane = sends[0]
     mine = last_call(own, over_depth(sends), BF16, "image_depth")
+    after_depth = mine
     parts = over_plane(mine)
     ipanel, gram = gram_call("col", list(parts), me, list(parts.values()), "image_gram")
     igrams = [gram] + over_depth([gram] * len(depths))
 
     columns = image_rows(image_order, probe_image.shape[0])
     keep, send = panel_call(
-        me, image_feats, text_feats, image_parts, columns, groups, 1, "text_panel"
+        me, image_feats, text_feats, image_parts, columns, groups, n_row, "text_panel"
     )
     swapped, _ = lax.optimization_barrier((col_swap(send, 1), image_sends[0]))
-    own, *sends = sums_call("col", 0, chips, me, [keep, swapped], "text_cores")
-    own, sends = own[0], [x[0] for x in sends]
+    own, *sends = sums_call("row", 1, depths, me, [keep, swapped], "text_cores")
     own, _ = lax.optimization_barrier((own, after_plane))
+    own, *sends = sums_call("col", 0, chips, me, [own] + over_depth(sends), "text_depth")
+    own, _ = lax.optimization_barrier((own, after_depth))
     mine = last_call(own, over_chips(sends), BF16, "text_plane")
-    tpanel, gram = text_gram_call([mine] + over_depth([mine] * len(depths)))
+    parts = [mine] + over_depth([mine] * len(depths))
+    tpanel, gram = gram_call("row", [0] + depths, me, parts, "text_gram")
     gram = last_call(gram, [col_swap(gram, 1)], F32, "text_gram_cores")
     tgrams = [gram] + over_chips([gram] * len(chips))
 

time: 92.4 us -> 99.4 us (1.076)
  starting transfers between devices: 42.2 us -> 46.7 us
  Pallas kernels: 24 us -> 25.4 us
  waiting for transfers between devices: 23.3 us -> 24.3 us
    ppermute x10 -> x13, starting transfers between devices: 16 us -> 22.6 us  [per_device(): lax.ppermute(x, 'row', [(i, i ^ s) for i in range(n_row)])]
    ppermute x10 -> x13, waiting for transfers between devices: 2.8 us -> 8.05 us  [per_device(): lax.ppermute(x, 'row', [(i, i ^ s) for i in range(n_row)])]
    ppermute x28, waiting for transfers between devices: 20.5 us -> 16.2 us  [per_device(): lax.ppermute(x, 'col', [(i, i ^ s) for i in range(n_col)])]
    ppermute x28, starting transfers between devices: 23.1 us -> 21 us  [per_device(): lax.ppermute(x, 'col', [(i, i ^ s) for i in range(n_col)])]
    pallas_call x3 -> x4, Pallas kernels: 1.97 us -> 2.57 us  [sums_call(): pl.pallas_call(functools.partial(sums_kernel, which, axis, shifts, len(te...]
  transfers between devices with their start and end apart: 39 -> 42, of which waited for: 14 -> 14; matrix products, arithmetic and copies ran while one was open for 1% -> 1% of each run, Pallas kernels for 18% -> 18%
where the time goes in v9:
time: 99.4 us; the launch traced here: 99.2 us
  starting transfers between devices  46.7 us (47%)
  Pallas kernels  25.4 us (26%)
  waiting for transfers between devices  24.3 us (24%)
  local copies, waits for them, and re-layouts  1.89 us (2%)
    ppermute x13, starting transfers between devices, per_device(): lax.ppermute(x, 'row', [(i, i ^ s) for i in range(n_row)])  22.6 us
    ppermute x28, starting transfers between devices, per_device(): lax.ppermute(x, 'col', [(i, i ^ s) for i in range(n_col)])  21 us
    ppermute x28, waiting for transfers between devices, per_device(): lax.ppermute(x, 'col', [(i, i ^ s) for i in range(n_col)])  16.2 us
    pallas_call x2, Pallas kernels, panel_call(): pl.pallas_call(functools.partial(panel_kernel, rows, len(parts), n_in, bl...  13.5 us
    ppermute x13, waiting for transfers between devices, per_device(): lax.ppermute(x, 'row', [(i, i ^ s) for i in range(n_row)])  8.05 us
    pallas_call x1, Pallas kernels, finish_call(): pl.pallas_call(functools.partial(finish_kernel, widths, len(igrams)), in_...  7.58 us
    ppermute x1, starting transfers between devices, split_swap(): return lax.ppermute(x, ('row', 'col'), pairs)  3.09 us
    pallas_call x4, Pallas kernels, sums_call(): pl.pallas_call(functools.partial(sums_kernel, which, axis, shifts, len(te...  2.57 us
  transfers between devices with their start and end apart: 42, of which 14 were waited for; matrix products, arithmetic and copies ran while one was open for 1% of the time, Pallas kernels for 18%

profile of v9, /device:TPU:0, one launch (start us, length us, event | category | flops | bytes accessed | tf_op | source)
XLA Modules:
  0.0 99.2 jit_solution(8889433178761685331)
XLA Ops:
  0.6 3.1 %collective-permute-start = (bf16[1536,128]{1,0:T(8,128)(2,1)}, bf16[1536,128]{1,0:T(8,128)(2,1)S(1)}, u32[]{:S(2)}, u32[]{:S(2)}) collective-permute-start(bf16[1536,128]{1,0:T(8,128)(2,1)} %refs_0_.3), channel_id=1, source_target_pairs={{0,8},{1,17},{2,10},{3,19},{4,12},{5,21},{6,14},{7,23},{8,0},{9,25... | collective-permute-start | bytes 1179656 | tf_op jit(solution)/shard_map/ppermute | solution.py:284
  3.7 2.4 %collective-permute-start.3 = (bf16[512,128]{1,0:T(8,128)(2,1)}, bf16[512,128]{1,0:T(8,128)(2,1)S(1)}, u32[]{:S(2)}, u32[]{:S(2)}) collective-permute-start(bf16[512,128]{1,0:T(8,128)(2,1)} %refs_0_.2), channel_id=1, source_target_pairs={{0,6},{1,7},{2,4},{3,5},{4,2},{5,3},{6,0},{7,1},{8,14},{9,15},{10,... | collective-permute-start | bytes 393224 | tf_op jit(solution)/shard_map/ppermute | solution.py:265
  8.2 3.0 %collective-permute-done.3.refs_3_ = bf16[512,128]{1,0:T(8,128)(2,1)S(1)} collective-permute-done((bf16[512,128]{1,0:T(8,128)(2,1)}, bf16[512,128]{1,0:T(8,128)(2,1)S(1)}, u32[]{:S(2)}, u32[]{:S(2)}) %collective-permute-start.3) | collective-permute-done | bytes 131104 | tf_op jit(solution)/shard_map/ppermute | solution.py:265
  11.1 2.6 %collective-permute-done.1.refs_1_ = bf16[512,128]{1,0:T(8,128)(2,1)S(1)} collective-permute-done((bf16[512,128]{1,0:T(8,128)(2,1)}, bf16[512,128]{1,0:T(8,128)(2,1)S(1)}, u32[]{:S(2)}, u32[]{:S(2)}) %collective-permute-start.1) | collective-permute-done | bytes 131104 | tf_op jit(solution)/shard_map/ppermute | solution.py:265
  14.2 3.6 %collective-permute-start.8 = (bf16[768,128]{1,0:T(8,128)(2,1)S(1)}, bf16[768,128]{1,0:T(8,128)(2,1)S(1)}, u32[]{:S(2)}, u32[]{:S(2)}) collective-permute-start(bf16[768,128]{1,0:T(8,128)(2,1)S(1)} %constant_dynamic-slice_fusion), channel_id=1, source_target_pairs={{0,24},{8,16},{16,8},{24,0},{1,25},{9,17},{17,9},{25,1},{2,26},{10... | collective-permute-start | bytes 589832 | tf_op jit(solution)/shard_map/ppermute | solution.py:266
  18.9 6.3 %image_panel.1 = (f32[4,4,192,128]{3,2,1,0:T(8,128)S(1)}, f32[4,4,192,128]{3,2,1,0:T(8,128)S(1)}) custom-call(s32[2]{0:T(128)S(1)} %pad_add_fusion.me_ref, bf16[576,4096]{1,0:T(8,128)(2,1)} %b_hbm.3, bf16[576,6144]{1,0:T(8,128)(2,1)} %a_hbm.3, bf16[512,128]{1,0:T(8,128)(2,1)S(1)} %copy-done.1, bf16[512,128]{1,0:T(8,128)(2,1)S(1)} %collective-permute-done.1.refs_1_, ...), custom_call_target="tpu_custom_call" | custom-call | flops 1509949440 | bytes 11796480 | tf_op jit(solution)/shard_map/image_panel/pallas_call | solution.py:91
  25.8 1.5 %collective-permute-done.9.refs_4_ = bf16[768,128]{1,0:T(8,128)(2,1)S(1)} collective-permute-done((bf16[768,128]{1,0:T(8,128)(2,1)S(1)}, bf16[768,128]{1,0:T(8,128)(2,1)S(1)}, u32[]{:S(2)}, u32[]{:S(2)}) %collective-permute-start.9) | collective-permute-done | bytes 196640 | tf_op jit(solution)/shard_map/ppermute | solution.py:265
  27.4 7.2 %text_panel.1 = (f32[4,4,128,128]{3,2,1,0:T(8,128)S(1)}, f32[4,4,128,128]{3,2,1,0:T(8,128)S(1)}) custom-call(s32[2]{0:T(128)S(1)} %pad_add_fusion.me_ref, bf16[576,6144]{1,0:T(8,128)(2,1)} %a_hbm.3, bf16[576,4096]{1,0:T(8,128)(2,1)} %b_hbm.3, bf16[1536,128]{1,0:T(8,128)(2,1)S(1)} %copy-done, bf16[1536,128]{1,0:T(8,128)(2,1)S(1)} %collective-permute-done.refs_1_, ...), custom_call_target="tpu_custom_call" | custom-call | flops 1509949440 | bytes 11796480 | tf_op jit(solution)/shard_map/text_panel/pallas_call | solution.py:91
  35.8 1.5 %collective-permute-start.12 = (bf16[4,192,128]{2,1,0:T(8,128)(2,1)S(1)}, bf16[4,192,128]{2,1,0:T(8,128)(2,1)S(1)}, u32[]{:S(2)}, u32[]{:S(2)}) collective-permute-start(bf16[4,192,128]{2,1,0:T(8,128)(2,1)S(1)} %get-tuple-element.50), channel_id=1, source_target_pairs={{0,2},{1,3},{2,0},{3,1},{4,6},{5,7},{6,4},{7,5},{8,10},{9,11},{10,... | collective-permute-start | bytes 589832 | tf_op jit(solution)/shard_map/ppermute | solution.py:265
  37.3 1.5 %collective-permute-start.13 = (bf16[4,192,128]{2,1,0:T(8,128)(2,1)S(1)}, bf16[4,192,128]{2,1,0:T(8,128)(2,1)S(1)}, u32[]{:S(2)}, u32[]{:S(2)}) collective-permute-start(bf16[4,192,128]{2,1,0:T(8,128)(2,1)S(1)} %get-tuple-element.51), channel_id=1, source_target_pairs={{0,4},{1,5},{2,6},{3,7},{4,0},{5,1},{6,2},{7,3},{8,12},{9,13},{10,... | collective-permute-start | bytes 589832 | tf_op jit(solution)/shard_map/ppermute | solution.py:265
  41.0 1.3 %collective-permute-start.27 = (bf16[4,128,128]{2,1,0:T(8,128)(2,1)S(1)}, bf16[4,128,128]{2,1,0:T(8,128)(2,1)S(1)}, u32[]{:S(2)}, u32[]{:S(2)}) collective-permute-start(bf16[4,128,128]{2,1,0:T(8,128)(2,1)S(1)} %get-tuple-element.66), channel_id=1, source_target_pairs={{0,16},{8,24},{16,0},{24,8},{1,17},{9,25},{17,1},{25,9},{2,18},{10... | collective-permute-start | bytes 393224 | tf_op jit(solution)/shard_map/ppermute | solution.py:266
  42.3 1.3 %collective-permute-done.12.refs_1_ = bf16[4,192,128]{2,1,0:T(8,128)(2,1)S(1)} collective-permute-done((bf16[4,192,128]{2,1,0:T(8,128)(2,1)S(1)}, bf16[4,192,128]{2,1,0:T(8,128)(2,1)S(1)}, u32[]{:S(2)}, u32[]{:S(2)}) %collective-permute-start.12) | collective-permute-done | bytes 196640 | tf_op jit(solution)/shard_map/ppermute | solution.py:265
  44.5 3.7 %collective-permute-done.13.refs_2_ = bf16[4,192,128]{2,1,0:T(8,128)(2,1)S(1)} collective-permute-done((bf16[4,192,128]{2,1,0:T(8,128)(2,1)S(1)}, bf16[4,192,128]{2,1,0:T(8,128)(2,1)S(1)}, u32[]{:S(2)}, u32[]{:S(2)}) %collective-permute-start.13) | collective-permute-done | bytes 196640 | tf_op jit(solution)/shard_map/ppermute | solution.py:265
  48.9 1.0 %collective-permute-start.15 = (bf16[192,128]{1,0:T(8,128)(2,1)S(1)}, bf16[192,128]{1,0:T(8,128)(2,1)S(1)}, u32[]{:S(2)}, u32[]{:S(2)}) collective-permute-start(bf16[192,128]{1,0:T(8,128)(2,1)S(1)} %get-tuple-element.54), channel_id=1, source_target_pairs={{0,8},{8,0},{16,24},{24,16},{1,9},{9,1},{17,25},{25,17},{2,10},{10... | collective-permute-start | bytes 147464 | tf_op jit(solution)/shard_map/ppermute | solution.py:266
  49.9 1.3 %collective-permute-start.16 = (bf16[192,128]{1,0:T(8,128)(2,1)S(1)}, bf16[192,128]{1,0:T(8,128)(2,1)S(1)}, u32[]{:S(2)}, u32[]{:S(2)}) collective-permute-start(bf16[192,128]{1,0:T(8,128)(2,1)S(1)} %get-tuple-element.55), channel_id=1, source_target_pairs={{0,16},{8,24},{16,0},{24,8},{1,17},{9,25},{17,1},{25,9},{2,18},{10... | collective-permute-start | bytes 147464 | tf_op jit(solution)/shard_map/ppermute | solution.py:266
  51.1 2.2 %collective-permute-start.17 = (bf16[192,128]{1,0:T(8,128)(2,1)S(1)}, bf16[192,128]{1,0:T(8,128)(2,1)S(1)}, u32[]{:S(2)}, u32[]{:S(2)}) collective-permute-start(bf16[192,128]{1,0:T(8,128)(2,1)S(1)} %get-tuple-element.56), channel_id=1, source_target_pairs={{0,24},{8,16},{16,8},{24,0},{1,25},{9,17},{17,9},{25,1},{2,26},{10... | collective-permute-start | bytes 147464 | tf_op jit(solution)/shard_map/ppermute | solution.py:266
  54.6 1.6 %collective-permute-start.29 = (bf16[128,128]{1,0:T(8,128)(2,1)S(1)}, bf16[128,128]{1,0:T(8,128)(2,1)S(1)}, u32[]{:S(2)}, u32[]{:S(2)}) collective-permute-start(bf16[128,128]{1,0:T(8,128)(2,1)S(1)} %get-tuple-element.70), channel_id=1, source_target_pairs={{0,2},{1,3},{2,0},{3,1},{4,6},{5,7},{6,4},{7,5},{8,10},{9,11},{10,... | collective-permute-start | bytes 98312 | tf_op jit(solution)/shard_map/ppermute | solution.py:265
  56.1 2.6 %collective-permute-start.30 = (bf16[128,128]{1,0:T(8,128)(2,1)S(1)}, bf16[128,128]{1,0:T(8,128)(2,1)S(1)}, u32[]{:S(2)}, u32[]{:S(2)}) collective-permute-start(bf16[128,128]{1,0:T(8,128)(2,1)S(1)} %get-tuple-element.71), channel_id=1, source_target_pairs={{0,4},{1,5},{2,6},{3,7},{4,0},{5,1},{6,2},{7,3},{8,12},{9,13},{10,... | collective-permute-start | bytes 98312 | tf_op jit(solution)/shard_map/ppermute | solution.py:265
  58.8 1.5 %collective-permute-start.18 = (bf16[192,128]{1,0:T(8,128)(2,1)S(1)}, bf16[192,128]{1,0:T(8,128)(2,1)S(1)}, u32[]{:S(2)}, u32[]{:S(2)}) collective-permute-start(bf16[192,128]{1,0:T(8,128)(2,1)S(1)} %image_depth.1.refs_0_), channel_id=1, source_target_pairs={{0,2},{1,3},{2,0},{3,1},{4,6},{5,7},{6,4},{7,5},{8,10},{9,11},{10,... | collective-permute-start | bytes 147464 | tf_op jit(solution)/shard_map/ppermute | solution.py:265
  60.3 2.0 %collective-permute-start.19 = (bf16[192,128]{1,0:T(8,128)(2,1)S(1)}, bf16[192,128]{1,0:T(8,128)(2,1)S(1)}, u32[]{:S(2)}, u32[]{:S(2)}) collective-permute-start(bf16[192,128]{1,0:T(8,128)(2,1)S(1)} %image_depth.1.refs_0_), channel_id=1, source_target_pairs={{0,4},{1,5},{2,6},{3,7},{4,0},{5,1},{6,2},{7,3},{8,12},{9,13},{10,... | collective-permute-start | bytes 147464 | tf_op jit(solution)/shard_map/ppermute | solution.py:265
  62.3 1.2 %collective-permute-done.31.refs_2_ = bf16[128,128]{1,0:T(8,128)(2,1)S(1)} collective-permute-done((bf16[128,128]{1,0:T(8,128)(2,1)S(1)}, bf16[128,128]{1,0:T(8,128)(2,1)S(1)}, u32[]{:S(2)}, u32[]{:S(2)}) %collective-permute-start.31) | collective-permute-done | bytes 32800 | tf_op jit(solution)/shard_map/ppermute | solution.py:265
  63.6 3.5 %collective-permute-start.32 = (bf16[128,128]{1,0:T(8,128)(2,1)S(1)}, bf16[128,128]{1,0:T(8,128)(2,1)S(1)}, u32[]{:S(2)}, u32[]{:S(2)}) collective-permute-start(bf16[128,128]{1,0:T(8,128)(2,1)S(1)} %text_plane.1.refs_0_), channel_id=1, source_target_pairs={{0,8},{8,0},{16,24},{24,16},{1,9},{9,1},{17,25},{25,17},{2,10},{10... | collective-permute-start | bytes 98312 | tf_op jit(solution)/shard_map/ppermute | solution.py:266
  67.1 1.1 %collective-permute-start.33 = (bf16[128,128]{1,0:T(8,128)(2,1)S(1)}, bf16[128,128]{1,0:T(8,128)(2,1)S(1)}, u32[]{:S(2)}, u32[]{:S(2)}) collective-permute-start(bf16[128,128]{1,0:T(8,128)(2,1)S(1)} %text_plane.1.refs_0_), channel_id=1, source_target_pairs={{0,16},{8,24},{16,0},{24,8},{1,17},{9,25},{17,1},{25,9},{2,18},{10... | collective-permute-start | bytes 98312 | tf_op jit(solution)/shard_map/ppermute | solution.py:266
  70.0 2.2 %collective-permute-done.33.refs_2_ = bf16[128,128]{1,0:T(8,128)(2,1)S(1)} collective-permute-done((bf16[128,128]{1,0:T(8,128)(2,1)S(1)}, bf16[128,128]{1,0:T(8,128)(2,1)S(1)}, u32[]{:S(2)}, u32[]{:S(2)}) %collective-permute-start.33) | collective-permute-done | bytes 32800 | tf_op jit(solution)/shard_map/ppermute | solution.py:266
  72.2 2.2 %collective-permute-start.34 = (bf16[128,128]{1,0:T(8,128)(2,1)S(1)}, bf16[128,128]{1,0:T(8,128)(2,1)S(1)}, u32[]{:S(2)}, u32[]{:S(2)}) collective-permute-start(bf16[128,128]{1,0:T(8,128)(2,1)S(1)} %text_plane.1.refs_0_), channel_id=1, source_target_pairs={{0,24},{8,16},{16,8},{24,0},{1,25},{9,17},{17,9},{25,1},{2,26},{10... | collective-permute-start | bytes 98312 | tf_op jit(solution)/shard_map/ppermute | solution.py:266
  74.4 3.5 %collective-permute-done.34.refs_3_ = bf16[128,128]{1,0:T(8,128)(2,1)S(1)} collective-permute-done((bf16[128,128]{1,0:T(8,128)(2,1)S(1)}, bf16[128,128]{1,0:T(8,128)(2,1)S(1)}, u32[]{:S(2)}, u32[]{:S(2)}) %collective-permute-start.34) | collective-permute-done | bytes 32800 | tf_op jit(solution)/shard_map/ppermute | solution.py:266
  79.8 2.8 %collective-permute-start.36 = (f32[128,128]{1,0:T(8,128)S(1)}, f32[128,128]{1,0:T(8,128)S(1)}, u32[]{:S(2)}, u32[]{:S(2)}) collective-permute-start(f32[128,128]{1,0:T(8,128)S(1)} %get-tuple-element.74.refs_0_), channel_id=1, source_target_pairs={{0,16},{8,24},{16,0},{24,8},{1,17},{9,25},{17,1},{25,9},{2,18},{10... | collective-permute-start | bytes 196616 | tf_op jit(solution)/shard_map/ppermute | solution.py:266
  82.6 1.6 %collective-permute-start.37 = (f32[128,128]{1,0:T(8,128)S(1)}, f32[128,128]{1,0:T(8,128)S(1)}, u32[]{:S(2)}, u32[]{:S(2)}) collective-permute-start(f32[128,128]{1,0:T(8,128)S(1)} %get-tuple-element.74.refs_0_), channel_id=1, source_target_pairs={{0,24},{8,16},{16,8},{24,0},{1,25},{9,17},{17,9},{25,1},{2,26},{10... | collective-permute-start | bytes 196616 | tf_op jit(solution)/shard_map/ppermute | solution.py:266
  84.9 1.6 %collective-permute-start.40 = (f32[128,128]{1,0:T(8,128)S(1)}, f32[128,128]{1,0:T(8,128)S(1)}, u32[]{:S(2)}, u32[]{:S(2)}) collective-permute-start(f32[128,128]{1,0:T(8,128)S(1)} %text_gram_cores.1.refs_4_), channel_id=1, source_target_pairs={{0,4},{1,5},{2,6},{3,7},{4,0},{5,1},{6,2},{7,3},{8,12},{9,13},{10,... | collective-permute-start | bytes 196616 | tf_op jit(solution)/shard_map/ppermute | solution.py:265
  86.5 1.3 %collective-permute-start.41 = (f32[128,128]{1,0:T(8,128)S(1)}, f32[128,128]{1,0:T(8,128)S(1)}, u32[]{:S(2)}, u32[]{:S(2)}) collective-permute-start(f32[128,128]{1,0:T(8,128)S(1)} %text_gram_cores.1.refs_4_), channel_id=1, source_target_pairs={{0,6},{1,7},{2,4},{3,5},{4,2},{5,3},{6,0},{7,1},{8,14},{9,15},{10,... | collective-permute-start | bytes 196616 | tf_op jit(solution)/shard_map/ppermute | solution.py:265
  89.9 1.8 %collective-permute-done.41.refs_7_ = f32[128,128]{1,0:T(8,128)S(1)} collective-permute-done((f32[128,128]{1,0:T(8,128)S(1)}, f32[128,128]{1,0:T(8,128)S(1)}, u32[]{:S(2)}, u32[]{:S(2)}) %collective-permute-start.41) | collective-permute-done | bytes 65568 | tf_op jit(solution)/shard_map/ppermute | solution.py:265
  91.6 7.6 %finish.1 = (f32[1536,128]{1,0:T(8,128)}, f32[512,128]{1,0:T(8,128)}) custom-call(bf16[8,192,128]{2,1,0:T(8,128)(2,1)S(1)} %get-tuple-element.57.ipanel, bf16[4,128,128]{2,1,0:T(8,128)(2,1)S(1)} %get-tuple-element.73.tpanel, f32[128,128]{1,0:T(8,128)S(1)} %get-tuple-element.74.refs_0_, f32[128,128]{1,0:T(8,128)S(1)} %collective-permute-done.35.refs_1_, ...), custom_call_target="tpu_custom_call" | custom-call | flops 10000000000 | bytes 1179648 | tf_op jit(solution)/shard_map/finish/pallas_call | solution.py:251
  (70 shorter events, 16.9 us)
Async XLA Ops:
  0.6 13.6 %collective-permute-start = (bf16[1536,128]{1,0:T(8,128)(2,1)}, bf16[1536,128]{1,0:T(8,128)(2,1)S(1)}, u32[]{:S(2)}, u32[]{:S(2)}) collective-permute-start(bf16[1536,128]{1,0:T(8,128)(2,1)} %refs_0_.3), channel_id=1, source_target_pairs={{0,8},{1,17},{2,10},{3,19},{4,12},{5,21},{6,14},{7,23},{8,0},{9,25... | collective-permute-start | bytes 1179656 | tf_op jit(solution)/shard_map/ppermute | solution.py:284
  3.7 7.4 %collective-permute-start.3 = (bf16[512,128]{1,0:T(8,128)(2,1)}, bf16[512,128]{1,0:T(8,128)(2,1)S(1)}, u32[]{:S(2)}, u32[]{:S(2)}) collective-permute-start(bf16[512,128]{1,0:T(8,128)(2,1)} %refs_0_.2), channel_id=1, source_target_pairs={{0,6},{1,7},{2,4},{3,5},{4,2},{5,3},{6,0},{7,1},{8,14},{9,15},{10,... | collective-permute-start | bytes 393224 | tf_op jit(solution)/shard_map/ppermute | solution.py:265
  6.2 7.5 %collective-permute-start.1 = (bf16[512,128]{1,0:T(8,128)(2,1)}, bf16[512,128]{1,0:T(8,128)(2,1)S(1)}, u32[]{:S(2)}, u32[]{:S(2)}) collective-permute-start(bf16[512,128]{1,0:T(8,128)(2,1)} %refs_0_.2), channel_id=1, source_target_pairs={{0,2},{1,3},{2,0},{3,1},{4,6},{5,7},{6,4},{7,5},{8,10},{9,11},{10,... | collective-permute-start | bytes 393224 | tf_op jit(solution)/shard_map/ppermute | solution.py:265
  6.7 7.0 %collective-permute-start.2 = (bf16[512,128]{1,0:T(8,128)(2,1)}, bf16[512,128]{1,0:T(8,128)(2,1)S(1)}, u32[]{:S(2)}, u32[]{:S(2)}) collective-permute-start(bf16[512,128]{1,0:T(8,128)(2,1)} %refs_0_.2), channel_id=1, source_target_pairs={{0,4},{1,5},{2,6},{3,7},{4,0},{5,1},{6,2},{7,3},{8,12},{9,13},{10,... | collective-permute-start | bytes 393224 | tf_op jit(solution)/shard_map/ppermute | solution.py:265
  7.2 10.7 %collective-permute-start.4 = (bf16[512,128]{1,0:T(8,128)(2,1)}, bf16[512,128]{1,0:T(8,128)(2,1)S(1)}, u32[]{:S(2)}, u32[]{:S(2)}) collective-permute-start(bf16[512,128]{1,0:T(8,128)(2,1)} %refs_0_.2), channel_id=1, source_target_pairs={{0,1},{1,0},{2,3},{3,2},{4,5},{5,4},{6,7},{7,6},{8,9},{9,8},{10,11... | collective-permute-start | bytes 393224 | tf_op jit(solution)/shard_map/ppermute | solution.py:265
  14.2 11.0 %collective-permute-start.8 = (bf16[768,128]{1,0:T(8,128)(2,1)S(1)}, bf16[768,128]{1,0:T(8,128)(2,1)S(1)}, u32[]{:S(2)}, u32[]{:S(2)}) collective-permute-start(bf16[768,128]{1,0:T(8,128)(2,1)S(1)} %constant_dynamic-slice_fusion), channel_id=1, source_target_pairs={{0,24},{8,16},{16,8},{24,0},{1,25},{9,17},{17,9},{25,1},{2,26},{10... | collective-permute-start | bytes 589832 | tf_op jit(solution)/shard_map/ppermute | solution.py:266
  27.3 7.8 %collective-permute-start.11 = (f32[4,4,192,128]{3,2,1,0:T(8,128)S(1)}, f32[4,4,192,128]{3,2,1,0:T(8,128)S(1)}, u32[]{:S(2)}, u32[]{:S(2)}) collective-permute-start(f32[4,4,192,128]{3,2,1,0:T(8,128)S(1)} %get-tuple-element.48), channel_id=1, source_target_pairs={{0,1},{1,0},{2,3},{3,2},{4,5},{5,4},{6,7},{7,6},{8,9},{9,8},{10,11... | collective-permute-start | bytes 4718600 | tf_op jit(solution)/shard_map/ppermute | solution.py:265
  35.8 7.8 %collective-permute-start.12 = (bf16[4,192,128]{2,1,0:T(8,128)(2,1)S(1)}, bf16[4,192,128]{2,1,0:T(8,128)(2,1)S(1)}, u32[]{:S(2)}, u32[]{:S(2)}) collective-permute-start(bf16[4,192,128]{2,1,0:T(8,128)(2,1)S(1)} %get-tuple-element.50), channel_id=1, source_target_pairs={{0,2},{1,3},{2,0},{3,1},{4,6},{5,7},{6,4},{7,5},{8,10},{9,11},{10,... | collective-permute-start | bytes 589832 | tf_op jit(solution)/shard_map/ppermute | solution.py:265
  37.3 10.9 %collective-permute-start.13 = (bf16[4,192,128]{2,1,0:T(8,128)(2,1)S(1)}, bf16[4,192,128]{2,1,0:T(8,128)(2,1)S(1)}, u32[]{:S(2)}, u32[]{:S(2)}) collective-permute-start(bf16[4,192,128]{2,1,0:T(8,128)(2,1)S(1)} %get-tuple-element.51), channel_id=1, source_target_pairs={{0,4},{1,5},{2,6},{3,7},{4,0},{5,1},{6,2},{7,3},{8,12},{9,13},{10,... | collective-permute-start | bytes 589832 | tf_op jit(solution)/shard_map/ppermute | solution.py:265
  38.9 9.4 %collective-permute-start.14 = (bf16[4,192,128]{2,1,0:T(8,128)(2,1)S(1)}, bf16[4,192,128]{2,1,0:T(8,128)(2,1)S(1)}, u32[]{:S(2)}, u32[]{:S(2)}) collective-permute-start(bf16[4,192,128]{2,1,0:T(8,128)(2,1)S(1)} %get-tuple-element.52), channel_id=1, source_target_pairs={{0,6},{1,7},{2,4},{3,5},{4,2},{5,3},{6,0},{7,1},{8,14},{9,15},{10,... | collective-permute-start | bytes 589832 | tf_op jit(solution)/shard_map/ppermute | solution.py:265
  40.0 11.1 %collective-permute-start.26 = (bf16[4,128,128]{2,1,0:T(8,128)(2,1)S(1)}, bf16[4,128,128]{2,1,0:T(8,128)(2,1)S(1)}, u32[]{:S(2)}, u32[]{:S(2)}) collective-permute-start(bf16[4,128,128]{2,1,0:T(8,128)(2,1)S(1)} %get-tuple-element.65), channel_id=1, source_target_pairs={{0,8},{8,0},{16,24},{24,16},{1,9},{9,1},{17,25},{25,17},{2,10},{10... | collective-permute-start | bytes 393224 | tf_op jit(solution)/shard_map/ppermute | solution.py:266
  41.0 13.0 %collective-permute-start.27 = (bf16[4,128,128]{2,1,0:T(8,128)(2,1)S(1)}, bf16[4,128,128]{2,1,0:T(8,128)(2,1)S(1)}, u32[]{:S(2)}, u32[]{:S(2)}) collective-permute-start(bf16[4,128,128]{2,1,0:T(8,128)(2,1)S(1)} %get-tuple-element.66), channel_id=1, source_target_pairs={{0,16},{8,24},{16,0},{24,8},{1,17},{9,25},{17,1},{25,9},{2,18},{10... | collective-permute-start | bytes 393224 | tf_op jit(solution)/shard_map/ppermute | solution.py:266
  43.6 10.4 %collective-permute-start.28 = (bf16[4,128,128]{2,1,0:T(8,128)(2,1)S(1)}, bf16[4,128,128]{2,1,0:T(8,128)(2,1)S(1)}, u32[]{:S(2)}, u32[]{:S(2)}) collective-permute-start(bf16[4,128,128]{2,1,0:T(8,128)(2,1)S(1)} %get-tuple-element.67), channel_id=1, source_target_pairs={{0,24},{8,16},{16,8},{24,0},{1,25},{9,17},{17,9},{25,1},{2,26},{10... | collective-permute-start | bytes 393224 | tf_op jit(solution)/shard_map/ppermute | solution.py:266
  48.9 9.9 %collective-permute-start.15 = (bf16[192,128]{1,0:T(8,128)(2,1)S(1)}, bf16[192,128]{1,0:T(8,128)(2,1)S(1)}, u32[]{:S(2)}, u32[]{:S(2)}) collective-permute-start(bf16[192,128]{1,0:T(8,128)(2,1)S(1)} %get-tuple-element.54), channel_id=1, source_target_pairs={{0,8},{8,0},{16,24},{24,16},{1,9},{9,1},{17,25},{25,17},{2,10},{10... | collective-permute-start | bytes 147464 | tf_op jit(solution)/shard_map/ppermute | solution.py:266
  49.9 8.9 %collective-permute-start.16 = (bf16[192,128]{1,0:T(8,128)(2,1)S(1)}, bf16[192,128]{1,0:T(8,128)(2,1)S(1)}, u32[]{:S(2)}, u32[]{:S(2)}) collective-permute-start(bf16[192,128]{1,0:T(8,128)(2,1)S(1)} %get-tuple-element.55), channel_id=1, source_target_pairs={{0,16},{8,24},{16,0},{24,8},{1,17},{9,25},{17,1},{25,9},{2,18},{10... | collective-permute-start | bytes 147464 | tf_op jit(solution)/shard_map/ppermute | solution.py:266
  51.1 7.6 %collective-permute-start.17 = (bf16[192,128]{1,0:T(8,128)(2,1)S(1)}, bf16[192,128]{1,0:T(8,128)(2,1)S(1)}, u32[]{:S(2)}, u32[]{:S(2)}) collective-permute-start(bf16[192,128]{1,0:T(8,128)(2,1)S(1)} %get-tuple-element.56), channel_id=1, source_target_pairs={{0,24},{8,16},{16,8},{24,0},{1,25},{9,17},{17,9},{25,1},{2,26},{10... | collective-permute-start | bytes 147464 | tf_op jit(solution)/shard_map/ppermute | solution.py:266
  54.6 7.7 %collective-permute-start.29 = (bf16[128,128]{1,0:T(8,128)(2,1)S(1)}, bf16[128,128]{1,0:T(8,128)(2,1)S(1)}, u32[]{:S(2)}, u32[]{:S(2)}) collective-permute-start(bf16[128,128]{1,0:T(8,128)(2,1)S(1)} %get-tuple-element.70), channel_id=1, source_target_pairs={{0,2},{1,3},{2,0},{3,1},{4,6},{5,7},{6,4},{7,5},{8,10},{9,11},{10,... | collective-permute-start | bytes 98312 | tf_op jit(solution)/shard_map/ppermute | solution.py:265
  56.1 6.2 %collective-permute-start.30 = (bf16[128,128]{1,0:T(8,128)(2,1)S(1)}, bf16[128,128]{1,0:T(8,128)(2,1)S(1)}, u32[]{:S(2)}, u32[]{:S(2)}) collective-permute-start(bf16[128,128]{1,0:T(8,128)(2,1)S(1)} %get-tuple-element.71), channel_id=1, source_target_pairs={{0,4},{1,5},{2,6},{3,7},{4,0},{5,1},{6,2},{7,3},{8,12},{9,13},{10,... | collective-permute-start | bytes 98312 | tf_op jit(solution)/shard_map/ppermute | solution.py:265
  58.8 10.2 %collective-permute-start.18 = (bf16[192,128]{1,0:T(8,128)(2,1)S(1)}, bf16[192,128]{1,0:T(8,128)(2,1)S(1)}, u32[]{:S(2)}, u32[]{:S(2)}) collective-permute-start(bf16[192,128]{1,0:T(8,128)(2,1)S(1)} %image_depth.1.refs_0_), channel_id=1, source_target_pairs={{0,2},{1,3},{2,0},{3,1},{4,6},{5,7},{6,4},{7,5},{8,10},{9,11},{10,... | collective-permute-start | bytes 147464 | tf_op jit(solution)/shard_map/ppermute | solution.py:265
  60.3 9.2 %collective-permute-start.19 = (bf16[192,128]{1,0:T(8,128)(2,1)S(1)}, bf16[192,128]{1,0:T(8,128)(2,1)S(1)}, u32[]{:S(2)}, u32[]{:S(2)}) collective-permute-start(bf16[192,128]{1,0:T(8,128)(2,1)S(1)} %image_depth.1.refs_0_), channel_id=1, source_target_pairs={{0,4},{1,5},{2,6},{3,7},{4,0},{5,1},{6,2},{7,3},{8,12},{9,13},{10,... | collective-permute-start | bytes 147464 | tf_op jit(solution)/shard_map/ppermute | solution.py:265
  62.3 7.2 %collective-permute-start.20 = (bf16[192,128]{1,0:T(8,128)(2,1)S(1)}, bf16[192,128]{1,0:T(8,128)(2,1)S(1)}, u32[]{:S(2)}, u32[]{:S(2)}) collective-permute-start(bf16[192,128]{1,0:T(8,128)(2,1)S(1)} %image_depth.1.refs_0_), channel_id=1, source_target_pairs={{0,6},{1,7},{2,4},{3,5},{4,2},{5,3},{6,0},{7,1},{8,14},{9,15},{10,... | collective-permute-start | bytes 147464 | tf_op jit(solution)/shard_map/ppermute | solution.py:265
  63.6 5.4 %collective-permute-start.32 = (bf16[128,128]{1,0:T(8,128)(2,1)S(1)}, bf16[128,128]{1,0:T(8,128)(2,1)S(1)}, u32[]{:S(2)}, u32[]{:S(2)}) collective-permute-start(bf16[128,128]{1,0:T(8,128)(2,1)S(1)} %text_plane.1.refs_0_), channel_id=1, source_target_pairs={{0,8},{8,0},{16,24},{24,16},{1,9},{9,1},{17,25},{25,17},{2,10},{10... | collective-permute-start | bytes 98312 | tf_op jit(solution)/shard_map/ppermute | solution.py:266
  69.0 9.8 %collective-permute-start.21 = (bf16[192,128]{1,0:T(8,128)(2,1)S(1)}, bf16[192,128]{1,0:T(8,128)(2,1)S(1)}, u32[]{:S(2)}, u32[]{:S(2)}) collective-permute-start(bf16[192,128]{1,0:T(8,128)(2,1)S(1)} %image_depth.1.refs_0_), channel_id=1, source_target_pairs={{0,1},{1,0},{2,3},{3,2},{4,5},{5,4},{6,7},{7,6},{8,9},{9,8},{10,11... | collective-permute-start | bytes 147464 | tf_op jit(solution)/shard_map/ppermute | solution.py:265
  69.0 9.8 %collective-permute-start.22 = (bf16[192,128]{1,0:T(8,128)(2,1)S(1)}, bf16[192,128]{1,0:T(8,128)(2,1)S(1)}, u32[]{:S(2)}, u32[]{:S(2)}) collective-permute-start(bf16[192,128]{1,0:T(8,128)(2,1)S(1)} %collective-permute-done.18.refs_1_), channel_id=1, source_target_pairs={{0,1},{1,0},{2,3},{3,2},{4,5},{5,4},{6,7},{7,6},{8,9},{9,8},{10,11... | collective-permute-start | bytes 147464 | tf_op jit(solution)/shard_map/ppermute | solution.py:265
  69.5 9.3 %collective-permute-start.23 = (bf16[192,128]{1,0:T(8,128)(2,1)S(1)}, bf16[192,128]{1,0:T(8,128)(2,1)S(1)}, u32[]{:S(2)}, u32[]{:S(2)}) collective-permute-start(bf16[192,128]{1,0:T(8,128)(2,1)S(1)} %collective-permute-done.19.refs_2_), channel_id=1, source_target_pairs={{0,1},{1,0},{2,3},{3,2},{4,5},{5,4},{6,7},{7,6},{8,9},{9,8},{10,11... | collective-permute-start | bytes 147464 | tf_op jit(solution)/shard_map/ppermute | solution.py:265
  69.5 9.3 %collective-permute-start.24 = (bf16[192,128]{1,0:T(8,128)(2,1)S(1)}, bf16[192,128]{1,0:T(8,128)(2,1)S(1)}, u32[]{:S(2)}, u32[]{:S(2)}) collective-permute-start(bf16[192,128]{1,0:T(8,128)(2,1)S(1)} %collective-permute-done.20.refs_3_), channel_id=1, source_target_pairs={{0,1},{1,0},{2,3},{3,2},{4,5},{5,4},{6,7},{7,6},{8,9},{9,8},{10,11... | collective-permute-start | bytes 147464 | tf_op jit(solution)/shard_map/ppermute | solution.py:265
  72.2 5.7 %collective-permute-start.34 = (bf16[128,128]{1,0:T(8,128)(2,1)S(1)}, bf16[128,128]{1,0:T(8,128)(2,1)S(1)}, u32[]{:S(2)}, u32[]{:S(2)}) collective-permute-start(bf16[128,128]{1,0:T(8,128)(2,1)S(1)} %text_plane.1.refs_0_), channel_id=1, source_target_pairs={{0,24},{8,16},{16,8},{24,0},{1,25},{9,17},{17,9},{25,1},{2,26},{10... | collective-permute-start | bytes 98312 | tf_op jit(solution)/shard_map/ppermute | solution.py:266
  78.7 5.5 %collective-permute-start.38 = (f32[128,128]{1,0:T(8,128)S(1)}, f32[128,128]{1,0:T(8,128)S(1)}, u32[]{:S(2)}, u32[]{:S(2)}) collective-permute-start(f32[128,128]{1,0:T(8,128)S(1)} %get-tuple-element.75.own_ref), channel_id=1, source_target_pairs={{0,1},{1,0},{2,3},{3,2},{4,5},{5,4},{6,7},{7,6},{8,9},{9,8},{10,11... | collective-permute-start | bytes 196616 | tf_op jit(solution)/shard_map/ppermute | solution.py:265
  79.7 6.8 %collective-permute-start.35 = (f32[128,128]{1,0:T(8,128)S(1)}, f32[128,128]{1,0:T(8,128)S(1)}, u32[]{:S(2)}, u32[]{:S(2)}) collective-permute-start(f32[128,128]{1,0:T(8,128)S(1)} %get-tuple-element.74.refs_0_), channel_id=1, source_target_pairs={{0,8},{8,0},{16,24},{24,16},{1,9},{9,1},{17,25},{25,17},{2,10},{10... | collective-permute-start | bytes 196616 | tf_op jit(solution)/shard_map/ppermute | solution.py:266
  79.8 8.0 %collective-permute-start.36 = (f32[128,128]{1,0:T(8,128)S(1)}, f32[128,128]{1,0:T(8,128)S(1)}, u32[]{:S(2)}, u32[]{:S(2)}) collective-permute-start(f32[128,128]{1,0:T(8,128)S(1)} %get-tuple-element.74.refs_0_), channel_id=1, source_target_pairs={{0,16},{8,24},{16,0},{24,8},{1,17},{9,25},{17,1},{25,9},{2,18},{10... | collective-permute-start | bytes 196616 | tf_op jit(solution)/shard_map/ppermute | solution.py:266
  82.6 6.1 %collective-permute-start.37 = (f32[128,128]{1,0:T(8,128)S(1)}, f32[128,128]{1,0:T(8,128)S(1)}, u32[]{:S(2)}, u32[]{:S(2)}) collective-permute-start(f32[128,128]{1,0:T(8,128)S(1)} %get-tuple-element.74.refs_0_), channel_id=1, source_target_pairs={{0,24},{8,16},{16,8},{24,0},{1,25},{9,17},{17,9},{25,1},{2,26},{10... | collective-permute-start | bytes 196616 | tf_op jit(solution)/shard_map/ppermute | solution.py:266
  86.5 5.2 %collective-permute-start.41 = (f32[128,128]{1,0:T(8,128)S(1)}, f32[128,128]{1,0:T(8,128)S(1)}, u32[]{:S(2)}, u32[]{:S(2)}) collective-permute-start(f32[128,128]{1,0:T(8,128)S(1)} %text_gram_cores.1.refs_4_), channel_id=1, source_target_pairs={{0,6},{1,7},{2,4},{3,5},{4,2},{5,3},{6,0},{7,1},{8,14},{9,15},{10,... | collective-permute-start | bytes 196616 | tf_op jit(solution)/shard_map/ppermute | solution.py:265
  (12 other events, 51.1 us)

commit v10 on v9

--- a/solution.py
+++ b/solution.py
@@ -184,6 +184,34 @@
         cost_estimate=cost(2 * n * rows * rank * rank, 4 * n * rows * rank),
         name=name,
     )(me, *parts)
+
+
+def tree_sum(values):
+    while len(values) > 1:
+        values = [x + y for x, y in zip(values[::2], values[1::2])]
+    return values[0]
+
+
+def text_gram_kernel(*refs):
+    *parts, panel_ref, gram_ref = refs
+    panel = tree_sum([part[...].astype(F32) for part in parts]).astype(BF16)
+    panel_ref[0] = panel
+    gram_ref[...] = lax.dot_general(
+        panel, panel, (((0,), (0,)), ((), ())), preferred_element_type=F32
+    )
+
+
+def text_gram_call(parts):
+    rows, rank = parts[0].shape
+    return pl.pallas_call(
+        text_gram_kernel,
+        in_specs=[VMEM] * len(parts),
+        out_specs=[VMEM, VMEM],
+        out_shape=[sds((1, rows, rank), BF16), sds((rank, rank), F32)],
+        compiler_params=params(),
+        cost_estimate=cost(2 * rows * rank * rank, 4 * rows * rank),
+        name="text_gram",
+    )(*parts)
 
 
 def inverse_factor(gram):
@@ -227,8 +255,8 @@
 
     def total(refs):
         value = refs[0][...]
-        for ref in refs[1:]:
-            value = value + ref[...]
+        for even, odd in zip(refs[1::2], refs[2::2]):
+            value = value + (even[...] + odd[...])
         return value
 
     inverses = None
@@ -280,10 +308,16 @@
         pairs = []
         for r in range(n_row):
             for c in range(n_col):
-                pairs.append((r * n_col + c, (r ^ (odd if c % 2 else even)) * n_col + c))
+                shift = odd if c % 2 else even
+                if shift is not None:
+                    pairs.append((r * n_col + c, (r ^ shift[0]) * n_col + (c ^ shift[1])))
         return lax.ppermute(x, ("row", "col"), pairs)
 
-    fetched = [(t, t + 1, split_swap(probe_image, t, t + 1)) for t in depths[:-1:2]]
+    def shared_sums(x, shifts):
+        got = [split_swap(x, *pair) for pair in zip(shifts[::2], shifts[1::2] + [None])]
+        return [term for block in got for term in (block, col_swap(block, 1))]
+
+    fetched = [(t, t + 1, split_swap(probe_image, (t, 0), (t + 1, 0))) for t in depths[:-1:2]]
     half = probe_image.shape[0] // 2
     mine = lax.dynamic_slice_in_dim(probe_image, me[0] % 2 * half, half, 0)
     received = over_chips([probe_text] * len(chips))
@@ -311,25 +345,20 @@
     own, *sends = sums_call("row", 0, depths, me, [own] + over_chips(image_sends), "image_plane")
     after_plane = sends[0]
     mine = last_call(own, over_depth(sends), BF16, "image_depth")
-    after_depth = mine
     parts = over_plane(mine)
     ipanel, gram = gram_call("col", list(parts), me, list(parts.values()), "image_gram")
-    igrams = [gram] + over_depth([gram] * len(depths))
-
-    columns = image_rows(image_order, probe_image.shape[0])
-    keep, send = panel_call(
-        me, image_feats, text_feats, image_parts, columns, groups, n_row, "text_panel"
-    )
+    igrams = [gram] + shared_sums(gram, [(t, 0) for t in depths])
+
+    rows = image_rows(image_order, probe_image.shape[0])
+    keep, send = panel_call(me, image_feats, text_feats, image_parts, rows, groups, 1, "text_panel")
     swapped, _ = lax.optimization_barrier((col_swap(send, 1), image_sends[0]))
-    own, *sends = sums_call("row", 1, depths, me, [keep, swapped], "text_cores")
+    own, *sends = sums_call("col", 0, chips, me, [keep, swapped], "text_cores")
+    own, sends = own[0], [x[0] for x in sends]
     own, _ = lax.optimization_barrier((own, after_plane))
-    own, *sends = sums_call("col", 0, chips, me, [own] + over_depth(sends), "text_depth")
-    own, _ = lax.optimization_barrier((own, after_depth))
     mine = last_call(own, over_chips(sends), BF16, "text_plane")
-    parts = [mine] + over_depth([mine] * len(depths))
-    tpanel, gram = gram_call("row", [0] + depths, me, parts, "text_gram")
+    tpanel, gram = text_gram_call([mine] + over_depth([mine] * len(depths)))
     gram = last_call(gram, [col_swap(gram, 1)], F32, "text_gram_cores")
-    tgrams = [gram] + over_chips([gram] * len(chips))
+    tgrams = [gram] + shared_sums(gram, [(0, 2 * s) for s in chips])
 
     widths = (image_feats.shape[1], text_feats.shape[1])
     return finish_call(widths, ipanel, igrams, tpanel, tgrams)

time: 99.4 us -> 104 us (1.046)
  waiting for transfers between devices: 24.3 us -> 33 us
  starting transfers between devices: 46.7 us -> 43.6 us
  Pallas kernels: 25.4 us -> 24.3 us
    ppermute x13 -> x7, starting transfers between devices: 22.6 us -> 11.3 us  [per_device(): lax.ppermute(x, 'row', [(i, i ^ s) for i in range(n_row)])]
    ppermute x1 -> x5, starting transfers between devices: 3.09 us -> 13.1 us  [split_swap(): return lax.ppermute(x, ('row', 'col'), pairs)]
    ppermute x28 -> x29, waiting for transfers between devices: 16.2 us -> 19.7 us  [per_device(): lax.ppermute(x, 'col', [(i, i ^ s) for i in range(n_col)])]
    ppermute x13 -> x7, waiting for transfers between devices: 8.05 us -> 11.4 us  [per_device(): lax.ppermute(x, 'row', [(i, i ^ s) for i in range(n_row)])]
    ppermute x28 -> x29, starting transfers between devices: 21 us -> 19.1 us  [per_device(): lax.ppermute(x, 'col', [(i, i ^ s) for i in range(n_col)])]
    ppermute x1 -> x5, waiting for transfers between devices: 0.01 us -> 1.84 us  [split_swap(): return lax.ppermute(x, ('row', 'col'), pairs)]
    pallas_call x4 -> x3, Pallas kernels: 2.57 us -> 1.97 us  [sums_call(): pl.pallas_call(functools.partial(sums_kernel, which, axis, shifts, len(te...]
  transfers between devices with their start and end apart: 42 -> 41, of which waited for: 14 -> 14; matrix products, arithmetic and copies ran while one was open for 1% -> 1% of each run, Pallas kernels for 18% -> 16%
where the time goes in v10:
time: 104 us
  starting transfers between devices  43.6 us (42%)
  waiting for transfers between devices  33 us (32%)
  Pallas kernels  24.3 us (23%)
  local copies, waits for them, and re-layouts  1.89 us (2%)
    ppermute x29, waiting for transfers between devices, per_device(): lax.ppermute(x, 'col', [(i, i ^ s) for i in range(n_col)])  19.7 us
    ppermute x29, starting transfers between devices, per_device(): lax.ppermute(x, 'col', [(i, i ^ s) for i in range(n_col)])  19.1 us
    pallas_call x2, Pallas kernels, panel_call(): pl.pallas_call(functools.partial(panel_kernel, rows, len(parts), n_in, bl...  13.5 us
    ppermute x5, starting transfers between devices, split_swap(): return lax.ppermute(x, ('row', 'col'), pairs)  13.1 us
    ppermute x7, waiting for transfers between devices, per_device(): lax.ppermute(x, 'row', [(i, i ^ s) for i in range(n_row)])  11.4 us
    ppermute x7, starting transfers between devices, per_device(): lax.ppermute(x, 'row', [(i, i ^ s) for i in range(n_row)])  11.3 us
    pallas_call x1, Pallas kernels, finish_call(): pl.pallas_call(functools.partial(finish_kernel, widths, len(igrams)), in_...  7.58 us
  transfers between devices with their start and end apart: 41, of which 14 were waited for; matrix products, arithmetic and copies ran while one was open for 1% of the time, Pallas kernels for 16%

profile of v10, /device:TPU:0, one launch (start us, length us, event | category | flops | bytes accessed | tf_op | source)
XLA Modules:
  0.0 103.6 jit_solution(6268161321339900329)
XLA Ops:
  0.6 3.1 %collective-permute-start = (bf16[1536,128]{1,0:T(8,128)(2,1)}, bf16[1536,128]{1,0:T(8,128)(2,1)S(1)}, u32[]{:S(2)}, u32[]{:S(2)}) collective-permute-start(bf16[1536,128]{1,0:T(8,128)(2,1)} %refs_0_.3), channel_id=1, source_target_pairs={{0,8},{1,17},{2,10},{3,19},{4,12},{5,21},{6,14},{7,23},{8,0},{9,25... | collective-permute-start | bytes 1179656 | tf_op jit(solution)/shard_map/ppermute | solution.py:314
  3.7 2.4 %collective-permute-start.3 = (bf16[512,128]{1,0:T(8,128)(2,1)}, bf16[512,128]{1,0:T(8,128)(2,1)S(1)}, u32[]{:S(2)}, u32[]{:S(2)}) collective-permute-start(bf16[512,128]{1,0:T(8,128)(2,1)} %refs_0_.2), channel_id=1, source_target_pairs={{0,6},{1,7},{2,4},{3,5},{4,2},{5,3},{6,0},{7,1},{8,14},{9,15},{10,... | collective-permute-start | bytes 393224 | tf_op jit(solution)/shard_map/ppermute | solution.py:293
  8.2 3.0 %collective-permute-done.3.refs_3_ = bf16[512,128]{1,0:T(8,128)(2,1)S(1)} collective-permute-done((bf16[512,128]{1,0:T(8,128)(2,1)}, bf16[512,128]{1,0:T(8,128)(2,1)S(1)}, u32[]{:S(2)}, u32[]{:S(2)}) %collective-permute-start.3) | collective-permute-done | bytes 131104 | tf_op jit(solution)/shard_map/ppermute | solution.py:293
  11.1 2.6 %collective-permute-done.1.refs_1_ = bf16[512,128]{1,0:T(8,128)(2,1)S(1)} collective-permute-done((bf16[512,128]{1,0:T(8,128)(2,1)}, bf16[512,128]{1,0:T(8,128)(2,1)S(1)}, u32[]{:S(2)}, u32[]{:S(2)}) %collective-permute-start.1) | collective-permute-done | bytes 131104 | tf_op jit(solution)/shard_map/ppermute | solution.py:293
  14.2 3.6 %collective-permute-start.8 = (bf16[768,128]{1,0:T(8,128)(2,1)S(1)}, bf16[768,128]{1,0:T(8,128)(2,1)S(1)}, u32[]{:S(2)}, u32[]{:S(2)}) collective-permute-start(bf16[768,128]{1,0:T(8,128)(2,1)S(1)} %constant_dynamic-slice_fusion), channel_id=1, source_target_pairs={{0,24},{8,16},{16,8},{24,0},{1,25},{9,17},{17,9},{25,1},{2,26},{10... | collective-permute-start | bytes 589832 | tf_op jit(solution)/shard_map/ppermute | solution.py:294
  18.9 6.3 %image_panel.1 = (f32[4,4,192,128]{3,2,1,0:T(8,128)S(1)}, f32[4,4,192,128]{3,2,1,0:T(8,128)S(1)}) custom-call(s32[2]{0:T(128)S(1)} %pad_add_fusion.me_ref, bf16[576,4096]{1,0:T(8,128)(2,1)} %b_hbm.3, bf16[576,6144]{1,0:T(8,128)(2,1)} %a_hbm.3, bf16[512,128]{1,0:T(8,128)(2,1)S(1)} %copy-done.1, bf16[512,128]{1,0:T(8,128)(2,1)S(1)} %collective-permute-done.1.refs_1_, ...), custom_call_target="tpu_custom_call" | custom-call | flops 1509949440 | bytes 11796480 | tf_op jit(solution)/shard_map/image_panel/pallas_call | solution.py:91
  25.8 1.5 %collective-permute-done.9.refs_4_ = bf16[768,128]{1,0:T(8,128)(2,1)S(1)} collective-permute-done((bf16[768,128]{1,0:T(8,128)(2,1)S(1)}, bf16[768,128]{1,0:T(8,128)(2,1)S(1)}, u32[]{:S(2)}, u32[]{:S(2)}) %collective-permute-start.9) | collective-permute-done | bytes 196640 | tf_op jit(solution)/shard_map/ppermute | solution.py:293
  27.4 7.1 %text_panel.1 = (f32[4,1,512,128]{3,2,1,0:T(8,128)S(1)}, f32[4,1,512,128]{3,2,1,0:T(8,128)S(1)}) custom-call(s32[2]{0:T(128)S(1)} %pad_add_fusion.me_ref, bf16[576,6144]{1,0:T(8,128)(2,1)} %a_hbm.3, bf16[576,4096]{1,0:T(8,128)(2,1)} %b_hbm.3, bf16[1536,128]{1,0:T(8,128)(2,1)S(1)} %copy-done, bf16[1536,128]{1,0:T(8,128)(2,1)S(1)} %collective-permute-done.refs_1_, ...), custom_call_target="tpu_custom_call" | custom-call | flops 1509949440 | bytes 11796480 | tf_op jit(solution)/shard_map/text_panel/pallas_call | solution.py:91
  35.7 1.5 %collective-permute-start.12 = (bf16[4,192,128]{2,1,0:T(8,128)(2,1)S(1)}, bf16[4,192,128]{2,1,0:T(8,128)(2,1)S(1)}, u32[]{:S(2)}, u32[]{:S(2)}) collective-permute-start(bf16[4,192,128]{2,1,0:T(8,128)(2,1)S(1)} %get-tuple-element.45), channel_id=1, source_target_pairs={{0,2},{1,3},{2,0},{3,1},{4,6},{5,7},{6,4},{7,5},{8,10},{9,11},{10,... | collective-permute-start | bytes 589832 | tf_op jit(solution)/shard_map/ppermute | solution.py:293
  37.3 1.5 %collective-permute-start.13 = (bf16[4,192,128]{2,1,0:T(8,128)(2,1)S(1)}, bf16[4,192,128]{2,1,0:T(8,128)(2,1)S(1)}, u32[]{:S(2)}, u32[]{:S(2)}) collective-permute-start(bf16[4,192,128]{2,1,0:T(8,128)(2,1)S(1)} %get-tuple-element.46), channel_id=1, source_target_pairs={{0,4},{1,5},{2,6},{3,7},{4,0},{5,1},{6,2},{7,3},{8,12},{9,13},{10,... | collective-permute-start | bytes 589832 | tf_op jit(solution)/shard_map/ppermute | solution.py:293
  40.0 1.5 %collective-permute-start.26 = (bf16[512,128]{1,0:T(8,128)(2,1)S(1)}, bf16[512,128]{1,0:T(8,128)(2,1)S(1)}, u32[]{:S(2)}, u32[]{:S(2)}) collective-permute-start(bf16[512,128]{1,0:T(8,128)(2,1)S(1)} %bitcast.9), channel_id=1, source_target_pairs={{0,2},{1,3},{2,0},{3,1},{4,6},{5,7},{6,4},{7,5},{8,10},{9,11},{10,... | collective-permute-start | bytes 393224 | tf_op jit(solution)/shard_map/ppermute | solution.py:293
  41.5 1.5 %collective-permute-start.27 = (bf16[512,128]{1,0:T(8,128)(2,1)S(1)}, bf16[512,128]{1,0:T(8,128)(2,1)S(1)}, u32[]{:S(2)}, u32[]{:S(2)}) collective-permute-start(bf16[512,128]{1,0:T(8,128)(2,1)S(1)} %bitcast.8), channel_id=1, source_target_pairs={{0,4},{1,5},{2,6},{3,7},{4,0},{5,1},{6,2},{7,3},{8,12},{9,13},{10,... | collective-permute-start | bytes 393224 | tf_op jit(solution)/shard_map/ppermute | solution.py:293
  43.6 2.4 %collective-permute-start.28 = (bf16[512,128]{1,0:T(8,128)(2,1)S(1)}, bf16[512,128]{1,0:T(8,128)(2,1)S(1)}, u32[]{:S(2)}, u32[]{:S(2)}) collective-permute-start(bf16[512,128]{1,0:T(8,128)(2,1)S(1)} %bitcast.7), channel_id=1, source_target_pairs={{0,6},{1,7},{2,4},{3,5},{4,2},{5,3},{6,0},{7,1},{8,14},{9,15},{10,... | collective-permute-start | bytes 393224 | tf_op jit(solution)/shard_map/ppermute | solution.py:293
  46.0 3.0 %collective-permute-done.13.refs_2_ = bf16[4,192,128]{2,1,0:T(8,128)(2,1)S(1)} collective-permute-done((bf16[4,192,128]{2,1,0:T(8,128)(2,1)S(1)}, bf16[4,192,128]{2,1,0:T(8,128)(2,1)S(1)}, u32[]{:S(2)}, u32[]{:S(2)}) %collective-permute-start.13) | collective-permute-done | bytes 196640 | tf_op jit(solution)/shard_map/ppermute | solution.py:293
  50.6 3.1 %collective-permute-done.27.refs_1_ = bf16[512,128]{1,0:T(8,128)(2,1)S(1)} collective-permute-done((bf16[512,128]{1,0:T(8,128)(2,1)S(1)}, bf16[512,128]{1,0:T(8,128)(2,1)S(1)}, u32[]{:S(2)}, u32[]{:S(2)}) %collective-permute-start.27) | collective-permute-done | bytes 131104 | tf_op jit(solution)/shard_map/ppermute | solution.py:293
  54.9 1.1 %collective-permute-start.15 = (bf16[192,128]{1,0:T(8,128)(2,1)S(1)}, bf16[192,128]{1,0:T(8,128)(2,1)S(1)}, u32[]{:S(2)}, u32[]{:S(2)}) collective-permute-start(bf16[192,128]{1,0:T(8,128)(2,1)S(1)} %get-tuple-element.49), channel_id=1, source_target_pairs={{0,8},{8,0},{16,24},{24,16},{1,9},{9,1},{17,25},{25,17},{2,10},{10... | collective-permute-start | bytes 147464 | tf_op jit(solution)/shard_map/ppermute | solution.py:294
  55.9 2.1 %collective-permute-start.30 = (bf16[512,128]{1,0:T(8,128)(2,1)S(1)}, bf16[512,128]{1,0:T(8,128)(2,1)S(1)}, u32[]{:S(2)}, u32[]{:S(2)}) collective-permute-start(bf16[512,128]{1,0:T(8,128)(2,1)S(1)} %text_plane.1.refs_0_), channel_id=1, source_target_pairs={{0,16},{8,24},{16,0},{24,8},{1,17},{9,25},{17,1},{25,9},{2,18},{10... | collective-permute-start | bytes 393224 | tf_op jit(solution)/shard_map/ppermute | solution.py:294
  58.1 1.2 %collective-permute-start.31 = (bf16[512,128]{1,0:T(8,128)(2,1)S(1)}, bf16[512,128]{1,0:T(8,128)(2,1)S(1)}, u32[]{:S(2)}, u32[]{:S(2)}) collective-permute-start(bf16[512,128]{1,0:T(8,128)(2,1)S(1)} %text_plane.1.refs_0_), channel_id=1, source_target_pairs={{0,24},{8,16},{16,8},{24,0},{1,25},{9,17},{17,9},{25,1},{2,26},{10... | collective-permute-start | bytes 393224 | tf_op jit(solution)/shard_map/ppermute | solution.py:294
  59.6 1.4 %collective-permute-done.15.refs_0_ = bf16[192,128]{1,0:T(8,128)(2,1)S(1)} collective-permute-done((bf16[192,128]{1,0:T(8,128)(2,1)S(1)}, bf16[192,128]{1,0:T(8,128)(2,1)S(1)}, u32[]{:S(2)}, u32[]{:S(2)}) %collective-permute-start.15) | collective-permute-done | bytes 49184 | tf_op jit(solution)/shard_map/ppermute | solution.py:294
  61.0 2.0 %collective-permute-start.17 = (bf16[192,128]{1,0:T(8,128)(2,1)S(1)}, bf16[192,128]{1,0:T(8,128)(2,1)S(1)}, u32[]{:S(2)}, u32[]{:S(2)}) collective-permute-start(bf16[192,128]{1,0:T(8,128)(2,1)S(1)} %get-tuple-element.51), channel_id=1, source_target_pairs={{0,24},{8,16},{16,8},{24,0},{1,25},{9,17},{17,9},{25,1},{2,26},{10... | collective-permute-start | bytes 147464 | tf_op jit(solution)/shard_map/ppermute | solution.py:294
  63.0 10.0 %collective-permute-done.16.refs_1_ = bf16[192,128]{1,0:T(8,128)(2,1)S(1)} collective-permute-done((bf16[192,128]{1,0:T(8,128)(2,1)S(1)}, bf16[192,128]{1,0:T(8,128)(2,1)S(1)}, u32[]{:S(2)}, u32[]{:S(2)}) %collective-permute-start.16) | collective-permute-done | bytes 49184 | tf_op jit(solution)/shard_map/ppermute | solution.py:294
  73.0 1.5 %collective-permute-start.18 = (bf16[192,128]{1,0:T(8,128)(2,1)S(1)}, bf16[192,128]{1,0:T(8,128)(2,1)S(1)}, u32[]{:S(2)}, u32[]{:S(2)}) collective-permute-start(bf16[192,128]{1,0:T(8,128)(2,1)S(1)} %image_depth.1.refs_0_), channel_id=1, source_target_pairs={{0,2},{1,3},{2,0},{3,1},{4,6},{5,7},{6,4},{7,5},{8,10},{9,11},{10,... | collective-permute-start | bytes 147464 | tf_op jit(solution)/shard_map/ppermute | solution.py:293
  75.1 1.5 %collective-permute-start.20 = (bf16[192,128]{1,0:T(8,128)(2,1)S(1)}, bf16[192,128]{1,0:T(8,128)(2,1)S(1)}, u32[]{:S(2)}, u32[]{:S(2)}) collective-permute-start(bf16[192,128]{1,0:T(8,128)(2,1)S(1)} %image_depth.1.refs_0_), channel_id=1, source_target_pairs={{0,6},{1,7},{2,4},{3,5},{4,2},{5,3},{6,0},{7,1},{8,14},{9,15},{10,... | collective-permute-start | bytes 147464 | tf_op jit(solution)/shard_map/ppermute | solution.py:293
  77.5 1.1 %collective-permute-done.19.refs_2_ = bf16[192,128]{1,0:T(8,128)(2,1)S(1)} collective-permute-done((bf16[192,128]{1,0:T(8,128)(2,1)S(1)}, bf16[192,128]{1,0:T(8,128)(2,1)S(1)}, u32[]{:S(2)}, u32[]{:S(2)}) %collective-permute-start.19) | collective-permute-done | bytes 49184 | tf_op jit(solution)/shard_map/ppermute | solution.py:293
  78.6 1.4 %collective-permute-done.20.refs_3_ = bf16[192,128]{1,0:T(8,128)(2,1)S(1)} collective-permute-done((bf16[192,128]{1,0:T(8,128)(2,1)S(1)}, bf16[192,128]{1,0:T(8,128)(2,1)S(1)}, u32[]{:S(2)}, u32[]{:S(2)}) %collective-permute-start.20) | collective-permute-done | bytes 49184 | tf_op jit(solution)/shard_map/ppermute | solution.py:293
  80.1 1.2 %collective-permute-done.24.refs_7_ = bf16[192,128]{1,0:T(8,128)(2,1)S(1)} collective-permute-done((bf16[192,128]{1,0:T(8,128)(2,1)S(1)}, bf16[192,128]{1,0:T(8,128)(2,1)S(1)}, u32[]{:S(2)}, u32[]{:S(2)}) %collective-permute-start.24) | collective-permute-done | bytes 49184 | tf_op jit(solution)/shard_map/ppermute | solution.py:293
  82.2 1.2 %collective-permute-start.32 = (f32[128,128]{1,0:T(8,128)S(1)}, f32[128,128]{1,0:T(8,128)S(1)}, u32[]{:S(2)}, u32[]{:S(2)}) collective-permute-start(f32[128,128]{1,0:T(8,128)S(1)} %get-tuple-element.64.refs_0_), channel_id=1, source_target_pairs={{0,8},{1,17},{2,10},{3,19},{4,12},{5,21},{6,14},{7,23},{8,0},{9,25... | collective-permute-start | bytes 196616 | tf_op jit(solution)/shard_map/ppermute | solution.py:314
  83.4 3.8 %collective-permute-start.34 = (f32[128,128]{1,0:T(8,128)S(1)}, f32[128,128]{1,0:T(8,128)S(1)}, u32[]{:S(2)}, u32[]{:S(2)}) collective-permute-start(f32[128,128]{1,0:T(8,128)S(1)} %get-tuple-element.64.refs_0_), channel_id=1, source_target_pairs={{0,24},{2,26},{4,28},{6,30},{8,16},{10,18},{12,20},{14,22},{16,8},... | collective-permute-start | bytes 196616 | tf_op jit(solution)/shard_map/ppermute | solution.py:314
  87.8 4.5 %collective-permute-start.39 = (f32[128,128]{1,0:T(8,128)S(1)}, f32[128,128]{1,0:T(8,128)S(1)}, u32[]{:S(2)}, u32[]{:S(2)}) collective-permute-start(f32[128,128]{1,0:T(8,128)S(1)} %text_gram_cores.1.refs_5_), channel_id=1, source_target_pairs={{0,6},{2,4},{4,2},{6,0},{8,14},{10,12},{12,10},{14,8},{16,22},{18,... | collective-permute-start | bytes 196616 | tf_op jit(solution)/shard_map/ppermute | solution.py:314
  93.0 1.8 %collective-permute-done.39.refs_8_ = f32[128,128]{1,0:T(8,128)S(1)} collective-permute-done((f32[128,128]{1,0:T(8,128)S(1)}, f32[128,128]{1,0:T(8,128)S(1)}, u32[]{:S(2)}, u32[]{:S(2)}) %collective-permute-start.39) | collective-permute-done | bytes 65568 | tf_op jit(solution)/shard_map/ppermute | solution.py:314
  94.8 1.2 %collective-permute-done.40.refs_9_ = f32[128,128]{1,0:T(8,128)S(1)} collective-permute-done((f32[128,128]{1,0:T(8,128)S(1)}, f32[128,128]{1,0:T(8,128)S(1)}, u32[]{:S(2)}, u32[]{:S(2)}) %collective-permute-start.40) | collective-permute-done | bytes 65568 | tf_op jit(solution)/shard_map/ppermute | solution.py:293
  96.1 7.6 %finish.1 = (f32[1536,128]{1,0:T(8,128)}, f32[512,128]{1,0:T(8,128)}) custom-call(bf16[8,192,128]{2,1,0:T(8,128)(2,1)S(1)} %get-tuple-element.52.ipanel, bf16[1,512,128]{2,1,0:T(8,128)(2,1)S(1)} %get-tuple-element.63.tpanel, f32[128,128]{1,0:T(8,128)S(1)} %get-tuple-element.64.refs_0_, f32[128,128]{1,0:T(8,128)S(1)} %collective-permute-done.32.refs_1_, ...), custom_call_target="tpu_custom_call" | custom-call | flops 10000000000 | bytes 1179648 | tf_op jit(solution)/shard_map/finish/pallas_call | solution.py:279
  (67 shorter events, 13.7 us)
Async XLA Ops:
  0.6 13.6 %collective-permute-start = (bf16[1536,128]{1,0:T(8,128)(2,1)}, bf16[1536,128]{1,0:T(8,128)(2,1)S(1)}, u32[]{:S(2)}, u32[]{:S(2)}) collective-permute-start(bf16[1536,128]{1,0:T(8,128)(2,1)} %refs_0_.3), channel_id=1, source_target_pairs={{0,8},{1,17},{2,10},{3,19},{4,12},{5,21},{6,14},{7,23},{8,0},{9,25... | collective-permute-start | bytes 1179656 | tf_op jit(solution)/shard_map/ppermute | solution.py:314
  3.7 7.4 %collective-permute-start.3 = (bf16[512,128]{1,0:T(8,128)(2,1)}, bf16[512,128]{1,0:T(8,128)(2,1)S(1)}, u32[]{:S(2)}, u32[]{:S(2)}) collective-permute-start(bf16[512,128]{1,0:T(8,128)(2,1)} %refs_0_.2), channel_id=1, source_target_pairs={{0,6},{1,7},{2,4},{3,5},{4,2},{5,3},{6,0},{7,1},{8,14},{9,15},{10,... | collective-permute-start | bytes 393224 | tf_op jit(solution)/shard_map/ppermute | solution.py:293
  6.2 7.5 %collective-permute-start.1 = (bf16[512,128]{1,0:T(8,128)(2,1)}, bf16[512,128]{1,0:T(8,128)(2,1)S(1)}, u32[]{:S(2)}, u32[]{:S(2)}) collective-permute-start(bf16[512,128]{1,0:T(8,128)(2,1)} %refs_0_.2), channel_id=1, source_target_pairs={{0,2},{1,3},{2,0},{3,1},{4,6},{5,7},{6,4},{7,5},{8,10},{9,11},{10,... | collective-permute-start | bytes 393224 | tf_op jit(solution)/shard_map/ppermute | solution.py:293
  6.7 7.0 %collective-permute-start.2 = (bf16[512,128]{1,0:T(8,128)(2,1)}, bf16[512,128]{1,0:T(8,128)(2,1)S(1)}, u32[]{:S(2)}, u32[]{:S(2)}) collective-permute-start(bf16[512,128]{1,0:T(8,128)(2,1)} %refs_0_.2), channel_id=1, source_target_pairs={{0,4},{1,5},{2,6},{3,7},{4,0},{5,1},{6,2},{7,3},{8,12},{9,13},{10,... | collective-permute-start | bytes 393224 | tf_op jit(solution)/shard_map/ppermute | solution.py:293
  7.2 10.7 %collective-permute-start.4 = (bf16[512,128]{1,0:T(8,128)(2,1)}, bf16[512,128]{1,0:T(8,128)(2,1)S(1)}, u32[]{:S(2)}, u32[]{:S(2)}) collective-permute-start(bf16[512,128]{1,0:T(8,128)(2,1)} %refs_0_.2), channel_id=1, source_target_pairs={{0,1},{1,0},{2,3},{3,2},{4,5},{5,4},{6,7},{7,6},{8,9},{9,8},{10,11... | collective-permute-start | bytes 393224 | tf_op jit(solution)/shard_map/ppermute | solution.py:293
  13.7 4.2 %collective-permute-start.5 = (bf16[512,128]{1,0:T(8,128)(2,1)S(1)}, bf16[512,128]{1,0:T(8,128)(2,1)S(1)}, u32[]{:S(2)}, u32[]{:S(2)}) collective-permute-start(bf16[512,128]{1,0:T(8,128)(2,1)S(1)} %collective-permute-done.1.refs_1_), channel_id=1, source_target_pairs={{0,1},{1,0},{2,3},{3,2},{4,5},{5,4},{6,7},{7,6},{8,9},{9,8},{10,11... | collective-permute-start | bytes 393224 | tf_op jit(solution)/shard_map/ppermute | solution.py:293
  13.7 4.2 %collective-permute-start.6 = (bf16[512,128]{1,0:T(8,128)(2,1)S(1)}, bf16[512,128]{1,0:T(8,128)(2,1)S(1)}, u32[]{:S(2)}, u32[]{:S(2)}) collective-permute-start(bf16[512,128]{1,0:T(8,128)(2,1)S(1)} %collective-permute-done.2.refs_2_), channel_id=1, source_target_pairs={{0,1},{1,0},{2,3},{3,2},{4,5},{5,4},{6,7},{7,6},{8,9},{9,8},{10,11... | collective-permute-start | bytes 393224 | tf_op jit(solution)/shard_map/ppermute | solution.py:293
  14.2 3.7 %collective-permute-start.7 = (bf16[512,128]{1,0:T(8,128)(2,1)S(1)}, bf16[512,128]{1,0:T(8,128)(2,1)S(1)}, u32[]{:S(2)}, u32[]{:S(2)}) collective-permute-start(bf16[512,128]{1,0:T(8,128)(2,1)S(1)} %collective-permute-done.3.refs_3_), channel_id=1, source_target_pairs={{0,1},{1,0},{2,3},{3,2},{4,5},{5,4},{6,7},{7,6},{8,9},{9,8},{10,11... | collective-permute-start | bytes 393224 | tf_op jit(solution)/shard_map/ppermute | solution.py:293
  14.2 11.0 %collective-permute-start.8 = (bf16[768,128]{1,0:T(8,128)(2,1)S(1)}, bf16[768,128]{1,0:T(8,128)(2,1)S(1)}, u32[]{:S(2)}, u32[]{:S(2)}) collective-permute-start(bf16[768,128]{1,0:T(8,128)(2,1)S(1)} %constant_dynamic-slice_fusion), channel_id=1, source_target_pairs={{0,24},{8,16},{16,8},{24,0},{1,25},{9,17},{17,9},{25,1},{2,26},{10... | collective-permute-start | bytes 589832 | tf_op jit(solution)/shard_map/ppermute | solution.py:294
  27.3 7.7 %collective-permute-start.11 = (f32[4,4,192,128]{3,2,1,0:T(8,128)S(1)}, f32[4,4,192,128]{3,2,1,0:T(8,128)S(1)}, u32[]{:S(2)}, u32[]{:S(2)}) collective-permute-start(f32[4,4,192,128]{3,2,1,0:T(8,128)S(1)} %get-tuple-element.43), channel_id=1, source_target_pairs={{0,1},{1,0},{2,3},{3,2},{4,5},{5,4},{6,7},{7,6},{8,9},{9,8},{10,11... | collective-permute-start | bytes 4718600 | tf_op jit(solution)/shard_map/ppermute | solution.py:293
  34.6 4.7 %collective-permute-start.25 = (f32[4,1,512,128]{3,2,1,0:T(8,128)S(1)}, f32[4,1,512,128]{3,2,1,0:T(8,128)S(1)}, u32[]{:S(2)}, u32[]{:S(2)}) collective-permute-start(f32[4,1,512,128]{3,2,1,0:T(8,128)S(1)} %get-tuple-element.56), channel_id=1, source_target_pairs={{0,1},{1,0},{2,3},{3,2},{4,5},{5,4},{6,7},{7,6},{8,9},{9,8},{10,11... | collective-permute-start | bytes 3145736 | tf_op jit(solution)/shard_map/ppermute | solution.py:293
  35.7 7.8 %collective-permute-start.12 = (bf16[4,192,128]{2,1,0:T(8,128)(2,1)S(1)}, bf16[4,192,128]{2,1,0:T(8,128)(2,1)S(1)}, u32[]{:S(2)}, u32[]{:S(2)}) collective-permute-start(bf16[4,192,128]{2,1,0:T(8,128)(2,1)S(1)} %get-tuple-element.45), channel_id=1, source_target_pairs={{0,2},{1,3},{2,0},{3,1},{4,6},{5,7},{6,4},{7,5},{8,10},{9,11},{10,... | collective-permute-start | bytes 589832 | tf_op jit(solution)/shard_map/ppermute | solution.py:293
  37.3 11.7 %collective-permute-start.13 = (bf16[4,192,128]{2,1,0:T(8,128)(2,1)S(1)}, bf16[4,192,128]{2,1,0:T(8,128)(2,1)S(1)}, u32[]{:S(2)}, u32[]{:S(2)}) collective-permute-start(bf16[4,192,128]{2,1,0:T(8,128)(2,1)S(1)} %get-tuple-element.46), channel_id=1, source_target_pairs={{0,4},{1,5},{2,6},{3,7},{4,0},{5,1},{6,2},{7,3},{8,12},{9,13},{10,... | collective-permute-start | bytes 589832 | tf_op jit(solution)/shard_map/ppermute | solution.py:293
  38.8 10.2 %collective-permute-start.14 = (bf16[4,192,128]{2,1,0:T(8,128)(2,1)S(1)}, bf16[4,192,128]{2,1,0:T(8,128)(2,1)S(1)}, u32[]{:S(2)}, u32[]{:S(2)}) collective-permute-start(bf16[4,192,128]{2,1,0:T(8,128)(2,1)S(1)} %get-tuple-element.47), channel_id=1, source_target_pairs={{0,6},{1,7},{2,4},{3,5},{4,2},{5,3},{6,0},{7,1},{8,14},{9,15},{10,... | collective-permute-start | bytes 589832 | tf_op jit(solution)/shard_map/ppermute | solution.py:293
  40.0 10.7 %collective-permute-start.26 = (bf16[512,128]{1,0:T(8,128)(2,1)S(1)}, bf16[512,128]{1,0:T(8,128)(2,1)S(1)}, u32[]{:S(2)}, u32[]{:S(2)}) collective-permute-start(bf16[512,128]{1,0:T(8,128)(2,1)S(1)} %bitcast.9), channel_id=1, source_target_pairs={{0,2},{1,3},{2,0},{3,1},{4,6},{5,7},{6,4},{7,5},{8,10},{9,11},{10,... | collective-permute-start | bytes 393224 | tf_op jit(solution)/shard_map/ppermute | solution.py:293
  41.5 12.3 %collective-permute-start.27 = (bf16[512,128]{1,0:T(8,128)(2,1)S(1)}, bf16[512,128]{1,0:T(8,128)(2,1)S(1)}, u32[]{:S(2)}, u32[]{:S(2)}) collective-permute-start(bf16[512,128]{1,0:T(8,128)(2,1)S(1)} %bitcast.8), channel_id=1, source_target_pairs={{0,4},{1,5},{2,6},{3,7},{4,0},{5,1},{6,2},{7,3},{8,12},{9,13},{10,... | collective-permute-start | bytes 393224 | tf_op jit(solution)/shard_map/ppermute | solution.py:293
  43.6 10.2 %collective-permute-start.28 = (bf16[512,128]{1,0:T(8,128)(2,1)S(1)}, bf16[512,128]{1,0:T(8,128)(2,1)S(1)}, u32[]{:S(2)}, u32[]{:S(2)}) collective-permute-start(bf16[512,128]{1,0:T(8,128)(2,1)S(1)} %bitcast.7), channel_id=1, source_target_pairs={{0,6},{1,7},{2,4},{3,5},{4,2},{5,3},{6,0},{7,1},{8,14},{9,15},{10,... | collective-permute-start | bytes 393224 | tf_op jit(solution)/shard_map/ppermute | solution.py:293
  53.9 21.2 %collective-permute-start.29 = (bf16[512,128]{1,0:T(8,128)(2,1)S(1)}, bf16[512,128]{1,0:T(8,128)(2,1)S(1)}, u32[]{:S(2)}, u32[]{:S(2)}) collective-permute-start(bf16[512,128]{1,0:T(8,128)(2,1)S(1)} %text_plane.1.refs_0_), channel_id=1, source_target_pairs={{0,8},{8,0},{16,24},{24,16},{1,9},{9,1},{17,25},{25,17},{2,10},{10... | collective-permute-start | bytes 393224 | tf_op jit(solution)/shard_map/ppermute | solution.py:294
  54.9 6.2 %collective-permute-start.15 = (bf16[192,128]{1,0:T(8,128)(2,1)S(1)}, bf16[192,128]{1,0:T(8,128)(2,1)S(1)}, u32[]{:S(2)}, u32[]{:S(2)}) collective-permute-start(bf16[192,128]{1,0:T(8,128)(2,1)S(1)} %get-tuple-element.49), channel_id=1, source_target_pairs={{0,8},{8,0},{16,24},{24,16},{1,9},{9,1},{17,25},{25,17},{2,10},{10... | collective-permute-start | bytes 147464 | tf_op jit(solution)/shard_map/ppermute | solution.py:294
  55.9 20.6 %collective-permute-start.30 = (bf16[512,128]{1,0:T(8,128)(2,1)S(1)}, bf16[512,128]{1,0:T(8,128)(2,1)S(1)}, u32[]{:S(2)}, u32[]{:S(2)}) collective-permute-start(bf16[512,128]{1,0:T(8,128)(2,1)S(1)} %text_plane.1.refs_0_), channel_id=1, source_target_pairs={{0,16},{8,24},{16,0},{24,8},{1,17},{9,25},{17,1},{25,9},{2,18},{10... | collective-permute-start | bytes 393224 | tf_op jit(solution)/shard_map/ppermute | solution.py:294
  58.1 18.5 %collective-permute-start.31 = (bf16[512,128]{1,0:T(8,128)(2,1)S(1)}, bf16[512,128]{1,0:T(8,128)(2,1)S(1)}, u32[]{:S(2)}, u32[]{:S(2)}) collective-permute-start(bf16[512,128]{1,0:T(8,128)(2,1)S(1)} %text_plane.1.refs_0_), channel_id=1, source_target_pairs={{0,24},{8,16},{16,8},{24,0},{1,25},{9,17},{17,9},{25,1},{2,26},{10... | collective-permute-start | bytes 393224 | tf_op jit(solution)/shard_map/ppermute | solution.py:294
  59.3 13.7 %collective-permute-start.16 = (bf16[192,128]{1,0:T(8,128)(2,1)S(1)}, bf16[192,128]{1,0:T(8,128)(2,1)S(1)}, u32[]{:S(2)}, u32[]{:S(2)}) collective-permute-start(bf16[192,128]{1,0:T(8,128)(2,1)S(1)} %get-tuple-element.50), channel_id=1, source_target_pairs={{0,16},{8,24},{16,0},{24,8},{1,17},{9,25},{17,1},{25,9},{2,18},{10... | collective-permute-start | bytes 147464 | tf_op jit(solution)/shard_map/ppermute | solution.py:294
  61.0 12.0 %collective-permute-start.17 = (bf16[192,128]{1,0:T(8,128)(2,1)S(1)}, bf16[192,128]{1,0:T(8,128)(2,1)S(1)}, u32[]{:S(2)}, u32[]{:S(2)}) collective-permute-start(bf16[192,128]{1,0:T(8,128)(2,1)S(1)} %get-tuple-element.51), channel_id=1, source_target_pairs={{0,24},{8,16},{16,8},{24,0},{1,25},{9,17},{17,9},{25,1},{2,26},{10... | collective-permute-start | bytes 147464 | tf_op jit(solution)/shard_map/ppermute | solution.py:294
  73.0 4.4 %collective-permute-start.18 = (bf16[192,128]{1,0:T(8,128)(2,1)S(1)}, bf16[192,128]{1,0:T(8,128)(2,1)S(1)}, u32[]{:S(2)}, u32[]{:S(2)}) collective-permute-start(bf16[192,128]{1,0:T(8,128)(2,1)S(1)} %image_depth.1.refs_0_), channel_id=1, source_target_pairs={{0,2},{1,3},{2,0},{3,1},{4,6},{5,7},{6,4},{7,5},{8,10},{9,11},{10,... | collective-permute-start | bytes 147464 | tf_op jit(solution)/shard_map/ppermute | solution.py:293
  74.5 4.1 %collective-permute-start.19 = (bf16[192,128]{1,0:T(8,128)(2,1)S(1)}, bf16[192,128]{1,0:T(8,128)(2,1)S(1)}, u32[]{:S(2)}, u32[]{:S(2)}) collective-permute-start(bf16[192,128]{1,0:T(8,128)(2,1)S(1)} %image_depth.1.refs_0_), channel_id=1, source_target_pairs={{0,4},{1,5},{2,6},{3,7},{4,0},{5,1},{6,2},{7,3},{8,12},{9,13},{10,... | collective-permute-start | bytes 147464 | tf_op jit(solution)/shard_map/ppermute | solution.py:293
  75.1 5.0 %collective-permute-start.20 = (bf16[192,128]{1,0:T(8,128)(2,1)S(1)}, bf16[192,128]{1,0:T(8,128)(2,1)S(1)}, u32[]{:S(2)}, u32[]{:S(2)}) collective-permute-start(bf16[192,128]{1,0:T(8,128)(2,1)S(1)} %image_depth.1.refs_0_), channel_id=1, source_target_pairs={{0,6},{1,7},{2,4},{3,5},{4,2},{5,3},{6,0},{7,1},{8,14},{9,15},{10,... | collective-permute-start | bytes 147464 | tf_op jit(solution)/shard_map/ppermute | solution.py:293
  76.9 10.3 %collective-permute-start.36 = (f32[128,128]{1,0:T(8,128)S(1)}, f32[128,128]{1,0:T(8,128)S(1)}, u32[]{:S(2)}, u32[]{:S(2)}) collective-permute-start(f32[128,128]{1,0:T(8,128)S(1)} %get-tuple-element.65.own_ref), channel_id=1, source_target_pairs={{0,1},{1,0},{2,3},{3,2},{4,5},{5,4},{6,7},{7,6},{8,9},{9,8},{10,11... | collective-permute-start | bytes 196616 | tf_op jit(solution)/shard_map/ppermute | solution.py:293
  76.9 3.1 %collective-permute-start.21 = (bf16[192,128]{1,0:T(8,128)(2,1)S(1)}, bf16[192,128]{1,0:T(8,128)(2,1)S(1)}, u32[]{:S(2)}, u32[]{:S(2)}) collective-permute-start(bf16[192,128]{1,0:T(8,128)(2,1)S(1)} %image_depth.1.refs_0_), channel_id=1, source_target_pairs={{0,1},{1,0},{2,3},{3,2},{4,5},{5,4},{6,7},{7,6},{8,9},{9,8},{10,11... | collective-permute-start | bytes 147464 | tf_op jit(solution)/shard_map/ppermute | solution.py:293
  82.2 10.1 %collective-permute-start.32 = (f32[128,128]{1,0:T(8,128)S(1)}, f32[128,128]{1,0:T(8,128)S(1)}, u32[]{:S(2)}, u32[]{:S(2)}) collective-permute-start(f32[128,128]{1,0:T(8,128)S(1)} %get-tuple-element.64.refs_0_), channel_id=1, source_target_pairs={{0,8},{1,17},{2,10},{3,19},{4,12},{5,21},{6,14},{7,23},{8,0},{9,25... | collective-permute-start | bytes 196616 | tf_op jit(solution)/shard_map/ppermute | solution.py:314
  83.4 9.0 %collective-permute-start.34 = (f32[128,128]{1,0:T(8,128)S(1)}, f32[128,128]{1,0:T(8,128)S(1)}, u32[]{:S(2)}, u32[]{:S(2)}) collective-permute-start(f32[128,128]{1,0:T(8,128)S(1)} %get-tuple-element.64.refs_0_), channel_id=1, source_target_pairs={{0,24},{2,26},{4,28},{6,30},{8,16},{10,18},{12,20},{14,22},{16,8},... | collective-permute-start | bytes 196616 | tf_op jit(solution)/shard_map/ppermute | solution.py:314
  87.2 5.7 %collective-permute-start.37 = (f32[128,128]{1,0:T(8,128)S(1)}, f32[128,128]{1,0:T(8,128)S(1)}, u32[]{:S(2)}, u32[]{:S(2)}) collective-permute-start(f32[128,128]{1,0:T(8,128)S(1)} %text_gram_cores.1.refs_5_), channel_id=1, source_target_pairs={{0,2},{1,5},{2,0},{3,7},{4,6},{5,1},{6,4},{7,3},{8,10},{9,13},{10,... | collective-permute-start | bytes 196616 | tf_op jit(solution)/shard_map/ppermute | solution.py:314
  87.8 7.0 %collective-permute-start.39 = (f32[128,128]{1,0:T(8,128)S(1)}, f32[128,128]{1,0:T(8,128)S(1)}, u32[]{:S(2)}, u32[]{:S(2)}) collective-permute-start(f32[128,128]{1,0:T(8,128)S(1)} %text_gram_cores.1.refs_5_), channel_id=1, source_target_pairs={{0,6},{2,4},{4,2},{6,0},{8,14},{10,12},{12,10},{14,8},{16,22},{18,... | collective-permute-start | bytes 196616 | tf_op jit(solution)/shard_map/ppermute | solution.py:314
  (11 other events, 28.0 us)

commit v11 on v10

--- a/solution.py
+++ b/solution.py
@@ -48,8 +48,27 @@
     return rows
 
 
+def load_kernel(hbm_ref, out_ref, sem):
+    move = pltpu.make_async_copy(hbm_ref, out_ref, sem)
+    move.start()
+    move.wait()
+
+
+def load_call(x):
+    return pl.pallas_call(
+        load_kernel,
+        in_specs=[pl.BlockSpec(memory_space=pltpu.HBM)],
+        out_specs=VMEM,
+        out_shape=sds(x.shape, x.dtype),
+        scratch_shapes=[pltpu.SemaphoreType.DMA],
+        compiler_params=params(),
+        cost_estimate=cost(1, 4 * x.size),
+        name="load",
+    )(x)
+
+
 def panel_kernel(rows, n, n_in, n_out, me_ref, a_hbm, b_hbm, *refs):
-    parts, (keep_ref, send_ref, a_ref, b_ref, probe, a_sem, b_sem, own_sem) = refs[:n], refs[n:]
+    parts, (keep_ref, send_ref, a_ref, b_ref, probe, a_sem, b_sem) = refs[:n], refs[n:]
     core = me_ref[0] % 2
     tall = a_ref.shape[0] // n_in
     cols = b_ref.shape[1] // n_out // 2
@@ -61,13 +80,10 @@
         span = pl.ds(2 * i * cols, 2 * cols)
         moves.append(pltpu.make_async_copy(b_hbm.at[:, span], b_ref.at[:, span], b_sem.at[i]))
     places = rows(me_ref)
-    own = pltpu.make_async_copy(parts[0], probe.at[pl.ds(places[0], parts[0].shape[0])], own_sem)
-    own.start()
     for move in moves:
         move.start()
-    for at, part in zip(places[1:], parts[1:]):
+    for at, part in zip(places, parts):
         probe[pl.ds(at, part.shape[0]), :] = part[...]
-    own.wait()
     sketches = []
     for i in range(n_in):
         moves[i].wait()
@@ -90,7 +106,7 @@
     n_in = 3 if pairs % 48 == 0 else 1
     return pl.pallas_call(
         functools.partial(panel_kernel, rows, len(parts), n_in, blocks),
-        in_specs=[SMEM, hbm, hbm, hbm] + [VMEM] * (len(parts) - 1),
+        in_specs=[SMEM, hbm, hbm] + [VMEM] * len(parts),
         out_specs=[VMEM, VMEM],
         out_shape=[out, out],
         scratch_shapes=[
@@ -99,7 +115,6 @@
             pltpu.VMEM((a.shape[1], rank), BF16),
             pltpu.SemaphoreType.DMA((n_in,)),
             pltpu.SemaphoreType.DMA((blocks,)),
-            pltpu.SemaphoreType.DMA,
         ],
         compiler_params=pltpu.CompilerParams(vmem_limit_bytes=PANEL_LIMIT),
         cost_estimate=cost(2 * pairs * rank * (width + a.shape[1]), 2 * pairs * (width + a.shape[1])),
@@ -156,6 +171,29 @@
         cost_estimate=cost(own.size, 12 * own.size),
         name=name,
     )(own, *recv)
+
+
+def pack(gram):
+    half = gram.shape[0] // 2
+    top, low = gram[:half], gram[half:]
+    row = lax.broadcasted_iota(jnp.int32, top.shape, 0)
+    lane = lax.broadcasted_iota(jnp.int32, top.shape, 1)
+    body = jnp.where(row + half >= lane, low, pltpu.roll(top, half, 1))
+    diagonal = jnp.sum(jnp.where(row == lane, top, 0.0), axis=0, keepdims=True)
+    return jnp.concatenate([body, jnp.broadcast_to(diagonal, (8, gram.shape[1]))], axis=0)
+
+
+def unpack(packed):
+    half = packed.shape[0] - 8
+    body, diagonal = packed[:half], packed[half : half + 1]
+    row = lax.broadcasted_iota(jnp.int32, body.shape, 0)
+    lane = lax.broadcasted_iota(jnp.int32, body.shape, 1)
+    upper = jnp.where(jnp.logical_and(lane < half, row < lane), pltpu.roll(body, half, 1), 0.0)
+    lower = jnp.where(row + half > lane, body, 0.0)
+    strict = jnp.concatenate([upper, lower], axis=0)
+    first = jnp.where(row == lane, jnp.broadcast_to(diagonal, body.shape), 0.0)
+    last = jnp.where(row + half == lane, body, 0.0)
+    return strict + strict.T + jnp.concatenate([first, last], axis=0)
 
 
 def gram_kernel(which, order, me_ref, *refs):
@@ -166,10 +204,9 @@
         else:
             spot = me_ref[0] ^ s
             panel_ref[spot % 2 * (len(order) // 2) + spot // 2] = part[...]
-    panel = panel_ref[...].reshape(-1, gram_ref.shape[0])
-    gram_ref[...] = lax.dot_general(
-        panel, panel, (((0,), (0,)), ((), ())), preferred_element_type=F32
-    )
+    panel = panel_ref[...].reshape(-1, gram_ref.shape[1])
+    gram = lax.dot_general(panel, panel, (((0,), (0,)), ((), ())), preferred_element_type=F32)
+    gram_ref[...] = pack(gram)
 
 
 def gram_call(which, order, me, parts, name):
@@ -179,7 +216,7 @@
         functools.partial(gram_kernel, which, order),
         in_specs=[SMEM] + [VMEM] * n,
         out_specs=[VMEM, VMEM],
-        out_shape=[sds((n, rows, rank), BF16), sds((rank, rank), F32)],
+        out_shape=[sds((n, rows, rank), BF16), sds((rank // 2 + 8, rank), F32)],
         compiler_params=params(),
         cost_estimate=cost(2 * n * rows * rank * rank, 4 * n * rows * rank),
         name=name,
@@ -196,9 +233,8 @@
     *parts, panel_ref, gram_ref = refs
     panel = tree_sum([part[...].astype(F32) for part in parts]).astype(BF16)
     panel_ref[0] = panel
-    gram_ref[...] = lax.dot_general(
-        panel, panel, (((0,), (0,)), ((), ())), preferred_element_type=F32
-    )
+    gram = lax.dot_general(panel, panel, (((0,), (0,)), ((), ())), preferred_element_type=F32)
+    gram_ref[...] = pack(gram)
 
 
 def text_gram_call(parts):
@@ -207,7 +243,7 @@
         text_gram_kernel,
         in_specs=[VMEM] * len(parts),
         out_specs=[VMEM, VMEM],
-        out_shape=[sds((1, rows, rank), BF16), sds((rank, rank), F32)],
+        out_shape=[sds((1, rows, rank), BF16), sds((rank // 2 + 8, rank), F32)],
         compiler_params=params(),
         cost_estimate=cost(2 * rows * rank * rank, 4 * rows * rank),
         name="text_gram",
@@ -255,9 +291,9 @@
 
     def total(refs):
         value = refs[0][...]
-        for even, odd in zip(refs[1::2], refs[2::2]):
-            value = value + (even[...] + odd[...])
-        return value
+        for ref in refs[1:]:
+            value = value + ref[...]
+        return unpack(value)
 
     inverses = None
     for inverses in zip(inverse_factor(total(grams[:n_image])), inverse_factor(total(grams[n_image:]))):
@@ -308,21 +344,17 @@
         pairs = []
         for r in range(n_row):
             for c in range(n_col):
-                shift = odd if c % 2 else even
-                if shift is not None:
-                    pairs.append((r * n_col + c, (r ^ shift[0]) * n_col + (c ^ shift[1])))
+                pairs.append((r * n_col + c, (r ^ (odd if c % 2 else even)) * n_col + c))
         return lax.ppermute(x, ("row", "col"), pairs)
 
-    def shared_sums(x, shifts):
-        got = [split_swap(x, *pair) for pair in zip(shifts[::2], shifts[1::2] + [None])]
-        return [term for block in got for term in (block, col_swap(block, 1))]
-
-    fetched = [(t, t + 1, split_swap(probe_image, (t, 0), (t + 1, 0))) for t in depths[:-1:2]]
+    fetched = [(t, t + 1, split_swap(probe_image, t, t + 1)) for t in depths[:-1:2]]
     half = probe_image.shape[0] // 2
     mine = lax.dynamic_slice_in_dim(probe_image, me[0] % 2 * half, half, 0)
     received = over_chips([probe_text] * len(chips))
-    mine, received[-1] = lax.optimization_barrier((mine, received[-1]))
+    own = load_call(probe_text)
+    mine, own, received[-1] = lax.optimization_barrier((mine, own, received[-1]))
     text_parts = over_plane(probe_text, received)
+    text_parts[0] = own
     first, *blocks = lax.optimization_barrier((me, *[block for _, _, block in fetched]))
     last = depths[-1]
     mine = row_swap(mine, last)
@@ -343,22 +375,23 @@
     image_parts += [mine, other]
     own, *image_sends = sums_call("col", 1, chips, me, [keep, col_swap(send, 1)], "image_cores")
     own, *sends = sums_call("row", 0, depths, me, [own] + over_chips(image_sends), "image_plane")
-    after_plane = sends[0]
-    mine = last_call(own, over_depth(sends), BF16, "image_depth")
+    received = over_depth(sends)
+    after_depth = received
+    mine = last_call(own, received, BF16, "image_depth")
     parts = over_plane(mine)
     ipanel, gram = gram_call("col", list(parts), me, list(parts.values()), "image_gram")
-    igrams = [gram] + shared_sums(gram, [(t, 0) for t in depths])
+    igrams = [gram] + over_depth([gram] * len(depths))
 
     rows = image_rows(image_order, probe_image.shape[0])
     keep, send = panel_call(me, image_feats, text_feats, image_parts, rows, groups, 1, "text_panel")
     swapped, _ = lax.optimization_barrier((col_swap(send, 1), image_sends[0]))
     own, *sends = sums_call("col", 0, chips, me, [keep, swapped], "text_cores")
     own, sends = own[0], [x[0] for x in sends]
-    own, _ = lax.optimization_barrier((own, after_plane))
+    own, *_ = lax.optimization_barrier((own, *after_depth))
     mine = last_call(own, over_chips(sends), BF16, "text_plane")
     tpanel, gram = text_gram_call([mine] + over_depth([mine] * len(depths)))
     gram = last_call(gram, [col_swap(gram, 1)], F32, "text_gram_cores")
-    tgrams = [gram] + shared_sums(gram, [(0, 2 * s) for s in chips])
+    tgrams = [gram] + over_chips([gram] * len(chips))
 
     widths = (image_feats.shape[1], text_feats.shape[1])
     return finish_call(widths, ipanel, igrams, tpanel, tgrams)

time: 104 us -> 93.8 us (0.902)
  waiting for transfers between devices: 33 us -> 21.8 us
  starting transfers between devices: 43.6 us -> 45 us
    ppermute x5 -> x1, starting transfers between devices: 13.1 us -> 3.09 us  [split_swap(): return lax.ppermute(x, ('row', 'col'), pairs)]
    ppermute x7 -> x10, starting transfers between devices: 11.3 us -> 19.4 us  [per_device(): lax.ppermute(x, 'row', [(i, i ^ s) for i in range(n_row)])]
    ppermute x7 -> x10, waiting for transfers between devices: 11.4 us -> 4.52 us  [per_device(): lax.ppermute(x, 'row', [(i, i ^ s) for i in range(n_row)])]
    ppermute x29 -> x28, starting transfers between devices: 19.1 us -> 22.6 us  [per_device(): lax.ppermute(x, 'col', [(i, i ^ s) for i in range(n_col)])]
    ppermute x29 -> x28, waiting for transfers between devices: 19.7 us -> 17.3 us  [per_device(): lax.ppermute(x, 'col', [(i, i ^ s) for i in range(n_col)])]
    ppermute x5 -> x1, waiting for transfers between devices: 1.84 us -> 0.01 us  [split_swap(): return lax.ppermute(x, ('row', 'col'), pairs)]
  transfers between devices with their start and end apart: 41 -> 39, of which waited for: 14 -> 16; matrix products, arithmetic and copies ran while one was open for 1% -> 1% of each run, Pallas kernels for 16% -> 17%
where the time goes in v11:
time: 93.8 us; the launch traced here: 93.7 us
  starting transfers between devices  45 us (48%)
  Pallas kernels  24.1 us (26%)
  waiting for transfers between devices  21.8 us (23%)
  local copies, waits for them, and re-layouts  1.88 us (2%)
    ppermute x28, starting transfers between devices, per_device(): lax.ppermute(x, 'col', [(i, i ^ s) for i in range(n_col)])  22.6 us
    ppermute x10, starting transfers between devices, per_device(): lax.ppermute(x, 'row', [(i, i ^ s) for i in range(n_row)])  19.4 us
    ppermute x28, waiting for transfers between devices, per_device(): lax.ppermute(x, 'col', [(i, i ^ s) for i in range(n_col)])  17.3 us
    pallas_call x2, Pallas kernels, panel_call(): pl.pallas_call(functools.partial(panel_kernel, rows, len(parts), n_in, bl...  12.7 us
    pallas_call x1, Pallas kernels, finish_call(): pl.pallas_call(functools.partial(finish_kernel, widths, len(igrams)), in_...  7.92 us
    ppermute x10, waiting for transfers between devices, per_device(): lax.ppermute(x, 'row', [(i, i ^ s) for i in range(n_row)])  4.52 us
    ppermute x1, starting transfers between devices, split_swap(): return lax.ppermute(x, ('row', 'col'), pairs)  3.09 us
    pallas_call x3, Pallas kernels, sums_call(): pl.pallas_call(functools.partial(sums_kernel, which, axis, shifts, len(te...  1.97 us
  transfers between devices with their start and end apart: 39, of which 16 were waited for; matrix products, arithmetic and copies ran while one was open for 1% of the time, Pallas kernels for 17%

profile of v11, /device:TPU:0, one launch (start us, length us, event | category | flops | bytes accessed | tf_op | source)
XLA Modules:
  0.0 93.7 jit_solution(5301188238722280434)
XLA Ops:
  0.6 3.1 %collective-permute-start = (bf16[1536,128]{1,0:T(8,128)(2,1)}, bf16[1536,128]{1,0:T(8,128)(2,1)S(1)}, u32[]{:S(2)}, u32[]{:S(2)}) collective-permute-start(bf16[1536,128]{1,0:T(8,128)(2,1)} %refs_0_.1), channel_id=1, source_target_pairs={{0,8},{1,17},{2,10},{3,19},{4,12},{5,21},{6,14},{7,23},{8,0},{9,25... | collective-permute-start | bytes 1179656 | tf_op jit(solution)/shard_map/ppermute | solution.py:348
  3.7 2.4 %collective-permute-start.1 = (bf16[512,128]{1,0:T(8,128)(2,1)}, bf16[512,128]{1,0:T(8,128)(2,1)S(1)}, u32[]{:S(2)}, u32[]{:S(2)}) collective-permute-start(bf16[512,128]{1,0:T(8,128)(2,1)} %hbm_ref.1), channel_id=1, source_target_pairs={{0,6},{1,7},{2,4},{3,5},{4,2},{5,3},{6,0},{7,1},{8,14},{9,15},{10,... | collective-permute-start | bytes 393224 | tf_op jit(solution)/shard_map/ppermute | solution.py:329
  9.3 1.8 %collective-permute-done.1.refs_3_ = bf16[512,128]{1,0:T(8,128)(2,1)S(1)} collective-permute-done((bf16[512,128]{1,0:T(8,128)(2,1)}, bf16[512,128]{1,0:T(8,128)(2,1)S(1)}, u32[]{:S(2)}, u32[]{:S(2)}) %collective-permute-start.1) | collective-permute-done | bytes 131104 | tf_op jit(solution)/shard_map/ppermute | solution.py:329
  11.1 2.6 %collective-permute-done.2.refs_1_ = bf16[512,128]{1,0:T(8,128)(2,1)S(1)} collective-permute-done((bf16[512,128]{1,0:T(8,128)(2,1)}, bf16[512,128]{1,0:T(8,128)(2,1)S(1)}, u32[]{:S(2)}, u32[]{:S(2)}) %collective-permute-start.2) | collective-permute-done | bytes 131104 | tf_op jit(solution)/shard_map/ppermute | solution.py:329
  14.2 3.6 %collective-permute-start.8 = (bf16[768,128]{1,0:T(8,128)(2,1)S(1)}, bf16[768,128]{1,0:T(8,128)(2,1)S(1)}, u32[]{:S(2)}, u32[]{:S(2)}) collective-permute-start(bf16[768,128]{1,0:T(8,128)(2,1)S(1)} %constant_dynamic-slice_fusion), channel_id=1, source_target_pairs={{0,24},{8,16},{16,8},{24,0},{1,25},{9,17},{17,9},{25,1},{2,26},{10... | collective-permute-start | bytes 589832 | tf_op jit(solution)/shard_map/ppermute | solution.py:330
  17.9 6.1 %image_panel.1 = (f32[4,4,192,128]{3,2,1,0:T(8,128)S(1)}, f32[4,4,192,128]{3,2,1,0:T(8,128)S(1)}) custom-call(s32[2]{0:T(128)S(1)} %pad_add_fusion.me_ref, bf16[576,4096]{1,0:T(8,128)(2,1)} %b_hbm.3, bf16[576,6144]{1,0:T(8,128)(2,1)} %a_hbm.3, bf16[512,128]{1,0:T(8,128)(2,1)S(1)} %load.1.refs_0_, bf16[512,128]{1,0:T(8,128)(2,1)S(1)} %collective-permute-done.2.refs_1_, ...), custom_call_target="tpu_custom_call" | custom-call | flops 1509949440 | bytes 11796480 | tf_op jit(solution)/shard_map/image_panel/pallas_call | solution.py:107
  24.6 1.5 %collective-permute-done.9.refs_4_ = bf16[768,128]{1,0:T(8,128)(2,1)S(1)} collective-permute-done((bf16[768,128]{1,0:T(8,128)(2,1)S(1)}, bf16[768,128]{1,0:T(8,128)(2,1)S(1)}, u32[]{:S(2)}, u32[]{:S(2)}) %collective-permute-start.9) | collective-permute-done | bytes 196640 | tf_op jit(solution)/shard_map/ppermute | solution.py:329
  26.3 6.6 %text_panel.1 = (f32[4,1,512,128]{3,2,1,0:T(8,128)S(1)}, f32[4,1,512,128]{3,2,1,0:T(8,128)S(1)}) custom-call(s32[2]{0:T(128)S(1)} %pad_add_fusion.me_ref, bf16[576,6144]{1,0:T(8,128)(2,1)} %a_hbm.3, bf16[576,4096]{1,0:T(8,128)(2,1)} %b_hbm.3, bf16[1536,128]{1,0:T(8,128)(2,1)S(1)} %copy-done, bf16[1536,128]{1,0:T(8,128)(2,1)S(1)} %collective-permute-done.refs_1_, ...), custom_call_target="tpu_custom_call" | custom-call | flops 1509949440 | bytes 11796480 | tf_op jit(solution)/shard_map/text_panel/pallas_call | solution.py:107
  34.0 1.6 %collective-permute-start.12 = (bf16[4,192,128]{2,1,0:T(8,128)(2,1)S(1)}, bf16[4,192,128]{2,1,0:T(8,128)(2,1)S(1)}, u32[]{:S(2)}, u32[]{:S(2)}) collective-permute-start(bf16[4,192,128]{2,1,0:T(8,128)(2,1)S(1)} %get-tuple-element.47), channel_id=1, source_target_pairs={{0,2},{1,3},{2,0},{3,1},{4,6},{5,7},{6,4},{7,5},{8,10},{9,11},{10,... | collective-permute-start | bytes 589832 | tf_op jit(solution)/shard_map/ppermute | solution.py:329
  35.6 1.5 %collective-permute-start.13 = (bf16[4,192,128]{2,1,0:T(8,128)(2,1)S(1)}, bf16[4,192,128]{2,1,0:T(8,128)(2,1)S(1)}, u32[]{:S(2)}, u32[]{:S(2)}) collective-permute-start(bf16[4,192,128]{2,1,0:T(8,128)(2,1)S(1)} %get-tuple-element.48), channel_id=1, source_target_pairs={{0,4},{1,5},{2,6},{3,7},{4,0},{5,1},{6,2},{7,3},{8,12},{9,13},{10,... | collective-permute-start | bytes 589832 | tf_op jit(solution)/shard_map/ppermute | solution.py:329
  38.2 1.6 %collective-permute-start.26 = (bf16[512,128]{1,0:T(8,128)(2,1)S(1)}, bf16[512,128]{1,0:T(8,128)(2,1)S(1)}, u32[]{:S(2)}, u32[]{:S(2)}) collective-permute-start(bf16[512,128]{1,0:T(8,128)(2,1)S(1)} %bitcast.9), channel_id=1, source_target_pairs={{0,2},{1,3},{2,0},{3,1},{4,6},{5,7},{6,4},{7,5},{8,10},{9,11},{10,... | collective-permute-start | bytes 393224 | tf_op jit(solution)/shard_map/ppermute | solution.py:329
  39.8 1.5 %collective-permute-start.27 = (bf16[512,128]{1,0:T(8,128)(2,1)S(1)}, bf16[512,128]{1,0:T(8,128)(2,1)S(1)}, u32[]{:S(2)}, u32[]{:S(2)}) collective-permute-start(bf16[512,128]{1,0:T(8,128)(2,1)S(1)} %bitcast.8), channel_id=1, source_target_pairs={{0,4},{1,5},{2,6},{3,7},{4,0},{5,1},{6,2},{7,3},{8,12},{9,13},{10,... | collective-permute-start | bytes 393224 | tf_op jit(solution)/shard_map/ppermute | solution.py:329
  41.8 2.5 %collective-permute-start.28 = (bf16[512,128]{1,0:T(8,128)(2,1)S(1)}, bf16[512,128]{1,0:T(8,128)(2,1)S(1)}, u32[]{:S(2)}, u32[]{:S(2)}) collective-permute-start(bf16[512,128]{1,0:T(8,128)(2,1)S(1)} %bitcast.7), channel_id=1, source_target_pairs={{0,6},{1,7},{2,4},{3,5},{4,2},{5,3},{6,0},{7,1},{8,14},{9,15},{10,... | collective-permute-start | bytes 393224 | tf_op jit(solution)/shard_map/ppermute | solution.py:329
  44.3 3.0 %collective-permute-done.13.refs_2_ = bf16[4,192,128]{2,1,0:T(8,128)(2,1)S(1)} collective-permute-done((bf16[4,192,128]{2,1,0:T(8,128)(2,1)S(1)}, bf16[4,192,128]{2,1,0:T(8,128)(2,1)S(1)}, u32[]{:S(2)}, u32[]{:S(2)}) %collective-permute-start.13) | collective-permute-done | bytes 196640 | tf_op jit(solution)/shard_map/ppermute | solution.py:329
  48.0 2.2 %collective-permute-start.15 = (bf16[192,128]{1,0:T(8,128)(2,1)S(1)}, bf16[192,128]{1,0:T(8,128)(2,1)S(1)}, u32[]{:S(2)}, u32[]{:S(2)}) collective-permute-start(bf16[192,128]{1,0:T(8,128)(2,1)S(1)} %get-tuple-element.51), channel_id=1, source_target_pairs={{0,8},{8,0},{16,24},{24,16},{1,9},{9,1},{17,25},{25,17},{2,10},{10... | collective-permute-start | bytes 147464 | tf_op jit(solution)/shard_map/ppermute | solution.py:330
  50.1 1.3 %collective-permute-start.16 = (bf16[192,128]{1,0:T(8,128)(2,1)S(1)}, bf16[192,128]{1,0:T(8,128)(2,1)S(1)}, u32[]{:S(2)}, u32[]{:S(2)}) collective-permute-start(bf16[192,128]{1,0:T(8,128)(2,1)S(1)} %get-tuple-element.52), channel_id=1, source_target_pairs={{0,16},{8,24},{16,0},{24,8},{1,17},{9,25},{17,1},{25,9},{2,18},{10... | collective-permute-start | bytes 147464 | tf_op jit(solution)/shard_map/ppermute | solution.py:330
  51.4 1.2 %collective-permute-done.15.refs_0_ = bf16[192,128]{1,0:T(8,128)(2,1)S(1)} collective-permute-done((bf16[192,128]{1,0:T(8,128)(2,1)S(1)}, bf16[192,128]{1,0:T(8,128)(2,1)S(1)}, u32[]{:S(2)}, u32[]{:S(2)}) %collective-permute-start.15) | collective-permute-done | bytes 49184 | tf_op jit(solution)/shard_map/ppermute | solution.py:330
  52.6 2.8 %collective-permute-start.17 = (bf16[192,128]{1,0:T(8,128)(2,1)S(1)}, bf16[192,128]{1,0:T(8,128)(2,1)S(1)}, u32[]{:S(2)}, u32[]{:S(2)}) collective-permute-start(bf16[192,128]{1,0:T(8,128)(2,1)S(1)} %get-tuple-element.53), channel_id=1, source_target_pairs={{0,24},{8,16},{16,8},{24,0},{1,25},{9,17},{17,9},{25,1},{2,26},{10... | collective-permute-start | bytes 147464 | tf_op jit(solution)/shard_map/ppermute | solution.py:330
  55.9 2.7 %collective-permute-done.17.refs_2_ = bf16[192,128]{1,0:T(8,128)(2,1)S(1)} collective-permute-done((bf16[192,128]{1,0:T(8,128)(2,1)S(1)}, bf16[192,128]{1,0:T(8,128)(2,1)S(1)}, u32[]{:S(2)}, u32[]{:S(2)}) %collective-permute-start.17) | collective-permute-done | bytes 49184 | tf_op jit(solution)/shard_map/ppermute | solution.py:330
  58.7 3.7 %collective-permute-start.30 = (bf16[512,128]{1,0:T(8,128)(2,1)S(1)}, bf16[512,128]{1,0:T(8,128)(2,1)S(1)}, u32[]{:S(2)}, u32[]{:S(2)}) collective-permute-start(bf16[512,128]{1,0:T(8,128)(2,1)S(1)} %text_plane.1.refs_0_), channel_id=1, source_target_pairs={{0,16},{8,24},{16,0},{24,8},{1,17},{9,25},{17,1},{25,9},{2,18},{10... | collective-permute-start | bytes 393224 | tf_op jit(solution)/shard_map/ppermute | solution.py:330
  63.2 1.3 %collective-permute-start.31 = (bf16[512,128]{1,0:T(8,128)(2,1)S(1)}, bf16[512,128]{1,0:T(8,128)(2,1)S(1)}, u32[]{:S(2)}, u32[]{:S(2)}) collective-permute-start(bf16[512,128]{1,0:T(8,128)(2,1)S(1)} %text_plane.1.refs_0_), channel_id=1, source_target_pairs={{0,24},{8,16},{16,8},{24,0},{1,25},{9,17},{17,9},{25,1},{2,26},{10... | collective-permute-start | bytes 393224 | tf_op jit(solution)/shard_map/ppermute | solution.py:330
  64.6 1.5 %collective-permute-start.19 = (bf16[192,128]{1,0:T(8,128)(2,1)S(1)}, bf16[192,128]{1,0:T(8,128)(2,1)S(1)}, u32[]{:S(2)}, u32[]{:S(2)}) collective-permute-start(bf16[192,128]{1,0:T(8,128)(2,1)S(1)} %image_depth.1.refs_0_), channel_id=1, source_target_pairs={{0,4},{1,5},{2,6},{3,7},{4,0},{5,1},{6,2},{7,3},{8,12},{9,13},{10,... | collective-permute-start | bytes 147464 | tf_op jit(solution)/shard_map/ppermute | solution.py:329
  66.6 1.4 %collective-permute-start.20 = (bf16[192,128]{1,0:T(8,128)(2,1)S(1)}, bf16[192,128]{1,0:T(8,128)(2,1)S(1)}, u32[]{:S(2)}, u32[]{:S(2)}) collective-permute-start(bf16[192,128]{1,0:T(8,128)(2,1)S(1)} %image_depth.1.refs_0_), channel_id=1, source_target_pairs={{0,6},{1,7},{2,4},{3,5},{4,2},{5,3},{6,0},{7,1},{8,14},{9,15},{10,... | collective-permute-start | bytes 147464 | tf_op jit(solution)/shard_map/ppermute | solution.py:329
  68.7 3.0 %collective-permute-done.20.refs_3_ = bf16[192,128]{1,0:T(8,128)(2,1)S(1)} collective-permute-done((bf16[192,128]{1,0:T(8,128)(2,1)S(1)}, bf16[192,128]{1,0:T(8,128)(2,1)S(1)}, u32[]{:S(2)}, u32[]{:S(2)}) %collective-permute-start.20) | collective-permute-done | bytes 49184 | tf_op jit(solution)/shard_map/ppermute | solution.py:329
  73.4 1.0 %image_gram.1 = (bf16[8,192,128]{2,1,0:T(8,128)(2,1)S(1)}, f32[72,128]{1,0:T(8,128)S(1)}) custom-call(s32[2]{0:T(128)S(1)} %pad_add_fusion.me_ref, bf16[192,128]{1,0:T(8,128)(2,1)S(1)} %image_depth.1.refs_0_, bf16[192,128]{1,0:T(8,128)(2,1)S(1)} %collective-permute-done.18.refs_1_, bf16[192,128]{1,0:T(8,128)(2,1)S(1)} %collective-permute-done.19.refs_2_, ...), custom_call_target="tpu_custom_call" | custom-call | flops 50331648 | bytes 786432 | tf_op jit(solution)/shard_map/image_gram/pallas_call | solution.py:215
  74.9 1.8 %collective-permute-start.33 = (f32[72,128]{1,0:T(8,128)S(1)}, f32[72,128]{1,0:T(8,128)S(1)}, u32[]{:S(2)}, u32[]{:S(2)}) collective-permute-start(f32[72,128]{1,0:T(8,128)S(1)} %get-tuple-element.66.refs_0_), channel_id=1, source_target_pairs={{0,16},{8,24},{16,0},{24,8},{1,17},{9,25},{17,1},{25,9},{2,18},{10... | collective-permute-start | bytes 110600 | tf_op jit(solution)/shard_map/ppermute | solution.py:330
  76.7 2.1 %collective-permute-start.34 = (f32[72,128]{1,0:T(8,128)S(1)}, f32[72,128]{1,0:T(8,128)S(1)}, u32[]{:S(2)}, u32[]{:S(2)}) collective-permute-start(f32[72,128]{1,0:T(8,128)S(1)} %get-tuple-element.66.refs_0_), channel_id=1, source_target_pairs={{0,24},{8,16},{16,8},{24,0},{1,25},{9,17},{17,9},{25,1},{2,26},{10... | collective-permute-start | bytes 110600 | tf_op jit(solution)/shard_map/ppermute | solution.py:330
  78.8 1.4 %collective-permute-start.36 = (f32[72,128]{1,0:T(8,128)S(1)}, f32[72,128]{1,0:T(8,128)S(1)}, u32[]{:S(2)}, u32[]{:S(2)}) collective-permute-start(f32[72,128]{1,0:T(8,128)S(1)} %text_gram_cores.1.refs_4_), channel_id=1, source_target_pairs={{0,2},{1,3},{2,0},{3,1},{4,6},{5,7},{6,4},{7,5},{8,10},{9,11},{10,... | collective-permute-start | bytes 110600 | tf_op jit(solution)/shard_map/ppermute | solution.py:329
  80.9 1.5 %collective-permute-start.38 = (f32[72,128]{1,0:T(8,128)S(1)}, f32[72,128]{1,0:T(8,128)S(1)}, u32[]{:S(2)}, u32[]{:S(2)}) collective-permute-start(f32[72,128]{1,0:T(8,128)S(1)} %text_gram_cores.1.refs_4_), channel_id=1, source_target_pairs={{0,6},{1,7},{2,4},{3,5},{4,2},{5,3},{6,0},{7,1},{8,14},{9,15},{10,... | collective-permute-start | bytes 110600 | tf_op jit(solution)/shard_map/ppermute | solution.py:329
  82.8 1.6 %collective-permute-done.37.refs_6_ = f32[72,128]{1,0:T(8,128)S(1)} collective-permute-done((f32[72,128]{1,0:T(8,128)S(1)}, f32[72,128]{1,0:T(8,128)S(1)}, u32[]{:S(2)}, u32[]{:S(2)}) %collective-permute-start.37) | collective-permute-done | bytes 36896 | tf_op jit(solution)/shard_map/ppermute | solution.py:329
  84.4 1.3 %collective-permute-done.38.refs_7_ = f32[72,128]{1,0:T(8,128)S(1)} collective-permute-done((f32[72,128]{1,0:T(8,128)S(1)}, f32[72,128]{1,0:T(8,128)S(1)}, u32[]{:S(2)}, u32[]{:S(2)}) %collective-permute-start.38) | collective-permute-done | bytes 36896 | tf_op jit(solution)/shard_map/ppermute | solution.py:329
  85.7 7.9 %finish.1 = (f32[1536,128]{1,0:T(8,128)}, f32[512,128]{1,0:T(8,128)}) custom-call(bf16[8,192,128]{2,1,0:T(8,128)(2,1)S(1)} %get-tuple-element.54.ipanel, bf16[1,512,128]{2,1,0:T(8,128)(2,1)S(1)} %get-tuple-element.65.tpanel, f32[72,128]{1,0:T(8,128)S(1)} %get-tuple-element.66.refs_0_, f32[72,128]{1,0:T(8,128)S(1)} %collective-permute-done.32.refs_1_, ...), custom_call_target="tpu_custom_call" | custom-call | flops 10000000000 | bytes 1179648 | tf_op jit(solution)/shard_map/finish/pallas_call | solution.py:315
  (64 shorter events, 13.8 us)
Async XLA Ops:
  0.6 13.6 %collective-permute-start = (bf16[1536,128]{1,0:T(8,128)(2,1)}, bf16[1536,128]{1,0:T(8,128)(2,1)S(1)}, u32[]{:S(2)}, u32[]{:S(2)}) collective-permute-start(bf16[1536,128]{1,0:T(8,128)(2,1)} %refs_0_.1), channel_id=1, source_target_pairs={{0,8},{1,17},{2,10},{3,19},{4,12},{5,21},{6,14},{7,23},{8,0},{9,25... | collective-permute-start | bytes 1179656 | tf_op jit(solution)/shard_map/ppermute | solution.py:348
  3.7 7.4 %collective-permute-start.1 = (bf16[512,128]{1,0:T(8,128)(2,1)}, bf16[512,128]{1,0:T(8,128)(2,1)S(1)}, u32[]{:S(2)}, u32[]{:S(2)}) collective-permute-start(bf16[512,128]{1,0:T(8,128)(2,1)} %hbm_ref.1), channel_id=1, source_target_pairs={{0,6},{1,7},{2,4},{3,5},{4,2},{5,3},{6,0},{7,1},{8,14},{9,15},{10,... | collective-permute-start | bytes 393224 | tf_op jit(solution)/shard_map/ppermute | solution.py:329
  6.2 7.5 %collective-permute-start.2 = (bf16[512,128]{1,0:T(8,128)(2,1)}, bf16[512,128]{1,0:T(8,128)(2,1)S(1)}, u32[]{:S(2)}, u32[]{:S(2)}) collective-permute-start(bf16[512,128]{1,0:T(8,128)(2,1)} %hbm_ref.1), channel_id=1, source_target_pairs={{0,2},{1,3},{2,0},{3,1},{4,6},{5,7},{6,4},{7,5},{8,10},{9,11},{10,... | collective-permute-start | bytes 393224 | tf_op jit(solution)/shard_map/ppermute | solution.py:329
  6.7 7.0 %collective-permute-start.3 = (bf16[512,128]{1,0:T(8,128)(2,1)}, bf16[512,128]{1,0:T(8,128)(2,1)S(1)}, u32[]{:S(2)}, u32[]{:S(2)}) collective-permute-start(bf16[512,128]{1,0:T(8,128)(2,1)} %hbm_ref.1), channel_id=1, source_target_pairs={{0,4},{1,5},{2,6},{3,7},{4,0},{5,1},{6,2},{7,3},{8,12},{9,13},{10,... | collective-permute-start | bytes 393224 | tf_op jit(solution)/shard_map/ppermute | solution.py:329
  7.2 10.7 %collective-permute-start.4 = (bf16[512,128]{1,0:T(8,128)(2,1)}, bf16[512,128]{1,0:T(8,128)(2,1)S(1)}, u32[]{:S(2)}, u32[]{:S(2)}) collective-permute-start(bf16[512,128]{1,0:T(8,128)(2,1)} %hbm_ref.1), channel_id=1, source_target_pairs={{0,1},{1,0},{2,3},{3,2},{4,5},{5,4},{6,7},{7,6},{8,9},{9,8},{10,11... | collective-permute-start | bytes 393224 | tf_op jit(solution)/shard_map/ppermute | solution.py:329
  13.7 4.2 %collective-permute-start.5 = (bf16[512,128]{1,0:T(8,128)(2,1)S(1)}, bf16[512,128]{1,0:T(8,128)(2,1)S(1)}, u32[]{:S(2)}, u32[]{:S(2)}) collective-permute-start(bf16[512,128]{1,0:T(8,128)(2,1)S(1)} %collective-permute-done.2.refs_1_), channel_id=1, source_target_pairs={{0,1},{1,0},{2,3},{3,2},{4,5},{5,4},{6,7},{7,6},{8,9},{9,8},{10,11... | collective-permute-start | bytes 393224 | tf_op jit(solution)/shard_map/ppermute | solution.py:329
  13.7 4.2 %collective-permute-start.6 = (bf16[512,128]{1,0:T(8,128)(2,1)S(1)}, bf16[512,128]{1,0:T(8,128)(2,1)S(1)}, u32[]{:S(2)}, u32[]{:S(2)}) collective-permute-start(bf16[512,128]{1,0:T(8,128)(2,1)S(1)} %collective-permute-done.3.refs_2_), channel_id=1, source_target_pairs={{0,1},{1,0},{2,3},{3,2},{4,5},{5,4},{6,7},{7,6},{8,9},{9,8},{10,11... | collective-permute-start | bytes 393224 | tf_op jit(solution)/shard_map/ppermute | solution.py:329
  14.2 9.8 %collective-permute-start.8 = (bf16[768,128]{1,0:T(8,128)(2,1)S(1)}, bf16[768,128]{1,0:T(8,128)(2,1)S(1)}, u32[]{:S(2)}, u32[]{:S(2)}) collective-permute-start(bf16[768,128]{1,0:T(8,128)(2,1)S(1)} %constant_dynamic-slice_fusion), channel_id=1, source_target_pairs={{0,24},{8,16},{16,8},{24,0},{1,25},{9,17},{17,9},{25,1},{2,26},{10... | collective-permute-start | bytes 589832 | tf_op jit(solution)/shard_map/ppermute | solution.py:330
  26.1 7.2 %collective-permute-start.11 = (f32[4,4,192,128]{3,2,1,0:T(8,128)S(1)}, f32[4,4,192,128]{3,2,1,0:T(8,128)S(1)}, u32[]{:S(2)}, u32[]{:S(2)}) collective-permute-start(f32[4,4,192,128]{3,2,1,0:T(8,128)S(1)} %get-tuple-element.45), channel_id=1, source_target_pairs={{0,1},{1,0},{2,3},{3,2},{4,5},{5,4},{6,7},{7,6},{8,9},{9,8},{10,11... | collective-permute-start | bytes 4718600 | tf_op jit(solution)/shard_map/ppermute | solution.py:329
  32.9 4.7 %collective-permute-start.25 = (f32[4,1,512,128]{3,2,1,0:T(8,128)S(1)}, f32[4,1,512,128]{3,2,1,0:T(8,128)S(1)}, u32[]{:S(2)}, u32[]{:S(2)}) collective-permute-start(f32[4,1,512,128]{3,2,1,0:T(8,128)S(1)} %get-tuple-element.58), channel_id=1, source_target_pairs={{0,1},{1,0},{2,3},{3,2},{4,5},{5,4},{6,7},{7,6},{8,9},{9,8},{10,11... | collective-permute-start | bytes 3145736 | tf_op jit(solution)/shard_map/ppermute | solution.py:329
  34.0 7.8 %collective-permute-start.12 = (bf16[4,192,128]{2,1,0:T(8,128)(2,1)S(1)}, bf16[4,192,128]{2,1,0:T(8,128)(2,1)S(1)}, u32[]{:S(2)}, u32[]{:S(2)}) collective-permute-start(bf16[4,192,128]{2,1,0:T(8,128)(2,1)S(1)} %get-tuple-element.47), channel_id=1, source_target_pairs={{0,2},{1,3},{2,0},{3,1},{4,6},{5,7},{6,4},{7,5},{8,10},{9,11},{10,... | collective-permute-start | bytes 589832 | tf_op jit(solution)/shard_map/ppermute | solution.py:329
  35.6 11.7 %collective-permute-start.13 = (bf16[4,192,128]{2,1,0:T(8,128)(2,1)S(1)}, bf16[4,192,128]{2,1,0:T(8,128)(2,1)S(1)}, u32[]{:S(2)}, u32[]{:S(2)}) collective-permute-start(bf16[4,192,128]{2,1,0:T(8,128)(2,1)S(1)} %get-tuple-element.48), channel_id=1, source_target_pairs={{0,4},{1,5},{2,6},{3,7},{4,0},{5,1},{6,2},{7,3},{8,12},{9,13},{10,... | collective-permute-start | bytes 589832 | tf_op jit(solution)/shard_map/ppermute | solution.py:329
  37.1 10.2 %collective-permute-start.14 = (bf16[4,192,128]{2,1,0:T(8,128)(2,1)S(1)}, bf16[4,192,128]{2,1,0:T(8,128)(2,1)S(1)}, u32[]{:S(2)}, u32[]{:S(2)}) collective-permute-start(bf16[4,192,128]{2,1,0:T(8,128)(2,1)S(1)} %get-tuple-element.49), channel_id=1, source_target_pairs={{0,6},{1,7},{2,4},{3,5},{4,2},{5,3},{6,0},{7,1},{8,14},{9,15},{10,... | collective-permute-start | bytes 589832 | tf_op jit(solution)/shard_map/ppermute | solution.py:329
  38.2 20.4 %collective-permute-start.26 = (bf16[512,128]{1,0:T(8,128)(2,1)S(1)}, bf16[512,128]{1,0:T(8,128)(2,1)S(1)}, u32[]{:S(2)}, u32[]{:S(2)}) collective-permute-start(bf16[512,128]{1,0:T(8,128)(2,1)S(1)} %bitcast.9), channel_id=1, source_target_pairs={{0,2},{1,3},{2,0},{3,1},{4,6},{5,7},{6,4},{7,5},{8,10},{9,11},{10,... | collective-permute-start | bytes 393224 | tf_op jit(solution)/shard_map/ppermute | solution.py:329
  39.8 18.8 %collective-permute-start.27 = (bf16[512,128]{1,0:T(8,128)(2,1)S(1)}, bf16[512,128]{1,0:T(8,128)(2,1)S(1)}, u32[]{:S(2)}, u32[]{:S(2)}) collective-permute-start(bf16[512,128]{1,0:T(8,128)(2,1)S(1)} %bitcast.8), channel_id=1, source_target_pairs={{0,4},{1,5},{2,6},{3,7},{4,0},{5,1},{6,2},{7,3},{8,12},{9,13},{10,... | collective-permute-start | bytes 393224 | tf_op jit(solution)/shard_map/ppermute | solution.py:329
  41.8 16.8 %collective-permute-start.28 = (bf16[512,128]{1,0:T(8,128)(2,1)S(1)}, bf16[512,128]{1,0:T(8,128)(2,1)S(1)}, u32[]{:S(2)}, u32[]{:S(2)}) collective-permute-start(bf16[512,128]{1,0:T(8,128)(2,1)S(1)} %bitcast.7), channel_id=1, source_target_pairs={{0,6},{1,7},{2,4},{3,5},{4,2},{5,3},{6,0},{7,1},{8,14},{9,15},{10,... | collective-permute-start | bytes 393224 | tf_op jit(solution)/shard_map/ppermute | solution.py:329
  48.0 4.6 %collective-permute-start.15 = (bf16[192,128]{1,0:T(8,128)(2,1)S(1)}, bf16[192,128]{1,0:T(8,128)(2,1)S(1)}, u32[]{:S(2)}, u32[]{:S(2)}) collective-permute-start(bf16[192,128]{1,0:T(8,128)(2,1)S(1)} %get-tuple-element.51), channel_id=1, source_target_pairs={{0,8},{8,0},{16,24},{24,16},{1,9},{9,1},{17,25},{25,17},{2,10},{10... | collective-permute-start | bytes 147464 | tf_op jit(solution)/shard_map/ppermute | solution.py:330
  50.1 5.8 %collective-permute-start.16 = (bf16[192,128]{1,0:T(8,128)(2,1)S(1)}, bf16[192,128]{1,0:T(8,128)(2,1)S(1)}, u32[]{:S(2)}, u32[]{:S(2)}) collective-permute-start(bf16[192,128]{1,0:T(8,128)(2,1)S(1)} %get-tuple-element.52), channel_id=1, source_target_pairs={{0,16},{8,24},{16,0},{24,8},{1,17},{9,25},{17,1},{25,9},{2,18},{10... | collective-permute-start | bytes 147464 | tf_op jit(solution)/shard_map/ppermute | solution.py:330
  52.6 6.0 %collective-permute-start.17 = (bf16[192,128]{1,0:T(8,128)(2,1)S(1)}, bf16[192,128]{1,0:T(8,128)(2,1)S(1)}, u32[]{:S(2)}, u32[]{:S(2)}) collective-permute-start(bf16[192,128]{1,0:T(8,128)(2,1)S(1)} %get-tuple-element.53), channel_id=1, source_target_pairs={{0,24},{8,16},{16,8},{24,0},{1,25},{9,17},{17,9},{25,1},{2,26},{10... | collective-permute-start | bytes 147464 | tf_op jit(solution)/shard_map/ppermute | solution.py:330
  58.7 13.0 %collective-permute-start.29 = (bf16[512,128]{1,0:T(8,128)(2,1)S(1)}, bf16[512,128]{1,0:T(8,128)(2,1)S(1)}, u32[]{:S(2)}, u32[]{:S(2)}) collective-permute-start(bf16[512,128]{1,0:T(8,128)(2,1)S(1)} %text_plane.1.refs_0_), channel_id=1, source_target_pairs={{0,8},{8,0},{16,24},{24,16},{1,9},{9,1},{17,25},{25,17},{2,10},{10... | collective-permute-start | bytes 393224 | tf_op jit(solution)/shard_map/ppermute | solution.py:330
  58.7 13.4 %collective-permute-start.30 = (bf16[512,128]{1,0:T(8,128)(2,1)S(1)}, bf16[512,128]{1,0:T(8,128)(2,1)S(1)}, u32[]{:S(2)}, u32[]{:S(2)}) collective-permute-start(bf16[512,128]{1,0:T(8,128)(2,1)S(1)} %text_plane.1.refs_0_), channel_id=1, source_target_pairs={{0,16},{8,24},{16,0},{24,8},{1,17},{9,25},{17,1},{25,9},{2,18},{10... | collective-permute-start | bytes 393224 | tf_op jit(solution)/shard_map/ppermute | solution.py:330
  62.5 4.2 %collective-permute-start.18 = (bf16[192,128]{1,0:T(8,128)(2,1)S(1)}, bf16[192,128]{1,0:T(8,128)(2,1)S(1)}, u32[]{:S(2)}, u32[]{:S(2)}) collective-permute-start(bf16[192,128]{1,0:T(8,128)(2,1)S(1)} %image_depth.1.refs_0_), channel_id=1, source_target_pairs={{0,2},{1,3},{2,0},{3,1},{4,6},{5,7},{6,4},{7,5},{8,10},{9,11},{10,... | collective-permute-start | bytes 147464 | tf_op jit(solution)/shard_map/ppermute | solution.py:329
  63.2 9.0 %collective-permute-start.31 = (bf16[512,128]{1,0:T(8,128)(2,1)S(1)}, bf16[512,128]{1,0:T(8,128)(2,1)S(1)}, u32[]{:S(2)}, u32[]{:S(2)}) collective-permute-start(bf16[512,128]{1,0:T(8,128)(2,1)S(1)} %text_plane.1.refs_0_), channel_id=1, source_target_pairs={{0,24},{8,16},{16,8},{24,0},{1,25},{9,17},{17,9},{25,1},{2,26},{10... | collective-permute-start | bytes 393224 | tf_op jit(solution)/shard_map/ppermute | solution.py:330
  64.6 4.1 %collective-permute-start.19 = (bf16[192,128]{1,0:T(8,128)(2,1)S(1)}, bf16[192,128]{1,0:T(8,128)(2,1)S(1)}, u32[]{:S(2)}, u32[]{:S(2)}) collective-permute-start(bf16[192,128]{1,0:T(8,128)(2,1)S(1)} %image_depth.1.refs_0_), channel_id=1, source_target_pairs={{0,4},{1,5},{2,6},{3,7},{4,0},{5,1},{6,2},{7,3},{8,12},{9,13},{10,... | collective-permute-start | bytes 147464 | tf_op jit(solution)/shard_map/ppermute | solution.py:329
  66.6 5.0 %collective-permute-start.20 = (bf16[192,128]{1,0:T(8,128)(2,1)S(1)}, bf16[192,128]{1,0:T(8,128)(2,1)S(1)}, u32[]{:S(2)}, u32[]{:S(2)}) collective-permute-start(bf16[192,128]{1,0:T(8,128)(2,1)S(1)} %image_depth.1.refs_0_), channel_id=1, source_target_pairs={{0,6},{1,7},{2,4},{3,5},{4,2},{5,3},{6,0},{7,1},{8,14},{9,15},{10,... | collective-permute-start | bytes 147464 | tf_op jit(solution)/shard_map/ppermute | solution.py:329
  68.6 4.4 %collective-permute-start.21 = (bf16[192,128]{1,0:T(8,128)(2,1)S(1)}, bf16[192,128]{1,0:T(8,128)(2,1)S(1)}, u32[]{:S(2)}, u32[]{:S(2)}) collective-permute-start(bf16[192,128]{1,0:T(8,128)(2,1)S(1)} %image_depth.1.refs_0_), channel_id=1, source_target_pairs={{0,1},{1,0},{2,3},{3,2},{4,5},{5,4},{6,7},{7,6},{8,9},{9,8},{10,11... | collective-permute-start | bytes 147464 | tf_op jit(solution)/shard_map/ppermute | solution.py:329
  72.5 6.3 %collective-permute-start.35 = (f32[72,128]{1,0:T(8,128)S(1)}, f32[72,128]{1,0:T(8,128)S(1)}, u32[]{:S(2)}, u32[]{:S(2)}) collective-permute-start(f32[72,128]{1,0:T(8,128)S(1)} %get-tuple-element.67.own_ref), channel_id=1, source_target_pairs={{0,1},{1,0},{2,3},{3,2},{4,5},{5,4},{6,7},{7,6},{8,9},{9,8},{10,11... | collective-permute-start | bytes 110600 | tf_op jit(solution)/shard_map/ppermute | solution.py:329
  74.3 6.5 %collective-permute-start.32 = (f32[72,128]{1,0:T(8,128)S(1)}, f32[72,128]{1,0:T(8,128)S(1)}, u32[]{:S(2)}, u32[]{:S(2)}) collective-permute-start(f32[72,128]{1,0:T(8,128)S(1)} %get-tuple-element.66.refs_0_), channel_id=1, source_target_pairs={{0,8},{8,0},{16,24},{24,16},{1,9},{9,1},{17,25},{25,17},{2,10},{10... | collective-permute-start | bytes 110600 | tf_op jit(solution)/shard_map/ppermute | solution.py:330
  74.9 7.5 %collective-permute-start.33 = (f32[72,128]{1,0:T(8,128)S(1)}, f32[72,128]{1,0:T(8,128)S(1)}, u32[]{:S(2)}, u32[]{:S(2)}) collective-permute-start(f32[72,128]{1,0:T(8,128)S(1)} %get-tuple-element.66.refs_0_), channel_id=1, source_target_pairs={{0,16},{8,24},{16,0},{24,8},{1,17},{9,25},{17,1},{25,9},{2,18},{10... | collective-permute-start | bytes 110600 | tf_op jit(solution)/shard_map/ppermute | solution.py:330
  76.7 5.8 %collective-permute-start.34 = (f32[72,128]{1,0:T(8,128)S(1)}, f32[72,128]{1,0:T(8,128)S(1)}, u32[]{:S(2)}, u32[]{:S(2)}) collective-permute-start(f32[72,128]{1,0:T(8,128)S(1)} %get-tuple-element.66.refs_0_), channel_id=1, source_target_pairs={{0,24},{8,16},{16,8},{24,0},{1,25},{9,17},{17,9},{25,1},{2,26},{10... | collective-permute-start | bytes 110600 | tf_op jit(solution)/shard_map/ppermute | solution.py:330
  80.2 4.2 %collective-permute-start.37 = (f32[72,128]{1,0:T(8,128)S(1)}, f32[72,128]{1,0:T(8,128)S(1)}, u32[]{:S(2)}, u32[]{:S(2)}) collective-permute-start(f32[72,128]{1,0:T(8,128)S(1)} %text_gram_cores.1.refs_4_), channel_id=1, source_target_pairs={{0,4},{1,5},{2,6},{3,7},{4,0},{5,1},{6,2},{7,3},{8,12},{9,13},{10,... | collective-permute-start | bytes 110600 | tf_op jit(solution)/shard_map/ppermute | solution.py:329
  80.9 4.9 %collective-permute-start.38 = (f32[72,128]{1,0:T(8,128)S(1)}, f32[72,128]{1,0:T(8,128)S(1)}, u32[]{:S(2)}, u32[]{:S(2)}) collective-permute-start(f32[72,128]{1,0:T(8,128)S(1)} %text_gram_cores.1.refs_4_), channel_id=1, source_target_pairs={{0,6},{1,7},{2,4},{3,5},{4,2},{5,3},{6,0},{7,1},{8,14},{9,15},{10,... | collective-permute-start | bytes 110600 | tf_op jit(solution)/shard_map/ppermute | solution.py:329
  (9 other events, 25.2 us)

commit v12 on v11

--- a/solution.py
+++ b/solution.py
@@ -117,7 +117,7 @@
             pltpu.SemaphoreType.DMA((blocks,)),
         ],
         compiler_params=pltpu.CompilerParams(vmem_limit_bytes=PANEL_LIMIT),
-        cost_estimate=cost(2 * pairs * rank * (width + a.shape[1]), 2 * pairs * (width + a.shape[1])),
+        cost_estimate=cost(1, 1),
         name=name,
     )(me, a, b, *parts)
 
@@ -355,7 +355,7 @@
     mine, own, received[-1] = lax.optimization_barrier((mine, own, received[-1]))
     text_parts = over_plane(probe_text, received)
     text_parts[0] = own
-    first, *blocks = lax.optimization_barrier((me, *[block for _, _, block in fetched]))
+    blocks = [block for _, _, block in fetched]
     last = depths[-1]
     mine = row_swap(mine, last)
     image_order = [(0, 0, None)]
@@ -363,7 +363,7 @@
 
     columns = text_rows(list(text_parts), probe_text.shape[0])
     keep, send = panel_call(
-        first, text_feats, image_feats, list(text_parts.values()), columns, n_row, groups, "image_panel"
+        me, text_feats, image_feats, list(text_parts.values()), columns, n_row, groups, "image_panel"
     )
     send, mine, *blocks = lax.optimization_barrier((send, mine, *blocks))
     swapped = [col_swap(block, 1) for block in blocks]
@@ -375,8 +375,8 @@
     image_parts += [mine, other]
     own, *image_sends = sums_call("col", 1, chips, me, [keep, col_swap(send, 1)], "image_cores")
     own, *sends = sums_call("row", 0, depths, me, [own] + over_chips(image_sends), "image_plane")
+    after_plane = sends[0]
     received = over_depth(sends)
-    after_depth = received
     mine = last_call(own, received, BF16, "image_depth")
     parts = over_plane(mine)
     ipanel, gram = gram_call("col", list(parts), me, list(parts.values()), "image_gram")
@@ -387,7 +387,7 @@
     swapped, _ = lax.optimization_barrier((col_swap(send, 1), image_sends[0]))
     own, *sends = sums_call("col", 0, chips, me, [keep, swapped], "text_cores")
     own, sends = own[0], [x[0] for x in sends]
-    own, *_ = lax.optimization_barrier((own, *after_depth))
+    own, _ = lax.optimization_barrier((own, after_plane))
     mine = last_call(own, over_chips(sends), BF16, "text_plane")
     tpanel, gram = text_gram_call([mine] + over_depth([mine] * len(depths)))
     gram = last_call(gram, [col_swap(gram, 1)], F32, "text_gram_cores")

time: 93.8 us -> 87 us (0.928)
  waiting for transfers between devices: 21.8 us -> 17.9 us
  starting transfers between devices: 45 us -> 42.1 us
    ppermute x10, starting transfers between devices: 19.4 us -> 16.1 us  [per_device(): lax.ppermute(x, 'row', [(i, i ^ s) for i in range(n_row)])]
    ppermute x10, waiting for transfers between devices: 4.52 us -> 2.11 us  [per_device(): lax.ppermute(x, 'row', [(i, i ^ s) for i in range(n_row)])]
    ppermute x28, waiting for transfers between devices: 17.3 us -> 15.8 us  [per_device(): lax.ppermute(x, 'col', [(i, i ^ s) for i in range(n_col)])]
  transfers between devices with their start and end apart: 39 -> 39, of which waited for: 16 -> 16; matrix products, arithmetic and copies ran while one was open for 1% -> 1% of each run, Pallas kernels for 17% -> 19%
where the time goes in v12:
time: 87 us; the launch traced here: 86.8 us
  starting transfers between devices  42.1 us (48%)
  Pallas kernels  24.1 us (28%)
  waiting for transfers between devices  17.9 us (21%)
  local copies, waits for them, and re-layouts  1.88 us (2%)
    ppermute x28, starting transfers between devices, per_device(): lax.ppermute(x, 'col', [(i, i ^ s) for i in range(n_col)])  22.9 us
    ppermute x10, starting transfers between devices, per_device(): lax.ppermute(x, 'row', [(i, i ^ s) for i in range(n_row)])  16.1 us
    ppermute x28, waiting for transfers between devices, per_device(): lax.ppermute(x, 'col', [(i, i ^ s) for i in range(n_col)])  15.8 us
    pallas_call x2, Pallas kernels, panel_call(): pl.pallas_call(functools.partial(panel_kernel, rows, len(parts), n_in, bl...  12.7 us
    pallas_call x1, Pallas kernels, finish_call(): pl.pallas_call(functools.partial(finish_kernel, widths, len(igrams)), in_...  7.93 us
    ppermute x1, starting transfers between devices, split_swap(): return lax.ppermute(x, ('row', 'col'), pairs)  3.09 us
    ppermute x10, waiting for transfers between devices, per_device(): lax.ppermute(x, 'row', [(i, i ^ s) for i in range(n_row)])  2.11 us
    pallas_call x3, Pallas kernels, sums_call(): pl.pallas_call(functools.partial(sums_kernel, which, axis, shifts, len(te...  1.97 us
  transfers between devices with their start and end apart: 39, of which 16 were waited for; matrix products, arithmetic and copies ran while one was open for 1% of the time, Pallas kernels for 19%

profile of v12, /device:TPU:0, one launch (start us, length us, event | category | flops | bytes accessed | tf_op | source)
XLA Modules:
  0.0 86.8 jit_solution(2591692961176036844)
XLA Ops:
  0.6 3.1 %collective-permute-start.8 = (bf16[1536,128]{1,0:T(8,128)(2,1)}, bf16[1536,128]{1,0:T(8,128)(2,1)S(1)}, u32[]{:S(2)}, u32[]{:S(2)}) collective-permute-start(bf16[1536,128]{1,0:T(8,128)(2,1)} %refs_0_.1), channel_id=1, source_target_pairs={{0,8},{1,17},{2,10},{3,19},{4,12},{5,21},{6,14},{7,23},{8,0},{9,25... | collective-permute-start | bytes 1179656 | tf_op jit(solution)/shard_map/ppermute | solution.py:348
  3.7 2.4 %collective-permute-start = (bf16[512,128]{1,0:T(8,128)(2,1)}, bf16[512,128]{1,0:T(8,128)(2,1)S(1)}, u32[]{:S(2)}, u32[]{:S(2)}) collective-permute-start(bf16[512,128]{1,0:T(8,128)(2,1)} %hbm_ref.1), channel_id=1, source_target_pairs={{0,6},{1,7},{2,4},{3,5},{4,2},{5,3},{6,0},{7,1},{8,14},{9,15},{10,... | collective-permute-start | bytes 393224 | tf_op jit(solution)/shard_map/ppermute | solution.py:329
  9.3 1.8 %collective-permute-done.refs_3_ = bf16[512,128]{1,0:T(8,128)(2,1)S(1)} collective-permute-done((bf16[512,128]{1,0:T(8,128)(2,1)}, bf16[512,128]{1,0:T(8,128)(2,1)S(1)}, u32[]{:S(2)}, u32[]{:S(2)}) %collective-permute-start) | collective-permute-done | bytes 131104 | tf_op jit(solution)/shard_map/ppermute | solution.py:329
  11.1 2.6 %collective-permute-start.7 = (bf16[768,128]{1,0:T(8,128)(2,1)S(1)}, bf16[768,128]{1,0:T(8,128)(2,1)S(1)}, u32[]{:S(2)}, u32[]{:S(2)}) collective-permute-start(bf16[768,128]{1,0:T(8,128)(2,1)S(1)} %constant_dynamic-slice_fusion), channel_id=1, source_target_pairs={{0,24},{8,16},{16,8},{24,0},{1,25},{9,17},{17,9},{25,1},{2,26},{10... | collective-permute-start | bytes 589832 | tf_op jit(solution)/shard_map/ppermute | solution.py:330
  15.6 6.1 %image_panel.1 = (f32[4,4,192,128]{3,2,1,0:T(8,128)S(1)}, f32[4,4,192,128]{3,2,1,0:T(8,128)S(1)}) custom-call(s32[2]{0:T(128)S(1)} %pad_add_fusion.me_ref, bf16[576,4096]{1,0:T(8,128)(2,1)} %b_hbm.3, bf16[576,6144]{1,0:T(8,128)(2,1)} %a_hbm.3, bf16[512,128]{1,0:T(8,128)(2,1)S(1)} %load.1.refs_0_, bf16[512,128]{1,0:T(8,128)(2,1)S(1)} %collective-permute-done.1.refs_1_, ...), custom_call_target="tpu_custom_call" | custom-call | flops 1 | bytes 1 | tf_op jit(solution)/shard_map/image_panel/pallas_call | solution.py:107
  22.3 1.5 %collective-permute-done.9.refs_4_ = bf16[768,128]{1,0:T(8,128)(2,1)S(1)} collective-permute-done((bf16[768,128]{1,0:T(8,128)(2,1)S(1)}, bf16[768,128]{1,0:T(8,128)(2,1)S(1)}, u32[]{:S(2)}, u32[]{:S(2)}) %collective-permute-start.9) | collective-permute-done | bytes 196640 | tf_op jit(solution)/shard_map/ppermute | solution.py:329
  24.0 6.6 %text_panel.1 = (f32[4,1,512,128]{3,2,1,0:T(8,128)S(1)}, f32[4,1,512,128]{3,2,1,0:T(8,128)S(1)}) custom-call(s32[2]{0:T(128)S(1)} %pad_add_fusion.me_ref, bf16[576,6144]{1,0:T(8,128)(2,1)} %a_hbm.3, bf16[576,4096]{1,0:T(8,128)(2,1)} %b_hbm.3, bf16[1536,128]{1,0:T(8,128)(2,1)S(1)} %copy-done, bf16[1536,128]{1,0:T(8,128)(2,1)S(1)} %collective-permute-done.8.refs_1_, ...), custom_call_target="tpu_custom_call" | custom-call | flops 1 | bytes 1 | tf_op jit(solution)/shard_map/text_panel/pallas_call | solution.py:107
  31.7 1.5 %collective-permute-start.12 = (bf16[4,192,128]{2,1,0:T(8,128)(2,1)S(1)}, bf16[4,192,128]{2,1,0:T(8,128)(2,1)S(1)}, u32[]{:S(2)}, u32[]{:S(2)}) collective-permute-start(bf16[4,192,128]{2,1,0:T(8,128)(2,1)S(1)} %get-tuple-element.43), channel_id=1, source_target_pairs={{0,2},{1,3},{2,0},{3,1},{4,6},{5,7},{6,4},{7,5},{8,10},{9,11},{10,... | collective-permute-start | bytes 589832 | tf_op jit(solution)/shard_map/ppermute | solution.py:329
  33.2 1.4 %collective-permute-start.13 = (bf16[4,192,128]{2,1,0:T(8,128)(2,1)S(1)}, bf16[4,192,128]{2,1,0:T(8,128)(2,1)S(1)}, u32[]{:S(2)}, u32[]{:S(2)}) collective-permute-start(bf16[4,192,128]{2,1,0:T(8,128)(2,1)S(1)} %get-tuple-element.44), channel_id=1, source_target_pairs={{0,4},{1,5},{2,6},{3,7},{4,0},{5,1},{6,2},{7,3},{8,12},{9,13},{10,... | collective-permute-start | bytes 589832 | tf_op jit(solution)/shard_map/ppermute | solution.py:329
  35.9 1.5 %collective-permute-start.26 = (bf16[512,128]{1,0:T(8,128)(2,1)S(1)}, bf16[512,128]{1,0:T(8,128)(2,1)S(1)}, u32[]{:S(2)}, u32[]{:S(2)}) collective-permute-start(bf16[512,128]{1,0:T(8,128)(2,1)S(1)} %bitcast.9), channel_id=1, source_target_pairs={{0,2},{1,3},{2,0},{3,1},{4,6},{5,7},{6,4},{7,5},{8,10},{9,11},{10,... | collective-permute-start | bytes 393224 | tf_op jit(solution)/shard_map/ppermute | solution.py:329
  37.4 1.4 %collective-permute-start.27 = (bf16[512,128]{1,0:T(8,128)(2,1)S(1)}, bf16[512,128]{1,0:T(8,128)(2,1)S(1)}, u32[]{:S(2)}, u32[]{:S(2)}) collective-permute-start(bf16[512,128]{1,0:T(8,128)(2,1)S(1)} %bitcast.8), channel_id=1, source_target_pairs={{0,4},{1,5},{2,6},{3,7},{4,0},{5,1},{6,2},{7,3},{8,12},{9,13},{10,... | collective-permute-start | bytes 393224 | tf_op jit(solution)/shard_map/ppermute | solution.py:329
  39.5 2.3 %collective-permute-start.28 = (bf16[512,128]{1,0:T(8,128)(2,1)S(1)}, bf16[512,128]{1,0:T(8,128)(2,1)S(1)}, u32[]{:S(2)}, u32[]{:S(2)}) collective-permute-start(bf16[512,128]{1,0:T(8,128)(2,1)S(1)} %bitcast.7), channel_id=1, source_target_pairs={{0,6},{1,7},{2,4},{3,5},{4,2},{5,3},{6,0},{7,1},{8,14},{9,15},{10,... | collective-permute-start | bytes 393224 | tf_op jit(solution)/shard_map/ppermute | solution.py:329
  41.8 3.3 %collective-permute-done.13.refs_2_ = bf16[4,192,128]{2,1,0:T(8,128)(2,1)S(1)} collective-permute-done((bf16[4,192,128]{2,1,0:T(8,128)(2,1)S(1)}, bf16[4,192,128]{2,1,0:T(8,128)(2,1)S(1)}, u32[]{:S(2)}, u32[]{:S(2)}) %collective-permute-start.13) | collective-permute-done | bytes 196640 | tf_op jit(solution)/shard_map/ppermute | solution.py:329
  45.7 1.4 %collective-permute-start.15 = (bf16[192,128]{1,0:T(8,128)(2,1)S(1)}, bf16[192,128]{1,0:T(8,128)(2,1)S(1)}, u32[]{:S(2)}, u32[]{:S(2)}) collective-permute-start(bf16[192,128]{1,0:T(8,128)(2,1)S(1)} %get-tuple-element.47), channel_id=1, source_target_pairs={{0,8},{8,0},{16,24},{24,16},{1,9},{9,1},{17,25},{25,17},{2,10},{10... | collective-permute-start | bytes 147464 | tf_op jit(solution)/shard_map/ppermute | solution.py:330
  47.1 1.8 %collective-permute-start.16 = (bf16[192,128]{1,0:T(8,128)(2,1)S(1)}, bf16[192,128]{1,0:T(8,128)(2,1)S(1)}, u32[]{:S(2)}, u32[]{:S(2)}) collective-permute-start(bf16[192,128]{1,0:T(8,128)(2,1)S(1)} %get-tuple-element.48), channel_id=1, source_target_pairs={{0,16},{8,24},{16,0},{24,8},{1,17},{9,25},{17,1},{25,9},{2,18},{10... | collective-permute-start | bytes 147464 | tf_op jit(solution)/shard_map/ppermute | solution.py:330
  48.9 1.4 %collective-permute-start.17 = (bf16[192,128]{1,0:T(8,128)(2,1)S(1)}, bf16[192,128]{1,0:T(8,128)(2,1)S(1)}, u32[]{:S(2)}, u32[]{:S(2)}) collective-permute-start(bf16[192,128]{1,0:T(8,128)(2,1)S(1)} %get-tuple-element.49), channel_id=1, source_target_pairs={{0,24},{8,16},{16,8},{24,0},{1,25},{9,17},{17,9},{25,1},{2,26},{10... | collective-permute-start | bytes 147464 | tf_op jit(solution)/shard_map/ppermute | solution.py:330
  51.2 2.2 %collective-permute-start.30 = (bf16[512,128]{1,0:T(8,128)(2,1)S(1)}, bf16[512,128]{1,0:T(8,128)(2,1)S(1)}, u32[]{:S(2)}, u32[]{:S(2)}) collective-permute-start(bf16[512,128]{1,0:T(8,128)(2,1)S(1)} %text_plane.1.refs_0_), channel_id=1, source_target_pairs={{0,16},{8,24},{16,0},{24,8},{1,17},{9,25},{17,1},{25,9},{2,18},{10... | collective-permute-start | bytes 393224 | tf_op jit(solution)/shard_map/ppermute | solution.py:330
  53.4 1.9 %collective-permute-done.17.refs_2_ = bf16[192,128]{1,0:T(8,128)(2,1)S(1)} collective-permute-done((bf16[192,128]{1,0:T(8,128)(2,1)S(1)}, bf16[192,128]{1,0:T(8,128)(2,1)S(1)}, u32[]{:S(2)}, u32[]{:S(2)}) %collective-permute-start.17) | collective-permute-done | bytes 49184 | tf_op jit(solution)/shard_map/ppermute | solution.py:330
  55.3 1.1 %collective-permute-start.18 = (bf16[192,128]{1,0:T(8,128)(2,1)S(1)}, bf16[192,128]{1,0:T(8,128)(2,1)S(1)}, u32[]{:S(2)}, u32[]{:S(2)}) collective-permute-start(bf16[192,128]{1,0:T(8,128)(2,1)S(1)} %image_depth.1.refs_0_), channel_id=1, source_target_pairs={{0,2},{1,3},{2,0},{3,1},{4,6},{5,7},{6,4},{7,5},{8,10},{9,11},{10,... | collective-permute-start | bytes 147464 | tf_op jit(solution)/shard_map/ppermute | solution.py:329
  56.5 1.4 %collective-permute-start.31 = (bf16[512,128]{1,0:T(8,128)(2,1)S(1)}, bf16[512,128]{1,0:T(8,128)(2,1)S(1)}, u32[]{:S(2)}, u32[]{:S(2)}) collective-permute-start(bf16[512,128]{1,0:T(8,128)(2,1)S(1)} %text_plane.1.refs_0_), channel_id=1, source_target_pairs={{0,24},{8,16},{16,8},{24,0},{1,25},{9,17},{17,9},{25,1},{2,26},{10... | collective-permute-start | bytes 393224 | tf_op jit(solution)/shard_map/ppermute | solution.py:330
  57.9 1.2 %collective-permute-start.19 = (bf16[192,128]{1,0:T(8,128)(2,1)S(1)}, bf16[192,128]{1,0:T(8,128)(2,1)S(1)}, u32[]{:S(2)}, u32[]{:S(2)}) collective-permute-start(bf16[192,128]{1,0:T(8,128)(2,1)S(1)} %image_depth.1.refs_0_), channel_id=1, source_target_pairs={{0,4},{1,5},{2,6},{3,7},{4,0},{5,1},{6,2},{7,3},{8,12},{9,13},{10,... | collective-permute-start | bytes 147464 | tf_op jit(solution)/shard_map/ppermute | solution.py:329
  59.5 1.7 %collective-permute-start.20 = (bf16[192,128]{1,0:T(8,128)(2,1)S(1)}, bf16[192,128]{1,0:T(8,128)(2,1)S(1)}, u32[]{:S(2)}, u32[]{:S(2)}) collective-permute-start(bf16[192,128]{1,0:T(8,128)(2,1)S(1)} %image_depth.1.refs_0_), channel_id=1, source_target_pairs={{0,6},{1,7},{2,4},{3,5},{4,2},{5,3},{6,0},{7,1},{8,14},{9,15},{10,... | collective-permute-start | bytes 147464 | tf_op jit(solution)/shard_map/ppermute | solution.py:329
  62.0 2.5 %collective-permute-done.20.refs_3_ = bf16[192,128]{1,0:T(8,128)(2,1)S(1)} collective-permute-done((bf16[192,128]{1,0:T(8,128)(2,1)S(1)}, bf16[192,128]{1,0:T(8,128)(2,1)S(1)}, u32[]{:S(2)}, u32[]{:S(2)}) %collective-permute-start.20) | collective-permute-done | bytes 49184 | tf_op jit(solution)/shard_map/ppermute | solution.py:329
  66.2 1.0 %image_gram.1 = (bf16[8,192,128]{2,1,0:T(8,128)(2,1)S(1)}, f32[72,128]{1,0:T(8,128)S(1)}) custom-call(s32[2]{0:T(128)S(1)} %pad_add_fusion.me_ref, bf16[192,128]{1,0:T(8,128)(2,1)S(1)} %image_depth.1.refs_0_, bf16[192,128]{1,0:T(8,128)(2,1)S(1)} %collective-permute-done.18.refs_1_, bf16[192,128]{1,0:T(8,128)(2,1)S(1)} %collective-permute-done.19.refs_2_, ...), custom_call_target="tpu_custom_call" | custom-call | flops 50331648 | bytes 786432 | tf_op jit(solution)/shard_map/image_gram/pallas_call | solution.py:215
  67.2 1.0 %collective-permute-start.32 = (f32[72,128]{1,0:T(8,128)S(1)}, f32[72,128]{1,0:T(8,128)S(1)}, u32[]{:S(2)}, u32[]{:S(2)}) collective-permute-start(f32[72,128]{1,0:T(8,128)S(1)} %get-tuple-element.62.refs_0_), channel_id=1, source_target_pairs={{0,8},{8,0},{16,24},{24,16},{1,9},{9,1},{17,25},{25,17},{2,10},{10... | collective-permute-start | bytes 110600 | tf_op jit(solution)/shard_map/ppermute | solution.py:330
  68.2 1.6 %collective-permute-start.33 = (f32[72,128]{1,0:T(8,128)S(1)}, f32[72,128]{1,0:T(8,128)S(1)}, u32[]{:S(2)}, u32[]{:S(2)}) collective-permute-start(f32[72,128]{1,0:T(8,128)S(1)} %get-tuple-element.62.refs_0_), channel_id=1, source_target_pairs={{0,16},{8,24},{16,0},{24,8},{1,17},{9,25},{17,1},{25,9},{2,18},{10... | collective-permute-start | bytes 110600 | tf_op jit(solution)/shard_map/ppermute | solution.py:330
  69.9 1.8 %collective-permute-start.34 = (f32[72,128]{1,0:T(8,128)S(1)}, f32[72,128]{1,0:T(8,128)S(1)}, u32[]{:S(2)}, u32[]{:S(2)}) collective-permute-start(f32[72,128]{1,0:T(8,128)S(1)} %get-tuple-element.62.refs_0_), channel_id=1, source_target_pairs={{0,24},{8,16},{16,8},{24,0},{1,25},{9,17},{17,9},{25,1},{2,26},{10... | collective-permute-start | bytes 110600 | tf_op jit(solution)/shard_map/ppermute | solution.py:330
  71.7 1.6 %collective-permute-start.36 = (f32[72,128]{1,0:T(8,128)S(1)}, f32[72,128]{1,0:T(8,128)S(1)}, u32[]{:S(2)}, u32[]{:S(2)}) collective-permute-start(f32[72,128]{1,0:T(8,128)S(1)} %text_gram_cores.1.refs_4_), channel_id=1, source_target_pairs={{0,2},{1,3},{2,0},{3,1},{4,6},{5,7},{6,4},{7,5},{8,10},{9,11},{10,... | collective-permute-start | bytes 110600 | tf_op jit(solution)/shard_map/ppermute | solution.py:329
  74.0 1.4 %collective-permute-start.38 = (f32[72,128]{1,0:T(8,128)S(1)}, f32[72,128]{1,0:T(8,128)S(1)}, u32[]{:S(2)}, u32[]{:S(2)}) collective-permute-start(f32[72,128]{1,0:T(8,128)S(1)} %text_gram_cores.1.refs_4_), channel_id=1, source_target_pairs={{0,6},{1,7},{2,4},{3,5},{4,2},{5,3},{6,0},{7,1},{8,14},{9,15},{10,... | collective-permute-start | bytes 110600 | tf_op jit(solution)/shard_map/ppermute | solution.py:329
  75.7 1.7 %collective-permute-done.37.refs_6_ = f32[72,128]{1,0:T(8,128)S(1)} collective-permute-done((f32[72,128]{1,0:T(8,128)S(1)}, f32[72,128]{1,0:T(8,128)S(1)}, u32[]{:S(2)}, u32[]{:S(2)}) %collective-permute-start.37) | collective-permute-done | bytes 36896 | tf_op jit(solution)/shard_map/ppermute | solution.py:329
  77.4 1.5 %collective-permute-done.38.refs_7_ = f32[72,128]{1,0:T(8,128)S(1)} collective-permute-done((f32[72,128]{1,0:T(8,128)S(1)}, f32[72,128]{1,0:T(8,128)S(1)}, u32[]{:S(2)}, u32[]{:S(2)}) %collective-permute-start.38) | collective-permute-done | bytes 36896 | tf_op jit(solution)/shard_map/ppermute | solution.py:329
  78.9 7.9 %finish.1 = (f32[1536,128]{1,0:T(8,128)}, f32[512,128]{1,0:T(8,128)}) custom-call(bf16[8,192,128]{2,1,0:T(8,128)(2,1)S(1)} %get-tuple-element.50.ipanel, bf16[1,512,128]{2,1,0:T(8,128)(2,1)S(1)} %get-tuple-element.61.tpanel, f32[72,128]{1,0:T(8,128)S(1)} %get-tuple-element.62.refs_0_, f32[72,128]{1,0:T(8,128)S(1)} %collective-permute-done.32.refs_1_, ...), custom_call_target="tpu_custom_call" | custom-call | flops 10000000000 | bytes 1179648 | tf_op jit(solution)/shard_map/finish/pallas_call | solution.py:315
  (64 shorter events, 14.3 us)
Async XLA Ops:
  0.6 21.1 %collective-permute-start.8 = (bf16[1536,128]{1,0:T(8,128)(2,1)}, bf16[1536,128]{1,0:T(8,128)(2,1)S(1)}, u32[]{:S(2)}, u32[]{:S(2)}) collective-permute-start(bf16[1536,128]{1,0:T(8,128)(2,1)} %refs_0_.1), channel_id=1, source_target_pairs={{0,8},{1,17},{2,10},{3,19},{4,12},{5,21},{6,14},{7,23},{8,0},{9,25... | collective-permute-start | bytes 1179656 | tf_op jit(solution)/shard_map/ppermute | solution.py:348
  3.7 7.4 %collective-permute-start = (bf16[512,128]{1,0:T(8,128)(2,1)}, bf16[512,128]{1,0:T(8,128)(2,1)S(1)}, u32[]{:S(2)}, u32[]{:S(2)}) collective-permute-start(bf16[512,128]{1,0:T(8,128)(2,1)} %hbm_ref.1), channel_id=1, source_target_pairs={{0,6},{1,7},{2,4},{3,5},{4,2},{5,3},{6,0},{7,1},{8,14},{9,15},{10,... | collective-permute-start | bytes 393224 | tf_op jit(solution)/shard_map/ppermute | solution.py:329
  6.2 7.5 %collective-permute-start.1 = (bf16[512,128]{1,0:T(8,128)(2,1)}, bf16[512,128]{1,0:T(8,128)(2,1)S(1)}, u32[]{:S(2)}, u32[]{:S(2)}) collective-permute-start(bf16[512,128]{1,0:T(8,128)(2,1)} %hbm_ref.1), channel_id=1, source_target_pairs={{0,2},{1,3},{2,0},{3,1},{4,6},{5,7},{6,4},{7,5},{8,10},{9,11},{10,... | collective-permute-start | bytes 393224 | tf_op jit(solution)/shard_map/ppermute | solution.py:329
  6.7 7.0 %collective-permute-start.2 = (bf16[512,128]{1,0:T(8,128)(2,1)}, bf16[512,128]{1,0:T(8,128)(2,1)S(1)}, u32[]{:S(2)}, u32[]{:S(2)}) collective-permute-start(bf16[512,128]{1,0:T(8,128)(2,1)} %hbm_ref.1), channel_id=1, source_target_pairs={{0,4},{1,5},{2,6},{3,7},{4,0},{5,1},{6,2},{7,3},{8,12},{9,13},{10,... | collective-permute-start | bytes 393224 | tf_op jit(solution)/shard_map/ppermute | solution.py:329
  7.2 7.0 %collective-permute-start.3 = (bf16[512,128]{1,0:T(8,128)(2,1)}, bf16[512,128]{1,0:T(8,128)(2,1)S(1)}, u32[]{:S(2)}, u32[]{:S(2)}) collective-permute-start(bf16[512,128]{1,0:T(8,128)(2,1)} %hbm_ref.1), channel_id=1, source_target_pairs={{0,1},{1,0},{2,3},{3,2},{4,5},{5,4},{6,7},{7,6},{8,9},{9,8},{10,11... | collective-permute-start | bytes 393224 | tf_op jit(solution)/shard_map/ppermute | solution.py:329
  11.1 10.6 %collective-permute-start.7 = (bf16[768,128]{1,0:T(8,128)(2,1)S(1)}, bf16[768,128]{1,0:T(8,128)(2,1)S(1)}, u32[]{:S(2)}, u32[]{:S(2)}) collective-permute-start(bf16[768,128]{1,0:T(8,128)(2,1)S(1)} %constant_dynamic-slice_fusion), channel_id=1, source_target_pairs={{0,24},{8,16},{16,8},{24,0},{1,25},{9,17},{17,9},{25,1},{2,26},{10... | collective-permute-start | bytes 589832 | tf_op jit(solution)/shard_map/ppermute | solution.py:330
  21.7 2.1 %collective-permute-start.10 = (bf16[1536,128]{1,0:T(8,128)(2,1)S(1)}, bf16[1536,128]{1,0:T(8,128)(2,1)S(1)}, u32[]{:S(2)}, u32[]{:S(2)}) collective-permute-start(bf16[1536,128]{1,0:T(8,128)(2,1)S(1)} %collective-permute-done.8.refs_1_), channel_id=1, source_target_pairs={{0,1},{1,0},{2,3},{3,2},{4,5},{5,4},{6,7},{7,6},{8,9},{9,8},{10,11... | collective-permute-start | bytes 1179656 | tf_op jit(solution)/shard_map/ppermute | solution.py:329
  23.8 7.2 %collective-permute-start.11 = (f32[4,4,192,128]{3,2,1,0:T(8,128)S(1)}, f32[4,4,192,128]{3,2,1,0:T(8,128)S(1)}, u32[]{:S(2)}, u32[]{:S(2)}) collective-permute-start(f32[4,4,192,128]{3,2,1,0:T(8,128)S(1)} %get-tuple-element.41), channel_id=1, source_target_pairs={{0,1},{1,0},{2,3},{3,2},{4,5},{5,4},{6,7},{7,6},{8,9},{9,8},{10,11... | collective-permute-start | bytes 4718600 | tf_op jit(solution)/shard_map/ppermute | solution.py:329
  30.5 4.7 %collective-permute-start.25 = (f32[4,1,512,128]{3,2,1,0:T(8,128)S(1)}, f32[4,1,512,128]{3,2,1,0:T(8,128)S(1)}, u32[]{:S(2)}, u32[]{:S(2)}) collective-permute-start(f32[4,1,512,128]{3,2,1,0:T(8,128)S(1)} %get-tuple-element.54), channel_id=1, source_target_pairs={{0,1},{1,0},{2,3},{3,2},{4,5},{5,4},{6,7},{7,6},{8,9},{9,8},{10,11... | collective-permute-start | bytes 3145736 | tf_op jit(solution)/shard_map/ppermute | solution.py:329
  31.7 7.8 %collective-permute-start.12 = (bf16[4,192,128]{2,1,0:T(8,128)(2,1)S(1)}, bf16[4,192,128]{2,1,0:T(8,128)(2,1)S(1)}, u32[]{:S(2)}, u32[]{:S(2)}) collective-permute-start(bf16[4,192,128]{2,1,0:T(8,128)(2,1)S(1)} %get-tuple-element.43), channel_id=1, source_target_pairs={{0,2},{1,3},{2,0},{3,1},{4,6},{5,7},{6,4},{7,5},{8,10},{9,11},{10,... | collective-permute-start | bytes 589832 | tf_op jit(solution)/shard_map/ppermute | solution.py:329
  33.2 11.8 %collective-permute-start.13 = (bf16[4,192,128]{2,1,0:T(8,128)(2,1)S(1)}, bf16[4,192,128]{2,1,0:T(8,128)(2,1)S(1)}, u32[]{:S(2)}, u32[]{:S(2)}) collective-permute-start(bf16[4,192,128]{2,1,0:T(8,128)(2,1)S(1)} %get-tuple-element.44), channel_id=1, source_target_pairs={{0,4},{1,5},{2,6},{3,7},{4,0},{5,1},{6,2},{7,3},{8,12},{9,13},{10,... | collective-permute-start | bytes 589832 | tf_op jit(solution)/shard_map/ppermute | solution.py:329
  34.6 10.4 %collective-permute-start.14 = (bf16[4,192,128]{2,1,0:T(8,128)(2,1)S(1)}, bf16[4,192,128]{2,1,0:T(8,128)(2,1)S(1)}, u32[]{:S(2)}, u32[]{:S(2)}) collective-permute-start(bf16[4,192,128]{2,1,0:T(8,128)(2,1)S(1)} %get-tuple-element.45), channel_id=1, source_target_pairs={{0,6},{1,7},{2,4},{3,5},{4,2},{5,3},{6,0},{7,1},{8,14},{9,15},{10,... | collective-permute-start | bytes 589832 | tf_op jit(solution)/shard_map/ppermute | solution.py:329
  35.9 13.0 %collective-permute-start.26 = (bf16[512,128]{1,0:T(8,128)(2,1)S(1)}, bf16[512,128]{1,0:T(8,128)(2,1)S(1)}, u32[]{:S(2)}, u32[]{:S(2)}) collective-permute-start(bf16[512,128]{1,0:T(8,128)(2,1)S(1)} %bitcast.9), channel_id=1, source_target_pairs={{0,2},{1,3},{2,0},{3,1},{4,6},{5,7},{6,4},{7,5},{8,10},{9,11},{10,... | collective-permute-start | bytes 393224 | tf_op jit(solution)/shard_map/ppermute | solution.py:329
  37.4 12.9 %collective-permute-start.27 = (bf16[512,128]{1,0:T(8,128)(2,1)S(1)}, bf16[512,128]{1,0:T(8,128)(2,1)S(1)}, u32[]{:S(2)}, u32[]{:S(2)}) collective-permute-start(bf16[512,128]{1,0:T(8,128)(2,1)S(1)} %bitcast.8), channel_id=1, source_target_pairs={{0,4},{1,5},{2,6},{3,7},{4,0},{5,1},{6,2},{7,3},{8,12},{9,13},{10,... | collective-permute-start | bytes 393224 | tf_op jit(solution)/shard_map/ppermute | solution.py:329
  39.5 10.8 %collective-permute-start.28 = (bf16[512,128]{1,0:T(8,128)(2,1)S(1)}, bf16[512,128]{1,0:T(8,128)(2,1)S(1)}, u32[]{:S(2)}, u32[]{:S(2)}) collective-permute-start(bf16[512,128]{1,0:T(8,128)(2,1)S(1)} %bitcast.7), channel_id=1, source_target_pairs={{0,6},{1,7},{2,4},{3,5},{4,2},{5,3},{6,0},{7,1},{8,14},{9,15},{10,... | collective-permute-start | bytes 393224 | tf_op jit(solution)/shard_map/ppermute | solution.py:329
  45.7 7.7 %collective-permute-start.15 = (bf16[192,128]{1,0:T(8,128)(2,1)S(1)}, bf16[192,128]{1,0:T(8,128)(2,1)S(1)}, u32[]{:S(2)}, u32[]{:S(2)}) collective-permute-start(bf16[192,128]{1,0:T(8,128)(2,1)S(1)} %get-tuple-element.47), channel_id=1, source_target_pairs={{0,8},{8,0},{16,24},{24,16},{1,9},{9,1},{17,25},{25,17},{2,10},{10... | collective-permute-start | bytes 147464 | tf_op jit(solution)/shard_map/ppermute | solution.py:330
  47.1 6.4 %collective-permute-start.16 = (bf16[192,128]{1,0:T(8,128)(2,1)S(1)}, bf16[192,128]{1,0:T(8,128)(2,1)S(1)}, u32[]{:S(2)}, u32[]{:S(2)}) collective-permute-start(bf16[192,128]{1,0:T(8,128)(2,1)S(1)} %get-tuple-element.48), channel_id=1, source_target_pairs={{0,16},{8,24},{16,0},{24,8},{1,17},{9,25},{17,1},{25,9},{2,18},{10... | collective-permute-start | bytes 147464 | tf_op jit(solution)/shard_map/ppermute | solution.py:330
  48.9 6.4 %collective-permute-start.17 = (bf16[192,128]{1,0:T(8,128)(2,1)S(1)}, bf16[192,128]{1,0:T(8,128)(2,1)S(1)}, u32[]{:S(2)}, u32[]{:S(2)}) collective-permute-start(bf16[192,128]{1,0:T(8,128)(2,1)S(1)} %get-tuple-element.49), channel_id=1, source_target_pairs={{0,24},{8,16},{16,8},{24,0},{1,25},{9,17},{17,9},{25,1},{2,26},{10... | collective-permute-start | bytes 147464 | tf_op jit(solution)/shard_map/ppermute | solution.py:330
  50.4 14.1 %collective-permute-start.29 = (bf16[512,128]{1,0:T(8,128)(2,1)S(1)}, bf16[512,128]{1,0:T(8,128)(2,1)S(1)}, u32[]{:S(2)}, u32[]{:S(2)}) collective-permute-start(bf16[512,128]{1,0:T(8,128)(2,1)S(1)} %text_plane.1.refs_0_), channel_id=1, source_target_pairs={{0,8},{8,0},{16,24},{24,16},{1,9},{9,1},{17,25},{25,17},{2,10},{10... | collective-permute-start | bytes 393224 | tf_op jit(solution)/shard_map/ppermute | solution.py:330
  51.2 13.8 %collective-permute-start.30 = (bf16[512,128]{1,0:T(8,128)(2,1)S(1)}, bf16[512,128]{1,0:T(8,128)(2,1)S(1)}, u32[]{:S(2)}, u32[]{:S(2)}) collective-permute-start(bf16[512,128]{1,0:T(8,128)(2,1)S(1)} %text_plane.1.refs_0_), channel_id=1, source_target_pairs={{0,16},{8,24},{16,0},{24,8},{1,17},{9,25},{17,1},{25,9},{2,18},{10... | collective-permute-start | bytes 393224 | tf_op jit(solution)/shard_map/ppermute | solution.py:330
  55.3 4.2 %collective-permute-start.18 = (bf16[192,128]{1,0:T(8,128)(2,1)S(1)}, bf16[192,128]{1,0:T(8,128)(2,1)S(1)}, u32[]{:S(2)}, u32[]{:S(2)}) collective-permute-start(bf16[192,128]{1,0:T(8,128)(2,1)S(1)} %image_depth.1.refs_0_), channel_id=1, source_target_pairs={{0,2},{1,3},{2,0},{3,1},{4,6},{5,7},{6,4},{7,5},{8,10},{9,11},{10,... | collective-permute-start | bytes 147464 | tf_op jit(solution)/shard_map/ppermute | solution.py:329
  56.5 8.6 %collective-permute-start.31 = (bf16[512,128]{1,0:T(8,128)(2,1)S(1)}, bf16[512,128]{1,0:T(8,128)(2,1)S(1)}, u32[]{:S(2)}, u32[]{:S(2)}) collective-permute-start(bf16[512,128]{1,0:T(8,128)(2,1)S(1)} %text_plane.1.refs_0_), channel_id=1, source_target_pairs={{0,24},{8,16},{16,8},{24,0},{1,25},{9,17},{17,9},{25,1},{2,26},{10... | collective-permute-start | bytes 393224 | tf_op jit(solution)/shard_map/ppermute | solution.py:330
  57.9 4.1 %collective-permute-start.19 = (bf16[192,128]{1,0:T(8,128)(2,1)S(1)}, bf16[192,128]{1,0:T(8,128)(2,1)S(1)}, u32[]{:S(2)}, u32[]{:S(2)}) collective-permute-start(bf16[192,128]{1,0:T(8,128)(2,1)S(1)} %image_depth.1.refs_0_), channel_id=1, source_target_pairs={{0,4},{1,5},{2,6},{3,7},{4,0},{5,1},{6,2},{7,3},{8,12},{9,13},{10,... | collective-permute-start | bytes 147464 | tf_op jit(solution)/shard_map/ppermute | solution.py:329
  59.5 5.0 %collective-permute-start.20 = (bf16[192,128]{1,0:T(8,128)(2,1)S(1)}, bf16[192,128]{1,0:T(8,128)(2,1)S(1)}, u32[]{:S(2)}, u32[]{:S(2)}) collective-permute-start(bf16[192,128]{1,0:T(8,128)(2,1)S(1)} %image_depth.1.refs_0_), channel_id=1, source_target_pairs={{0,6},{1,7},{2,4},{3,5},{4,2},{5,3},{6,0},{7,1},{8,14},{9,15},{10,... | collective-permute-start | bytes 147464 | tf_op jit(solution)/shard_map/ppermute | solution.py:329
  62.0 3.9 %collective-permute-start.21 = (bf16[192,128]{1,0:T(8,128)(2,1)S(1)}, bf16[192,128]{1,0:T(8,128)(2,1)S(1)}, u32[]{:S(2)}, u32[]{:S(2)}) collective-permute-start(bf16[192,128]{1,0:T(8,128)(2,1)S(1)} %image_depth.1.refs_0_), channel_id=1, source_target_pairs={{0,1},{1,0},{2,3},{3,2},{4,5},{5,4},{6,7},{7,6},{8,9},{9,8},{10,11... | collective-permute-start | bytes 147464 | tf_op jit(solution)/shard_map/ppermute | solution.py:329
  65.4 6.3 %collective-permute-start.35 = (f32[72,128]{1,0:T(8,128)S(1)}, f32[72,128]{1,0:T(8,128)S(1)}, u32[]{:S(2)}, u32[]{:S(2)}) collective-permute-start(f32[72,128]{1,0:T(8,128)S(1)} %get-tuple-element.63.own_ref), channel_id=1, source_target_pairs={{0,1},{1,0},{2,3},{3,2},{4,5},{5,4},{6,7},{7,6},{8,9},{9,8},{10,11... | collective-permute-start | bytes 110600 | tf_op jit(solution)/shard_map/ppermute | solution.py:329
  67.2 6.8 %collective-permute-start.32 = (f32[72,128]{1,0:T(8,128)S(1)}, f32[72,128]{1,0:T(8,128)S(1)}, u32[]{:S(2)}, u32[]{:S(2)}) collective-permute-start(f32[72,128]{1,0:T(8,128)S(1)} %get-tuple-element.62.refs_0_), channel_id=1, source_target_pairs={{0,8},{8,0},{16,24},{24,16},{1,9},{9,1},{17,25},{25,17},{2,10},{10... | collective-permute-start | bytes 110600 | tf_op jit(solution)/shard_map/ppermute | solution.py:330
  68.2 7.2 %collective-permute-start.33 = (f32[72,128]{1,0:T(8,128)S(1)}, f32[72,128]{1,0:T(8,128)S(1)}, u32[]{:S(2)}, u32[]{:S(2)}) collective-permute-start(f32[72,128]{1,0:T(8,128)S(1)} %get-tuple-element.62.refs_0_), channel_id=1, source_target_pairs={{0,16},{8,24},{16,0},{24,8},{1,17},{9,25},{17,1},{25,9},{2,18},{10... | collective-permute-start | bytes 110600 | tf_op jit(solution)/shard_map/ppermute | solution.py:330
  69.9 5.8 %collective-permute-start.34 = (f32[72,128]{1,0:T(8,128)S(1)}, f32[72,128]{1,0:T(8,128)S(1)}, u32[]{:S(2)}, u32[]{:S(2)}) collective-permute-start(f32[72,128]{1,0:T(8,128)S(1)} %get-tuple-element.62.refs_0_), channel_id=1, source_target_pairs={{0,24},{8,16},{16,8},{24,0},{1,25},{9,17},{17,9},{25,1},{2,26},{10... | collective-permute-start | bytes 110600 | tf_op jit(solution)/shard_map/ppermute | solution.py:330
  71.7 4.0 %collective-permute-start.36 = (f32[72,128]{1,0:T(8,128)S(1)}, f32[72,128]{1,0:T(8,128)S(1)}, u32[]{:S(2)}, u32[]{:S(2)}) collective-permute-start(f32[72,128]{1,0:T(8,128)S(1)} %text_gram_cores.1.refs_4_), channel_id=1, source_target_pairs={{0,2},{1,3},{2,0},{3,1},{4,6},{5,7},{6,4},{7,5},{8,10},{9,11},{10,... | collective-permute-start | bytes 110600 | tf_op jit(solution)/shard_map/ppermute | solution.py:329
  73.3 4.1 %collective-permute-start.37 = (f32[72,128]{1,0:T(8,128)S(1)}, f32[72,128]{1,0:T(8,128)S(1)}, u32[]{:S(2)}, u32[]{:S(2)}) collective-permute-start(f32[72,128]{1,0:T(8,128)S(1)} %text_gram_cores.1.refs_4_), channel_id=1, source_target_pairs={{0,4},{1,5},{2,6},{3,7},{4,0},{5,1},{6,2},{7,3},{8,12},{9,13},{10,... | collective-permute-start | bytes 110600 | tf_op jit(solution)/shard_map/ppermute | solution.py:329
  74.0 4.9 %collective-permute-start.38 = (f32[72,128]{1,0:T(8,128)S(1)}, f32[72,128]{1,0:T(8,128)S(1)}, u32[]{:S(2)}, u32[]{:S(2)}) collective-permute-start(f32[72,128]{1,0:T(8,128)S(1)} %text_gram_cores.1.refs_4_), channel_id=1, source_target_pairs={{0,6},{1,7},{2,4},{3,5},{4,2},{5,3},{6,0},{7,1},{8,14},{9,15},{10,... | collective-permute-start | bytes 110600 | tf_op jit(solution)/shard_map/ppermute | solution.py:329
  (9 other events, 20.6 us)

commit v13 on v12

--- a/solution.py
+++ b/solution.py
@@ -286,41 +286,35 @@
     yield jnp.concatenate(rows, axis=0)
 
 
-def finish_kernel(widths, n_image, ipanel, tpanel, *refs):
-    *grams, iout, tout = refs
-
-    def total(refs):
-        value = refs[0][...]
-        for ref in refs[1:]:
-            value = value + ref[...]
-        return unpack(value)
-
-    inverses = None
-    for inverses in zip(inverse_factor(total(grams[:n_image])), inverse_factor(total(grams[n_image:]))):
+def finish_kernel(width, panel_ref, *refs):
+    *grams, out_ref = refs
+    total = grams[0][...]
+    for ref in grams[1:]:
+        total = total + ref[...]
+    inverse = None
+    for inverse in inverse_factor(unpack(total)):
         pass
+    inverse = inverse * math.sqrt(width)
+    high = inverse.astype(BF16)
+    low = (inverse - high.astype(F32)).astype(BF16)
     dims = (((1,), (1,)), ((), ()))
-    for inverse, width, panel_ref, out_ref in zip(inverses, widths, (ipanel, tpanel), (iout, tout)):
-        inverse = inverse * math.sqrt(width)
-        high = inverse.astype(BF16)
-        low = (inverse - high.astype(F32)).astype(BF16)
-        panel = panel_ref[...].reshape(out_ref.shape)
-        out_ref[...] = lax.dot_general(panel, high, dims, preferred_element_type=F32) + lax.dot_general(
-            panel, low, dims, preferred_element_type=F32
-        )
-
-
-def finish_call(widths, ipanel, igrams, tpanel, tgrams):
-    rank = ipanel.shape[-1]
-    outs = [sds((math.prod(p.shape[:-1]), rank), F32) for p in (ipanel, tpanel)]
-    return pl.pallas_call(
-        functools.partial(finish_kernel, widths, len(igrams)),
-        in_specs=[VMEM] * (2 + len(igrams) + len(tgrams)),
-        out_specs=[VMEM] * 2,
-        out_shape=outs,
-        compiler_params=params(),
-        cost_estimate=cost(10**10, 6 * ipanel.size),
-        name="finish",
-    )(ipanel, tpanel, *igrams, *tgrams)
+    panel = panel_ref[...].reshape(out_ref.shape)
+    out_ref[...] = lax.dot_general(panel, high, dims, preferred_element_type=F32) + lax.dot_general(
+        panel, low, dims, preferred_element_type=F32
+    )
+
+
+def finish_call(width, panel, grams, name):
+    n, rows, rank = panel.shape
+    return pl.pallas_call(
+        functools.partial(finish_kernel, width),
+        in_specs=[VMEM] * (1 + len(grams)),
+        out_specs=VMEM,
+        out_shape=sds((n * rows, rank), F32),
+        compiler_params=params(),
+        cost_estimate=cost(5 * 10**9, 6 * n * rows * rank),
+        name=name,
+    )(panel, *grams)
 
 
 def per_device(n_row, n_col, image_feats, text_feats, probe_image, probe_text):
@@ -393,8 +387,10 @@
     gram = last_call(gram, [col_swap(gram, 1)], F32, "text_gram_cores")
     tgrams = [gram] + over_chips([gram] * len(chips))
 
-    widths = (image_feats.shape[1], text_feats.shape[1])
-    return finish_call(widths, ipanel, igrams, tpanel, tgrams)
+    return (
+        finish_call(image_feats.shape[1], ipanel, igrams, "image_finish"),
+        finish_call(text_feats.shape[1], tpanel, tgrams, "text_finish"),
+    )
 
 
 def solution(mesh):

time: 87 us -> 87.8 us (level)
  Pallas kernels: 24.1 us -> 28.1 us
  waiting for transfers between devices: 17.9 us -> 14.6 us
    pallas_call x1 -> x2, Pallas kernels: 7.93 us -> 12 us  [finish_call(): pl.pallas_call(functools.partial(finish_kernel, width), in_specs=[VMEM] *...]
    ppermute x28, waiting for transfers between devices: 15.8 us -> 12.5 us  [per_device(): lax.ppermute(x, 'col', [(i, i ^ s) for i in range(n_col)])]
  transfers between devices with their start and end apart: 39 -> 39, of which waited for: 16 -> 13; matrix products, arithmetic and copies ran while one was open for 1% -> 1% of each run, Pallas kernels for 19% -> 26%
where the time goes in v13:
time: 87.8 us; the launch traced here: 87.6 us
  starting transfers between devices  42.1 us (48%)
  Pallas kernels  28.1 us (32%)
  waiting for transfers between devices  14.6 us (17%)
  local copies, waits for them, and re-layouts  1.88 us (2%)
    ppermute x28, starting transfers between devices, per_device(): lax.ppermute(x, 'col', [(i, i ^ s) for i in range(n_col)])  22.9 us
    ppermute x10, starting transfers between devices, per_device(): lax.ppermute(x, 'row', [(i, i ^ s) for i in range(n_row)])  16.1 us
    pallas_call x2, Pallas kernels, panel_call(): pl.pallas_call(functools.partial(panel_kernel, rows, len(parts), n_in, bl...  12.7 us
    ppermute x28, waiting for transfers between devices, per_device(): lax.ppermute(x, 'col', [(i, i ^ s) for i in range(n_col)])  12.5 us
    pallas_call x2, Pallas kernels, finish_call(): pl.pallas_call(functools.partial(finish_kernel, width), in_specs=[VMEM] *...  12 us
    ppermute x1, starting transfers between devices, split_swap(): return lax.ppermute(x, ('row', 'col'), pairs)  3.09 us
    ppermute x10, waiting for transfers between devices, per_device(): lax.ppermute(x, 'row', [(i, i ^ s) for i in range(n_row)])  2.11 us
    pallas_call x3, Pallas kernels, sums_call(): pl.pallas_call(functools.partial(sums_kernel, which, axis, shifts, len(te...  1.97 us
  transfers between devices with their start and end apart: 39, of which 13 were waited for; matrix products, arithmetic and copies ran while one was open for 1% of the time, Pallas kernels for 26%

profile of v13, /device:TPU:0, one launch (start us, length us, event | category | flops | bytes accessed | tf_op | source)
XLA Modules:
  0.0 87.6 jit_solution(15542574096815351009)
XLA Ops:
  0.6 3.1 %collective-permute-start.8 = (bf16[1536,128]{1,0:T(8,128)(2,1)}, bf16[1536,128]{1,0:T(8,128)(2,1)S(1)}, u32[]{:S(2)}, u32[]{:S(2)}) collective-permute-start(bf16[1536,128]{1,0:T(8,128)(2,1)} %refs_0_.1), channel_id=1, source_target_pairs={{0,8},{1,17},{2,10},{3,19},{4,12},{5,21},{6,14},{7,23},{8,0},{9,25... | collective-permute-start | bytes 1179656 | tf_op jit(solution)/shard_map/ppermute | solution.py:342
  3.7 2.4 %collective-permute-start = (bf16[512,128]{1,0:T(8,128)(2,1)}, bf16[512,128]{1,0:T(8,128)(2,1)S(1)}, u32[]{:S(2)}, u32[]{:S(2)}) collective-permute-start(bf16[512,128]{1,0:T(8,128)(2,1)} %hbm_ref.1), channel_id=1, source_target_pairs={{0,6},{1,7},{2,4},{3,5},{4,2},{5,3},{6,0},{7,1},{8,14},{9,15},{10,... | collective-permute-start | bytes 393224 | tf_op jit(solution)/shard_map/ppermute | solution.py:323
  8.3 0.9 %constant_dynamic-slice_fusion = bf16[768,128]{1,0:T(8,128)(2,1)S(1)} fusion(bf16[1536,128]{1,0:T(8,128)(2,1)} %refs_0_.1, s32[]{:T(128)S(6)} %select_n.11), kind=kLoop, calls=%fused_computation.1 | loop fusion | bytes 393220 | tf_op jit(solution)/shard_map/dynamic_slice | solution.py:346
  9.3 1.8 %collective-permute-done.refs_3_ = bf16[512,128]{1,0:T(8,128)(2,1)S(1)} collective-permute-done((bf16[512,128]{1,0:T(8,128)(2,1)}, bf16[512,128]{1,0:T(8,128)(2,1)S(1)}, u32[]{:S(2)}, u32[]{:S(2)}) %collective-permute-start) | collective-permute-done | bytes 131104 | tf_op jit(solution)/shard_map/ppermute | solution.py:323
  11.1 2.6 %collective-permute-start.7 = (bf16[768,128]{1,0:T(8,128)(2,1)S(1)}, bf16[768,128]{1,0:T(8,128)(2,1)S(1)}, u32[]{:S(2)}, u32[]{:S(2)}) collective-permute-start(bf16[768,128]{1,0:T(8,128)(2,1)S(1)} %constant_dynamic-slice_fusion), channel_id=1, source_target_pairs={{0,24},{8,16},{16,8},{24,0},{1,25},{9,17},{17,9},{25,1},{2,26},{10... | collective-permute-start | bytes 589832 | tf_op jit(solution)/shard_map/ppermute | solution.py:324
  15.6 6.1 %image_panel.1 = (f32[4,4,192,128]{3,2,1,0:T(8,128)S(1)}, f32[4,4,192,128]{3,2,1,0:T(8,128)S(1)}) custom-call(s32[2]{0:T(128)S(1)} %pad_add_fusion.me_ref, bf16[576,4096]{1,0:T(8,128)(2,1)} %b_hbm.3, bf16[576,6144]{1,0:T(8,128)(2,1)} %a_hbm.3, bf16[512,128]{1,0:T(8,128)(2,1)S(1)} %load.1.refs_0_, bf16[512,128]{1,0:T(8,128)(2,1)S(1)} %collective-permute-done.1.refs_1_, ...), custom_call_target="tpu_custom_call" | custom-call | flops 1 | bytes 1 | tf_op jit(solution)/shard_map/image_panel/pallas_call | solution.py:107
  22.3 1.5 %collective-permute-done.9.refs_4_ = bf16[768,128]{1,0:T(8,128)(2,1)S(1)} collective-permute-done((bf16[768,128]{1,0:T(8,128)(2,1)S(1)}, bf16[768,128]{1,0:T(8,128)(2,1)S(1)}, u32[]{:S(2)}, u32[]{:S(2)}) %collective-permute-start.9) | collective-permute-done | bytes 196640 | tf_op jit(solution)/shard_map/ppermute | solution.py:323
  24.0 6.6 %text_panel.1 = (f32[4,1,512,128]{3,2,1,0:T(8,128)S(1)}, f32[4,1,512,128]{3,2,1,0:T(8,128)S(1)}) custom-call(s32[2]{0:T(128)S(1)} %pad_add_fusion.me_ref, bf16[576,6144]{1,0:T(8,128)(2,1)} %a_hbm.3, bf16[576,4096]{1,0:T(8,128)(2,1)} %b_hbm.3, bf16[1536,128]{1,0:T(8,128)(2,1)S(1)} %copy-done, bf16[1536,128]{1,0:T(8,128)(2,1)S(1)} %collective-permute-done.8.refs_1_, ...), custom_call_target="tpu_custom_call" | custom-call | flops 1 | bytes 1 | tf_op jit(solution)/shard_map/text_panel/pallas_call | solution.py:107
  31.7 1.5 %collective-permute-start.12 = (bf16[4,192,128]{2,1,0:T(8,128)(2,1)S(1)}, bf16[4,192,128]{2,1,0:T(8,128)(2,1)S(1)}, u32[]{:S(2)}, u32[]{:S(2)}) collective-permute-start(bf16[4,192,128]{2,1,0:T(8,128)(2,1)S(1)} %get-tuple-element.43), channel_id=1, source_target_pairs={{0,2},{1,3},{2,0},{3,1},{4,6},{5,7},{6,4},{7,5},{8,10},{9,11},{10,... | collective-permute-start | bytes 589832 | tf_op jit(solution)/shard_map/ppermute | solution.py:323
  33.2 1.4 %collective-permute-start.13 = (bf16[4,192,128]{2,1,0:T(8,128)(2,1)S(1)}, bf16[4,192,128]{2,1,0:T(8,128)(2,1)S(1)}, u32[]{:S(2)}, u32[]{:S(2)}) collective-permute-start(bf16[4,192,128]{2,1,0:T(8,128)(2,1)S(1)} %get-tuple-element.44), channel_id=1, source_target_pairs={{0,4},{1,5},{2,6},{3,7},{4,0},{5,1},{6,2},{7,3},{8,12},{9,13},{10,... | collective-permute-start | bytes 589832 | tf_op jit(solution)/shard_map/ppermute | solution.py:323
  35.9 1.5 %collective-permute-start.29 = (bf16[512,128]{1,0:T(8,128)(2,1)S(1)}, bf16[512,128]{1,0:T(8,128)(2,1)S(1)}, u32[]{:S(2)}, u32[]{:S(2)}) collective-permute-start(bf16[512,128]{1,0:T(8,128)(2,1)S(1)} %bitcast.9), channel_id=1, source_target_pairs={{0,2},{1,3},{2,0},{3,1},{4,6},{5,7},{6,4},{7,5},{8,10},{9,11},{10,... | collective-permute-start | bytes 393224 | tf_op jit(solution)/shard_map/ppermute | solution.py:323
  37.4 1.4 %collective-permute-start.30 = (bf16[512,128]{1,0:T(8,128)(2,1)S(1)}, bf16[512,128]{1,0:T(8,128)(2,1)S(1)}, u32[]{:S(2)}, u32[]{:S(2)}) collective-permute-start(bf16[512,128]{1,0:T(8,128)(2,1)S(1)} %bitcast.8), channel_id=1, source_target_pairs={{0,4},{1,5},{2,6},{3,7},{4,0},{5,1},{6,2},{7,3},{8,12},{9,13},{10,... | collective-permute-start | bytes 393224 | tf_op jit(solution)/shard_map/ppermute | solution.py:323
  39.5 2.3 %collective-permute-start.31 = (bf16[512,128]{1,0:T(8,128)(2,1)S(1)}, bf16[512,128]{1,0:T(8,128)(2,1)S(1)}, u32[]{:S(2)}, u32[]{:S(2)}) collective-permute-start(bf16[512,128]{1,0:T(8,128)(2,1)S(1)} %bitcast.7), channel_id=1, source_target_pairs={{0,6},{1,7},{2,4},{3,5},{4,2},{5,3},{6,0},{7,1},{8,14},{9,15},{10,... | collective-permute-start | bytes 393224 | tf_op jit(solution)/shard_map/ppermute | solution.py:323
  41.8 3.3 %collective-permute-done.13.refs_2_ = bf16[4,192,128]{2,1,0:T(8,128)(2,1)S(1)} collective-permute-done((bf16[4,192,128]{2,1,0:T(8,128)(2,1)S(1)}, bf16[4,192,128]{2,1,0:T(8,128)(2,1)S(1)}, u32[]{:S(2)}, u32[]{:S(2)}) %collective-permute-start.13) | collective-permute-done | bytes 196640 | tf_op jit(solution)/shard_map/ppermute | solution.py:323
  45.7 1.4 %collective-permute-start.15 = (bf16[192,128]{1,0:T(8,128)(2,1)S(1)}, bf16[192,128]{1,0:T(8,128)(2,1)S(1)}, u32[]{:S(2)}, u32[]{:S(2)}) collective-permute-start(bf16[192,128]{1,0:T(8,128)(2,1)S(1)} %get-tuple-element.47), channel_id=1, source_target_pairs={{0,8},{8,0},{16,24},{24,16},{1,9},{9,1},{17,25},{25,17},{2,10},{10... | collective-permute-start | bytes 147464 | tf_op jit(solution)/shard_map/ppermute | solution.py:324
  47.1 1.8 %collective-permute-start.16 = (bf16[192,128]{1,0:T(8,128)(2,1)S(1)}, bf16[192,128]{1,0:T(8,128)(2,1)S(1)}, u32[]{:S(2)}, u32[]{:S(2)}) collective-permute-start(bf16[192,128]{1,0:T(8,128)(2,1)S(1)} %get-tuple-element.48), channel_id=1, source_target_pairs={{0,16},{8,24},{16,0},{24,8},{1,17},{9,25},{17,1},{25,9},{2,18},{10... | collective-permute-start | bytes 147464 | tf_op jit(solution)/shard_map/ppermute | solution.py:324
  48.9 1.4 %collective-permute-start.17 = (bf16[192,128]{1,0:T(8,128)(2,1)S(1)}, bf16[192,128]{1,0:T(8,128)(2,1)S(1)}, u32[]{:S(2)}, u32[]{:S(2)}) collective-permute-start(bf16[192,128]{1,0:T(8,128)(2,1)S(1)} %get-tuple-element.49), channel_id=1, source_target_pairs={{0,24},{8,16},{16,8},{24,0},{1,25},{9,17},{17,9},{25,1},{2,26},{10... | collective-permute-start | bytes 147464 | tf_op jit(solution)/shard_map/ppermute | solution.py:324
  51.2 2.2 %collective-permute-start.33 = (bf16[512,128]{1,0:T(8,128)(2,1)S(1)}, bf16[512,128]{1,0:T(8,128)(2,1)S(1)}, u32[]{:S(2)}, u32[]{:S(2)}) collective-permute-start(bf16[512,128]{1,0:T(8,128)(2,1)S(1)} %text_plane.1.refs_0_), channel_id=1, source_target_pairs={{0,16},{8,24},{16,0},{24,8},{1,17},{9,25},{17,1},{25,9},{2,18},{10... | collective-permute-start | bytes 393224 | tf_op jit(solution)/shard_map/ppermute | solution.py:324
  53.4 1.9 %collective-permute-done.17.refs_2_ = bf16[192,128]{1,0:T(8,128)(2,1)S(1)} collective-permute-done((bf16[192,128]{1,0:T(8,128)(2,1)S(1)}, bf16[192,128]{1,0:T(8,128)(2,1)S(1)}, u32[]{:S(2)}, u32[]{:S(2)}) %collective-permute-start.17) | collective-permute-done | bytes 49184 | tf_op jit(solution)/shard_map/ppermute | solution.py:324
  55.3 1.1 %collective-permute-start.18 = (bf16[192,128]{1,0:T(8,128)(2,1)S(1)}, bf16[192,128]{1,0:T(8,128)(2,1)S(1)}, u32[]{:S(2)}, u32[]{:S(2)}) collective-permute-start(bf16[192,128]{1,0:T(8,128)(2,1)S(1)} %image_depth.1.refs_0_), channel_id=1, source_target_pairs={{0,2},{1,3},{2,0},{3,1},{4,6},{5,7},{6,4},{7,5},{8,10},{9,11},{10,... | collective-permute-start | bytes 147464 | tf_op jit(solution)/shard_map/ppermute | solution.py:323
  56.5 1.4 %collective-permute-start.34 = (bf16[512,128]{1,0:T(8,128)(2,1)S(1)}, bf16[512,128]{1,0:T(8,128)(2,1)S(1)}, u32[]{:S(2)}, u32[]{:S(2)}) collective-permute-start(bf16[512,128]{1,0:T(8,128)(2,1)S(1)} %text_plane.1.refs_0_), channel_id=1, source_target_pairs={{0,24},{8,16},{16,8},{24,0},{1,25},{9,17},{17,9},{25,1},{2,26},{10... | collective-permute-start | bytes 393224 | tf_op jit(solution)/shard_map/ppermute | solution.py:324
  57.9 1.2 %collective-permute-start.19 = (bf16[192,128]{1,0:T(8,128)(2,1)S(1)}, bf16[192,128]{1,0:T(8,128)(2,1)S(1)}, u32[]{:S(2)}, u32[]{:S(2)}) collective-permute-start(bf16[192,128]{1,0:T(8,128)(2,1)S(1)} %image_depth.1.refs_0_), channel_id=1, source_target_pairs={{0,4},{1,5},{2,6},{3,7},{4,0},{5,1},{6,2},{7,3},{8,12},{9,13},{10,... | collective-permute-start | bytes 147464 | tf_op jit(solution)/shard_map/ppermute | solution.py:323
  59.5 1.7 %collective-permute-start.20 = (bf16[192,128]{1,0:T(8,128)(2,1)S(1)}, bf16[192,128]{1,0:T(8,128)(2,1)S(1)}, u32[]{:S(2)}, u32[]{:S(2)}) collective-permute-start(bf16[192,128]{1,0:T(8,128)(2,1)S(1)} %image_depth.1.refs_0_), channel_id=1, source_target_pairs={{0,6},{1,7},{2,4},{3,5},{4,2},{5,3},{6,0},{7,1},{8,14},{9,15},{10,... | collective-permute-start | bytes 147464 | tf_op jit(solution)/shard_map/ppermute | solution.py:323
  62.0 2.5 %collective-permute-done.20.refs_3_ = bf16[192,128]{1,0:T(8,128)(2,1)S(1)} collective-permute-done((bf16[192,128]{1,0:T(8,128)(2,1)S(1)}, bf16[192,128]{1,0:T(8,128)(2,1)S(1)}, u32[]{:S(2)}, u32[]{:S(2)}) %collective-permute-start.20) | collective-permute-done | bytes 49184 | tf_op jit(solution)/shard_map/ppermute | solution.py:323
  66.2 1.0 %image_gram.1 = (bf16[8,192,128]{2,1,0:T(8,128)(2,1)S(1)}, f32[72,128]{1,0:T(8,128)S(1)}) custom-call(s32[2]{0:T(128)S(1)} %pad_add_fusion.me_ref, bf16[192,128]{1,0:T(8,128)(2,1)S(1)} %image_depth.1.refs_0_, bf16[192,128]{1,0:T(8,128)(2,1)S(1)} %collective-permute-done.18.refs_1_, bf16[192,128]{1,0:T(8,128)(2,1)S(1)} %collective-permute-done.19.refs_2_, ...), custom_call_target="tpu_custom_call" | custom-call | flops 50331648 | bytes 786432 | tf_op jit(solution)/shard_map/image_gram/pallas_call | solution.py:215
  67.2 1.0 %collective-permute-start.25 = (f32[72,128]{1,0:T(8,128)S(1)}, f32[72,128]{1,0:T(8,128)S(1)}, u32[]{:S(2)}, u32[]{:S(2)}) collective-permute-start(f32[72,128]{1,0:T(8,128)S(1)} %get-tuple-element.51.refs_0_), channel_id=1, source_target_pairs={{0,8},{8,0},{16,24},{24,16},{1,9},{9,1},{17,25},{25,17},{2,10},{10... | collective-permute-start | bytes 110600 | tf_op jit(solution)/shard_map/ppermute | solution.py:324
  68.2 1.6 %collective-permute-start.26 = (f32[72,128]{1,0:T(8,128)S(1)}, f32[72,128]{1,0:T(8,128)S(1)}, u32[]{:S(2)}, u32[]{:S(2)}) collective-permute-start(f32[72,128]{1,0:T(8,128)S(1)} %get-tuple-element.51.refs_0_), channel_id=1, source_target_pairs={{0,16},{8,24},{16,0},{24,8},{1,17},{9,25},{17,1},{25,9},{2,18},{10... | collective-permute-start | bytes 110600 | tf_op jit(solution)/shard_map/ppermute | solution.py:324
  69.9 1.8 %collective-permute-start.27 = (f32[72,128]{1,0:T(8,128)S(1)}, f32[72,128]{1,0:T(8,128)S(1)}, u32[]{:S(2)}, u32[]{:S(2)}) collective-permute-start(f32[72,128]{1,0:T(8,128)S(1)} %get-tuple-element.51.refs_0_), channel_id=1, source_target_pairs={{0,24},{8,16},{16,8},{24,0},{1,25},{9,17},{17,9},{25,1},{2,26},{10... | collective-permute-start | bytes 110600 | tf_op jit(solution)/shard_map/ppermute | solution.py:324
  71.7 1.6 %collective-permute-start.36 = (f32[72,128]{1,0:T(8,128)S(1)}, f32[72,128]{1,0:T(8,128)S(1)}, u32[]{:S(2)}, u32[]{:S(2)}) collective-permute-start(f32[72,128]{1,0:T(8,128)S(1)} %text_gram_cores.1.refs_0_), channel_id=1, source_target_pairs={{0,2},{1,3},{2,0},{3,1},{4,6},{5,7},{6,4},{7,5},{8,10},{9,11},{10,... | collective-permute-start | bytes 110600 | tf_op jit(solution)/shard_map/ppermute | solution.py:323
  74.0 1.4 %collective-permute-start.38 = (f32[72,128]{1,0:T(8,128)S(1)}, f32[72,128]{1,0:T(8,128)S(1)}, u32[]{:S(2)}, u32[]{:S(2)}) collective-permute-start(f32[72,128]{1,0:T(8,128)S(1)} %text_gram_cores.1.refs_0_), channel_id=1, source_target_pairs={{0,6},{1,7},{2,4},{3,5},{4,2},{5,3},{6,0},{7,1},{8,14},{9,15},{10,... | collective-permute-start | bytes 110600 | tf_op jit(solution)/shard_map/ppermute | solution.py:323
  75.6 6.2 %image_finish.1 = f32[1536,128]{1,0:T(8,128)} custom-call(bf16[8,192,128]{2,1,0:T(8,128)(2,1)S(1)} %get-tuple-element.50.panel_ref, f32[72,128]{1,0:T(8,128)S(1)} %get-tuple-element.51.refs_0_, f32[72,128]{1,0:T(8,128)S(1)} %collective-permute-done.25.refs_1_, f32[72,128]{1,0:T(8,128)S(1)} %collective-permute-done.26.refs_2_, ...), custom_call_target="tpu_custom_call" | custom-call | flops 5000000000 | bytes 1179648 | tf_op jit(solution)/shard_map/image_finish/pallas_call | solution.py:309
  81.9 5.8 %text_finish.1 = f32[512,128]{1,0:T(8,128)} custom-call(bf16[1,512,128]{2,1,0:T(8,128)(2,1)S(1)} %get-tuple-element.62.panel_ref, f32[72,128]{1,0:T(8,128)S(1)} %text_gram_cores.1.refs_0_, f32[72,128]{1,0:T(8,128)S(1)} %collective-permute-done.36.refs_1_, f32[72,128]{1,0:T(8,128)S(1)} %collective-permute-done.37.refs_2_, ...), custom_call_target="tpu_custom_call" | custom-call | flops 5000000000 | bytes 393216 | tf_op jit(solution)/shard_map/text_finish/pallas_call | solution.py:309
  (65 shorter events, 13.3 us)
Async XLA Ops:
  0.6 21.1 %collective-permute-start.8 = (bf16[1536,128]{1,0:T(8,128)(2,1)}, bf16[1536,128]{1,0:T(8,128)(2,1)S(1)}, u32[]{:S(2)}, u32[]{:S(2)}) collective-permute-start(bf16[1536,128]{1,0:T(8,128)(2,1)} %refs_0_.1), channel_id=1, source_target_pairs={{0,8},{1,17},{2,10},{3,19},{4,12},{5,21},{6,14},{7,23},{8,0},{9,25... | collective-permute-start | bytes 1179656 | tf_op jit(solution)/shard_map/ppermute | solution.py:342
  3.7 7.4 %collective-permute-start = (bf16[512,128]{1,0:T(8,128)(2,1)}, bf16[512,128]{1,0:T(8,128)(2,1)S(1)}, u32[]{:S(2)}, u32[]{:S(2)}) collective-permute-start(bf16[512,128]{1,0:T(8,128)(2,1)} %hbm_ref.1), channel_id=1, source_target_pairs={{0,6},{1,7},{2,4},{3,5},{4,2},{5,3},{6,0},{7,1},{8,14},{9,15},{10,... | collective-permute-start | bytes 393224 | tf_op jit(solution)/shard_map/ppermute | solution.py:323
  6.2 7.5 %collective-permute-start.1 = (bf16[512,128]{1,0:T(8,128)(2,1)}, bf16[512,128]{1,0:T(8,128)(2,1)S(1)}, u32[]{:S(2)}, u32[]{:S(2)}) collective-permute-start(bf16[512,128]{1,0:T(8,128)(2,1)} %hbm_ref.1), channel_id=1, source_target_pairs={{0,2},{1,3},{2,0},{3,1},{4,6},{5,7},{6,4},{7,5},{8,10},{9,11},{10,... | collective-permute-start | bytes 393224 | tf_op jit(solution)/shard_map/ppermute | solution.py:323
  6.7 7.0 %collective-permute-start.2 = (bf16[512,128]{1,0:T(8,128)(2,1)}, bf16[512,128]{1,0:T(8,128)(2,1)S(1)}, u32[]{:S(2)}, u32[]{:S(2)}) collective-permute-start(bf16[512,128]{1,0:T(8,128)(2,1)} %hbm_ref.1), channel_id=1, source_target_pairs={{0,4},{1,5},{2,6},{3,7},{4,0},{5,1},{6,2},{7,3},{8,12},{9,13},{10,... | collective-permute-start | bytes 393224 | tf_op jit(solution)/shard_map/ppermute | solution.py:323
  7.2 7.0 %collective-permute-start.3 = (bf16[512,128]{1,0:T(8,128)(2,1)}, bf16[512,128]{1,0:T(8,128)(2,1)S(1)}, u32[]{:S(2)}, u32[]{:S(2)}) collective-permute-start(bf16[512,128]{1,0:T(8,128)(2,1)} %hbm_ref.1), channel_id=1, source_target_pairs={{0,1},{1,0},{2,3},{3,2},{4,5},{5,4},{6,7},{7,6},{8,9},{9,8},{10,11... | collective-permute-start | bytes 393224 | tf_op jit(solution)/shard_map/ppermute | solution.py:323
  11.1 10.6 %collective-permute-start.7 = (bf16[768,128]{1,0:T(8,128)(2,1)S(1)}, bf16[768,128]{1,0:T(8,128)(2,1)S(1)}, u32[]{:S(2)}, u32[]{:S(2)}) collective-permute-start(bf16[768,128]{1,0:T(8,128)(2,1)S(1)} %constant_dynamic-slice_fusion), channel_id=1, source_target_pairs={{0,24},{8,16},{16,8},{24,0},{1,25},{9,17},{17,9},{25,1},{2,26},{10... | collective-permute-start | bytes 589832 | tf_op jit(solution)/shard_map/ppermute | solution.py:324
  21.7 2.1 %collective-permute-start.10 = (bf16[1536,128]{1,0:T(8,128)(2,1)S(1)}, bf16[1536,128]{1,0:T(8,128)(2,1)S(1)}, u32[]{:S(2)}, u32[]{:S(2)}) collective-permute-start(bf16[1536,128]{1,0:T(8,128)(2,1)S(1)} %collective-permute-done.8.refs_1_), channel_id=1, source_target_pairs={{0,1},{1,0},{2,3},{3,2},{4,5},{5,4},{6,7},{7,6},{8,9},{9,8},{10,11... | collective-permute-start | bytes 1179656 | tf_op jit(solution)/shard_map/ppermute | solution.py:323
  23.8 7.2 %collective-permute-start.11 = (f32[4,4,192,128]{3,2,1,0:T(8,128)S(1)}, f32[4,4,192,128]{3,2,1,0:T(8,128)S(1)}, u32[]{:S(2)}, u32[]{:S(2)}) collective-permute-start(f32[4,4,192,128]{3,2,1,0:T(8,128)S(1)} %get-tuple-element.41), channel_id=1, source_target_pairs={{0,1},{1,0},{2,3},{3,2},{4,5},{5,4},{6,7},{7,6},{8,9},{9,8},{10,11... | collective-permute-start | bytes 4718600 | tf_op jit(solution)/shard_map/ppermute | solution.py:323
  30.5 4.7 %collective-permute-start.28 = (f32[4,1,512,128]{3,2,1,0:T(8,128)S(1)}, f32[4,1,512,128]{3,2,1,0:T(8,128)S(1)}, u32[]{:S(2)}, u32[]{:S(2)}) collective-permute-start(f32[4,1,512,128]{3,2,1,0:T(8,128)S(1)} %get-tuple-element.55), channel_id=1, source_target_pairs={{0,1},{1,0},{2,3},{3,2},{4,5},{5,4},{6,7},{7,6},{8,9},{9,8},{10,11... | collective-permute-start | bytes 3145736 | tf_op jit(solution)/shard_map/ppermute | solution.py:323
  31.7 7.8 %collective-permute-start.12 = (bf16[4,192,128]{2,1,0:T(8,128)(2,1)S(1)}, bf16[4,192,128]{2,1,0:T(8,128)(2,1)S(1)}, u32[]{:S(2)}, u32[]{:S(2)}) collective-permute-start(bf16[4,192,128]{2,1,0:T(8,128)(2,1)S(1)} %get-tuple-element.43), channel_id=1, source_target_pairs={{0,2},{1,3},{2,0},{3,1},{4,6},{5,7},{6,4},{7,5},{8,10},{9,11},{10,... | collective-permute-start | bytes 589832 | tf_op jit(solution)/shard_map/ppermute | solution.py:323
  33.2 11.8 %collective-permute-start.13 = (bf16[4,192,128]{2,1,0:T(8,128)(2,1)S(1)}, bf16[4,192,128]{2,1,0:T(8,128)(2,1)S(1)}, u32[]{:S(2)}, u32[]{:S(2)}) collective-permute-start(bf16[4,192,128]{2,1,0:T(8,128)(2,1)S(1)} %get-tuple-element.44), channel_id=1, source_target_pairs={{0,4},{1,5},{2,6},{3,7},{4,0},{5,1},{6,2},{7,3},{8,12},{9,13},{10,... | collective-permute-start | bytes 589832 | tf_op jit(solution)/shard_map/ppermute | solution.py:323
  34.6 10.4 %collective-permute-start.14 = (bf16[4,192,128]{2,1,0:T(8,128)(2,1)S(1)}, bf16[4,192,128]{2,1,0:T(8,128)(2,1)S(1)}, u32[]{:S(2)}, u32[]{:S(2)}) collective-permute-start(bf16[4,192,128]{2,1,0:T(8,128)(2,1)S(1)} %get-tuple-element.45), channel_id=1, source_target_pairs={{0,6},{1,7},{2,4},{3,5},{4,2},{5,3},{6,0},{7,1},{8,14},{9,15},{10,... | collective-permute-start | bytes 589832 | tf_op jit(solution)/shard_map/ppermute | solution.py:323
  35.9 13.0 %collective-permute-start.29 = (bf16[512,128]{1,0:T(8,128)(2,1)S(1)}, bf16[512,128]{1,0:T(8,128)(2,1)S(1)}, u32[]{:S(2)}, u32[]{:S(2)}) collective-permute-start(bf16[512,128]{1,0:T(8,128)(2,1)S(1)} %bitcast.9), channel_id=1, source_target_pairs={{0,2},{1,3},{2,0},{3,1},{4,6},{5,7},{6,4},{7,5},{8,10},{9,11},{10,... | collective-permute-start | bytes 393224 | tf_op jit(solution)/shard_map/ppermute | solution.py:323
  37.4 12.9 %collective-permute-start.30 = (bf16[512,128]{1,0:T(8,128)(2,1)S(1)}, bf16[512,128]{1,0:T(8,128)(2,1)S(1)}, u32[]{:S(2)}, u32[]{:S(2)}) collective-permute-start(bf16[512,128]{1,0:T(8,128)(2,1)S(1)} %bitcast.8), channel_id=1, source_target_pairs={{0,4},{1,5},{2,6},{3,7},{4,0},{5,1},{6,2},{7,3},{8,12},{9,13},{10,... | collective-permute-start | bytes 393224 | tf_op jit(solution)/shard_map/ppermute | solution.py:323
  39.5 10.8 %collective-permute-start.31 = (bf16[512,128]{1,0:T(8,128)(2,1)S(1)}, bf16[512,128]{1,0:T(8,128)(2,1)S(1)}, u32[]{:S(2)}, u32[]{:S(2)}) collective-permute-start(bf16[512,128]{1,0:T(8,128)(2,1)S(1)} %bitcast.7), channel_id=1, source_target_pairs={{0,6},{1,7},{2,4},{3,5},{4,2},{5,3},{6,0},{7,1},{8,14},{9,15},{10,... | collective-permute-start | bytes 393224 | tf_op jit(solution)/shard_map/ppermute | solution.py:323
  45.7 7.7 %collective-permute-start.15 = (bf16[192,128]{1,0:T(8,128)(2,1)S(1)}, bf16[192,128]{1,0:T(8,128)(2,1)S(1)}, u32[]{:S(2)}, u32[]{:S(2)}) collective-permute-start(bf16[192,128]{1,0:T(8,128)(2,1)S(1)} %get-tuple-element.47), channel_id=1, source_target_pairs={{0,8},{8,0},{16,24},{24,16},{1,9},{9,1},{17,25},{25,17},{2,10},{10... | collective-permute-start | bytes 147464 | tf_op jit(solution)/shard_map/ppermute | solution.py:324
  47.1 6.4 %collective-permute-start.16 = (bf16[192,128]{1,0:T(8,128)(2,1)S(1)}, bf16[192,128]{1,0:T(8,128)(2,1)S(1)}, u32[]{:S(2)}, u32[]{:S(2)}) collective-permute-start(bf16[192,128]{1,0:T(8,128)(2,1)S(1)} %get-tuple-element.48), channel_id=1, source_target_pairs={{0,16},{8,24},{16,0},{24,8},{1,17},{9,25},{17,1},{25,9},{2,18},{10... | collective-permute-start | bytes 147464 | tf_op jit(solution)/shard_map/ppermute | solution.py:324
  48.9 6.4 %collective-permute-start.17 = (bf16[192,128]{1,0:T(8,128)(2,1)S(1)}, bf16[192,128]{1,0:T(8,128)(2,1)S(1)}, u32[]{:S(2)}, u32[]{:S(2)}) collective-permute-start(bf16[192,128]{1,0:T(8,128)(2,1)S(1)} %get-tuple-element.49), channel_id=1, source_target_pairs={{0,24},{8,16},{16,8},{24,0},{1,25},{9,17},{17,9},{25,1},{2,26},{10... | collective-permute-start | bytes 147464 | tf_op jit(solution)/shard_map/ppermute | solution.py:324
  50.4 14.1 %collective-permute-start.32 = (bf16[512,128]{1,0:T(8,128)(2,1)S(1)}, bf16[512,128]{1,0:T(8,128)(2,1)S(1)}, u32[]{:S(2)}, u32[]{:S(2)}) collective-permute-start(bf16[512,128]{1,0:T(8,128)(2,1)S(1)} %text_plane.1.refs_0_), channel_id=1, source_target_pairs={{0,8},{8,0},{16,24},{24,16},{1,9},{9,1},{17,25},{25,17},{2,10},{10... | collective-permute-start | bytes 393224 | tf_op jit(solution)/shard_map/ppermute | solution.py:324
  51.2 13.8 %collective-permute-start.33 = (bf16[512,128]{1,0:T(8,128)(2,1)S(1)}, bf16[512,128]{1,0:T(8,128)(2,1)S(1)}, u32[]{:S(2)}, u32[]{:S(2)}) collective-permute-start(bf16[512,128]{1,0:T(8,128)(2,1)S(1)} %text_plane.1.refs_0_), channel_id=1, source_target_pairs={{0,16},{8,24},{16,0},{24,8},{1,17},{9,25},{17,1},{25,9},{2,18},{10... | collective-permute-start | bytes 393224 | tf_op jit(solution)/shard_map/ppermute | solution.py:324
  55.3 4.2 %collective-permute-start.18 = (bf16[192,128]{1,0:T(8,128)(2,1)S(1)}, bf16[192,128]{1,0:T(8,128)(2,1)S(1)}, u32[]{:S(2)}, u32[]{:S(2)}) collective-permute-start(bf16[192,128]{1,0:T(8,128)(2,1)S(1)} %image_depth.1.refs_0_), channel_id=1, source_target_pairs={{0,2},{1,3},{2,0},{3,1},{4,6},{5,7},{6,4},{7,5},{8,10},{9,11},{10,... | collective-permute-start | bytes 147464 | tf_op jit(solution)/shard_map/ppermute | solution.py:323
  56.5 8.6 %collective-permute-start.34 = (bf16[512,128]{1,0:T(8,128)(2,1)S(1)}, bf16[512,128]{1,0:T(8,128)(2,1)S(1)}, u32[]{:S(2)}, u32[]{:S(2)}) collective-permute-start(bf16[512,128]{1,0:T(8,128)(2,1)S(1)} %text_plane.1.refs_0_), channel_id=1, source_target_pairs={{0,24},{8,16},{16,8},{24,0},{1,25},{9,17},{17,9},{25,1},{2,26},{10... | collective-permute-start | bytes 393224 | tf_op jit(solution)/shard_map/ppermute | solution.py:324
  57.9 4.1 %collective-permute-start.19 = (bf16[192,128]{1,0:T(8,128)(2,1)S(1)}, bf16[192,128]{1,0:T(8,128)(2,1)S(1)}, u32[]{:S(2)}, u32[]{:S(2)}) collective-permute-start(bf16[192,128]{1,0:T(8,128)(2,1)S(1)} %image_depth.1.refs_0_), channel_id=1, source_target_pairs={{0,4},{1,5},{2,6},{3,7},{4,0},{5,1},{6,2},{7,3},{8,12},{9,13},{10,... | collective-permute-start | bytes 147464 | tf_op jit(solution)/shard_map/ppermute | solution.py:323
  59.5 5.0 %collective-permute-start.20 = (bf16[192,128]{1,0:T(8,128)(2,1)S(1)}, bf16[192,128]{1,0:T(8,128)(2,1)S(1)}, u32[]{:S(2)}, u32[]{:S(2)}) collective-permute-start(bf16[192,128]{1,0:T(8,128)(2,1)S(1)} %image_depth.1.refs_0_), channel_id=1, source_target_pairs={{0,6},{1,7},{2,4},{3,5},{4,2},{5,3},{6,0},{7,1},{8,14},{9,15},{10,... | collective-permute-start | bytes 147464 | tf_op jit(solution)/shard_map/ppermute | solution.py:323
  62.0 3.9 %collective-permute-start.21 = (bf16[192,128]{1,0:T(8,128)(2,1)S(1)}, bf16[192,128]{1,0:T(8,128)(2,1)S(1)}, u32[]{:S(2)}, u32[]{:S(2)}) collective-permute-start(bf16[192,128]{1,0:T(8,128)(2,1)S(1)} %image_depth.1.refs_0_), channel_id=1, source_target_pairs={{0,1},{1,0},{2,3},{3,2},{4,5},{5,4},{6,7},{7,6},{8,9},{9,8},{10,11... | collective-permute-start | bytes 147464 | tf_op jit(solution)/shard_map/ppermute | solution.py:323
  65.4 6.3 %collective-permute-start.35 = (f32[72,128]{1,0:T(8,128)S(1)}, f32[72,128]{1,0:T(8,128)S(1)}, u32[]{:S(2)}, u32[]{:S(2)}) collective-permute-start(f32[72,128]{1,0:T(8,128)S(1)} %get-tuple-element.63.own_ref), channel_id=1, source_target_pairs={{0,1},{1,0},{2,3},{3,2},{4,5},{5,4},{6,7},{7,6},{8,9},{9,8},{10,11... | collective-permute-start | bytes 110600 | tf_op jit(solution)/shard_map/ppermute | solution.py:323
  67.2 6.8 %collective-permute-start.25 = (f32[72,128]{1,0:T(8,128)S(1)}, f32[72,128]{1,0:T(8,128)S(1)}, u32[]{:S(2)}, u32[]{:S(2)}) collective-permute-start(f32[72,128]{1,0:T(8,128)S(1)} %get-tuple-element.51.refs_0_), channel_id=1, source_target_pairs={{0,8},{8,0},{16,24},{24,16},{1,9},{9,1},{17,25},{25,17},{2,10},{10... | collective-permute-start | bytes 110600 | tf_op jit(solution)/shard_map/ppermute | solution.py:324
  68.2 7.2 %collective-permute-start.26 = (f32[72,128]{1,0:T(8,128)S(1)}, f32[72,128]{1,0:T(8,128)S(1)}, u32[]{:S(2)}, u32[]{:S(2)}) collective-permute-start(f32[72,128]{1,0:T(8,128)S(1)} %get-tuple-element.51.refs_0_), channel_id=1, source_target_pairs={{0,16},{8,24},{16,0},{24,8},{1,17},{9,25},{17,1},{25,9},{2,18},{10... | collective-permute-start | bytes 110600 | tf_op jit(solution)/shard_map/ppermute | solution.py:324
  69.9 5.8 %collective-permute-start.27 = (f32[72,128]{1,0:T(8,128)S(1)}, f32[72,128]{1,0:T(8,128)S(1)}, u32[]{:S(2)}, u32[]{:S(2)}) collective-permute-start(f32[72,128]{1,0:T(8,128)S(1)} %get-tuple-element.51.refs_0_), channel_id=1, source_target_pairs={{0,24},{8,16},{16,8},{24,0},{1,25},{9,17},{17,9},{25,1},{2,26},{10... | collective-permute-start | bytes 110600 | tf_op jit(solution)/shard_map/ppermute | solution.py:324
  71.7 10.2 %collective-permute-start.36 = (f32[72,128]{1,0:T(8,128)S(1)}, f32[72,128]{1,0:T(8,128)S(1)}, u32[]{:S(2)}, u32[]{:S(2)}) collective-permute-start(f32[72,128]{1,0:T(8,128)S(1)} %text_gram_cores.1.refs_0_), channel_id=1, source_target_pairs={{0,2},{1,3},{2,0},{3,1},{4,6},{5,7},{6,4},{7,5},{8,10},{9,11},{10,... | collective-permute-start | bytes 110600 | tf_op jit(solution)/shard_map/ppermute | solution.py:323
  73.3 8.6 %collective-permute-start.37 = (f32[72,128]{1,0:T(8,128)S(1)}, f32[72,128]{1,0:T(8,128)S(1)}, u32[]{:S(2)}, u32[]{:S(2)}) collective-permute-start(f32[72,128]{1,0:T(8,128)S(1)} %text_gram_cores.1.refs_0_), channel_id=1, source_target_pairs={{0,4},{1,5},{2,6},{3,7},{4,0},{5,1},{6,2},{7,3},{8,12},{9,13},{10,... | collective-permute-start | bytes 110600 | tf_op jit(solution)/shard_map/ppermute | solution.py:323
  74.0 7.8 %collective-permute-start.38 = (f32[72,128]{1,0:T(8,128)S(1)}, f32[72,128]{1,0:T(8,128)S(1)}, u32[]{:S(2)}, u32[]{:S(2)}) collective-permute-start(f32[72,128]{1,0:T(8,128)S(1)} %text_gram_cores.1.refs_0_), channel_id=1, source_target_pairs={{0,6},{1,7},{2,4},{3,5},{4,2},{5,3},{6,0},{7,1},{8,14},{9,15},{10,... | collective-permute-start | bytes 110600 | tf_op jit(solution)/shard_map/ppermute | solution.py:323
  (9 other events, 20.6 us)

commit v14 on v12

--- a/solution.py
+++ b/solution.py
@@ -304,9 +304,9 @@
         high = inverse.astype(BF16)
         low = (inverse - high.astype(F32)).astype(BF16)
         panel = panel_ref[...].reshape(out_ref.shape)
-        out_ref[...] = lax.dot_general(panel, high, dims, preferred_element_type=F32) + lax.dot_general(
-            panel, low, dims, preferred_element_type=F32
-        )
+        panel = jnp.concatenate([panel, panel], axis=1)
+        both = jnp.concatenate([high, low], axis=1)
+        out_ref[...] = lax.dot_general(panel, both, dims, preferred_element_type=F32)
 
 
 def finish_call(widths, ipanel, igrams, tpanel, tgrams):

time: 87 us -> 87 us (level)
  no operation moved by 1% of the time
where the time goes in v14:
time: 87 us; the launch traced here: 86.8 us
  starting transfers between devices  42.1 us (48%)
  Pallas kernels  24.1 us (28%)
  waiting for transfers between devices  17.9 us (21%)
  local copies, waits for them, and re-layouts  1.88 us (2%)
    ppermute x28, starting transfers between devices, per_device(): lax.ppermute(x, 'col', [(i, i ^ s) for i in range(n_col)])  22.9 us
    ppermute x10, starting transfers between devices, per_device(): lax.ppermute(x, 'row', [(i, i ^ s) for i in range(n_row)])  16.1 us
    ppermute x28, waiting for transfers between devices, per_device(): lax.ppermute(x, 'col', [(i, i ^ s) for i in range(n_col)])  15.8 us
    pallas_call x2, Pallas kernels, panel_call(): pl.pallas_call(functools.partial(panel_kernel, rows, len(parts), n_in, bl...  12.7 us
    pallas_call x1, Pallas kernels, finish_call(): pl.pallas_call(functools.partial(finish_kernel, widths, len(igrams)), in_...  7.96 us
    ppermute x1, starting transfers between devices, split_swap(): return lax.ppermute(x, ('row', 'col'), pairs)  3.09 us
    ppermute x10, waiting for transfers between devices, per_device(): lax.ppermute(x, 'row', [(i, i ^ s) for i in range(n_row)])  2.11 us
    pallas_call x3, Pallas kernels, sums_call(): pl.pallas_call(functools.partial(sums_kernel, which, axis, shifts, len(te...  1.97 us
  transfers between devices with their start and end apart: 39, of which 16 were waited for; matrix products, arithmetic and copies ran while one was open for 1% of the time, Pallas kernels for 19%

profile of v14, /device:TPU:0, one launch (start us, length us, event | category | flops | bytes accessed | tf_op | source)
XLA Modules:
  0.0 86.8 jit_solution(5289747495728886009)
XLA Ops:
  0.6 3.1 %collective-permute-start.8 = (bf16[1536,128]{1,0:T(8,128)(2,1)}, bf16[1536,128]{1,0:T(8,128)(2,1)S(1)}, u32[]{:S(2)}, u32[]{:S(2)}) collective-permute-start(bf16[1536,128]{1,0:T(8,128)(2,1)} %refs_0_.1), channel_id=1, source_target_pairs={{0,8},{1,17},{2,10},{3,19},{4,12},{5,21},{6,14},{7,23},{8,0},{9,25... | collective-permute-start | bytes 1179656 | tf_op jit(solution)/shard_map/ppermute | solution.py:348
  3.7 2.4 %collective-permute-start = (bf16[512,128]{1,0:T(8,128)(2,1)}, bf16[512,128]{1,0:T(8,128)(2,1)S(1)}, u32[]{:S(2)}, u32[]{:S(2)}) collective-permute-start(bf16[512,128]{1,0:T(8,128)(2,1)} %hbm_ref.1), channel_id=1, source_target_pairs={{0,6},{1,7},{2,4},{3,5},{4,2},{5,3},{6,0},{7,1},{8,14},{9,15},{10,... | collective-permute-start | bytes 393224 | tf_op jit(solution)/shard_map/ppermute | solution.py:329
  9.3 1.8 %collective-permute-done.refs_3_ = bf16[512,128]{1,0:T(8,128)(2,1)S(1)} collective-permute-done((bf16[512,128]{1,0:T(8,128)(2,1)}, bf16[512,128]{1,0:T(8,128)(2,1)S(1)}, u32[]{:S(2)}, u32[]{:S(2)}) %collective-permute-start) | collective-permute-done | bytes 131104 | tf_op jit(solution)/shard_map/ppermute | solution.py:329
  11.1 2.6 %collective-permute-start.7 = (bf16[768,128]{1,0:T(8,128)(2,1)S(1)}, bf16[768,128]{1,0:T(8,128)(2,1)S(1)}, u32[]{:S(2)}, u32[]{:S(2)}) collective-permute-start(bf16[768,128]{1,0:T(8,128)(2,1)S(1)} %constant_dynamic-slice_fusion), channel_id=1, source_target_pairs={{0,24},{8,16},{16,8},{24,0},{1,25},{9,17},{17,9},{25,1},{2,26},{10... | collective-permute-start | bytes 589832 | tf_op jit(solution)/shard_map/ppermute | solution.py:330
  15.6 6.1 %image_panel.1 = (f32[4,4,192,128]{3,2,1,0:T(8,128)S(1)}, f32[4,4,192,128]{3,2,1,0:T(8,128)S(1)}) custom-call(s32[2]{0:T(128)S(1)} %pad_add_fusion.me_ref, bf16[576,4096]{1,0:T(8,128)(2,1)} %b_hbm.3, bf16[576,6144]{1,0:T(8,128)(2,1)} %a_hbm.3, bf16[512,128]{1,0:T(8,128)(2,1)S(1)} %load.1.refs_0_, bf16[512,128]{1,0:T(8,128)(2,1)S(1)} %collective-permute-done.1.refs_1_, ...), custom_call_target="tpu_custom_call" | custom-call | flops 1 | bytes 1 | tf_op jit(solution)/shard_map/image_panel/pallas_call | solution.py:107
  22.3 1.5 %collective-permute-done.9.refs_4_ = bf16[768,128]{1,0:T(8,128)(2,1)S(1)} collective-permute-done((bf16[768,128]{1,0:T(8,128)(2,1)S(1)}, bf16[768,128]{1,0:T(8,128)(2,1)S(1)}, u32[]{:S(2)}, u32[]{:S(2)}) %collective-permute-start.9) | collective-permute-done | bytes 196640 | tf_op jit(solution)/shard_map/ppermute | solution.py:329
  24.0 6.6 %text_panel.1 = (f32[4,1,512,128]{3,2,1,0:T(8,128)S(1)}, f32[4,1,512,128]{3,2,1,0:T(8,128)S(1)}) custom-call(s32[2]{0:T(128)S(1)} %pad_add_fusion.me_ref, bf16[576,6144]{1,0:T(8,128)(2,1)} %a_hbm.3, bf16[576,4096]{1,0:T(8,128)(2,1)} %b_hbm.3, bf16[1536,128]{1,0:T(8,128)(2,1)S(1)} %copy-done, bf16[1536,128]{1,0:T(8,128)(2,1)S(1)} %collective-permute-done.8.refs_1_, ...), custom_call_target="tpu_custom_call" | custom-call | flops 1 | bytes 1 | tf_op jit(solution)/shard_map/text_panel/pallas_call | solution.py:107
  31.7 1.5 %collective-permute-start.12 = (bf16[4,192,128]{2,1,0:T(8,128)(2,1)S(1)}, bf16[4,192,128]{2,1,0:T(8,128)(2,1)S(1)}, u32[]{:S(2)}, u32[]{:S(2)}) collective-permute-start(bf16[4,192,128]{2,1,0:T(8,128)(2,1)S(1)} %get-tuple-element.43), channel_id=1, source_target_pairs={{0,2},{1,3},{2,0},{3,1},{4,6},{5,7},{6,4},{7,5},{8,10},{9,11},{10,... | collective-permute-start | bytes 589832 | tf_op jit(solution)/shard_map/ppermute | solution.py:329
  33.2 1.4 %collective-permute-start.13 = (bf16[4,192,128]{2,1,0:T(8,128)(2,1)S(1)}, bf16[4,192,128]{2,1,0:T(8,128)(2,1)S(1)}, u32[]{:S(2)}, u32[]{:S(2)}) collective-permute-start(bf16[4,192,128]{2,1,0:T(8,128)(2,1)S(1)} %get-tuple-element.44), channel_id=1, source_target_pairs={{0,4},{1,5},{2,6},{3,7},{4,0},{5,1},{6,2},{7,3},{8,12},{9,13},{10,... | collective-permute-start | bytes 589832 | tf_op jit(solution)/shard_map/ppermute | solution.py:329
  35.9 1.5 %collective-permute-start.26 = (bf16[512,128]{1,0:T(8,128)(2,1)S(1)}, bf16[512,128]{1,0:T(8,128)(2,1)S(1)}, u32[]{:S(2)}, u32[]{:S(2)}) collective-permute-start(bf16[512,128]{1,0:T(8,128)(2,1)S(1)} %bitcast.9), channel_id=1, source_target_pairs={{0,2},{1,3},{2,0},{3,1},{4,6},{5,7},{6,4},{7,5},{8,10},{9,11},{10,... | collective-permute-start | bytes 393224 | tf_op jit(solution)/shard_map/ppermute | solution.py:329
  37.4 1.4 %collective-permute-start.27 = (bf16[512,128]{1,0:T(8,128)(2,1)S(1)}, bf16[512,128]{1,0:T(8,128)(2,1)S(1)}, u32[]{:S(2)}, u32[]{:S(2)}) collective-permute-start(bf16[512,128]{1,0:T(8,128)(2,1)S(1)} %bitcast.8), channel_id=1, source_target_pairs={{0,4},{1,5},{2,6},{3,7},{4,0},{5,1},{6,2},{7,3},{8,12},{9,13},{10,... | collective-permute-start | bytes 393224 | tf_op jit(solution)/shard_map/ppermute | solution.py:329
  39.5 2.3 %collective-permute-start.28 = (bf16[512,128]{1,0:T(8,128)(2,1)S(1)}, bf16[512,128]{1,0:T(8,128)(2,1)S(1)}, u32[]{:S(2)}, u32[]{:S(2)}) collective-permute-start(bf16[512,128]{1,0:T(8,128)(2,1)S(1)} %bitcast.7), channel_id=1, source_target_pairs={{0,6},{1,7},{2,4},{3,5},{4,2},{5,3},{6,0},{7,1},{8,14},{9,15},{10,... | collective-permute-start | bytes 393224 | tf_op jit(solution)/shard_map/ppermute | solution.py:329
  41.8 3.3 %collective-permute-done.13.refs_2_ = bf16[4,192,128]{2,1,0:T(8,128)(2,1)S(1)} collective-permute-done((bf16[4,192,128]{2,1,0:T(8,128)(2,1)S(1)}, bf16[4,192,128]{2,1,0:T(8,128)(2,1)S(1)}, u32[]{:S(2)}, u32[]{:S(2)}) %collective-permute-start.13) | collective-permute-done | bytes 196640 | tf_op jit(solution)/shard_map/ppermute | solution.py:329
  45.7 1.4 %collective-permute-start.15 = (bf16[192,128]{1,0:T(8,128)(2,1)S(1)}, bf16[192,128]{1,0:T(8,128)(2,1)S(1)}, u32[]{:S(2)}, u32[]{:S(2)}) collective-permute-start(bf16[192,128]{1,0:T(8,128)(2,1)S(1)} %get-tuple-element.47), channel_id=1, source_target_pairs={{0,8},{8,0},{16,24},{24,16},{1,9},{9,1},{17,25},{25,17},{2,10},{10... | collective-permute-start | bytes 147464 | tf_op jit(solution)/shard_map/ppermute | solution.py:330
  47.1 1.8 %collective-permute-start.16 = (bf16[192,128]{1,0:T(8,128)(2,1)S(1)}, bf16[192,128]{1,0:T(8,128)(2,1)S(1)}, u32[]{:S(2)}, u32[]{:S(2)}) collective-permute-start(bf16[192,128]{1,0:T(8,128)(2,1)S(1)} %get-tuple-element.48), channel_id=1, source_target_pairs={{0,16},{8,24},{16,0},{24,8},{1,17},{9,25},{17,1},{25,9},{2,18},{10... | collective-permute-start | bytes 147464 | tf_op jit(solution)/shard_map/ppermute | solution.py:330
  48.9 1.4 %collective-permute-start.17 = (bf16[192,128]{1,0:T(8,128)(2,1)S(1)}, bf16[192,128]{1,0:T(8,128)(2,1)S(1)}, u32[]{:S(2)}, u32[]{:S(2)}) collective-permute-start(bf16[192,128]{1,0:T(8,128)(2,1)S(1)} %get-tuple-element.49), channel_id=1, source_target_pairs={{0,24},{8,16},{16,8},{24,0},{1,25},{9,17},{17,9},{25,1},{2,26},{10... | collective-permute-start | bytes 147464 | tf_op jit(solution)/shard_map/ppermute | solution.py:330
  51.2 2.2 %collective-permute-start.30 = (bf16[512,128]{1,0:T(8,128)(2,1)S(1)}, bf16[512,128]{1,0:T(8,128)(2,1)S(1)}, u32[]{:S(2)}, u32[]{:S(2)}) collective-permute-start(bf16[512,128]{1,0:T(8,128)(2,1)S(1)} %text_plane.1.refs_0_), channel_id=1, source_target_pairs={{0,16},{8,24},{16,0},{24,8},{1,17},{9,25},{17,1},{25,9},{2,18},{10... | collective-permute-start | bytes 393224 | tf_op jit(solution)/shard_map/ppermute | solution.py:330
  53.4 1.9 %collective-permute-done.17.refs_2_ = bf16[192,128]{1,0:T(8,128)(2,1)S(1)} collective-permute-done((bf16[192,128]{1,0:T(8,128)(2,1)S(1)}, bf16[192,128]{1,0:T(8,128)(2,1)S(1)}, u32[]{:S(2)}, u32[]{:S(2)}) %collective-permute-start.17) | collective-permute-done | bytes 49184 | tf_op jit(solution)/shard_map/ppermute | solution.py:330
  55.3 1.1 %collective-permute-start.18 = (bf16[192,128]{1,0:T(8,128)(2,1)S(1)}, bf16[192,128]{1,0:T(8,128)(2,1)S(1)}, u32[]{:S(2)}, u32[]{:S(2)}) collective-permute-start(bf16[192,128]{1,0:T(8,128)(2,1)S(1)} %image_depth.1.refs_0_), channel_id=1, source_target_pairs={{0,2},{1,3},{2,0},{3,1},{4,6},{5,7},{6,4},{7,5},{8,10},{9,11},{10,... | collective-permute-start | bytes 147464 | tf_op jit(solution)/shard_map/ppermute | solution.py:329
  56.5 1.4 %collective-permute-start.31 = (bf16[512,128]{1,0:T(8,128)(2,1)S(1)}, bf16[512,128]{1,0:T(8,128)(2,1)S(1)}, u32[]{:S(2)}, u32[]{:S(2)}) collective-permute-start(bf16[512,128]{1,0:T(8,128)(2,1)S(1)} %text_plane.1.refs_0_), channel_id=1, source_target_pairs={{0,24},{8,16},{16,8},{24,0},{1,25},{9,17},{17,9},{25,1},{2,26},{10... | collective-permute-start | bytes 393224 | tf_op jit(solution)/shard_map/ppermute | solution.py:330
  57.9 1.2 %collective-permute-start.19 = (bf16[192,128]{1,0:T(8,128)(2,1)S(1)}, bf16[192,128]{1,0:T(8,128)(2,1)S(1)}, u32[]{:S(2)}, u32[]{:S(2)}) collective-permute-start(bf16[192,128]{1,0:T(8,128)(2,1)S(1)} %image_depth.1.refs_0_), channel_id=1, source_target_pairs={{0,4},{1,5},{2,6},{3,7},{4,0},{5,1},{6,2},{7,3},{8,12},{9,13},{10,... | collective-permute-start | bytes 147464 | tf_op jit(solution)/shard_map/ppermute | solution.py:329
  59.5 1.7 %collective-permute-start.20 = (bf16[192,128]{1,0:T(8,128)(2,1)S(1)}, bf16[192,128]{1,0:T(8,128)(2,1)S(1)}, u32[]{:S(2)}, u32[]{:S(2)}) collective-permute-start(bf16[192,128]{1,0:T(8,128)(2,1)S(1)} %image_depth.1.refs_0_), channel_id=1, source_target_pairs={{0,6},{1,7},{2,4},{3,5},{4,2},{5,3},{6,0},{7,1},{8,14},{9,15},{10,... | collective-permute-start | bytes 147464 | tf_op jit(solution)/shard_map/ppermute | solution.py:329
  62.0 2.5 %collective-permute-done.20.refs_3_ = bf16[192,128]{1,0:T(8,128)(2,1)S(1)} collective-permute-done((bf16[192,128]{1,0:T(8,128)(2,1)S(1)}, bf16[192,128]{1,0:T(8,128)(2,1)S(1)}, u32[]{:S(2)}, u32[]{:S(2)}) %collective-permute-start.20) | collective-permute-done | bytes 49184 | tf_op jit(solution)/shard_map/ppermute | solution.py:329
  66.2 1.0 %image_gram.1 = (bf16[8,192,128]{2,1,0:T(8,128)(2,1)S(1)}, f32[72,128]{1,0:T(8,128)S(1)}) custom-call(s32[2]{0:T(128)S(1)} %pad_add_fusion.me_ref, bf16[192,128]{1,0:T(8,128)(2,1)S(1)} %image_depth.1.refs_0_, bf16[192,128]{1,0:T(8,128)(2,1)S(1)} %collective-permute-done.18.refs_1_, bf16[192,128]{1,0:T(8,128)(2,1)S(1)} %collective-permute-done.19.refs_2_, ...), custom_call_target="tpu_custom_call" | custom-call | flops 50331648 | bytes 786432 | tf_op jit(solution)/shard_map/image_gram/pallas_call | solution.py:215
  67.2 1.0 %collective-permute-start.32 = (f32[72,128]{1,0:T(8,128)S(1)}, f32[72,128]{1,0:T(8,128)S(1)}, u32[]{:S(2)}, u32[]{:S(2)}) collective-permute-start(f32[72,128]{1,0:T(8,128)S(1)} %get-tuple-element.62.refs_0_), channel_id=1, source_target_pairs={{0,8},{8,0},{16,24},{24,16},{1,9},{9,1},{17,25},{25,17},{2,10},{10... | collective-permute-start | bytes 110600 | tf_op jit(solution)/shard_map/ppermute | solution.py:330
  68.2 1.6 %collective-permute-start.33 = (f32[72,128]{1,0:T(8,128)S(1)}, f32[72,128]{1,0:T(8,128)S(1)}, u32[]{:S(2)}, u32[]{:S(2)}) collective-permute-start(f32[72,128]{1,0:T(8,128)S(1)} %get-tuple-element.62.refs_0_), channel_id=1, source_target_pairs={{0,16},{8,24},{16,0},{24,8},{1,17},{9,25},{17,1},{25,9},{2,18},{10... | collective-permute-start | bytes 110600 | tf_op jit(solution)/shard_map/ppermute | solution.py:330
  69.9 1.8 %collective-permute-start.34 = (f32[72,128]{1,0:T(8,128)S(1)}, f32[72,128]{1,0:T(8,128)S(1)}, u32[]{:S(2)}, u32[]{:S(2)}) collective-permute-start(f32[72,128]{1,0:T(8,128)S(1)} %get-tuple-element.62.refs_0_), channel_id=1, source_target_pairs={{0,24},{8,16},{16,8},{24,0},{1,25},{9,17},{17,9},{25,1},{2,26},{10... | collective-permute-start | bytes 110600 | tf_op jit(solution)/shard_map/ppermute | solution.py:330
  71.7 1.6 %collective-permute-start.36 = (f32[72,128]{1,0:T(8,128)S(1)}, f32[72,128]{1,0:T(8,128)S(1)}, u32[]{:S(2)}, u32[]{:S(2)}) collective-permute-start(f32[72,128]{1,0:T(8,128)S(1)} %text_gram_cores.1.refs_4_), channel_id=1, source_target_pairs={{0,2},{1,3},{2,0},{3,1},{4,6},{5,7},{6,4},{7,5},{8,10},{9,11},{10,... | collective-permute-start | bytes 110600 | tf_op jit(solution)/shard_map/ppermute | solution.py:329
  74.0 1.4 %collective-permute-start.38 = (f32[72,128]{1,0:T(8,128)S(1)}, f32[72,128]{1,0:T(8,128)S(1)}, u32[]{:S(2)}, u32[]{:S(2)}) collective-permute-start(f32[72,128]{1,0:T(8,128)S(1)} %text_gram_cores.1.refs_4_), channel_id=1, source_target_pairs={{0,6},{1,7},{2,4},{3,5},{4,2},{5,3},{6,0},{7,1},{8,14},{9,15},{10,... | collective-permute-start | bytes 110600 | tf_op jit(solution)/shard_map/ppermute | solution.py:329
  75.7 1.7 %collective-permute-done.37.refs_6_ = f32[72,128]{1,0:T(8,128)S(1)} collective-permute-done((f32[72,128]{1,0:T(8,128)S(1)}, f32[72,128]{1,0:T(8,128)S(1)}, u32[]{:S(2)}, u32[]{:S(2)}) %collective-permute-start.37) | collective-permute-done | bytes 36896 | tf_op jit(solution)/shard_map/ppermute | solution.py:329
  77.4 1.5 %collective-permute-done.38.refs_7_ = f32[72,128]{1,0:T(8,128)S(1)} collective-permute-done((f32[72,128]{1,0:T(8,128)S(1)}, f32[72,128]{1,0:T(8,128)S(1)}, u32[]{:S(2)}, u32[]{:S(2)}) %collective-permute-start.38) | collective-permute-done | bytes 36896 | tf_op jit(solution)/shard_map/ppermute | solution.py:329
  78.9 8.0 %finish.1 = (f32[1536,128]{1,0:T(8,128)}, f32[512,128]{1,0:T(8,128)}) custom-call(bf16[8,192,128]{2,1,0:T(8,128)(2,1)S(1)} %get-tuple-element.50.ipanel, bf16[1,512,128]{2,1,0:T(8,128)(2,1)S(1)} %get-tuple-element.61.tpanel, f32[72,128]{1,0:T(8,128)S(1)} %get-tuple-element.62.refs_0_, f32[72,128]{1,0:T(8,128)S(1)} %collective-permute-done.32.refs_1_, ...), custom_call_target="tpu_custom_call" | custom-call | flops 10000000000 | bytes 1179648 | tf_op jit(solution)/shard_map/finish/pallas_call | solution.py:315
  (64 shorter events, 14.3 us)
Async XLA Ops:
  0.6 21.1 %collective-permute-start.8 = (bf16[1536,128]{1,0:T(8,128)(2,1)}, bf16[1536,128]{1,0:T(8,128)(2,1)S(1)}, u32[]{:S(2)}, u32[]{:S(2)}) collective-permute-start(bf16[1536,128]{1,0:T(8,128)(2,1)} %refs_0_.1), channel_id=1, source_target_pairs={{0,8},{1,17},{2,10},{3,19},{4,12},{5,21},{6,14},{7,23},{8,0},{9,25... | collective-permute-start | bytes 1179656 | tf_op jit(solution)/shard_map/ppermute | solution.py:348
  3.7 7.4 %collective-permute-start = (bf16[512,128]{1,0:T(8,128)(2,1)}, bf16[512,128]{1,0:T(8,128)(2,1)S(1)}, u32[]{:S(2)}, u32[]{:S(2)}) collective-permute-start(bf16[512,128]{1,0:T(8,128)(2,1)} %hbm_ref.1), channel_id=1, source_target_pairs={{0,6},{1,7},{2,4},{3,5},{4,2},{5,3},{6,0},{7,1},{8,14},{9,15},{10,... | collective-permute-start | bytes 393224 | tf_op jit(solution)/shard_map/ppermute | solution.py:329
  6.2 7.5 %collective-permute-start.1 = (bf16[512,128]{1,0:T(8,128)(2,1)}, bf16[512,128]{1,0:T(8,128)(2,1)S(1)}, u32[]{:S(2)}, u32[]{:S(2)}) collective-permute-start(bf16[512,128]{1,0:T(8,128)(2,1)} %hbm_ref.1), channel_id=1, source_target_pairs={{0,2},{1,3},{2,0},{3,1},{4,6},{5,7},{6,4},{7,5},{8,10},{9,11},{10,... | collective-permute-start | bytes 393224 | tf_op jit(solution)/shard_map/ppermute | solution.py:329
  6.7 7.0 %collective-permute-start.2 = (bf16[512,128]{1,0:T(8,128)(2,1)}, bf16[512,128]{1,0:T(8,128)(2,1)S(1)}, u32[]{:S(2)}, u32[]{:S(2)}) collective-permute-start(bf16[512,128]{1,0:T(8,128)(2,1)} %hbm_ref.1), channel_id=1, source_target_pairs={{0,4},{1,5},{2,6},{3,7},{4,0},{5,1},{6,2},{7,3},{8,12},{9,13},{10,... | collective-permute-start | bytes 393224 | tf_op jit(solution)/shard_map/ppermute | solution.py:329
  7.2 7.0 %collective-permute-start.3 = (bf16[512,128]{1,0:T(8,128)(2,1)}, bf16[512,128]{1,0:T(8,128)(2,1)S(1)}, u32[]{:S(2)}, u32[]{:S(2)}) collective-permute-start(bf16[512,128]{1,0:T(8,128)(2,1)} %hbm_ref.1), channel_id=1, source_target_pairs={{0,1},{1,0},{2,3},{3,2},{4,5},{5,4},{6,7},{7,6},{8,9},{9,8},{10,11... | collective-permute-start | bytes 393224 | tf_op jit(solution)/shard_map/ppermute | solution.py:329
  11.1 10.6 %collective-permute-start.7 = (bf16[768,128]{1,0:T(8,128)(2,1)S(1)}, bf16[768,128]{1,0:T(8,128)(2,1)S(1)}, u32[]{:S(2)}, u32[]{:S(2)}) collective-permute-start(bf16[768,128]{1,0:T(8,128)(2,1)S(1)} %constant_dynamic-slice_fusion), channel_id=1, source_target_pairs={{0,24},{8,16},{16,8},{24,0},{1,25},{9,17},{17,9},{25,1},{2,26},{10... | collective-permute-start | bytes 589832 | tf_op jit(solution)/shard_map/ppermute | solution.py:330
  21.7 2.1 %collective-permute-start.10 = (bf16[1536,128]{1,0:T(8,128)(2,1)S(1)}, bf16[1536,128]{1,0:T(8,128)(2,1)S(1)}, u32[]{:S(2)}, u32[]{:S(2)}) collective-permute-start(bf16[1536,128]{1,0:T(8,128)(2,1)S(1)} %collective-permute-done.8.refs_1_), channel_id=1, source_target_pairs={{0,1},{1,0},{2,3},{3,2},{4,5},{5,4},{6,7},{7,6},{8,9},{9,8},{10,11... | collective-permute-start | bytes 1179656 | tf_op jit(solution)/shard_map/ppermute | solution.py:329
  23.8 7.2 %collective-permute-start.11 = (f32[4,4,192,128]{3,2,1,0:T(8,128)S(1)}, f32[4,4,192,128]{3,2,1,0:T(8,128)S(1)}, u32[]{:S(2)}, u32[]{:S(2)}) collective-permute-start(f32[4,4,192,128]{3,2,1,0:T(8,128)S(1)} %get-tuple-element.41), channel_id=1, source_target_pairs={{0,1},{1,0},{2,3},{3,2},{4,5},{5,4},{6,7},{7,6},{8,9},{9,8},{10,11... | collective-permute-start | bytes 4718600 | tf_op jit(solution)/shard_map/ppermute | solution.py:329
  30.5 4.7 %collective-permute-start.25 = (f32[4,1,512,128]{3,2,1,0:T(8,128)S(1)}, f32[4,1,512,128]{3,2,1,0:T(8,128)S(1)}, u32[]{:S(2)}, u32[]{:S(2)}) collective-permute-start(f32[4,1,512,128]{3,2,1,0:T(8,128)S(1)} %get-tuple-element.54), channel_id=1, source_target_pairs={{0,1},{1,0},{2,3},{3,2},{4,5},{5,4},{6,7},{7,6},{8,9},{9,8},{10,11... | collective-permute-start | bytes 3145736 | tf_op jit(solution)/shard_map/ppermute | solution.py:329
  31.7 7.8 %collective-permute-start.12 = (bf16[4,192,128]{2,1,0:T(8,128)(2,1)S(1)}, bf16[4,192,128]{2,1,0:T(8,128)(2,1)S(1)}, u32[]{:S(2)}, u32[]{:S(2)}) collective-permute-start(bf16[4,192,128]{2,1,0:T(8,128)(2,1)S(1)} %get-tuple-element.43), channel_id=1, source_target_pairs={{0,2},{1,3},{2,0},{3,1},{4,6},{5,7},{6,4},{7,5},{8,10},{9,11},{10,... | collective-permute-start | bytes 589832 | tf_op jit(solution)/shard_map/ppermute | solution.py:329
  33.2 11.8 %collective-permute-start.13 = (bf16[4,192,128]{2,1,0:T(8,128)(2,1)S(1)}, bf16[4,192,128]{2,1,0:T(8,128)(2,1)S(1)}, u32[]{:S(2)}, u32[]{:S(2)}) collective-permute-start(bf16[4,192,128]{2,1,0:T(8,128)(2,1)S(1)} %get-tuple-element.44), channel_id=1, source_target_pairs={{0,4},{1,5},{2,6},{3,7},{4,0},{5,1},{6,2},{7,3},{8,12},{9,13},{10,... | collective-permute-start | bytes 589832 | tf_op jit(solution)/shard_map/ppermute | solution.py:329
  34.6 10.4 %collective-permute-start.14 = (bf16[4,192,128]{2,1,0:T(8,128)(2,1)S(1)}, bf16[4,192,128]{2,1,0:T(8,128)(2,1)S(1)}, u32[]{:S(2)}, u32[]{:S(2)}) collective-permute-start(bf16[4,192,128]{2,1,0:T(8,128)(2,1)S(1)} %get-tuple-element.45), channel_id=1, source_target_pairs={{0,6},{1,7},{2,4},{3,5},{4,2},{5,3},{6,0},{7,1},{8,14},{9,15},{10,... | collective-permute-start | bytes 589832 | tf_op jit(solution)/shard_map/ppermute | solution.py:329
  35.9 13.0 %collective-permute-start.26 = (bf16[512,128]{1,0:T(8,128)(2,1)S(1)}, bf16[512,128]{1,0:T(8,128)(2,1)S(1)}, u32[]{:S(2)}, u32[]{:S(2)}) collective-permute-start(bf16[512,128]{1,0:T(8,128)(2,1)S(1)} %bitcast.9), channel_id=1, source_target_pairs={{0,2},{1,3},{2,0},{3,1},{4,6},{5,7},{6,4},{7,5},{8,10},{9,11},{10,... | collective-permute-start | bytes 393224 | tf_op jit(solution)/shard_map/ppermute | solution.py:329
  37.4 12.9 %collective-permute-start.27 = (bf16[512,128]{1,0:T(8,128)(2,1)S(1)}, bf16[512,128]{1,0:T(8,128)(2,1)S(1)}, u32[]{:S(2)}, u32[]{:S(2)}) collective-permute-start(bf16[512,128]{1,0:T(8,128)(2,1)S(1)} %bitcast.8), channel_id=1, source_target_pairs={{0,4},{1,5},{2,6},{3,7},{4,0},{5,1},{6,2},{7,3},{8,12},{9,13},{10,... | collective-permute-start | bytes 393224 | tf_op jit(solution)/shard_map/ppermute | solution.py:329
  39.5 10.8 %collective-permute-start.28 = (bf16[512,128]{1,0:T(8,128)(2,1)S(1)}, bf16[512,128]{1,0:T(8,128)(2,1)S(1)}, u32[]{:S(2)}, u32[]{:S(2)}) collective-permute-start(bf16[512,128]{1,0:T(8,128)(2,1)S(1)} %bitcast.7), channel_id=1, source_target_pairs={{0,6},{1,7},{2,4},{3,5},{4,2},{5,3},{6,0},{7,1},{8,14},{9,15},{10,... | collective-permute-start | bytes 393224 | tf_op jit(solution)/shard_map/ppermute | solution.py:329
  45.7 7.7 %collective-permute-start.15 = (bf16[192,128]{1,0:T(8,128)(2,1)S(1)}, bf16[192,128]{1,0:T(8,128)(2,1)S(1)}, u32[]{:S(2)}, u32[]{:S(2)}) collective-permute-start(bf16[192,128]{1,0:T(8,128)(2,1)S(1)} %get-tuple-element.47), channel_id=1, source_target_pairs={{0,8},{8,0},{16,24},{24,16},{1,9},{9,1},{17,25},{25,17},{2,10},{10... | collective-permute-start | bytes 147464 | tf_op jit(solution)/shard_map/ppermute | solution.py:330
  47.1 6.4 %collective-permute-start.16 = (bf16[192,128]{1,0:T(8,128)(2,1)S(1)}, bf16[192,128]{1,0:T(8,128)(2,1)S(1)}, u32[]{:S(2)}, u32[]{:S(2)}) collective-permute-start(bf16[192,128]{1,0:T(8,128)(2,1)S(1)} %get-tuple-element.48), channel_id=1, source_target_pairs={{0,16},{8,24},{16,0},{24,8},{1,17},{9,25},{17,1},{25,9},{2,18},{10... | collective-permute-start | bytes 147464 | tf_op jit(solution)/shard_map/ppermute | solution.py:330
  48.9 6.4 %collective-permute-start.17 = (bf16[192,128]{1,0:T(8,128)(2,1)S(1)}, bf16[192,128]{1,0:T(8,128)(2,1)S(1)}, u32[]{:S(2)}, u32[]{:S(2)}) collective-permute-start(bf16[192,128]{1,0:T(8,128)(2,1)S(1)} %get-tuple-element.49), channel_id=1, source_target_pairs={{0,24},{8,16},{16,8},{24,0},{1,25},{9,17},{17,9},{25,1},{2,26},{10... | collective-permute-start | bytes 147464 | tf_op jit(solution)/shard_map/ppermute | solution.py:330
  50.4 14.1 %collective-permute-start.29 = (bf16[512,128]{1,0:T(8,128)(2,1)S(1)}, bf16[512,128]{1,0:T(8,128)(2,1)S(1)}, u32[]{:S(2)}, u32[]{:S(2)}) collective-permute-start(bf16[512,128]{1,0:T(8,128)(2,1)S(1)} %text_plane.1.refs_0_), channel_id=1, source_target_pairs={{0,8},{8,0},{16,24},{24,16},{1,9},{9,1},{17,25},{25,17},{2,10},{10... | collective-permute-start | bytes 393224 | tf_op jit(solution)/shard_map/ppermute | solution.py:330
  51.2 13.8 %collective-permute-start.30 = (bf16[512,128]{1,0:T(8,128)(2,1)S(1)}, bf16[512,128]{1,0:T(8,128)(2,1)S(1)}, u32[]{:S(2)}, u32[]{:S(2)}) collective-permute-start(bf16[512,128]{1,0:T(8,128)(2,1)S(1)} %text_plane.1.refs_0_), channel_id=1, source_target_pairs={{0,16},{8,24},{16,0},{24,8},{1,17},{9,25},{17,1},{25,9},{2,18},{10... | collective-permute-start | bytes 393224 | tf_op jit(solution)/shard_map/ppermute | solution.py:330
  55.3 4.2 %collective-permute-start.18 = (bf16[192,128]{1,0:T(8,128)(2,1)S(1)}, bf16[192,128]{1,0:T(8,128)(2,1)S(1)}, u32[]{:S(2)}, u32[]{:S(2)}) collective-permute-start(bf16[192,128]{1,0:T(8,128)(2,1)S(1)} %image_depth.1.refs_0_), channel_id=1, source_target_pairs={{0,2},{1,3},{2,0},{3,1},{4,6},{5,7},{6,4},{7,5},{8,10},{9,11},{10,... | collective-permute-start | bytes 147464 | tf_op jit(solution)/shard_map/ppermute | solution.py:329
  56.5 8.6 %collective-permute-start.31 = (bf16[512,128]{1,0:T(8,128)(2,1)S(1)}, bf16[512,128]{1,0:T(8,128)(2,1)S(1)}, u32[]{:S(2)}, u32[]{:S(2)}) collective-permute-start(bf16[512,128]{1,0:T(8,128)(2,1)S(1)} %text_plane.1.refs_0_), channel_id=1, source_target_pairs={{0,24},{8,16},{16,8},{24,0},{1,25},{9,17},{17,9},{25,1},{2,26},{10... | collective-permute-start | bytes 393224 | tf_op jit(solution)/shard_map/ppermute | solution.py:330
  57.9 4.1 %collective-permute-start.19 = (bf16[192,128]{1,0:T(8,128)(2,1)S(1)}, bf16[192,128]{1,0:T(8,128)(2,1)S(1)}, u32[]{:S(2)}, u32[]{:S(2)}) collective-permute-start(bf16[192,128]{1,0:T(8,128)(2,1)S(1)} %image_depth.1.refs_0_), channel_id=1, source_target_pairs={{0,4},{1,5},{2,6},{3,7},{4,0},{5,1},{6,2},{7,3},{8,12},{9,13},{10,... | collective-permute-start | bytes 147464 | tf_op jit(solution)/shard_map/ppermute | solution.py:329
  59.5 5.0 %collective-permute-start.20 = (bf16[192,128]{1,0:T(8,128)(2,1)S(1)}, bf16[192,128]{1,0:T(8,128)(2,1)S(1)}, u32[]{:S(2)}, u32[]{:S(2)}) collective-permute-start(bf16[192,128]{1,0:T(8,128)(2,1)S(1)} %image_depth.1.refs_0_), channel_id=1, source_target_pairs={{0,6},{1,7},{2,4},{3,5},{4,2},{5,3},{6,0},{7,1},{8,14},{9,15},{10,... | collective-permute-start | bytes 147464 | tf_op jit(solution)/shard_map/ppermute | solution.py:329
  62.0 3.9 %collective-permute-start.21 = (bf16[192,128]{1,0:T(8,128)(2,1)S(1)}, bf16[192,128]{1,0:T(8,128)(2,1)S(1)}, u32[]{:S(2)}, u32[]{:S(2)}) collective-permute-start(bf16[192,128]{1,0:T(8,128)(2,1)S(1)} %image_depth.1.refs_0_), channel_id=1, source_target_pairs={{0,1},{1,0},{2,3},{3,2},{4,5},{5,4},{6,7},{7,6},{8,9},{9,8},{10,11... | collective-permute-start | bytes 147464 | tf_op jit(solution)/shard_map/ppermute | solution.py:329
  65.4 6.3 %collective-permute-start.35 = (f32[72,128]{1,0:T(8,128)S(1)}, f32[72,128]{1,0:T(8,128)S(1)}, u32[]{:S(2)}, u32[]{:S(2)}) collective-permute-start(f32[72,128]{1,0:T(8,128)S(1)} %get-tuple-element.63.own_ref), channel_id=1, source_target_pairs={{0,1},{1,0},{2,3},{3,2},{4,5},{5,4},{6,7},{7,6},{8,9},{9,8},{10,11... | collective-permute-start | bytes 110600 | tf_op jit(solution)/shard_map/ppermute | solution.py:329
  67.2 6.8 %collective-permute-start.32 = (f32[72,128]{1,0:T(8,128)S(1)}, f32[72,128]{1,0:T(8,128)S(1)}, u32[]{:S(2)}, u32[]{:S(2)}) collective-permute-start(f32[72,128]{1,0:T(8,128)S(1)} %get-tuple-element.62.refs_0_), channel_id=1, source_target_pairs={{0,8},{8,0},{16,24},{24,16},{1,9},{9,1},{17,25},{25,17},{2,10},{10... | collective-permute-start | bytes 110600 | tf_op jit(solution)/shard_map/ppermute | solution.py:330
  68.2 7.2 %collective-permute-start.33 = (f32[72,128]{1,0:T(8,128)S(1)}, f32[72,128]{1,0:T(8,128)S(1)}, u32[]{:S(2)}, u32[]{:S(2)}) collective-permute-start(f32[72,128]{1,0:T(8,128)S(1)} %get-tuple-element.62.refs_0_), channel_id=1, source_target_pairs={{0,16},{8,24},{16,0},{24,8},{1,17},{9,25},{17,1},{25,9},{2,18},{10... | collective-permute-start | bytes 110600 | tf_op jit(solution)/shard_map/ppermute | solution.py:330
  69.9 5.8 %collective-permute-start.34 = (f32[72,128]{1,0:T(8,128)S(1)}, f32[72,128]{1,0:T(8,128)S(1)}, u32[]{:S(2)}, u32[]{:S(2)}) collective-permute-start(f32[72,128]{1,0:T(8,128)S(1)} %get-tuple-element.62.refs_0_), channel_id=1, source_target_pairs={{0,24},{8,16},{16,8},{24,0},{1,25},{9,17},{17,9},{25,1},{2,26},{10... | collective-permute-start | bytes 110600 | tf_op jit(solution)/shard_map/ppermute | solution.py:330
  71.7 4.0 %collective-permute-start.36 = (f32[72,128]{1,0:T(8,128)S(1)}, f32[72,128]{1,0:T(8,128)S(1)}, u32[]{:S(2)}, u32[]{:S(2)}) collective-permute-start(f32[72,128]{1,0:T(8,128)S(1)} %text_gram_cores.1.refs_4_), channel_id=1, source_target_pairs={{0,2},{1,3},{2,0},{3,1},{4,6},{5,7},{6,4},{7,5},{8,10},{9,11},{10,... | collective-permute-start | bytes 110600 | tf_op jit(solution)/shard_map/ppermute | solution.py:329
  73.3 4.1 %collective-permute-start.37 = (f32[72,128]{1,0:T(8,128)S(1)}, f32[72,128]{1,0:T(8,128)S(1)}, u32[]{:S(2)}, u32[]{:S(2)}) collective-permute-start(f32[72,128]{1,0:T(8,128)S(1)} %text_gram_cores.1.refs_4_), channel_id=1, source_target_pairs={{0,4},{1,5},{2,6},{3,7},{4,0},{5,1},{6,2},{7,3},{8,12},{9,13},{10,... | collective-permute-start | bytes 110600 | tf_op jit(solution)/shard_map/ppermute | solution.py:329
  74.0 4.9 %collective-permute-start.38 = (f32[72,128]{1,0:T(8,128)S(1)}, f32[72,128]{1,0:T(8,128)S(1)}, u32[]{:S(2)}, u32[]{:S(2)}) collective-permute-start(f32[72,128]{1,0:T(8,128)S(1)} %text_gram_cores.1.refs_4_), channel_id=1, source_target_pairs={{0,6},{1,7},{2,4},{3,5},{4,2},{5,3},{6,0},{7,1},{8,14},{9,15},{10,... | collective-permute-start | bytes 110600 | tf_op jit(solution)/shard_map/ppermute | solution.py:329
  (9 other events, 20.6 us)
